TPU v7x, 32 devices: a whole 2x2x4 slice. The times are simulated.
32 devices in a mesh: domain: 8 (over y, x, core), band: 4 (over z).
Axes of the slice: x: 2, y: 2, z: 4, core: 2. Of those that a mesh axis runs over, the one named last changes fastest.
Arguments:
- states_block: bfloat16 [27648, 512], P('domain', 'band')
- cell_matrix: bfloat16 [343, 343], replicated, as said below
- cell_scale: float32 [128], P('domain'), may hold values from 0.5 to 2
- potential: float32 [27648], P('domain'), may hold values from -1 to 1
- connectivity: int32 [128, 343], P('domain'), may hold values from 0 to 3743, as said below
- boundary_nodes: int32 [2304], P('domain'), may hold values from 0 to 3455, as said below
Outputs:
- orthonormal_block: float32 [27648, 512], P('domain', 'band')
Inputs may be any that keep to these rules, and one draw needn't show every extreme that they name: `cell_matrix`: symmetric. `connectivity`: block d names rows of subdomain d's extended array: values under 3456 are its own nodes, 3456 + p the p-th entry of block d + 1 (cyclically) of boundary_nodes; only the last 8 cells of a block name values of 3456 or more; every own node of a block is named by some cell. `boundary_nodes`: each block holds 288 distinct nodes of its subdomain.
All inputs are finite; a program needn't handle non-finite values.
Results may differ from a plain program's by a relative error of at most 0.0057.
Values may be sent and summed in bfloat16 or wider, within the bound.
No kernel may reach another device: no remote copies, remote signals or barrier semaphores. Data moves between devices by JAX's collectives and lax.ppermute only.
A program may use at most 64 MiB of HBM per device.

v0:
```python
import jax
import jax.numpy as jnp
from jax import lax
from jax.sharding import PartitionSpec as P

CENTER = 1.5
HALF_WIDTH = 1.25


def passed_along(value, axis, steps):
    count = lax.axis_size(axis)
    pairs = [(source, (source + steps) % count) for source in range(count)]
    return lax.ppermute(value, axis, pairs)


def cell_sum(source, links, scales, cell_matrix, segments):
    picked = source[links]
    products = jnp.einsum("mn,cns->cms", cell_matrix, picked, preferred_element_type=jnp.float32)
    products = products * scales[:, None, None]
    return jax.ops.segment_sum(
        products.reshape(-1, products.shape[-1]), links.reshape(-1), num_segments=segments
    )


def apply_operator(
    rounded, widened, cell_matrix, cell_scale, potential, connectivity, boundary_nodes
):
    owned = rounded.shape[0]
    plane = boundary_nodes.shape[0]
    ghost_rows = passed_along(rounded[boundary_nodes], "domain", -1)
    extended = jnp.concatenate([rounded, ghost_rows], axis=0)
    assembled = cell_sum(extended, connectivity, cell_scale, cell_matrix, owned + plane)
    own_sums = assembled[:owned]
    returned = passed_along(assembled[owned:], "domain", 1)
    own_sums = own_sums.at[boundary_nodes].add(returned)
    return own_sums + potential[:, None] * widened


def shards(states_block, cell_matrix, cell_scale, potential, connectivity, boundary_nodes):
    previous = states_block.astype(jnp.float32)
    image = apply_operator(
        states_block, previous, cell_matrix, cell_scale, potential, connectivity, boundary_nodes
    )
    current = (image - CENTER * previous) / HALF_WIDTH
    image = apply_operator(
        current.astype(jnp.bfloat16),
        current,
        cell_matrix,
        cell_scale,
        potential,
        connectivity,
        boundary_nodes,
    )
    following = 2.0 * (image - CENTER * current) / HALF_WIDTH - previous
    previous, current = (current, following)
    node_total = current.shape[0] * lax.axis_size("domain")
    contract_rows = (((0,), (0,)), ((), ()))
    node_rows = lax.all_to_all(current, "band", split_axis=0, concat_axis=1, tiled=True)
    partial_gram = lax.dot_general(
        node_rows,
        node_rows,
        contract_rows,
        precision=lax.Precision.HIGHEST,
        preferred_element_type=jnp.float32,
    )
    gram = lax.psum(partial_gram, ("domain", "band")) / node_total
    lower = jnp.linalg.cholesky(gram)
    solved = jax.scipy.linalg.solve_triangular(lower, node_rows.T, lower=True).T
    result = lax.all_to_all(solved, "band", split_axis=1, concat_axis=0, tiled=True)
    return result


def solution(mesh):
    return jax.shard_map(
        shards,
        mesh=mesh,
        in_specs=(
            P("domain", "band"),
            P(),
            P("domain"),
            P("domain"),
            P("domain", None),
            P("domain"),
        ),
        out_specs=P("domain", "band"),
        check_vma=False,
    )
```

profile of v0, /device:TPU:26, one launch (start us, length us, event | category | flops | bytes accessed | tf_op | source)
XLA Modules:
  0.0 527.1 jit_solution(17498743524054363159)
XLA Ops:
  7.3 2.4 gather_fusion
  12.9 10.9 %gather_fusion.1 = bf16[5488,128]{1,0:T(8,128)(2,1)S(1)} fusion(bf16[3744,128]{1,0:T(8,128)(2,1)S(1)} %pad_maximum_fusion, s32[6144]{0:T(1024)S(1)} %pad_clamp_fusion), kind=kCustom, calls=%fused_computation.1 | custom fusion | bytes 2831808 | tf_op jit(solution)/shard_map/gather | solution.py:17
  25.2 2.2 multiply_bitcast_fusion.1
  29.2 32.3 %scatter_custom_fusion = f32[3744,128]{1,0:T(8,128)} fusion(s32[5488]{0:T(1024)S(1)} %reshape.124, f32[5488,128]{1,0:T(8,128)} %reshape.110, f32[]{:T(128)} %constant.152.clone.1), kind=kCustom, calls=%fused_computation.43 | custom fusion | flops 702464 | bytes 1917440 | tf_op jit(solution)/shard_map/scatter-add | solution.py:20
  62.4 2.6 collective-permute-start.1
  67.1 2.7 scatter_fusion
  71.0 2.4 gather_fusion.2
  77.1 12.2 %gather_fusion.3 = bf16[5488,128]{1,0:T(8,128)(2,1)} fusion(bf16[3744,128]{1,0:T(8,128)(2,1)S(1)} %pad_maximum_fusion.1, s32[6144]{0:T(1024)S(1)} %pad_clamp_fusion), kind=kCustom, calls=%fused_computation.3 | custom fusion | bytes 2831808 | tf_op jit(solution)/shard_map/gather | solution.py:17
  91.0 2.5 multiply_bitcast_fusion
  93.4 3.0 reshape.126
  96.5 32.3 %scatter_custom_fusion.2 = f32[3744,128]{1,0:T(8,128)} fusion(s32[5488]{0:T(1024)S(1)} %reshape.124, f32[5488,128]{1,0:T(8,128)} %reshape.126, f32[]{:T(128)} %constant.152.clone.1), kind=kCustom, calls=%fused_computation.41 | custom fusion | flops 702464 | bytes 1917440 | tf_op jit(solution)/shard_map/scatter-add | solution.py:20
  129.7 3.5 collective-permute-start.3
  133.2 3.2 slice_add_fusion
  136.4 4.6 scatter_fusion.1
  142.9 44.0 %all_to_all.38 = f32[4,864,128]{2,1,0:T(8,128)} all-to-all(f32[4,864,128]{2,1,0:T(8,128)S(1)} %bitcast.76), channel_id=1, replica_groups=mesh['domain'=8,'band'=4] {'band'}, dimensions={0} | all-to-all | bytes 3538944 | tf_op jit(solution)/shard_map/all_to_all | solution.py:58
  188.7 4.6 fusion.43
  195.2 128.1 %all-reduce.3.cloned.1.call-done = f32[512,512]{0,1:T(8,128)} async-done(((f32[512,512]{0,1:T(8,128)}), f32[512,512]{0,1:T(8,128)}) %all-reduce.3.cloned.1.call-update) | async-done | bytes 1048592 | tf_op jit(solution)/shard_map/psum | solution.py:66
  326.3 11.7 %cholesky.104 = f32[128,128]{1,0:T(8,128)S(1)} custom-call(f32[128,128]{1,0:T(8,128)S(1)} %cholesky.266), custom_call_target="Cholesky" | custom-call | tf_op jit(solution)/shard_map/jit(cholesky)/cholesky | solution.py:67
  338.2 9.8 %custom-call.31 = f32[1,128,128]{1,2,0:T(8,128)S(1)} custom-call(f32[1,128,128]{2,1,0:T(8,128)S(1)} %get-tuple-element.32), custom_call_target="InvertDiagBlocksLowerTriangular" | custom-call | tf_op jit(solution)/shard_map/jit(cholesky)/cholesky | solution.py:67
  350.5 11.7 %cholesky.217 = f32[128,128]{1,0:T(8,128)S(1)} custom-call(f32[128,128]{1,0:T(8,128)S(1)} %cholesky.270), custom_call_target="Cholesky" | custom-call | tf_op jit(solution)/shard_map/jit(cholesky)/cholesky | solution.py:67
  362.2 10.0 %custom-call.32 = f32[1,128,128]{1,2,0:T(8,128)S(1)} custom-call(f32[1,128,128]{2,1,0:T(8,128)S(1)} %get-tuple-element.29), custom_call_target="InvertDiagBlocksLowerTriangular" | custom-call | tf_op jit(solution)/shard_map/jit(cholesky)/cholesky | solution.py:67
  373.8 11.7 %cholesky.238 = f32[128,128]{1,0:T(8,128)S(1)} custom-call(f32[128,128]{1,0:T(8,128)S(1)} %cholesky.275), custom_call_target="Cholesky" | custom-call | tf_op jit(solution)/shard_map/jit(cholesky)/cholesky | solution.py:67
  386.3 9.8 %custom-call.33 = f32[1,128,128]{1,2,0:T(8,128)S(1)} custom-call(f32[1,128,128]{2,1,0:T(8,128)S(1)} %get-tuple-element.26), custom_call_target="InvertDiagBlocksLowerTriangular" | custom-call | tf_op jit(solution)/shard_map/jit(cholesky)/cholesky | solution.py:67
  397.7 11.7 %cholesky.255 = f32[128,128]{1,0:T(8,128)S(1)} custom-call(f32[128,128]{1,0:T(8,128)S(1)} %convolution_subtract_fusion.4), custom_call_target="Cholesky" | custom-call | tf_op jit(solution)/shard_map/jit(cholesky)/cholesky | solution.py:67
  414.6 14.1 %while.1 = (s32[]{:T(128)}, f32[512,512]{1,0:T(8,128)}, s32[4,2]{0,1:T(2,128)S(1)}, f32[4,128,128]{2,1,0:T(8,128)}, s32[]{:T(128)}) while((s32[]{:T(128)}, f32[512,512]{1,0:T(8,128)}, s32[4,2]{0,1:T(2,128)S(1)}, f32[4,128,128]{2,1,0:T(8,128)}, s32[]{:T(128)}) %tuple.27), condition=%wide.while_cond, body=%wide.while_body.sunk | while | flops 2 | bytes 132705 | solution.py:68
  415.3 2.9 bitcast_dynamic-update-slice_fusion.2
  418.8 2.9 bitcast_dynamic-update-slice_fusion.2
  422.4 2.9 bitcast_dynamic-update-slice_fusion.2
  425.9 2.8 bitcast_dynamic-update-slice_fusion.2
  428.7 40.1 %custom-call.34 = f32[4,128,128]{1,2,0:T(8,128)S(1)} custom-call(f32[4,128,128]{2,1,0:T(8,128)} %get-tuple-element.12), custom_call_target="InvertDiagBlocksLowerTriangular" | custom-call | tf_op jit(solution)/shard_map/jit(_solve_triangular)/triangular_solve | solution.py:68
  473.6 2.2 fusion.8
  476.4 42.2 %all_to_all.39 = f32[864,4,128]{2,0,1:T(8,128)S(1)} all-to-all(f32[864,4,128]{2,0,1:T(8,128)S(1)} %copy_bitcast_fusion), channel_id=1, replica_groups=mesh['domain'=8,'band'=4] {'band'}, dimensions={1} | all-to-all | bytes 3538944 | tf_op jit(solution)/shard_map/all_to_all | solution.py:69
  (83 shorter events, 44.4 us)
Async XLA Ops:
  6.5 18.7 %copy-start = (bf16[343,343]{1,0:T(8,128)(2,1)S(1)}, bf16[343,343]{1,0:T(8,128)(2,1)}, u32[]{:S(2)}) copy-start(bf16[343,343]{1,0:T(8,128)(2,1)} %param.7) | copy-start | bytes 705898
  6.5 316.7 %all-reduce.3.cloned.1.call-start = ((), (), s32[]{:S(2)}) async-start(), calls=%async_computation.2 | async-start | bytes 2097152 | tf_op jit(solution)/shard_map/psum | solution.py:66
  9.7 2.0 collective-permute-start
  23.9 1.3 copy-start.7
  29.1 35.8 %copy-start.1 = (bf16[3456,128]{1,0:T(8,128)(2,1)S(1)}, bf16[3456,128]{1,0:T(8,128)(2,1)}, u32[]{:S(2)}) copy-start(bf16[3456,128]{1,0:T(8,128)(2,1)} %param.6) | copy-start | bytes 2654212
  29.2 35.8 %copy-start.6 = (f32[3456]{0:T(1024)S(1)}, f32[3456]{0:T(1024)}, u32[]{:S(2)}) copy-start(f32[3456]{0:T(1024)} %param.9) | copy-start | bytes 41476
  62.4 4.7 collective-permute-start.1
  73.4 2.5 collective-permute-start.2
  96.5 36.7 %copy-start.2 = (bf16[3456,128]{1,0:T(8,128)(2,1)S(1)}, bf16[3456,128]{1,0:T(8,128)(2,1)}, u32[]{:S(2)}) copy-start(bf16[3456,128]{1,0:T(8,128)(2,1)} %param.6) | copy-start | bytes 2654212
  129.7 6.7 %collective-permute-start.3 = (f32[288,128]{1,0:T(8,128)S(1)}, f32[288,128]{1,0:T(8,128)S(1)}, u32[]{:S(2)}, u32[]{:S(2)}) collective-permute-start(f32[288,128]{1,0:T(8,128)S(1)} %slice.152), channel_id=1, source_target_pairs={{0,4},{4,8},{8,12},{12,16},{16,20},{20,24},{24,28},{28,0},{1,5},{5... | collective-permute-start | bytes 442376 | tf_op jit(solution)/shard_map/ppermute | solution.py:13
  323.2 1.8 copy-start.4
  325.3 1.0 copy-start.5
  396.1 72.8 %copy-start.3 = (f32[864,512]{1,0:T(8,128)S(1)}, f32[864,512]{1,0:T(8,128)}, u32[]{:S(2)}) copy-start(f32[864,512]{1,0:T(8,128)} %copy.17) | copy-start | bytes 5308420
Sparse Core Ops, SparseCore 0:
  193.5 129.7 all-reduce.2
where the time goes:
time: 538 us; the launch traced here: 527 us
  other arithmetic  206 us (38%)
  waiting for transfers between devices  130 us (24%)
  blocking collectives  86.2 us (16%)
  local copies, waits for them, and re-layouts  58.7 us (11%)
  matrix products  22.2 us (4%)
  between operations  16.7 us (3%)
  starting transfers between devices  6.64 us (1%)
    psum x1, waiting for transfers between devices, shards(): gram = lax.psum(partial_gram, ('domain', 'band')) / node_total  128 us
    another operation x14, other arithmetic, shards(): lower = jnp.linalg.cholesky(gram)  78.9 us
    scatter-add x2, other arithmetic, cell_sum(): jax.ops.segment_sum(products.reshape(-1, products.shape[-1]), links.resha...  64.6 us
    all_to_all x1, blocking collectives, shards(): lax.all_to_all(current, 'band', split_axis=0, concat_axis=1, tiled=True)  44 us
    all_to_all x1, blocking collectives, shards(): lax.all_to_all(solved, 'band', split_axis=1, concat_axis=0, tiled=True)  42.2 us
    another operation x3, other arithmetic, shards(): solved = jax.scipy.linalg.solve_triangular(lower, node_rows.T, lower=True).T  41.2 us
    gather x4, local copies, waits for them, and re-layouts, cell_sum(): picked = source[links]  26 us
    another operation x12, local copies, waits for them, and re-layouts  14.1 us
  transfers between devices with their start and end apart: 5, of which 4 were waited for; matrix products, arithmetic and copies ran while one was open for 2% of the time, Pallas kernels for 0%

commit v1 on v0

v1 whole, which is shorter than its diff:
```python
import functools

import jax
import jax.numpy as jnp
from jax import lax
from jax.experimental import pallas as pl
from jax.experimental.pallas import tpu as pltpu
from jax.sharding import PartitionSpec as P

CENTER = 1.5
HALF_WIDTH = 1.25
LANES = 128
CHAINS = 4
EXACT = lax.Precision.HIGHEST
F32 = jnp.float32
BF16 = jnp.bfloat16
VM = pl.BlockSpec(memory_space=pltpu.VMEM)
SM = pl.BlockSpec(memory_space=pltpu.SMEM)
PARAMS = pltpu.CompilerParams(vmem_limit_bytes=48 << 20)


def shifted(value, axis, steps):
    count = lax.axis_size(axis)
    return lax.ppermute(value, axis, [(i, (i + steps) % count) for i in range(count)])


def upward(value, axis, steps):
    count = lax.axis_size(axis)
    return lax.ppermute(value, axis, [(i, i + steps) for i in range(count - steps)])


def pick_kernel(nodes, rows_ref, out_ref, wide, picked):
    wide[...] = rows_ref[...].astype(F32)
    count = nodes.shape[0]

    def body(step, _):
        for k in range(16):
            i = step * 16 + k
            picked[pl.ds(i, 1), :] = wide[pl.ds(nodes[i], 1), :]
        return 0

    lax.fori_loop(0, count // 16, body, 0)
    out_ref[...] = picked[...].astype(BF16)


def pick(nodes, rows):
    count = nodes.shape[0]
    return pl.pallas_call(
        pick_kernel,
        out_shape=jax.ShapeDtypeStruct((count, LANES), BF16),
        in_specs=[SM, VM],
        out_specs=VM,
        scratch_shapes=[pltpu.VMEM(rows.shape, F32), pltpu.VMEM((count, LANES), F32)],
        compiler_params=PARAMS,
        name="pick",
    )(nodes, rows)


def cells_kernel(
    links, scale, rows_ref, ghost_ref, matrix_ref, potential_ref, out_ref, back_ref, ext, *scratch
):
    gathered, products, sums = scratch[:2], scratch[2:4], scratch[4:]
    owned = rows_ref.shape[0]
    cells, npc = links.shape
    for block in range(owned // LANES):
        here = slice(block * LANES, (block + 1) * LANES)
        wide = rows_ref[here, :].astype(F32)
        level = jnp.broadcast_to(potential_ref[block : block + 1, :], (LANES, LANES)).T
        sums[0][here, :] = (level - CENTER) * wide
        ext[here, :] = wide.astype(BF16).astype(F32)
    ext[owned:, :] = ghost_ref[...].astype(F32)
    sums[0][owned:, :] = jnp.zeros_like(ghost_ref[...], F32)
    for total in sums[1:]:
        total[...] = jnp.zeros_like(total)
    for rows in gathered:
        rows[npc:, :] = jnp.zeros_like(rows[npc:, :])

    def pair(step, _):
        for r in range(npc):
            for half in range(2):
                gathered[half][r : r + 1, :] = ext[pl.ds(links[2 * step + half, r], 1), :]
        both = jnp.concatenate([rows[...].astype(BF16) for rows in gathered], axis=1)
        made = jnp.dot(matrix_ref[...], both[:npc], preferred_element_type=F32)
        for half in range(2):
            products[half][0:npc, :] = (
                made[:, half * LANES : (half + 1) * LANES] * scale[2 * step + half]
            )
        for r in range(npc):
            for half in range(2):
                total = sums[(2 * r + half) % CHAINS]
                row = pl.ds(links[2 * step + half, r], 1)
                total[row, :] = total[row, :] + products[half][r : r + 1, :]
        return 0

    lax.fori_loop(0, cells // 2, pair, 0)
    out_ref[...] = sum(total[0:owned, :] for total in sums)
    back_ref[...] = sum(total[owned:, :] for total in sums)


def cells(links, scale, rows, ghost, matrix, potential):
    owned, plane, npc = rows.shape[0], ghost.shape[0], links.shape[1]
    padded = (npc + 15) // 16 * 16
    return pl.pallas_call(
        cells_kernel,
        out_shape=(
            jax.ShapeDtypeStruct((owned, LANES), F32),
            jax.ShapeDtypeStruct((plane, LANES), F32),
        ),
        in_specs=[SM, SM, VM, VM, VM, VM],
        out_specs=(VM, VM),
        scratch_shapes=[pltpu.VMEM((owned + plane, LANES), F32)]
        + [pltpu.VMEM((padded, LANES), F32)] * 4
        + [pltpu.VMEM((owned + plane, LANES), F32)] * CHAINS,
        compiler_params=PARAMS,
        name="cells",
    )(links, scale, rows, ghost, matrix, potential)


def add_back(nodes, target, back_ref, factor, picked=None):
    def body(step, _):
        at = [step * 16 + k for k in range(16)]
        rows = [pl.ds(nodes[i], 1) for i in at]
        new = [target[r, :] + factor * back_ref[pl.ds(i, 1), :] for i, r in zip(at, rows)]
        for i, r, value in zip(at, rows, new):
            target[r, :] = value
            if picked is not None:
                picked[pl.ds(i, 1), :] = value
        return 0

    lax.fori_loop(0, nodes.shape[0] // 16, body, 0)


def first_kernel(nodes, sums_ref, back_ref, out_ref, picked_ref, picked):
    out_ref[...] = sums_ref[...] * (1.0 / HALF_WIDTH)
    add_back(nodes, out_ref, back_ref, 1.0 / HALF_WIDTH, picked)
    picked_ref[...] = picked[...].astype(BF16)


def first_term(nodes, sums, back):
    return pl.pallas_call(
        first_kernel,
        out_shape=(
            jax.ShapeDtypeStruct(sums.shape, F32),
            jax.ShapeDtypeStruct(back.shape, BF16),
        ),
        in_specs=[SM, VM, VM],
        out_specs=(VM, VM),
        scratch_shapes=[pltpu.VMEM(back.shape, F32)],
        compiler_params=PARAMS,
        name="first_term",
    )(nodes, sums, back)


def second_kernel(band, nodes, sums_ref, back_ref, previous_ref, *refs):
    pieces, total = refs[:-1], refs[-1]
    total[...] = sums_ref[...] * (2.0 / HALF_WIDTH) - previous_ref[...].astype(F32)
    add_back(nodes, total, back_ref, 2.0 / HALF_WIDTH)
    count = len(pieces)
    rows = total.shape[0] // count
    for k, piece in enumerate(pieces):
        start = pl.multiple_of(lax.rem(band[0] + k, count) * rows, rows)
        piece[...] = total[pl.ds(start, rows), :].astype(BF16)


def second_term(band, nodes, sums, back, previous, count):
    owned = sums.shape[0]
    return pl.pallas_call(
        second_kernel,
        out_shape=[jax.ShapeDtypeStruct((owned // count, LANES), BF16)] * count,
        in_specs=[SM, SM, VM, VM, VM],
        out_specs=[VM] * count,
        scratch_shapes=[pltpu.VMEM(sums.shape, F32)],
        compiler_params=PARAMS,
        name="second_term",
    )(band, nodes, sums, back, previous)


def gram_kernel(band, *refs):
    pieces, out_ref, held = refs[:-2], refs[-2], refs[-1]
    count = len(pieces)
    for s, piece in enumerate(pieces):
        held[lax.rem(band[0] + (count - s), count)] = piece[...]
    at = 0
    for i in range(count):
        for j in range(i + 1):
            out_ref[at : at + LANES, :] = lax.dot_general(
                held[i], held[j], (((0,), (0,)), ((), ())), preferred_element_type=F32
            )
            at += LANES


def partial_gram(band, pieces):
    count = len(pieces)
    blocks = count * (count + 1) // 2
    return pl.pallas_call(
        gram_kernel,
        out_shape=jax.ShapeDtypeStruct((blocks * LANES, LANES), F32),
        in_specs=[SM] + [VM] * count,
        out_specs=VM,
        scratch_shapes=[pltpu.VMEM((count,) + pieces[0].shape, BF16)],
        compiler_params=PARAMS,
        name="partial_gram",
    )(band, *pieces)


def summed(value):
    count = lax.axis_size("domain")
    if count > 8:
        return lax.psum(value, ("domain", "band"))
    chunks = value.reshape(count, -1, LANES)
    me = lax.axis_index("domain")
    taken = [
        lax.dynamic_index_in_dim(chunks, lax.rem(me + k, count), 0, keepdims=False)
        for k in range(count)
    ]
    total = taken[0]
    for part in [shifted(taken[k], "domain", k) for k in range(1, count)]:
        total = total + part
    whole = total
    for k in range(1, lax.axis_size("band")):
        whole = whole + shifted(total, "band", k)
    parts = [whole] + [shifted(whole, "domain", k) for k in range(1, count)]
    order = lax.rem(me - jnp.arange(count) + count, count)
    return jnp.stack(parts)[order].reshape(value.shape)


def small_inverse(tiles, lane):
    count, tiles, done = len(tiles), list(tiles), []
    sub = lax.broadcasted_iota(jnp.int32, tiles[0].shape, 0)

    def along_lanes(tile, column):
        return jnp.broadcast_to(tile[:, column : column + 1], tile.shape)

    def along_rows(tile, row):
        return jnp.broadcast_to(tile[row : row + 1, :], tile.shape)

    for p in range(count):
        base = 8 * p
        group = (lane >= base) & (lane < base + 8)
        columns = [along_lanes(tiles[p], base + m) for m in range(8)]
        entry = {(i, j): along_rows(columns[j], i) for j in range(8) for i in range(j, 8)}
        start = jnp.where(group, (lane - base == sub).astype(F32), tiles[p])
        solved = [along_rows(start, i) for i in range(8)]
        following = None
        if p + 1 < count:
            ahead = [along_lanes(tiles[p + 1], base + m) for m in range(8)]
            following = jnp.where(group, 0.0, tiles[p + 1])
        inverse, factor = [], {}
        for j in range(8):
            pivot = 1.0 / entry[j, j]
            inverse.append(pivot)
            for i in range(j + 1, 8):
                factor[i, j] = entry[i, j] * pivot
            for i in range(j + 1, 8):
                for k in range(j + 1, i + 1):
                    entry[i, k] = entry[i, k] - factor[i, j] * entry[k, j]
                solved[i] = solved[i] - factor[i, j] * solved[j]
            if following is not None:
                scaled = ahead[j] * pivot
                following = following - scaled * solved[j]
                for m in range(j + 1, 8):
                    ahead[m] = ahead[m] - scaled * entry[m, j]
        result = solved[0] * lax.rsqrt(entry[0, 0])
        for i in range(1, 8):
            result = jnp.where(sub == i, solved[i] * lax.rsqrt(entry[i, i]), result)
        done.append(jnp.where(lane <= base + sub, result, 0.0))
        if p + 2 < count:
            back = [None] * 8
            for i in range(7, -1, -1):
                value = solved[i] * inverse[i]
                for k in range(i + 1, 8):
                    value = value - factor[k, i] * back[k]
                back[i] = value
            for i in range(p + 2, count):
                value = jnp.where(group, 0.0, tiles[i])
                for m in range(8):
                    value = value - along_lanes(tiles[i], base + m) * back[m]
                tiles[i] = value
        if following is not None:
            tiles[p + 1] = following
    return done


def exact_dot(a, b, dims=(((1,), (0,)), ((), ()))):
    return lax.dot_general(a, b, dims, precision=EXACT, preferred_element_type=F32)


def inverse_kernel(over, packed_ref, out_ref, work, small):
    size = work.shape[0]
    blocks = size // LANES
    at = 0
    for i in range(blocks):
        for j in range(i + 1):
            block = packed_ref[at : at + LANES, :] * over
            work[i * LANES : (i + 1) * LANES, j * LANES : (j + 1) * LANES] = block
            if i != j:
                work[j * LANES : (j + 1) * LANES, i * LANES : (i + 1) * LANES] = block.T
            at += LANES
    out_ref[...] = jnp.zeros_like(out_ref)
    lane = lax.broadcasted_iota(jnp.int32, (8, LANES), 1)

    def step(k, _):
        base = pl.multiple_of(k * LANES, LANES)
        tiles = [
            work[pl.ds(pl.multiple_of(base + 8 * i, 8), 8), pl.ds(base, LANES)]
            for i in range(LANES // 8)
        ]
        for i, tile in enumerate(small_inverse(tiles, lane)):
            small[8 * i : 8 * i + 8, :] = tile
        for which in range(blocks):

            @pl.when(k == which)
            def _():
                a, b = which * LANES, (which + 1) * LANES
                diagonal = small[...]
                out_ref[a:b, a:b] = diagonal
                if which:
                    left = exact_dot(diagonal, work[a:b, 0:a])
                    out_ref[a:b, 0:a] = left
                if b < size:
                    right = exact_dot(diagonal, work[a:b, b:size])
                    column = exact_dot(work[b:size, a:b], diagonal, (((1,), (1,)), ((), ())))
                    work[b:size, b:size] = work[b:size, b:size] - exact_dot(column, right)
                    work[b:size, a:b] = -exact_dot(column, diagonal)
                    if which:
                        work[b:size, 0:a] = work[b:size, 0:a] - exact_dot(column, left)

        return 0

    lax.fori_loop(0, blocks, step, 0)


def inverse_factor(packed, size, over):
    return pl.pallas_call(
        functools.partial(inverse_kernel, over),
        out_shape=jax.ShapeDtypeStruct((size, size), F32),
        in_specs=[VM],
        out_specs=VM,
        scratch_shapes=[pltpu.VMEM((size, size), F32), pltpu.VMEM((LANES, LANES), F32)],
        compiler_params=PARAMS,
        name="inverse_factor",
    )(packed)


def output_kernel(band, factor_ref, *refs):
    pieces, out_ref = refs[:-1], refs[-1]
    count = factor_ref.shape[0] // LANES
    total = None
    for s in range(count):
        source = band[0] - s
        there = source >= 0
        column = pl.multiple_of(jnp.maximum(source, 0) * LANES, LANES)
        row = pl.multiple_of(band[0] * LANES, LANES)
        block = factor_ref[pl.ds(row, LANES), pl.ds(column, LANES)]
        block = jnp.where(there, block, 0.0)
        high = block.astype(BF16)
        low = (block - high.astype(F32)).astype(BF16)
        dims = (((1,), (1,)), ((), ()))
        piece = pieces[s][...]
        part = lax.dot_general(piece, high, dims, preferred_element_type=F32)
        part = part + lax.dot_general(piece, low, dims, preferred_element_type=F32)
        total = part if total is None else total + part
    out_ref[...] = total


def output(band, factor, received):
    count = len(received)
    owned = received[0].shape[0]
    rows = owned // count
    return pl.pallas_call(
        output_kernel,
        out_shape=jax.ShapeDtypeStruct((owned, LANES), F32),
        grid_spec=pltpu.PrefetchScalarGridSpec(
            num_scalar_prefetch=1,
            grid=(count,),
            in_specs=[pl.BlockSpec(factor.shape, lambda j, band: (0, 0))]
            + [pl.BlockSpec((rows, LANES), lambda j, band: (j, 0))] * count,
            out_specs=pl.BlockSpec((rows, LANES), lambda j, band: (lax.rem(band[0] + j, count), 0)),
        ),
        compiler_params=PARAMS,
        name="output",
    )(band, factor, *received)


def shards(states_block, cell_matrix, cell_scale, potential, connectivity, boundary_nodes):
    owned = states_block.shape[0]
    count = lax.axis_size("band")
    band = lax.axis_index("band").astype(jnp.int32).reshape(1)
    levels = potential.reshape(owned // LANES, LANES)

    ghost = shifted(pick(boundary_nodes, states_block), "domain", -1)
    sums, back = cells(connectivity, cell_scale, states_block, ghost, cell_matrix, levels)
    current, edge = first_term(boundary_nodes, sums, shifted(back, "domain", 1))
    ghost = shifted(edge, "domain", -1)
    sums, back = cells(connectivity, cell_scale, current, ghost, cell_matrix, levels)
    back = shifted(back, "domain", 1)
    pieces = second_term(band, boundary_nodes, sums, back, states_block, count)

    arrived = [pieces[0]] + [shifted(pieces[s], "band", s) for s in range(1, count)]
    packed = summed(partial_gram(band, arrived))
    factor = inverse_factor(
        packed, count * LANES, 1.0 / (owned * lax.axis_size("domain"))
    )
    received = [jnp.concatenate(pieces)]
    for s in range(1, count):
        sent = jnp.concatenate([pieces[(j + s) % count] for j in range(1, count)])
        received.append(jnp.concatenate([arrived[s], upward(sent, "band", s)]))
    return output(band, factor, received)


def solution(mesh):
    return jax.shard_map(
        shards,
        mesh=mesh,
        in_specs=(
            P("domain", "band"),
            P(),
            P("domain"),
            P("domain"),
            P("domain", None),
            P("domain"),
        ),
        out_specs=P("domain", "band"),
        check_vma=False,
    )
```

time: 538 us -> 176 us (0.33)
  the two profiles are of different devices: /device:TPU:26 before, /device:TPU:17 now
where the time goes in v1:
time: 176 us
  waiting for transfers between devices  66.5 us (38%)
  Pallas kernels  65.6 us (37%)
  starting transfers between devices  31.2 us (18%)
  local copies, waits for them, and re-layouts  8.36 us (5%)
  other arithmetic  3.83 us (2%)
    ppermute x24, waiting for transfers between devices, shifted(): lax.ppermute(value, axis, [(i, (i + steps) % count) for i in range(count)])  57.3 us
    pallas_call x2, Pallas kernels, cells(): pl.pallas_call(cells_kernel, out_shape=(jax.ShapeDtypeStruct((owned, LANE...  36.5 us
    ppermute x24, starting transfers between devices, shifted(): lax.ppermute(value, axis, [(i, (i + steps) % count) for i in range(count)])  26.4 us
    pallas_call x1, Pallas kernels, inverse_factor(): pl.pallas_call(functools.partial(inverse_kernel, over), out_shape=jax.Sha...  20.9 us
    ppermute x3, waiting for transfers between devices, upward(): lax.ppermute(value, axis, [(i, i + steps) for i in range(count - steps)])  9.22 us
    unnamed x32, local copies, waits for them, and re-layouts  7.7 us
    ppermute x3, starting transfers between devices, upward(): lax.ppermute(value, axis, [(i, i + steps) for i in range(count - steps)])  4.75 us
  transfers between devices with their start and end apart: 27, of which 18 were waited for; matrix products, arithmetic and copies ran while one was open for 2% of the time, Pallas kernels for 12%

profile of v1, /device:TPU:17, one launch (start us, length us, event | category | flops | bytes accessed | tf_op | source)
XLA Modules:
  0.0 175.8 jit_solution(463078348508640287)
XLA Ops:
  3.6 3.1 %collective-permute-done.ghost_ref = bf16[288,128]{1,0:T(8,128)(2,1)S(1)} collective-permute-done((bf16[288,128]{1,0:T(8,128)(2,1)S(1)}, bf16[288,128]{1,0:T(8,128)(2,1)S(1)}, u32[]{:S(2)}, u32[]{:S(2)}) %collective-permute-start) | collective-permute-done | bytes 73760 | tf_op jit(solution)/shard_map/ppermute | solution.py:24
  11.0 18.3 %cells.2 = (f32[3456,128]{1,0:T(8,128)S(1)}, f32[288,128]{1,0:T(8,128)S(1)}) custom-call(s32[16,343]{1,0:T(8,128)S(1)} %copy-done.6, f32[16]{0:T(128)S(1)} %copy-done.11, bf16[3456,128]{1,0:T(8,128)(2,1)S(1)} %copy-done.1, bf16[288,128]{1,0:T(8,128)(2,1)S(1)} %collective-permute-done.ghost_ref, bf16[343,343]{1,0:T(8,128)(2,1)S(1)} %copy-done.3, ...), custom_call_target="tpu_custom_call" | custom-call | tf_op jit(solution)/shard_map/cells/pallas_call | solution.py:103
  29.3 2.1 %collective-permute-done.1.back_ref = f32[288,128]{1,0:T(8,128)S(1)} collective-permute-done((f32[288,128]{1,0:T(8,128)S(1)}, f32[288,128]{1,0:T(8,128)S(1)}, u32[]{:S(2)}, u32[]{:S(2)}) %collective-permute-start.1) | collective-permute-done | bytes 147488 | tf_op jit(solution)/shard_map/ppermute | solution.py:24
  31.4 1.4 first_term.1
  32.8 4.2 %collective-permute-start.2 = (bf16[288,128]{1,0:T(8,128)(2,1)S(1)}, bf16[288,128]{1,0:T(8,128)(2,1)S(1)}, u32[]{:S(2)}, u32[]{:S(2)}) collective-permute-start(bf16[288,128]{1,0:T(8,128)(2,1)S(1)} %get-tuple-element.18), channel_id=1, source_target_pairs={{0,28},{4,0},{8,4},{12,8},{16,12},{20,16},{24,20},{28,24},{1,29},{... | collective-permute-start | bytes 221192 | tf_op jit(solution)/shard_map/ppermute | solution.py:24
  37.9 18.3 %cells.3 = (f32[3456,128]{1,0:T(8,128)S(1)}, f32[288,128]{1,0:T(8,128)S(1)}) custom-call(s32[16,343]{1,0:T(8,128)S(1)} %copy-done.6, f32[16]{0:T(128)S(1)} %copy-done.12, f32[3456,128]{1,0:T(8,128)S(1)} %get-tuple-element.17.rows_ref, bf16[288,128]{1,0:T(8,128)(2,1)S(1)} %collective-permute-done.2.ghost_ref, bf16[343,343]{1,0:T(8,128)(2,1)S(1)} %copy-done.3, ...), custom_call_target="tpu_custom_call" | custom-call | tf_op jit(solution)/shard_map/cells/pallas_call | solution.py:103
  56.3 2.1 %collective-permute-done.3.back_ref = f32[288,128]{1,0:T(8,128)S(1)} collective-permute-done((f32[288,128]{1,0:T(8,128)S(1)}, f32[288,128]{1,0:T(8,128)S(1)}, u32[]{:S(2)}, u32[]{:S(2)}) %collective-permute-start.3) | collective-permute-done | bytes 147488 | tf_op jit(solution)/shard_map/ppermute | solution.py:24
  59.9 1.4 second_term.1
  61.3 1.3 collective-permute-start.4
  63.9 4.9 %collective-permute-done.4.refs_1_ = bf16[864,128]{1,0:T(8,128)(2,1)S(1)} collective-permute-done((bf16[864,128]{1,0:T(8,128)(2,1)S(1)}, bf16[864,128]{1,0:T(8,128)(2,1)S(1)}, u32[]{:S(2)}, u32[]{:S(2)}) %collective-permute-start.4) | collective-permute-done | bytes 221216 | tf_op jit(solution)/shard_map/ppermute | solution.py:24
  68.8 7.7 %collective-permute-done.5.refs_2_ = bf16[864,128]{1,0:T(8,128)(2,1)S(1)} collective-permute-done((bf16[864,128]{1,0:T(8,128)(2,1)S(1)}, bf16[864,128]{1,0:T(8,128)(2,1)S(1)}, u32[]{:S(2)}, u32[]{:S(2)}) %collective-permute-start.5) | collective-permute-done | bytes 221216 | tf_op jit(solution)/shard_map/ppermute | solution.py:24
  76.6 4.7 %collective-permute-done.6.refs_3_ = bf16[864,128]{1,0:T(8,128)(2,1)S(1)} collective-permute-done((bf16[864,128]{1,0:T(8,128)(2,1)S(1)}, bf16[864,128]{1,0:T(8,128)(2,1)S(1)}, u32[]{:S(2)}, u32[]{:S(2)}) %collective-permute-start.6) | collective-permute-done | bytes 221216 | tf_op jit(solution)/shard_map/ppermute | solution.py:24
  82.3 3.3 %collective-permute-start.7 = (f32[160,128]{1,0:T(8,128)S(1)}, f32[160,128]{1,0:T(8,128)S(1)}, u32[]{:S(2)}, u32[]{:S(2)}) collective-permute-start(f32[160,128]{1,0:T(8,128)S(1)} %get-tuple-element.27), channel_id=1, source_target_pairs={{0,4},{4,8},{8,12},{12,16},{16,20},{20,24},{24,28},{28,0},{1,5},{5... | collective-permute-start | bytes 245768 | tf_op jit(solution)/shard_map/ppermute | solution.py:24
  86.9 1.6 collective-permute-start.11
  92.5 3.2 %collective-permute-done.9 = f32[160,128]{1,0:T(8,128)S(1)} collective-permute-done((f32[160,128]{1,0:T(8,128)S(1)}, f32[160,128]{1,0:T(8,128)S(1)}, u32[]{:S(2)}, u32[]{:S(2)}) %collective-permute-start.9) | collective-permute-done | bytes 81952 | tf_op jit(solution)/shard_map/ppermute | solution.py:24
  95.9 2.2 %collective-permute-start.16 = (f32[160,128]{1,0:T(8,128)S(1)}, f32[160,128]{1,0:T(8,128)S(1)}, u32[]{:S(2)}, u32[]{:S(2)}) collective-permute-start(f32[160,128]{1,0:T(8,128)S(1)} %fusion.5), channel_id=1, source_target_pairs={{0,3},{1,0},{2,1},{3,2},{4,7},{5,4},{6,5},{7,6},{8,11},{9,8},{10,9... | collective-permute-start | bytes 245768 | tf_op jit(solution)/shard_map/ppermute | solution.py:24
  98.2 2.2 %collective-permute-start.15 = (f32[160,128]{1,0:T(8,128)S(1)}, f32[160,128]{1,0:T(8,128)S(1)}, u32[]{:S(2)}, u32[]{:S(2)}) collective-permute-start(f32[160,128]{1,0:T(8,128)S(1)} %fusion.5), channel_id=1, source_target_pairs={{0,2},{1,3},{2,0},{3,1},{4,6},{5,7},{6,4},{7,5},{8,10},{9,11},{10,... | collective-permute-start | bytes 245768 | tf_op jit(solution)/shard_map/ppermute | solution.py:24
  100.4 4.8 %collective-permute-done.15 = f32[160,128]{1,0:T(8,128)S(1)} collective-permute-done((f32[160,128]{1,0:T(8,128)S(1)}, f32[160,128]{1,0:T(8,128)S(1)}, u32[]{:S(2)}, u32[]{:S(2)}) %collective-permute-start.15) | collective-permute-done | bytes 81952 | tf_op jit(solution)/shard_map/ppermute | solution.py:24
  105.3 1.7 collective-permute-done.14
  107.0 1.3 collective-permute-start.17
  108.3 1.3 pad_maximum_fusion.6
  109.7 1.5 collective-permute-start.26
  112.4 2.0 %collective-permute-start.24 = (bf16[2592,128]{1,0:T(8,128)(2,1)}, bf16[2592,128]{1,0:T(8,128)(2,1)S(1)}, u32[]{:S(2)}, u32[]{:S(2)}) collective-permute-start(bf16[2592,128]{1,0:T(8,128)(2,1)} %get-tuple-element.36), channel_id=1, source_target_pairs={{0,1},{1,2},{2,3},{4,5},{5,6},{6,7},{8,9},{9,10},{10,11},{12,13},{... | collective-permute-start | bytes 1990664 | tf_op jit(solution)/shard_map/ppermute | solution.py:29
  114.4 2.3 %collective-permute-start.22 = (f32[160,128]{1,0:T(8,128)S(1)}, f32[160,128]{1,0:T(8,128)S(1)}, u32[]{:S(2)}, u32[]{:S(2)}) collective-permute-start(f32[160,128]{1,0:T(8,128)S(1)} %get-tuple-element.26), channel_id=1, source_target_pairs={{0,24},{4,28},{8,0},{12,4},{16,8},{20,12},{24,16},{28,20},{1,25},{... | collective-permute-start | bytes 245768 | tf_op jit(solution)/shard_map/ppermute | solution.py:24
  116.7 4.7 %collective-permute-done.18 = f32[160,128]{1,0:T(8,128)S(1)} collective-permute-done((f32[160,128]{1,0:T(8,128)S(1)}, f32[160,128]{1,0:T(8,128)S(1)}, u32[]{:S(2)}, u32[]{:S(2)}) %collective-permute-start.18) | collective-permute-done | bytes 81952 | tf_op jit(solution)/shard_map/ppermute | solution.py:24
  122.2 3.9 %collective-permute-done.19 = f32[160,128]{1,0:T(8,128)S(1)} collective-permute-done((f32[160,128]{1,0:T(8,128)S(1)}, f32[160,128]{1,0:T(8,128)S(1)}, u32[]{:S(2)}, u32[]{:S(2)}) %collective-permute-start.19) | collective-permute-done | bytes 81952 | tf_op jit(solution)/shard_map/ppermute | solution.py:24
  126.5 4.1 %collective-permute-done.20 = f32[160,128]{1,0:T(8,128)S(1)} collective-permute-done((f32[160,128]{1,0:T(8,128)S(1)}, f32[160,128]{1,0:T(8,128)S(1)}, u32[]{:S(2)}, u32[]{:S(2)}) %collective-permute-start.20) | collective-permute-done | bytes 81952 | tf_op jit(solution)/shard_map/ppermute | solution.py:24
  131.0 3.9 %collective-permute-done.21 = f32[160,128]{1,0:T(8,128)S(1)} collective-permute-done((f32[160,128]{1,0:T(8,128)S(1)}, f32[160,128]{1,0:T(8,128)S(1)}, u32[]{:S(2)}, u32[]{:S(2)}) %collective-permute-start.21) | collective-permute-done | bytes 81952 | tf_op jit(solution)/shard_map/ppermute | solution.py:24
  134.9 4.2 %collective-permute-done.23 = f32[160,128]{1,0:T(8,128)S(1)} collective-permute-done((f32[160,128]{1,0:T(8,128)S(1)}, f32[160,128]{1,0:T(8,128)S(1)}, u32[]{:S(2)}, u32[]{:S(2)}) %collective-permute-start.23) | collective-permute-done | bytes 81952 | tf_op jit(solution)/shard_map/ppermute | solution.py:24
  139.8 20.9 %inverse_factor.1.factor_ref = f32[512,512]{1,0:T(8,128)S(1)} custom-call(f32[1280,128]{1,0:T(8,128)S(1)} %bitcast.52), custom_call_target="tpu_custom_call" | custom-call | tf_op jit(solution)/shard_map/inverse_factor/pallas_call | solution.py:334
  163.0 9.2 %collective-permute-done.24 = bf16[2592,128]{1,0:T(8,128)(2,1)S(1)} collective-permute-done((bf16[2592,128]{1,0:T(8,128)(2,1)}, bf16[2592,128]{1,0:T(8,128)(2,1)S(1)}, u32[]{:S(2)}, u32[]{:S(2)}) %collective-permute-start.24) | collective-permute-done | bytes 663584 | tf_op jit(solution)/shard_map/ppermute | solution.py:29
  172.3 3.5 %output.1 = f32[3456,128]{1,0:T(8,128)} custom-call(s32[1]{0:T(128)} %bitcast.band, f32[512,512]{1,0:T(8,128)S(1)} %inverse_factor.1.factor_ref, bf16[3456,128]{1,0:T(8,128)(2,1)S(1)} %pad_maximum_fusion.refs_0_, bf16[3456,128]{1,0:T(8,128)(2,1)S(1)} %pad_maximum_fusion.1.refs_1_, bf16[3456,128]{1,0:T(8,128)(2,1)S(1)} %pad_maximum_fusion.2.refs_2_, ...), custom_call_target="tpu_custom_call" | custom-call | tf_op jit(solution)/shard_map/output/pallas_call | solution.py:370
  (74 shorter events, 24.0 us)
Async XLA Ops:
  1.9 29.6 %copy-start.10 = (s32[288]{0:T(512)S(1)}, s32[288]{0:T(512)}, u32[]{:S(2)}) copy-start(s32[288]{0:T(512)} %nodes.5) | copy-start | bytes 3460
  1.9 36.1 %copy-start.8 = (f32[3456]{0:T(1024)S(1)}, f32[3456]{0:T(1024)}, u32[]{:S(2)}) copy-start(f32[3456]{0:T(1024)} %param.9) | copy-start | bytes 41476
  2.8 35.1 %copy-start.12 = (f32[16]{0:T(128)S(1)}, f32[16]{0:T(128)}, u32[]{:S(2)}) copy-start(f32[16]{0:T(128)} %scale.3) | copy-start | bytes 196
  2.9 3.9 %collective-permute-start = (bf16[288,128]{1,0:T(8,128)(2,1)S(1)}, bf16[288,128]{1,0:T(8,128)(2,1)S(1)}, u32[]{:S(2)}, u32[]{:S(2)}) collective-permute-start(bf16[288,128]{1,0:T(8,128)(2,1)S(1)} %pick.1), channel_id=1, source_target_pairs={{0,28},{4,0},{8,4},{12,8},{16,12},{20,16},{24,20},{28,24},{1,29},{... | collective-permute-start | bytes 221192 | tf_op jit(solution)/shard_map/ppermute | solution.py:24
  6.7 1.2 copy-start.1
  29.2 2.2 %collective-permute-start.1 = (f32[288,128]{1,0:T(8,128)S(1)}, f32[288,128]{1,0:T(8,128)S(1)}, u32[]{:S(2)}, u32[]{:S(2)}) collective-permute-start(f32[288,128]{1,0:T(8,128)S(1)} %get-tuple-element.16), channel_id=1, source_target_pairs={{0,4},{4,8},{8,12},{12,16},{16,20},{20,24},{24,28},{28,0},{1,5},{5... | collective-permute-start | bytes 442376 | tf_op jit(solution)/shard_map/ppermute | solution.py:24
  31.4 27.6 %copy-start.2 = (bf16[3456,128]{1,0:T(8,128)(2,1)S(1)}, bf16[3456,128]{1,0:T(8,128)(2,1)}, u32[]{:S(2)}) copy-start(bf16[3456,128]{1,0:T(8,128)(2,1)} %previous_ref.1) | copy-start | bytes 2654212
  32.8 5.1 %collective-permute-start.2 = (bf16[288,128]{1,0:T(8,128)(2,1)S(1)}, bf16[288,128]{1,0:T(8,128)(2,1)S(1)}, u32[]{:S(2)}, u32[]{:S(2)}) collective-permute-start(bf16[288,128]{1,0:T(8,128)(2,1)S(1)} %get-tuple-element.18), channel_id=1, source_target_pairs={{0,28},{4,0},{8,4},{12,8},{16,12},{20,16},{24,20},{28,24},{1,29},{... | collective-permute-start | bytes 221192 | tf_op jit(solution)/shard_map/ppermute | solution.py:24
  56.2 2.2 %collective-permute-start.3 = (f32[288,128]{1,0:T(8,128)S(1)}, f32[288,128]{1,0:T(8,128)S(1)}, u32[]{:S(2)}, u32[]{:S(2)}) collective-permute-start(f32[288,128]{1,0:T(8,128)S(1)} %get-tuple-element.20), channel_id=1, source_target_pairs={{0,4},{4,8},{8,12},{12,16},{16,20},{20,24},{24,28},{28,0},{1,5},{5... | collective-permute-start | bytes 442376 | tf_op jit(solution)/shard_map/ppermute | solution.py:24
  61.3 7.5 %collective-permute-start.4 = (bf16[864,128]{1,0:T(8,128)(2,1)S(1)}, bf16[864,128]{1,0:T(8,128)(2,1)S(1)}, u32[]{:S(2)}, u32[]{:S(2)}) collective-permute-start(bf16[864,128]{1,0:T(8,128)(2,1)S(1)} %get-tuple-element.22), channel_id=1, source_target_pairs={{0,1},{1,2},{2,3},{3,0},{4,5},{5,6},{6,7},{7,4},{8,9},{9,10},{10,1... | collective-permute-start | bytes 663560 | tf_op jit(solution)/shard_map/ppermute | solution.py:24
  62.7 13.9 %collective-permute-start.5 = (bf16[864,128]{1,0:T(8,128)(2,1)S(1)}, bf16[864,128]{1,0:T(8,128)(2,1)S(1)}, u32[]{:S(2)}, u32[]{:S(2)}) collective-permute-start(bf16[864,128]{1,0:T(8,128)(2,1)S(1)} %get-tuple-element.23), channel_id=1, source_target_pairs={{0,2},{1,3},{2,0},{3,1},{4,6},{5,7},{6,4},{7,5},{8,10},{9,11},{10,... | collective-permute-start | bytes 663560 | tf_op jit(solution)/shard_map/ppermute | solution.py:24
  62.7 18.6 %collective-permute-start.6 = (bf16[864,128]{1,0:T(8,128)(2,1)S(1)}, bf16[864,128]{1,0:T(8,128)(2,1)S(1)}, u32[]{:S(2)}, u32[]{:S(2)}) collective-permute-start(bf16[864,128]{1,0:T(8,128)(2,1)S(1)} %get-tuple-element.24), channel_id=1, source_target_pairs={{0,3},{1,0},{2,1},{3,2},{4,7},{5,4},{6,5},{7,6},{8,11},{9,8},{10,9... | collective-permute-start | bytes 663560 | tf_op jit(solution)/shard_map/ppermute | solution.py:24
  82.3 7.3 %collective-permute-start.7 = (f32[160,128]{1,0:T(8,128)S(1)}, f32[160,128]{1,0:T(8,128)S(1)}, u32[]{:S(2)}, u32[]{:S(2)}) collective-permute-start(f32[160,128]{1,0:T(8,128)S(1)} %get-tuple-element.27), channel_id=1, source_target_pairs={{0,4},{4,8},{8,12},{12,16},{16,20},{20,24},{24,28},{28,0},{1,5},{5... | collective-permute-start | bytes 245768 | tf_op jit(solution)/shard_map/ppermute | solution.py:24
  85.7 4.8 %collective-permute-start.13 = (f32[160,128]{1,0:T(8,128)S(1)}, f32[160,128]{1,0:T(8,128)S(1)}, u32[]{:S(2)}, u32[]{:S(2)}) collective-permute-start(f32[160,128]{1,0:T(8,128)S(1)} %get-tuple-element.28), channel_id=1, source_target_pairs={{0,28},{4,0},{8,4},{12,8},{16,12},{20,16},{24,20},{28,24},{1,29},{... | collective-permute-start | bytes 245768 | tf_op jit(solution)/shard_map/ppermute | solution.py:24
  85.7 5.8 %collective-permute-start.12 = (f32[160,128]{1,0:T(8,128)S(1)}, f32[160,128]{1,0:T(8,128)S(1)}, u32[]{:S(2)}, u32[]{:S(2)}) collective-permute-start(f32[160,128]{1,0:T(8,128)S(1)} %get-tuple-element.29), channel_id=1, source_target_pairs={{0,24},{4,28},{8,0},{12,4},{16,8},{20,12},{24,16},{28,20},{1,25},{... | collective-permute-start | bytes 245768 | tf_op jit(solution)/shard_map/ppermute | solution.py:24
  86.9 4.6 %collective-permute-start.11 = (f32[160,128]{1,0:T(8,128)S(1)}, f32[160,128]{1,0:T(8,128)S(1)}, u32[]{:S(2)}, u32[]{:S(2)}) collective-permute-start(f32[160,128]{1,0:T(8,128)S(1)} %get-tuple-element.30), channel_id=1, source_target_pairs={{0,20},{4,24},{8,28},{12,0},{16,4},{20,8},{24,12},{28,16},{1,21},{... | collective-permute-start | bytes 245768 | tf_op jit(solution)/shard_map/ppermute | solution.py:24
  88.5 4.0 %collective-permute-start.10 = (f32[160,128]{1,0:T(8,128)S(1)}, f32[160,128]{1,0:T(8,128)S(1)}, u32[]{:S(2)}, u32[]{:S(2)}) collective-permute-start(f32[160,128]{1,0:T(8,128)S(1)} %get-tuple-element.31), channel_id=1, source_target_pairs={{0,16},{4,20},{8,24},{12,28},{16,0},{20,4},{24,8},{28,12},{1,17},{... | collective-permute-start | bytes 245768 | tf_op jit(solution)/shard_map/ppermute | solution.py:24
  89.6 6.0 %collective-permute-start.9 = (f32[160,128]{1,0:T(8,128)S(1)}, f32[160,128]{1,0:T(8,128)S(1)}, u32[]{:S(2)}, u32[]{:S(2)}) collective-permute-start(f32[160,128]{1,0:T(8,128)S(1)} %get-tuple-element.32), channel_id=1, source_target_pairs={{0,12},{4,16},{8,20},{12,24},{16,28},{20,0},{24,4},{28,8},{1,13},{... | collective-permute-start | bytes 245768 | tf_op jit(solution)/shard_map/ppermute | solution.py:24
  90.5 5.4 %collective-permute-start.8 = (f32[160,128]{1,0:T(8,128)S(1)}, f32[160,128]{1,0:T(8,128)S(1)}, u32[]{:S(2)}, u32[]{:S(2)}) collective-permute-start(f32[160,128]{1,0:T(8,128)S(1)} %get-tuple-element.33), channel_id=1, source_target_pairs={{0,8},{4,12},{8,16},{12,20},{16,24},{20,28},{24,0},{28,4},{1,9},{5... | collective-permute-start | bytes 245768 | tf_op jit(solution)/shard_map/ppermute | solution.py:24
  95.9 4.5 %collective-permute-start.16 = (f32[160,128]{1,0:T(8,128)S(1)}, f32[160,128]{1,0:T(8,128)S(1)}, u32[]{:S(2)}, u32[]{:S(2)}) collective-permute-start(f32[160,128]{1,0:T(8,128)S(1)} %fusion.5), channel_id=1, source_target_pairs={{0,3},{1,0},{2,1},{3,2},{4,7},{5,4},{6,5},{7,6},{8,11},{9,8},{10,9... | collective-permute-start | bytes 245768 | tf_op jit(solution)/shard_map/ppermute | solution.py:24
  98.2 7.1 %collective-permute-start.15 = (f32[160,128]{1,0:T(8,128)S(1)}, f32[160,128]{1,0:T(8,128)S(1)}, u32[]{:S(2)}, u32[]{:S(2)}) collective-permute-start(f32[160,128]{1,0:T(8,128)S(1)} %fusion.5), channel_id=1, source_target_pairs={{0,2},{1,3},{2,0},{3,1},{4,6},{5,7},{6,4},{7,5},{8,10},{9,11},{10,... | collective-permute-start | bytes 245768 | tf_op jit(solution)/shard_map/ppermute | solution.py:24
  100.4 6.6 %collective-permute-start.14 = (f32[160,128]{1,0:T(8,128)S(1)}, f32[160,128]{1,0:T(8,128)S(1)}, u32[]{:S(2)}, u32[]{:S(2)}) collective-permute-start(f32[160,128]{1,0:T(8,128)S(1)} %fusion.5), channel_id=1, source_target_pairs={{0,1},{1,2},{2,3},{3,0},{4,5},{5,6},{6,7},{7,4},{8,9},{9,10},{10,1... | collective-permute-start | bytes 245768 | tf_op jit(solution)/shard_map/ppermute | solution.py:24
  107.0 9.7 %collective-permute-start.17 = (f32[160,128]{1,0:T(8,128)S(1)}, f32[160,128]{1,0:T(8,128)S(1)}, u32[]{:S(2)}, u32[]{:S(2)}) collective-permute-start(f32[160,128]{1,0:T(8,128)S(1)} %get-tuple-element.26), channel_id=1, source_target_pairs={{0,4},{4,8},{8,12},{12,16},{16,20},{20,24},{24,28},{28,0},{1,5},{5... | collective-permute-start | bytes 245768 | tf_op jit(solution)/shard_map/ppermute | solution.py:24
  109.7 51.0 %collective-permute-start.26 = (bf16[2592,128]{1,0:T(8,128)(2,1)}, bf16[2592,128]{1,0:T(8,128)(2,1)}, u32[]{:S(2)}, u32[]{:S(2)}) collective-permute-start(bf16[2592,128]{1,0:T(8,128)(2,1)} %get-tuple-element.34), channel_id=1, source_target_pairs={{0,3},{4,7},{8,11},{12,15},{16,19},{20,23},{24,27},{28,31}} | collective-permute-start | bytes 1990664 | tf_op jit(solution)/shard_map/ppermute | solution.py:29
  111.2 50.7 %collective-permute-start.25 = (bf16[2592,128]{1,0:T(8,128)(2,1)}, bf16[2592,128]{1,0:T(8,128)(2,1)}, u32[]{:S(2)}, u32[]{:S(2)}) collective-permute-start(bf16[2592,128]{1,0:T(8,128)(2,1)} %get-tuple-element.35), channel_id=1, source_target_pairs={{0,2},{1,3},{4,6},{5,7},{8,10},{9,11},{12,14},{13,15},{16,18},{17,... | collective-permute-start | bytes 1990664 | tf_op jit(solution)/shard_map/ppermute | solution.py:29
  112.4 59.8 %collective-permute-start.24 = (bf16[2592,128]{1,0:T(8,128)(2,1)}, bf16[2592,128]{1,0:T(8,128)(2,1)S(1)}, u32[]{:S(2)}, u32[]{:S(2)}) collective-permute-start(bf16[2592,128]{1,0:T(8,128)(2,1)} %get-tuple-element.36), channel_id=1, source_target_pairs={{0,1},{1,2},{2,3},{4,5},{5,6},{6,7},{8,9},{9,10},{10,11},{12,13},{... | collective-permute-start | bytes 1990664 | tf_op jit(solution)/shard_map/ppermute | solution.py:29
  114.4 20.5 %collective-permute-start.22 = (f32[160,128]{1,0:T(8,128)S(1)}, f32[160,128]{1,0:T(8,128)S(1)}, u32[]{:S(2)}, u32[]{:S(2)}) collective-permute-start(f32[160,128]{1,0:T(8,128)S(1)} %get-tuple-element.26), channel_id=1, source_target_pairs={{0,24},{4,28},{8,0},{12,4},{16,8},{20,12},{24,16},{28,20},{1,25},{... | collective-permute-start | bytes 245768 | tf_op jit(solution)/shard_map/ppermute | solution.py:24
  116.7 4.7 %collective-permute-start.18 = (f32[160,128]{1,0:T(8,128)S(1)}, f32[160,128]{1,0:T(8,128)S(1)}, u32[]{:S(2)}, u32[]{:S(2)}) collective-permute-start(f32[160,128]{1,0:T(8,128)S(1)} %get-tuple-element.26), channel_id=1, source_target_pairs={{0,8},{4,12},{8,16},{12,20},{16,24},{20,28},{24,0},{28,4},{1,9},{5... | collective-permute-start | bytes 245768 | tf_op jit(solution)/shard_map/ppermute | solution.py:24
  121.4 4.8 %collective-permute-start.19 = (f32[160,128]{1,0:T(8,128)S(1)}, f32[160,128]{1,0:T(8,128)S(1)}, u32[]{:S(2)}, u32[]{:S(2)}) collective-permute-start(f32[160,128]{1,0:T(8,128)S(1)} %get-tuple-element.26), channel_id=1, source_target_pairs={{0,12},{4,16},{8,20},{12,24},{16,28},{20,0},{24,4},{28,8},{1,13},{... | collective-permute-start | bytes 245768 | tf_op jit(solution)/shard_map/ppermute | solution.py:24
  126.1 4.5 %collective-permute-start.20 = (f32[160,128]{1,0:T(8,128)S(1)}, f32[160,128]{1,0:T(8,128)S(1)}, u32[]{:S(2)}, u32[]{:S(2)}) collective-permute-start(f32[160,128]{1,0:T(8,128)S(1)} %get-tuple-element.26), channel_id=1, source_target_pairs={{0,16},{4,20},{8,24},{12,28},{16,0},{20,4},{24,8},{28,12},{1,17},{... | collective-permute-start | bytes 245768 | tf_op jit(solution)/shard_map/ppermute | solution.py:24
  130.6 4.3 %collective-permute-start.21 = (f32[160,128]{1,0:T(8,128)S(1)}, f32[160,128]{1,0:T(8,128)S(1)}, u32[]{:S(2)}, u32[]{:S(2)}) collective-permute-start(f32[160,128]{1,0:T(8,128)S(1)} %get-tuple-element.26), channel_id=1, source_target_pairs={{0,20},{4,24},{8,28},{12,0},{16,4},{20,8},{24,12},{28,16},{1,21},{... | collective-permute-start | bytes 245768 | tf_op jit(solution)/shard_map/ppermute | solution.py:24
  134.9 4.3 %collective-permute-start.23 = (f32[160,128]{1,0:T(8,128)S(1)}, f32[160,128]{1,0:T(8,128)S(1)}, u32[]{:S(2)}, u32[]{:S(2)}) collective-permute-start(f32[160,128]{1,0:T(8,128)S(1)} %get-tuple-element.26), channel_id=1, source_target_pairs={{0,28},{4,0},{8,4},{12,8},{16,12},{20,16},{24,20},{28,24},{1,29},{... | collective-permute-start | bytes 245768 | tf_op jit(solution)/shard_map/ppermute | solution.py:24
  (8 other events, 6.5 us)

commit v2 on v1

v2 whole, which is shorter than its diff:
```python
import functools

import jax
import jax.numpy as jnp
from jax import lax
from jax.experimental import pallas as pl
from jax.experimental.pallas import tpu as pltpu
from jax.sharding import PartitionSpec as P

CENTER = 1.5
HALF_WIDTH = 1.25
LANES = 128
CHAINS = 4
EXACT = lax.Precision.HIGHEST
F32 = jnp.float32
BF16 = jnp.bfloat16
VM = pl.BlockSpec(memory_space=pltpu.VMEM)
SM = pl.BlockSpec(memory_space=pltpu.SMEM)
PARAMS = pltpu.CompilerParams(vmem_limit_bytes=48 << 20)


def shifted(value, axis, steps):
    count = lax.axis_size(axis)
    return lax.ppermute(value, axis, [(i, (i + steps) % count) for i in range(count)])


def spread_levels(potential_ref, block):
    return jnp.broadcast_to(potential_ref[block : block + 1, :], (LANES, LANES)).T - CENTER


def rows_out(rows_of, potential_ref, owned, base_ref, ext_ref):
    for block in range(owned // LANES):
        here = slice(block * LANES, (block + 1) * LANES)
        wide = rows_of(here)
        base_ref[here, :] = spread_levels(potential_ref, block) * wide
        ext_ref[here, :] = wide.astype(BF16).astype(F32)
    base_ref[owned:, :] = jnp.zeros_like(base_ref[owned:, :])


def prepare_kernel(nodes, rows_ref, potential_ref, base_ref, ext_ref, edge_ref, picked):
    owned = rows_ref.shape[0]
    rows_out(lambda here: rows_ref[here, :].astype(F32), potential_ref, owned, base_ref, ext_ref)

    def body(step, _):
        for k in range(16):
            i = step * 16 + k
            picked[pl.ds(i, 1), :] = ext_ref[pl.ds(nodes[i], 1), :]
        return 0

    lax.fori_loop(0, nodes.shape[0] // 16, body, 0)
    edge_ref[...] = picked[...].astype(BF16)


def prepared_shapes(owned, plane):
    return (
        jax.ShapeDtypeStruct((owned + plane, LANES), F32),
        jax.ShapeDtypeStruct((owned + plane, LANES), F32),
        jax.ShapeDtypeStruct((plane, LANES), BF16),
    )


def prepare(nodes, rows, potential):
    owned, plane = rows.shape[0], nodes.shape[0]
    return pl.pallas_call(
        prepare_kernel,
        out_shape=prepared_shapes(owned, plane),
        in_specs=[SM, VM, VM],
        out_specs=(VM, VM, VM),
        scratch_shapes=[pltpu.VMEM((plane, LANES), F32)],
        compiler_params=PARAMS,
        name="prepare",
    )(nodes, rows, potential)


def gather_cells(links, ext_ref, gathered, first):
    cells, npc = gathered.shape[0], links.shape[1]

    def cell(c, _):
        for r in range(npc):
            gathered[c, r : r + 1, :] = ext_ref[pl.ds(links[first + c, r], 1), :]
        return 0

    lax.fori_loop(0, cells, cell, 0)


def multiply_cells(scale, matrix_ref, gathered, products, first):
    cells, npc = gathered.shape[0], matrix_ref.shape[0]
    for c in range(0, cells, 2):
        both = jnp.concatenate(
            [gathered[c, 0:npc, :].astype(BF16), gathered[c + 1, 0:npc, :].astype(BF16)], axis=1
        )
        made = jnp.dot(matrix_ref[...], both, preferred_element_type=F32)
        for half in range(2):
            products[c + half, 0:npc, :] = (
                made[:, half * LANES : (half + 1) * LANES] * scale[first + c + half]
            )


def scatter_cells(links, products, sums, first):
    cells, npc = products.shape[0], links.shape[1]
    chains = len(sums)

    def cell(c, _):
        for r in range(npc):
            total = sums[r % chains]
            row = pl.ds(links[first + c, r], 1)
            total[row, :] = total[row, :] + products[c, r : r + 1, :]
        return 0

    lax.fori_loop(0, cells, cell, 0)


def near_products_kernel(links, scale, ext_ref, matrix_ref, out_ref, gathered):
    gather_cells(links, ext_ref, gathered, 0)
    multiply_cells(scale, matrix_ref, gathered, out_ref, 0)


def far_cells_kernel(
    links, scale, ext_ref, ghost_ref, matrix_ref, base_ref, out_ref, back_ref, ext, gathered,
    products, *sums
):
    owned = out_ref.shape[0]
    half = gathered.shape[0]
    ext[0:owned, :] = ext_ref[0:owned, :]
    ext[owned:, :] = ghost_ref[...].astype(F32)
    sums[0][...] = base_ref[...]
    for total in sums[1:]:
        total[...] = jnp.zeros_like(total)
    gather_cells(links, ext, gathered, half)
    multiply_cells(scale, matrix_ref, gathered, products, half)
    scatter_cells(links, products, sums, half)
    back_ref[...] = sum(total[owned:, :] for total in sums)
    out_ref[...] = sum(total[0:owned, :] for total in sums)


def near_sums_kernel(links, products_ref, start_ref, out_ref, *sums):
    sums = (out_ref,) + sums
    out_ref[...] = start_ref[...]
    for total in sums[1:]:
        total[...] = jnp.zeros_like(total)
    scatter_cells(links, products_ref, sums, 0)
    out_ref[...] = sum(total[...] for total in sums)


def cost(flops, moved):
    return pl.CostEstimate(flops=flops, bytes_accessed=moved, transcendentals=0)


def apply_operator(links, scale, matrix, base, ext, edge):
    cells, npc = links.shape
    half, padded = cells // 2, (npc + 7) // 8 * 8
    plane = edge.shape[0]
    whole = base.shape
    owned = whole[0] - plane
    held = (half, padded, LANES)
    ghost = shifted(edge, "domain", -1)
    products = pl.pallas_call(
        near_products_kernel,
        out_shape=jax.ShapeDtypeStruct(held, F32),
        in_specs=[SM, SM, VM, VM],
        out_specs=VM,
        scratch_shapes=[pltpu.VMEM(held, F32)],
        compiler_params=PARAMS,
        cost_estimate=cost(0, 14 << 20),
        name="near_products",
    )(links, scale, ext, matrix)
    ghost, products = ordered(ghost, products)
    sums, back = pl.pallas_call(
        far_cells_kernel,
        out_shape=(
            jax.ShapeDtypeStruct((owned, LANES), F32),
            jax.ShapeDtypeStruct((plane, LANES), F32),
        ),
        in_specs=[SM, SM, VM, VM, VM, VM],
        out_specs=(VM, VM),
        scratch_shapes=[pltpu.VMEM(whole, F32), pltpu.VMEM(held, F32), pltpu.VMEM(held, F32)]
        + [pltpu.VMEM(whole, F32)] * CHAINS,
        compiler_params=PARAMS,
        cost_estimate=cost(0, 28 << 20),
        name="far_cells",
    )(links, scale, ext, ghost, matrix, base)
    back = shifted(back, "domain", 1)
    sums = pl.pallas_call(
        near_sums_kernel,
        out_shape=jax.ShapeDtypeStruct((owned, LANES), F32),
        in_specs=[SM, VM, VM],
        out_specs=VM,
        scratch_shapes=[pltpu.VMEM((owned, LANES), F32)] * (CHAINS - 1),
        compiler_params=PARAMS,
        cost_estimate=cost(0, 14 << 20),
        name="near_sums",
    )(links, products, sums)
    return sums, back


def add_back(nodes, target, back_ref, factor, picked=None):
    def body(step, _):
        at = [step * 16 + k for k in range(16)]
        rows = [pl.ds(nodes[i], 1) for i in at]
        new = [target[r, :] + factor * back_ref[pl.ds(i, 1), :] for i, r in zip(at, rows)]
        for i, r, value in zip(at, rows, new):
            target[r, :] = value
            if picked is not None:
                picked[pl.ds(i, 1), :] = value
        return 0

    lax.fori_loop(0, nodes.shape[0] // 16, body, 0)


def first_kernel(nodes, sums_ref, back_ref, potential_ref, base_ref, ext_ref, edge_ref, picked, term):
    owned = sums_ref.shape[0]
    term[...] = sums_ref[...] * (1.0 / HALF_WIDTH)
    add_back(nodes, term, back_ref, 1.0 / HALF_WIDTH, picked)
    edge_ref[...] = picked[...].astype(BF16)
    rows_out(lambda here: term[here, :], potential_ref, owned, base_ref, ext_ref)


def first_term(nodes, sums, back, potential):
    owned, plane = sums.shape[0], nodes.shape[0]
    return pl.pallas_call(
        first_kernel,
        out_shape=prepared_shapes(owned, plane),
        in_specs=[SM, VM, VM, VM],
        out_specs=(VM, VM, VM),
        scratch_shapes=[pltpu.VMEM((plane, LANES), F32), pltpu.VMEM(sums.shape, F32)],
        compiler_params=PARAMS,
        name="first_term",
    )(nodes, sums, back, potential)


def second_kernel(band, nodes, sums_ref, back_ref, previous_ref, *refs):
    pieces, rest_ref, total = refs[:-2], refs[-2], refs[-1]
    total[...] = sums_ref[...] * (2.0 / HALF_WIDTH) - previous_ref[...].astype(F32)
    add_back(nodes, total, back_ref, 2.0 / HALF_WIDTH)
    count = len(pieces)
    rows = total.shape[0] // count
    for k, piece in enumerate(pieces):
        start = pl.multiple_of(lax.rem(band[0] + k, count) * rows, rows)
        part = total[pl.ds(start, rows), :].astype(BF16)
        piece[...] = part
        if k:
            rest_ref[(k - 1) * rows : k * rows, :] = part


def second_term(band, nodes, sums, back, previous, count):
    owned = sums.shape[0]
    rows = owned // count
    made = pl.pallas_call(
        second_kernel,
        out_shape=[jax.ShapeDtypeStruct((rows, LANES), BF16)] * count
        + [jax.ShapeDtypeStruct((owned - rows, LANES), BF16)],
        in_specs=[SM, SM, VM, VM, VM],
        out_specs=[VM] * (count + 1),
        scratch_shapes=[pltpu.VMEM(sums.shape, F32)],
        compiler_params=PARAMS,
        name="second_term",
    )(band, nodes, sums, back, previous)
    return made[:count], made[count]


def gram_kernel(band, *refs):
    pieces, out_ref, held = refs[:-2], refs[-2], refs[-1]
    count = len(pieces)
    for s, piece in enumerate(pieces):
        held[lax.rem(band[0] + (count - s), count)] = piece[...]
    at = 0
    for i in range(count):
        for j in range(i + 1):
            out_ref[at : at + LANES, :] = lax.dot_general(
                held[i], held[j], (((0,), (0,)), ((), ())), preferred_element_type=F32
            )
            at += LANES


def partial_gram(band, pieces):
    count = len(pieces)
    blocks = count * (count + 1) // 2
    return pl.pallas_call(
        gram_kernel,
        out_shape=jax.ShapeDtypeStruct((blocks * LANES, LANES), F32),
        in_specs=[SM] + [VM] * count,
        out_specs=VM,
        scratch_shapes=[pltpu.VMEM((count,) + pieces[0].shape, BF16)],
        compiler_params=PARAMS,
        name="partial_gram",
    )(band, *pieces)


def paired(value, axis, mask):
    count = lax.axis_size(axis)
    return lax.ppermute(value, axis, [(i, i ^ mask) for i in range(count)])


def chunk(value, count, index):
    rows = value.shape[0] // count
    return lax.dynamic_slice_in_dim(value, index * rows, rows, 0)


def reduced(value):
    me = lax.axis_index("domain")
    side, place = me % 2, me // 2
    half = chunk(value, 2, side) + paired(chunk(value, 2, 1 - side), "domain", 1)
    total = chunk(half, 4, place)
    for part in [paired(chunk(half, 4, place ^ m), "domain", 2 * m) for m in (1, 2, 3)]:
        total = total + part
    return total


def gathered_back(total):
    me = lax.axis_index("domain")
    side, place = me % 2, me // 2
    parts = jnp.stack([total] + [paired(total, "domain", 2 * m) for m in (1, 2, 3)])
    half = parts[place ^ jnp.arange(4)].reshape(-1, LANES)
    other = paired(half, "domain", 1)
    pair = jnp.where(side == 0, jnp.stack([half, other]), jnp.stack([other, half]))
    return pair.reshape(-1, LANES)


def passed_up(rests, firsts, held):
    rows = firsts[held].shape[0]
    count = lax.axis_size("band")
    onward = jnp.concatenate([rests[held][rows:], firsts[held]])
    return lax.ppermute(onward, "band", [(i, i + 1) for i in range(held, count - 1)])


def ordered(*values):
    return lax.optimization_barrier(values)


def summed_beside(gram, rests, firsts):
    count = lax.axis_size("band")
    split = lax.axis_size("domain") == 8 and count == 4
    total = reduced(gram) if split else lax.psum(gram, "domain")
    first = passed_up(rests, firsts, 0)
    total, first = ordered(total, first)
    rests.append(first)
    if split:
        for mask in (1, 2):
            total = total + paired(total, "band", mask)
    else:
        total = lax.psum(total, "band")
    for held in range(1, count - 1):
        total, rests[held] = ordered(total, rests[held])
        onward = passed_up(rests, firsts, held)
        if held == 1 and split:
            total = gathered_back(total)
        rests.append(onward)
    return total


def small_inverse(tiles, lane):
    count, tiles, done = len(tiles), list(tiles), []
    sub = lax.broadcasted_iota(jnp.int32, tiles[0].shape, 0)

    def along_lanes(tile, column):
        return jnp.broadcast_to(tile[:, column : column + 1], tile.shape)

    def along_rows(tile, row):
        return jnp.broadcast_to(tile[row : row + 1, :], tile.shape)

    for p in range(count):
        base = 8 * p
        group = (lane >= base) & (lane < base + 8)
        columns = [along_lanes(tiles[p], base + m) for m in range(8)]
        entry = {(i, j): along_rows(columns[j], i) for j in range(8) for i in range(j, 8)}
        start = jnp.where(group, (lane - base == sub).astype(F32), tiles[p])
        solved = [along_rows(start, i) for i in range(8)]
        following = None
        if p + 1 < count:
            ahead = [along_lanes(tiles[p + 1], base + m) for m in range(8)]
            following = jnp.where(group, 0.0, tiles[p + 1])
        inverse, factor = [], {}
        for j in range(8):
            pivot = 1.0 / entry[j, j]
            inverse.append(pivot)
            for i in range(j + 1, 8):
                factor[i, j] = entry[i, j] * pivot
            for i in range(j + 1, 8):
                for k in range(j + 1, i + 1):
                    entry[i, k] = entry[i, k] - factor[i, j] * entry[k, j]
                solved[i] = solved[i] - factor[i, j] * solved[j]
            if following is not None:
                scaled = ahead[j] * pivot
                following = following - scaled * solved[j]
                for m in range(j + 1, 8):
                    ahead[m] = ahead[m] - scaled * entry[m, j]
        result = solved[0] * lax.rsqrt(entry[0, 0])
        for i in range(1, 8):
            result = jnp.where(sub == i, solved[i] * lax.rsqrt(entry[i, i]), result)
        done.append(jnp.where(lane <= base + sub, result, 0.0))
        if p + 2 < count:
            back = [None] * 8
            for i in range(7, -1, -1):
                value = solved[i] * inverse[i]
                for k in range(i + 1, 8):
                    value = value - factor[k, i] * back[k]
                back[i] = value
            for i in range(p + 2, count):
                value = jnp.where(group, 0.0, tiles[i])
                for m in range(8):
                    value = value - along_lanes(tiles[i], base + m) * back[m]
                tiles[i] = value
        if following is not None:
            tiles[p + 1] = following
    return done


def exact_dot(a, b, dims=(((1,), (0,)), ((), ()))):
    return lax.dot_general(a, b, dims, precision=EXACT, preferred_element_type=F32)


def inverse_kernel(over, packed_ref, out_ref, work, small):
    size = work.shape[0]
    blocks = size // LANES
    at = 0
    for i in range(blocks):
        for j in range(i + 1):
            block = packed_ref[at : at + LANES, :] * over
            work[i * LANES : (i + 1) * LANES, j * LANES : (j + 1) * LANES] = block
            if i != j:
                work[j * LANES : (j + 1) * LANES, i * LANES : (i + 1) * LANES] = block.T
            at += LANES
    out_ref[...] = jnp.zeros_like(out_ref)
    lane = lax.broadcasted_iota(jnp.int32, (8, LANES), 1)

    def step(k, _):
        base = pl.multiple_of(k * LANES, LANES)
        tiles = [
            work[pl.ds(pl.multiple_of(base + 8 * i, 8), 8), pl.ds(base, LANES)]
            for i in range(LANES // 8)
        ]
        for i, tile in enumerate(small_inverse(tiles, lane)):
            small[8 * i : 8 * i + 8, :] = tile
        for which in range(blocks):

            @pl.when(k == which)
            def _():
                a, b = which * LANES, (which + 1) * LANES
                diagonal = small[...]
                out_ref[a:b, a:b] = diagonal
                if which:
                    left = exact_dot(diagonal, work[a:b, 0:a])
                    out_ref[a:b, 0:a] = left
                if b < size:
                    right = exact_dot(diagonal, work[a:b, b:size])
                    column = exact_dot(work[b:size, a:b], diagonal, (((1,), (1,)), ((), ())))
                    work[b:size, b:size] = work[b:size, b:size] - exact_dot(column, right)
                    work[b:size, a:b] = -exact_dot(column, diagonal)
                    if which:
                        work[b:size, 0:a] = work[b:size, 0:a] - exact_dot(column, left)

        return 0

    lax.fori_loop(0, blocks, step, 0)


def inverse_factor(packed, size, over):
    return pl.pallas_call(
        functools.partial(inverse_kernel, over),
        out_shape=jax.ShapeDtypeStruct((size, size), F32),
        in_specs=[VM],
        out_specs=VM,
        scratch_shapes=[pltpu.VMEM((size, size), F32), pltpu.VMEM((LANES, LANES), F32)],
        compiler_params=PARAMS,
        cost_estimate=cost(0, 70 << 20),
        name="inverse_factor",
    )(packed)


def output_kernel(band, factor_ref, *refs):
    out_ref, high_ref, low_ref = refs[-3:]
    count = factor_ref.shape[0] // LANES
    firsts, rests = refs[:count], refs[count:-3]
    j = pl.program_id(0)

    @pl.when(j == 0)
    def _():
        for s in range(count):
            source = band[0] - s
            column = pl.multiple_of(jnp.maximum(source, 0) * LANES, LANES)
            row = pl.multiple_of(band[0] * LANES, LANES)
            block = factor_ref[pl.ds(row, LANES), pl.ds(column, LANES)]
            block = jnp.where(source >= 0, block, 0.0)
            high = block.astype(BF16)
            high_ref[s] = high
            low_ref[s] = (block - high.astype(F32)).astype(BF16)

    def put(pieces):
        total = None
        dims = (((1,), (1,)), ((), ()))
        for s, piece in enumerate(pieces):
            for factor in (high_ref, low_ref):
                part = lax.dot_general(piece, factor[s], dims, preferred_element_type=F32)
                total = part if total is None else total + part
        out_ref[...] = total

    rows = out_ref.shape[0]

    @pl.when(j == 0)
    def _():
        put([piece[...] for piece in firsts])

    @pl.when(j > 0)
    def _():
        here = pl.ds(pl.multiple_of((j - 1) * rows, rows), rows)
        put([piece[here, :] for piece in rests])


def output(band, factor, firsts, rests):
    count = len(firsts)
    rows = firsts[0].shape[0]
    return pl.pallas_call(
        output_kernel,
        out_shape=jax.ShapeDtypeStruct((rows * count, LANES), F32),
        grid_spec=pltpu.PrefetchScalarGridSpec(
            num_scalar_prefetch=1,
            grid=(count,),
            in_specs=[VM] * (1 + 2 * count),
            out_specs=pl.BlockSpec((rows, LANES), lambda j, band: (lax.rem(band[0] + j, count), 0)),
            scratch_shapes=[pltpu.VMEM((count, LANES, LANES), BF16)] * 2,
        ),
        compiler_params=PARAMS,
        name="output",
    )(band, factor, *firsts, *rests)


def shards(states_block, cell_matrix, cell_scale, potential, connectivity, boundary_nodes):
    owned = states_block.shape[0]
    count = lax.axis_size("band")
    band = lax.axis_index("band").astype(jnp.int32).reshape(1)
    levels = potential.reshape(owned // LANES, LANES)

    operator = functools.partial(apply_operator, connectivity, cell_scale, cell_matrix)
    sums, back = operator(*prepare(boundary_nodes, states_block, levels))
    sums, back = operator(*first_term(boundary_nodes, sums, back, levels))
    pieces, rest = second_term(band, boundary_nodes, sums, back, states_block, count)

    firsts = [pieces[0]] + [shifted(pieces[s], "band", s) for s in range(1, count)]
    firsts = list(ordered(*firsts))
    rests = [rest]
    packed = summed_beside(partial_gram(band, firsts), rests, firsts)
    factor = inverse_factor(packed, count * LANES, 1.0 / (owned * lax.axis_size("domain")))
    return output(band, factor, firsts, rests)


def solution(mesh):
    return jax.shard_map(
        shards,
        mesh=mesh,
        in_specs=(
            P("domain", "band"),
            P(),
            P("domain"),
            P("domain"),
            P("domain", None),
            P("domain"),
        ),
        out_specs=P("domain", "band"),
        check_vma=False,
    )
```

time: 176 us -> 152 us (0.86)
  the two profiles are of different devices: /device:TPU:17 before, /device:TPU:20 now
where the time goes in v2:
time: 152 us
  Pallas kernels  68.1 us (45%)
  waiting for transfers between devices  44.8 us (29%)
  starting transfers between devices  30.2 us (20%)
  local copies, waits for them, and re-layouts  6.29 us (4%)
  other arithmetic  2.03 us (1%)
    pallas_call x1, Pallas kernels, inverse_factor(): pl.pallas_call(functools.partial(inverse_kernel, over), out_shape=jax.Sha...  20.9 us
    pallas_call x2, Pallas kernels, apply_operator(): pl.pallas_call(far_cells_kernel, out_shape=(jax.ShapeDtypeStruct((owned,...  18.3 us
    ppermute x7, waiting for transfers between devices, shifted(): lax.ppermute(value, axis, [(i, (i + steps) % count) for i in range(count)])  17 us
    ppermute x3, waiting for transfers between devices, passed_up(): lax.ppermute(onward, 'band', [(i, i + 1) for i in range(held, count - 1)])  15.4 us
    ppermute x3, starting transfers between devices, passed_up(): lax.ppermute(onward, 'band', [(i, i + 1) for i in range(held, count - 1)])  12.9 us
    ppermute x10, waiting for transfers between devices, paired(): return lax.ppermute(value, axis, [(i, i ^ mask) for i in range(count)])  12.5 us
    pallas_call x2, Pallas kernels, apply_operator(): pl.pallas_call(near_sums_kernel, out_shape=jax.ShapeDtypeStruct((owned, L...  10.8 us
    ppermute x10, starting transfers between devices, paired(): return lax.ppermute(value, axis, [(i, i ^ mask) for i in range(count)])  10.3 us
  transfers between devices with their start and end apart: 20, of which 10 were waited for; matrix products, arithmetic and copies ran while one was open for 2% of the time, Pallas kernels for 27%

profile of v2, /device:TPU:20, one launch (start us, length us, event | category | flops | bytes accessed | tf_op | source)
XLA Modules:
  0.0 151.8 jit_solution(14884457951349918255)
XLA Ops:
  0.0 1.2 copy-done.2
  2.6 1.4 prepare.1
  7.3 4.6 %near_products.2.products_ref = f32[8,344,128]{2,1,0:T(8,128)S(1)} custom-call(s32[16,343]{1,0:T(8,128)S(1)} %copy-done.4, f32[16]{0:T(128)S(1)} %copy-done.10, f32[3744,128]{1,0:T(8,128)S(1)} %get-tuple-element.35.ext_ref, bf16[343,343]{1,0:T(8,128)(2,1)S(1)} %copy-done), custom_call_target="tpu_custom_call" | custom-call | bytes 14680064 | tf_op jit(solution)/shard_map/near_products/pallas_call | solution.py:157
  11.9 9.2 %far_cells.2 = (f32[3456,128]{1,0:T(8,128)S(1)}, f32[288,128]{1,0:T(8,128)S(1)}) custom-call(s32[16,343]{1,0:T(8,128)S(1)} %copy-done.5, f32[16]{0:T(128)S(1)} %copy-done.11, f32[3744,128]{1,0:T(8,128)S(1)} %get-tuple-element.35.ext_ref, bf16[288,128]{1,0:T(8,128)(2,1)S(1)} %collective-permute-done.ghost_ref, bf16[343,343]{1,0:T(8,128)(2,1)S(1)} %copy-done.1, ...), custom_call_target="tpu_custom_call" | custom-call | bytes 29360128 | tf_op jit(solution)/shard_map/far_cells/pallas_call | solution.py:168
  21.1 5.4 %near_sums.2.sums_ref = f32[3456,128]{1,0:T(8,128)S(1)} custom-call(s32[16,343]{1,0:T(8,128)S(1)} %copy-done.5, f32[8,344,128]{2,1,0:T(8,128)S(1)} %near_products.2.products_ref, f32[3456,128]{1,0:T(8,128)S(1)} %get-tuple-element.39.start_ref), custom_call_target="tpu_custom_call" | custom-call | bytes 14680064 | tf_op jit(solution)/shard_map/near_sums/pallas_call | solution.py:183
  26.6 1.8 %first_term.1 = (f32[3744,128]{1,0:T(8,128)S(1)}, f32[3744,128]{1,0:T(8,128)S(1)}, bf16[288,128]{1,0:T(8,128)(2,1)S(1)}) custom-call(s32[288]{0:T(512)S(1)} %copy-done.9, f32[3456,128]{1,0:T(8,128)S(1)} %near_sums.2.sums_ref, f32[288,128]{1,0:T(8,128)S(1)} %collective-permute-done.1.back_ref, f32[27,128]{1,0:T(8,128)S(1)} %bitcast.14), custom_call_target="tpu_custom_call" | custom-call | tf_op jit(solution)/shard_map/first_term/pallas_call | solution.py:220
  28.3 2.7 %collective-permute-start.2 = (bf16[288,128]{1,0:T(8,128)(2,1)S(1)}, bf16[288,128]{1,0:T(8,128)(2,1)S(1)}, u32[]{:S(2)}, u32[]{:S(2)}) collective-permute-start(bf16[288,128]{1,0:T(8,128)(2,1)S(1)} %get-tuple-element.41), channel_id=1, source_target_pairs={{0,28},{4,0},{8,4},{12,8},{16,12},{20,16},{24,20},{28,24},{1,29},{... | collective-permute-start | bytes 221192 | tf_op jit(solution)/shard_map/ppermute | solution.py:24
  31.0 4.6 %near_products.3.products_ref = f32[8,344,128]{2,1,0:T(8,128)S(1)} custom-call(s32[16,343]{1,0:T(8,128)S(1)} %copy-done.5, f32[16]{0:T(128)S(1)} %copy-done.11, f32[3744,128]{1,0:T(8,128)S(1)} %get-tuple-element.42.ext_ref, bf16[343,343]{1,0:T(8,128)(2,1)S(1)} %copy-done.1), custom_call_target="tpu_custom_call" | custom-call | bytes 14680064 | tf_op jit(solution)/shard_map/near_products/pallas_call | solution.py:157
  35.5 9.2 %far_cells.3 = (f32[3456,128]{1,0:T(8,128)S(1)}, f32[288,128]{1,0:T(8,128)S(1)}) custom-call(s32[16,343]{1,0:T(8,128)S(1)} %copy-done.5, f32[16]{0:T(128)S(1)} %copy-done.11, f32[3744,128]{1,0:T(8,128)S(1)} %get-tuple-element.42.ext_ref, bf16[288,128]{1,0:T(8,128)(2,1)S(1)} %collective-permute-done.2.ghost_ref, bf16[343,343]{1,0:T(8,128)(2,1)S(1)} %copy-done.1, ...), custom_call_target="tpu_custom_call" | custom-call | bytes 29360128 | tf_op jit(solution)/shard_map/far_cells/pallas_call | solution.py:168
  44.8 5.4 %near_sums.3.sums_ref = f32[3456,128]{1,0:T(8,128)S(1)} custom-call(s32[16,343]{1,0:T(8,128)S(1)} %copy-done.5, f32[8,344,128]{2,1,0:T(8,128)S(1)} %near_products.3.products_ref, f32[3456,128]{1,0:T(8,128)S(1)} %get-tuple-element.46.start_ref), custom_call_target="tpu_custom_call" | custom-call | bytes 14680064 | tf_op jit(solution)/shard_map/near_sums/pallas_call | solution.py:183
  50.2 1.4 second_term.1
  51.7 1.6 %collective-permute-start.4 = (bf16[864,128]{1,0:T(8,128)(2,1)S(1)}, bf16[864,128]{1,0:T(8,128)(2,1)S(1)}, u32[]{:S(2)}, u32[]{:S(2)}) collective-permute-start(bf16[864,128]{1,0:T(8,128)(2,1)S(1)} %get-tuple-element.49), channel_id=1, source_target_pairs={{0,1},{1,2},{2,3},{3,0},{4,5},{5,6},{6,7},{7,4},{8,9},{9,10},{10,1... | collective-permute-start | bytes 663560 | tf_op jit(solution)/shard_map/ppermute | solution.py:24
  53.6 1.3 collective-permute-start.6
  55.0 14.5 %collective-permute-done.4.refs_1_ = bf16[864,128]{1,0:T(8,128)(2,1)S(1)} collective-permute-done((bf16[864,128]{1,0:T(8,128)(2,1)S(1)}, bf16[864,128]{1,0:T(8,128)(2,1)S(1)}, u32[]{:S(2)}, u32[]{:S(2)}) %collective-permute-start.4) | collective-permute-done | bytes 221216 | tf_op jit(solution)/shard_map/ppermute | solution.py:24
  69.5 2.4 %collective-permute-done.6.refs_3_ = bf16[864,128]{1,0:T(8,128)(2,1)S(1)} collective-permute-done((bf16[864,128]{1,0:T(8,128)(2,1)S(1)}, bf16[864,128]{1,0:T(8,128)(2,1)S(1)}, u32[]{:S(2)}, u32[]{:S(2)}) %collective-permute-start.6) | collective-permute-done | bytes 221216 | tf_op jit(solution)/shard_map/ppermute | solution.py:24
  73.0 4.5 %collective-permute-start.11 = (bf16[2592,128]{1,0:T(8,128)(2,1)S(1)}, bf16[2592,128]{1,0:T(8,128)(2,1)S(1)}, u32[]{:S(2)}, u32[]{:S(2)}) collective-permute-start(bf16[2592,128]{1,0:T(8,128)(2,1)S(1)} %pad_maximum_fusion), channel_id=1, source_target_pairs={{0,1},{1,2},{2,3},{4,5},{5,6},{6,7},{8,9},{9,10},{10,11},{12,13},{... | collective-permute-start | bytes 1990664 | tf_op jit(solution)/shard_map/ppermute | solution.py:323
  78.3 1.4 collective-permute-start.10
  80.2 1.5 collective-permute-start.9
  81.8 2.9 %collective-permute-done.10 = f32[160,128]{1,0:T(8,128)S(1)} collective-permute-done((f32[160,128]{1,0:T(8,128)}, f32[160,128]{1,0:T(8,128)S(1)}, u32[]{:S(2)}, u32[]{:S(2)}) %collective-permute-start.10) | collective-permute-done | bytes 81952 | tf_op jit(solution)/shard_map/ppermute | solution.py:291
  86.7 6.3 %collective-permute-done.11.refs_5_ = bf16[2592,128]{1,0:T(8,128)(2,1)S(1)} collective-permute-done((bf16[2592,128]{1,0:T(8,128)(2,1)S(1)}, bf16[2592,128]{1,0:T(8,128)(2,1)S(1)}, u32[]{:S(2)}, u32[]{:S(2)}) %collective-permute-start.11) | collective-permute-done | bytes 663584 | tf_op jit(solution)/shard_map/ppermute | solution.py:323
  93.0 1.9 %collective-permute-start.12 = (f32[160,128]{1,0:T(8,128)S(1)}, f32[160,128]{1,0:T(8,128)S(1)}, u32[]{:S(2)}, u32[]{:S(2)}) collective-permute-start(f32[160,128]{1,0:T(8,128)S(1)} %add_add_fusion), channel_id=1, source_target_pairs={{0,1},{1,0},{2,3},{3,2},{4,5},{5,4},{6,7},{7,6},{8,9},{9,8},{10,11... | collective-permute-start | bytes 245768 | tf_op jit(solution)/shard_map/ppermute | solution.py:291
  94.8 2.6 %collective-permute-done.12 = f32[160,128]{1,0:T(8,128)S(1)} collective-permute-done((f32[160,128]{1,0:T(8,128)S(1)}, f32[160,128]{1,0:T(8,128)S(1)}, u32[]{:S(2)}, u32[]{:S(2)}) %collective-permute-start.12) | collective-permute-done | bytes 81952 | tf_op jit(solution)/shard_map/ppermute | solution.py:291
  97.4 1.2 collective-permute-start.13
  98.7 4.2 %collective-permute-done.13 = f32[160,128]{1,0:T(8,128)S(1)} collective-permute-done((f32[160,128]{1,0:T(8,128)S(1)}, f32[160,128]{1,0:T(8,128)S(1)}, u32[]{:S(2)}, u32[]{:S(2)}) %collective-permute-start.13) | collective-permute-done | bytes 81952 | tf_op jit(solution)/shard_map/ppermute | solution.py:291
  102.9 1.6 %collective-permute-start.14 = (f32[160,128]{1,0:T(8,128)S(1)}, f32[160,128]{1,0:T(8,128)S(1)}, u32[]{:S(2)}, u32[]{:S(2)}) collective-permute-start(f32[160,128]{1,0:T(8,128)S(1)} %add.64), channel_id=1, source_target_pairs={{0,8},{4,12},{8,0},{12,4},{16,24},{20,28},{24,16},{28,20},{1,9},{5... | collective-permute-start | bytes 245768 | tf_op jit(solution)/shard_map/ppermute | solution.py:291
  105.0 1.5 collective-permute-start.16
  107.4 4.2 %collective-permute-start.18 = (bf16[2592,128]{1,0:T(8,128)(2,1)}, bf16[2592,128]{1,0:T(8,128)(2,1)S(1)}, u32[]{:S(2)}, u32[]{:S(2)}) collective-permute-start(bf16[2592,128]{1,0:T(8,128)(2,1)} %pad_maximum_fusion.1), channel_id=1, source_target_pairs={{1,2},{2,3},{5,6},{6,7},{9,10},{10,11},{13,14},{14,15},{17,18},{18... | collective-permute-start | bytes 1990664 | tf_op jit(solution)/shard_map/ppermute | solution.py:323
  112.3 1.6 %collective-permute-done.17 = f32[640,128]{1,0:T(8,128)S(1)} collective-permute-done((f32[640,128]{1,0:T(8,128)S(1)}, f32[640,128]{1,0:T(8,128)S(1)}, u32[]{:S(2)}, u32[]{:S(2)}) %collective-permute-start.17) | collective-permute-done | bytes 327712 | tf_op jit(solution)/shard_map/ppermute | solution.py:291
  114.0 9.1 %collective-permute-done.18.refs_6_ = bf16[2592,128]{1,0:T(8,128)(2,1)S(1)} collective-permute-done((bf16[2592,128]{1,0:T(8,128)(2,1)}, bf16[2592,128]{1,0:T(8,128)(2,1)S(1)}, u32[]{:S(2)}, u32[]{:S(2)}) %collective-permute-start.18) | collective-permute-done | bytes 663584 | tf_op jit(solution)/shard_map/ppermute | solution.py:323
  123.2 4.2 %collective-permute-start.19 = (bf16[2592,128]{1,0:T(8,128)(2,1)S(1)}, bf16[2592,128]{1,0:T(8,128)(2,1)S(1)}, u32[]{:S(2)}, u32[]{:S(2)}) collective-permute-start(bf16[2592,128]{1,0:T(8,128)(2,1)S(1)} %pad_maximum_fusion.2), channel_id=1, source_target_pairs={{2,3},{6,7},{10,11},{14,15},{18,19},{22,23},{26,27},{30,31}} | collective-permute-start | bytes 1990664 | tf_op jit(solution)/shard_map/ppermute | solution.py:323
  127.4 20.9 %inverse_factor.1.factor_ref = f32[512,512]{1,0:T(8,128)S(1)} custom-call(f32[1280,128]{1,0:T(8,128)S(1)} %bitcast.12), custom_call_target="tpu_custom_call" | custom-call | bytes 73400320 | tf_op jit(solution)/shard_map/inverse_factor/pallas_call | solution.py:458
  148.3 3.5 %output.1 = f32[3456,128]{1,0:T(8,128)} custom-call(s32[1]{0:T(128)} %bitcast.band, f32[512,512]{1,0:T(8,128)S(1)} %inverse_factor.1.factor_ref, bf16[864,128]{1,0:T(8,128)(2,1)S(1)} %get-tuple-element.52.refs_0_, bf16[864,128]{1,0:T(8,128)(2,1)S(1)} %collective-permute-done.4.refs_1_, bf16[864,128]{1,0:T(8,128)(2,1)S(1)} %collective-permute-done.5.refs_2_, ...), custom_call_target="tpu_custom_call" | custom-call | tf_op jit(solution)/shard_map/output/pallas_call | solution.py:512
  (61 shorter events, 11.9 us)
Async XLA Ops:
  0.0 1.2 copy-start.2
  1.2 0.7 copy-start.6
  1.9 0.7 copy-start.8
  4.0 7.8 %collective-permute-start = (bf16[288,128]{1,0:T(8,128)(2,1)S(1)}, bf16[288,128]{1,0:T(8,128)(2,1)S(1)}, u32[]{:S(2)}, u32[]{:S(2)}) collective-permute-start(bf16[288,128]{1,0:T(8,128)(2,1)S(1)} %get-tuple-element.34), channel_id=1, source_target_pairs={{0,28},{4,0},{8,4},{12,8},{16,12},{20,16},{24,20},{28,24},{1,29},{... | collective-permute-start | bytes 221192 | tf_op jit(solution)/shard_map/ppermute | solution.py:24
  4.9 1.0 copy-start
  5.9 0.7 copy-start.4
  6.6 0.7 copy-start.10
  7.2 4.6 %copy-start.1 = (bf16[343,343]{1,0:T(8,128)(2,1)S(1)}, bf16[343,343]{1,0:T(8,128)(2,1)}, u32[]{:S(2)}) copy-start(bf16[343,343]{1,0:T(8,128)(2,1)} %matrix_ref.7) | copy-start | bytes 705898
  7.3 4.6 %copy-start.5 = (s32[16,343]{1,0:T(8,128)S(1)}, s32[16,343]{1,0:T(8,128)}, u32[]{:S(2)}) copy-start(s32[16,343]{1,0:T(8,128)} %links.11) | copy-start | bytes 65860
  7.3 4.6 %copy-start.11 = (f32[16]{0:T(128)S(1)}, f32[16]{0:T(128)}, u32[]{:S(2)}) copy-start(f32[16]{0:T(128)} %scale.7) | copy-start | bytes 196
  21.0 5.5 %collective-permute-start.1 = (f32[288,128]{1,0:T(8,128)S(1)}, f32[288,128]{1,0:T(8,128)S(1)}, u32[]{:S(2)}, u32[]{:S(2)}) collective-permute-start(f32[288,128]{1,0:T(8,128)S(1)} %get-tuple-element.40), channel_id=1, source_target_pairs={{0,4},{4,8},{8,12},{12,16},{16,20},{20,24},{24,28},{28,0},{1,5},{5... | collective-permute-start | bytes 442376 | tf_op jit(solution)/shard_map/ppermute | solution.py:24
  21.1 5.5 %copy-start.7 = (f32[3456]{0:T(1024)S(1)}, f32[3456]{0:T(1024)}, u32[]{:S(2)}) copy-start(f32[3456]{0:T(1024)} %param.9) | copy-start | bytes 41476
  21.1 5.4 %copy-start.9 = (s32[288]{0:T(512)S(1)}, s32[288]{0:T(512)}, u32[]{:S(2)}) copy-start(s32[288]{0:T(512)} %nodes.5) | copy-start | bytes 3460
  28.3 7.2 %collective-permute-start.2 = (bf16[288,128]{1,0:T(8,128)(2,1)S(1)}, bf16[288,128]{1,0:T(8,128)(2,1)S(1)}, u32[]{:S(2)}, u32[]{:S(2)}) collective-permute-start(bf16[288,128]{1,0:T(8,128)(2,1)S(1)} %get-tuple-element.41), channel_id=1, source_target_pairs={{0,28},{4,0},{8,4},{12,8},{16,12},{20,16},{24,20},{28,24},{1,29},{... | collective-permute-start | bytes 221192 | tf_op jit(solution)/shard_map/ppermute | solution.py:24
  44.7 5.5 %collective-permute-start.3 = (f32[288,128]{1,0:T(8,128)S(1)}, f32[288,128]{1,0:T(8,128)S(1)}, u32[]{:S(2)}, u32[]{:S(2)}) collective-permute-start(f32[288,128]{1,0:T(8,128)S(1)} %get-tuple-element.47), channel_id=1, source_target_pairs={{0,4},{4,8},{8,12},{12,16},{16,20},{20,24},{24,28},{28,0},{1,5},{5... | collective-permute-start | bytes 442376 | tf_op jit(solution)/shard_map/ppermute | solution.py:24
  44.8 5.5 %copy-start.3 = (bf16[3456,128]{1,0:T(8,128)(2,1)S(1)}, bf16[3456,128]{1,0:T(8,128)(2,1)}, u32[]{:S(2)}) copy-start(bf16[3456,128]{1,0:T(8,128)(2,1)} %previous_ref.1) | copy-start | bytes 2654212
  51.7 17.9 %collective-permute-start.4 = (bf16[864,128]{1,0:T(8,128)(2,1)S(1)}, bf16[864,128]{1,0:T(8,128)(2,1)S(1)}, u32[]{:S(2)}, u32[]{:S(2)}) collective-permute-start(bf16[864,128]{1,0:T(8,128)(2,1)S(1)} %get-tuple-element.49), channel_id=1, source_target_pairs={{0,1},{1,2},{2,3},{3,0},{4,5},{5,6},{6,7},{7,4},{8,9},{9,10},{10,1... | collective-permute-start | bytes 663560 | tf_op jit(solution)/shard_map/ppermute | solution.py:24
  53.3 16.2 %collective-permute-start.5 = (bf16[864,128]{1,0:T(8,128)(2,1)S(1)}, bf16[864,128]{1,0:T(8,128)(2,1)S(1)}, u32[]{:S(2)}, u32[]{:S(2)}) collective-permute-start(bf16[864,128]{1,0:T(8,128)(2,1)S(1)} %get-tuple-element.50), channel_id=1, source_target_pairs={{0,2},{1,3},{2,0},{3,1},{4,6},{5,7},{6,4},{7,5},{8,10},{9,11},{10,... | collective-permute-start | bytes 663560 | tf_op jit(solution)/shard_map/ppermute | solution.py:24
  53.6 18.3 %collective-permute-start.6 = (bf16[864,128]{1,0:T(8,128)(2,1)S(1)}, bf16[864,128]{1,0:T(8,128)(2,1)S(1)}, u32[]{:S(2)}, u32[]{:S(2)}) collective-permute-start(bf16[864,128]{1,0:T(8,128)(2,1)S(1)} %get-tuple-element.51), channel_id=1, source_target_pairs={{0,3},{1,0},{2,1},{3,2},{4,7},{5,4},{6,5},{7,6},{8,11},{9,8},{10,9... | collective-permute-start | bytes 663560 | tf_op jit(solution)/shard_map/ppermute | solution.py:24
  72.9 4.7 %collective-permute-start.7 = (f32[640,128]{1,0:T(8,128)S(1)}, f32[640,128]{1,0:T(8,128)S(1)}, u32[]{:S(2)}, u32[]{:S(2)}) collective-permute-start(f32[640,128]{1,0:T(8,128)S(1)} %constant_dynamic-slice_fusion.3), channel_id=1, source_target_pairs={{0,4},{4,0},{8,12},{12,8},{16,20},{20,16},{24,28},{28,24},{1,5},{5... | collective-permute-start | bytes 983048 | tf_op jit(solution)/shard_map/ppermute | solution.py:291
  73.0 19.9 %collective-permute-start.11 = (bf16[2592,128]{1,0:T(8,128)(2,1)S(1)}, bf16[2592,128]{1,0:T(8,128)(2,1)S(1)}, u32[]{:S(2)}, u32[]{:S(2)}) collective-permute-start(bf16[2592,128]{1,0:T(8,128)(2,1)S(1)} %pad_maximum_fusion), channel_id=1, source_target_pairs={{0,1},{1,2},{2,3},{4,5},{5,6},{6,7},{8,9},{9,10},{10,11},{12,13},{... | collective-permute-start | bytes 1990664 | tf_op jit(solution)/shard_map/ppermute | solution.py:323
  78.3 6.4 %collective-permute-start.10 = (f32[160,128]{1,0:T(8,128)}, f32[160,128]{1,0:T(8,128)S(1)}, u32[]{:S(2)}, u32[]{:S(2)}) collective-permute-start(f32[160,128]{1,0:T(8,128)} %get-tuple-element.64), channel_id=1, source_target_pairs={{0,24},{4,28},{8,16},{12,20},{16,8},{20,12},{24,0},{28,4},{1,25},{... | collective-permute-start | bytes 245768 | tf_op jit(solution)/shard_map/ppermute | solution.py:291
  79.7 5.1 %collective-permute-start.8 = (f32[160,128]{1,0:T(8,128)S(1)}, f32[160,128]{1,0:T(8,128)S(1)}, u32[]{:S(2)}, u32[]{:S(2)}) collective-permute-start(f32[160,128]{1,0:T(8,128)S(1)} %get-tuple-element.63), channel_id=1, source_target_pairs={{0,8},{4,12},{8,0},{12,4},{16,24},{20,28},{24,16},{28,20},{1,9},{5... | collective-permute-start | bytes 245768 | tf_op jit(solution)/shard_map/ppermute | solution.py:291
  80.2 5.6 %collective-permute-start.9 = (f32[160,128]{1,0:T(8,128)S(1)}, f32[160,128]{1,0:T(8,128)}, u32[]{:S(2)}, u32[]{:S(2)}) collective-permute-start(f32[160,128]{1,0:T(8,128)S(1)} %get-tuple-element.65), channel_id=1, source_target_pairs={{0,16},{4,20},{8,24},{12,28},{16,0},{20,4},{24,8},{28,12},{1,17},{... | collective-permute-start | bytes 245768 | tf_op jit(solution)/shard_map/ppermute | solution.py:291
  93.0 4.4 %collective-permute-start.12 = (f32[160,128]{1,0:T(8,128)S(1)}, f32[160,128]{1,0:T(8,128)S(1)}, u32[]{:S(2)}, u32[]{:S(2)}) collective-permute-start(f32[160,128]{1,0:T(8,128)S(1)} %add_add_fusion), channel_id=1, source_target_pairs={{0,1},{1,0},{2,3},{3,2},{4,5},{5,4},{6,7},{7,6},{8,9},{9,8},{10,11... | collective-permute-start | bytes 245768 | tf_op jit(solution)/shard_map/ppermute | solution.py:291
  97.4 5.5 %collective-permute-start.13 = (f32[160,128]{1,0:T(8,128)S(1)}, f32[160,128]{1,0:T(8,128)S(1)}, u32[]{:S(2)}, u32[]{:S(2)}) collective-permute-start(f32[160,128]{1,0:T(8,128)S(1)} %add.63), channel_id=1, source_target_pairs={{0,2},{1,3},{2,0},{3,1},{4,6},{5,7},{6,4},{7,5},{8,10},{9,11},{10,... | collective-permute-start | bytes 245768 | tf_op jit(solution)/shard_map/ppermute | solution.py:291
  102.9 8.7 %collective-permute-start.14 = (f32[160,128]{1,0:T(8,128)S(1)}, f32[160,128]{1,0:T(8,128)S(1)}, u32[]{:S(2)}, u32[]{:S(2)}) collective-permute-start(f32[160,128]{1,0:T(8,128)S(1)} %add.64), channel_id=1, source_target_pairs={{0,8},{4,12},{8,0},{12,4},{16,24},{20,28},{24,16},{28,20},{1,9},{5... | collective-permute-start | bytes 245768 | tf_op jit(solution)/shard_map/ppermute | solution.py:291
  104.5 7.1 %collective-permute-start.15 = (f32[160,128]{1,0:T(8,128)S(1)}, f32[160,128]{1,0:T(8,128)S(1)}, u32[]{:S(2)}, u32[]{:S(2)}) collective-permute-start(f32[160,128]{1,0:T(8,128)S(1)} %add.64), channel_id=1, source_target_pairs={{0,16},{4,20},{8,24},{12,28},{16,0},{20,4},{24,8},{28,12},{1,17},{... | collective-permute-start | bytes 245768 | tf_op jit(solution)/shard_map/ppermute | solution.py:291
  105.0 6.6 %collective-permute-start.16 = (f32[160,128]{1,0:T(8,128)S(1)}, f32[160,128]{1,0:T(8,128)S(1)}, u32[]{:S(2)}, u32[]{:S(2)}) collective-permute-start(f32[160,128]{1,0:T(8,128)S(1)} %add.64), channel_id=1, source_target_pairs={{0,24},{4,28},{8,16},{12,20},{16,8},{20,12},{24,0},{28,4},{1,25},{... | collective-permute-start | bytes 245768 | tf_op jit(solution)/shard_map/ppermute | solution.py:291
  107.4 15.7 %collective-permute-start.18 = (bf16[2592,128]{1,0:T(8,128)(2,1)}, bf16[2592,128]{1,0:T(8,128)(2,1)S(1)}, u32[]{:S(2)}, u32[]{:S(2)}) collective-permute-start(bf16[2592,128]{1,0:T(8,128)(2,1)} %pad_maximum_fusion.1), channel_id=1, source_target_pairs={{1,2},{2,3},{5,6},{6,7},{9,10},{10,11},{13,14},{14,15},{17,18},{18... | collective-permute-start | bytes 1990664 | tf_op jit(solution)/shard_map/ppermute | solution.py:323
  112.2 1.7 %collective-permute-start.17 = (f32[640,128]{1,0:T(8,128)S(1)}, f32[640,128]{1,0:T(8,128)S(1)}, u32[]{:S(2)}, u32[]{:S(2)}) collective-permute-start(f32[640,128]{1,0:T(8,128)S(1)} %bitcast.15), channel_id=1, source_target_pairs={{0,4},{4,0},{8,12},{12,8},{16,20},{20,16},{24,28},{28,24},{1,5},{5... | collective-permute-start | bytes 983048 | tf_op jit(solution)/shard_map/ppermute | solution.py:291
  123.2 25.1 %collective-permute-start.19 = (bf16[2592,128]{1,0:T(8,128)(2,1)S(1)}, bf16[2592,128]{1,0:T(8,128)(2,1)S(1)}, u32[]{:S(2)}, u32[]{:S(2)}) collective-permute-start(bf16[2592,128]{1,0:T(8,128)(2,1)S(1)} %pad_maximum_fusion.2), channel_id=1, source_target_pairs={{2,3},{6,7},{10,11},{14,15},{18,19},{22,23},{26,27},{30,31}} | collective-permute-start | bytes 1990664 | tf_op jit(solution)/shard_map/ppermute | solution.py:323

commit v3 on v2

--- a/solution.py
+++ b/solution.py
@@ -329,22 +329,19 @@
 
 def summed_beside(gram, rests, firsts):
     count = lax.axis_size("band")
-    split = lax.axis_size("domain") == 8 and count == 4
-    total = reduced(gram) if split else lax.psum(gram, "domain")
-    first = passed_up(rests, firsts, 0)
-    total, first = ordered(total, first)
-    rests.append(first)
-    if split:
-        for mask in (1, 2):
-            total = total + paired(total, "band", mask)
-    else:
-        total = lax.psum(total, "band")
-    for held in range(1, count - 1):
-        total, rests[held] = ordered(total, rests[held])
-        onward = passed_up(rests, firsts, held)
-        if held == 1 and split:
-            total = gathered_back(total)
-        rests.append(onward)
+    if lax.axis_size("domain") != 8 or count != 4:
+        for held in range(count - 1):
+            rests.append(passed_up(rests, firsts, held))
+        return lax.psum(gram, ("domain", "band"))
+    rests.append(passed_up(rests, firsts, 0))
+    total = reduced(gram)
+    total = total + paired(total, "band", 1)
+    total, rests[1] = ordered(total, rests[1])
+    rests.append(passed_up(rests, firsts, 1))
+    total = total + paired(total, "band", 2)
+    total = gathered_back(total)
+    total, rests[2] = ordered(total, rests[2])
+    rests.append(passed_up(rests, firsts, 2))
     return total
 
 

time: 152 us -> 144 us (0.947)
  the two profiles are of different devices: /device:TPU:20 before, /device:TPU:26 now
where the time goes in v3:
time: 144 us; the launch traced here: 141 us
  Pallas kernels  68.1 us (47%)
  waiting for transfers between devices  42.5 us (30%)
  starting transfers between devices  22.1 us (15%)
  local copies, waits for them, and re-layouts  6.28 us (4%)
  other arithmetic  2.03 us (1%)
    pallas_call x1, Pallas kernels, inverse_factor(): pl.pallas_call(functools.partial(inverse_kernel, over), out_shape=jax.Sha...  20.9 us
    ppermute x10, waiting for transfers between devices, paired(): return lax.ppermute(value, axis, [(i, i ^ mask) for i in range(count)])  19.6 us
    ppermute x7, waiting for transfers between devices, shifted(): lax.ppermute(value, axis, [(i, (i + steps) % count) for i in range(count)])  18.4 us
    pallas_call x2, Pallas kernels, apply_operator(): pl.pallas_call(far_cells_kernel, out_shape=(jax.ShapeDtypeStruct((owned,...  18.3 us
    ppermute x10, starting transfers between devices, paired(): return lax.ppermute(value, axis, [(i, i ^ mask) for i in range(count)])  13.1 us
    pallas_call x2, Pallas kernels, apply_operator(): pl.pallas_call(near_sums_kernel, out_shape=jax.ShapeDtypeStruct((owned, L...  10.8 us
    pallas_call x2, Pallas kernels, apply_operator(): pl.pallas_call(near_products_kernel, out_shape=jax.ShapeDtypeStruct(held,...  9.12 us
    ppermute x7, starting transfers between devices, shifted(): lax.ppermute(value, axis, [(i, (i + steps) % count) for i in range(count)])  5.18 us
  transfers between devices with their start and end apart: 20, of which 12 were waited for; matrix products, arithmetic and copies ran while one was open for 2% of the time, Pallas kernels for 29%

profile of v3, /device:TPU:26, one launch (start us, length us, event | category | flops | bytes accessed | tf_op | source)
XLA Modules:
  0.0 141.4 jit_solution(9771022300796688773)
XLA Ops:
  2.6 1.4 prepare.1
  6.4 4.6 %near_products.2.products_ref = f32[8,344,128]{2,1,0:T(8,128)S(1)} custom-call(s32[16,343]{1,0:T(8,128)S(1)} %copy-done.4, f32[16]{0:T(128)S(1)} %copy-done.10, f32[3744,128]{1,0:T(8,128)S(1)} %get-tuple-element.33.ext_ref, bf16[343,343]{1,0:T(8,128)(2,1)S(1)} %copy-done), custom_call_target="tpu_custom_call" | custom-call | bytes 14680064 | tf_op jit(solution)/shard_map/near_products/pallas_call | solution.py:157
  11.0 9.2 %far_cells.2 = (f32[3456,128]{1,0:T(8,128)S(1)}, f32[288,128]{1,0:T(8,128)S(1)}) custom-call(s32[16,343]{1,0:T(8,128)S(1)} %copy-done.5, f32[16]{0:T(128)S(1)} %copy-done.11, f32[3744,128]{1,0:T(8,128)S(1)} %get-tuple-element.33.ext_ref, bf16[288,128]{1,0:T(8,128)(2,1)S(1)} %collective-permute-done.ghost_ref, bf16[343,343]{1,0:T(8,128)(2,1)S(1)} %copy-done.1, ...), custom_call_target="tpu_custom_call" | custom-call | bytes 29360128 | tf_op jit(solution)/shard_map/far_cells/pallas_call | solution.py:168
  20.7 5.4 %near_sums.2.sums_ref = f32[3456,128]{1,0:T(8,128)S(1)} custom-call(s32[16,343]{1,0:T(8,128)S(1)} %copy-done.5, f32[8,344,128]{2,1,0:T(8,128)S(1)} %near_products.2.products_ref, f32[3456,128]{1,0:T(8,128)S(1)} %get-tuple-element.37.start_ref), custom_call_target="tpu_custom_call" | custom-call | bytes 14680064 | tf_op jit(solution)/shard_map/near_sums/pallas_call | solution.py:183
  26.1 1.8 %first_term.1 = (f32[3744,128]{1,0:T(8,128)S(1)}, f32[3744,128]{1,0:T(8,128)S(1)}, bf16[288,128]{1,0:T(8,128)(2,1)S(1)}) custom-call(s32[288]{0:T(512)S(1)} %copy-done.9, f32[3456,128]{1,0:T(8,128)S(1)} %near_sums.2.sums_ref, f32[288,128]{1,0:T(8,128)S(1)} %collective-permute-done.1.back_ref, f32[27,128]{1,0:T(8,128)S(1)} %bitcast.14), custom_call_target="tpu_custom_call" | custom-call | tf_op jit(solution)/shard_map/first_term/pallas_call | solution.py:220
  27.9 1.3 collective-permute-start.2
  29.2 4.6 %near_products.3.products_ref = f32[8,344,128]{2,1,0:T(8,128)S(1)} custom-call(s32[16,343]{1,0:T(8,128)S(1)} %copy-done.5, f32[16]{0:T(128)S(1)} %copy-done.11, f32[3744,128]{1,0:T(8,128)S(1)} %get-tuple-element.40.ext_ref, bf16[343,343]{1,0:T(8,128)(2,1)S(1)} %copy-done.1), custom_call_target="tpu_custom_call" | custom-call | bytes 14680064 | tf_op jit(solution)/shard_map/near_products/pallas_call | solution.py:157
  33.8 9.2 %far_cells.3 = (f32[3456,128]{1,0:T(8,128)S(1)}, f32[288,128]{1,0:T(8,128)S(1)}) custom-call(s32[16,343]{1,0:T(8,128)S(1)} %copy-done.5, f32[16]{0:T(128)S(1)} %copy-done.11, f32[3744,128]{1,0:T(8,128)S(1)} %get-tuple-element.40.ext_ref, bf16[288,128]{1,0:T(8,128)(2,1)S(1)} %collective-permute-done.2.ghost_ref, bf16[343,343]{1,0:T(8,128)(2,1)S(1)} %copy-done.1, ...), custom_call_target="tpu_custom_call" | custom-call | bytes 29360128 | tf_op jit(solution)/shard_map/far_cells/pallas_call | solution.py:168
  43.8 5.4 %near_sums.3.sums_ref = f32[3456,128]{1,0:T(8,128)S(1)} custom-call(s32[16,343]{1,0:T(8,128)S(1)} %copy-done.5, f32[8,344,128]{2,1,0:T(8,128)S(1)} %near_products.3.products_ref, f32[3456,128]{1,0:T(8,128)S(1)} %get-tuple-element.44.start_ref), custom_call_target="tpu_custom_call" | custom-call | bytes 14680064 | tf_op jit(solution)/shard_map/near_sums/pallas_call | solution.py:183
  49.2 1.4 second_term.1
  50.9 1.7 %collective-permute-start.5 = (bf16[864,128]{1,0:T(8,128)(2,1)S(1)}, bf16[864,128]{1,0:T(8,128)(2,1)S(1)}, u32[]{:S(2)}, u32[]{:S(2)}) collective-permute-start(bf16[864,128]{1,0:T(8,128)(2,1)S(1)} %get-tuple-element.48), channel_id=1, source_target_pairs={{0,2},{1,3},{2,0},{3,1},{4,6},{5,7},{6,4},{7,5},{8,10},{9,11},{10,... | collective-permute-start | bytes 663560 | tf_op jit(solution)/shard_map/ppermute | solution.py:24
  53.1 4.3 %collective-permute-done.4.refs_1_ = bf16[864,128]{1,0:T(8,128)(2,1)S(1)} collective-permute-done((bf16[864,128]{1,0:T(8,128)(2,1)S(1)}, bf16[864,128]{1,0:T(8,128)(2,1)S(1)}, u32[]{:S(2)}, u32[]{:S(2)}) %collective-permute-start.4) | collective-permute-done | bytes 221216 | tf_op jit(solution)/shard_map/ppermute | solution.py:24
  57.4 14.1 %collective-permute-done.5.refs_2_ = bf16[864,128]{1,0:T(8,128)(2,1)S(1)} collective-permute-done((bf16[864,128]{1,0:T(8,128)(2,1)S(1)}, bf16[864,128]{1,0:T(8,128)(2,1)S(1)}, u32[]{:S(2)}, u32[]{:S(2)}) %collective-permute-start.5) | collective-permute-done | bytes 221216 | tf_op jit(solution)/shard_map/ppermute | solution.py:24
  72.4 1.5 %collective-permute-start.7 = (f32[640,128]{1,0:T(8,128)S(1)}, f32[640,128]{1,0:T(8,128)S(1)}, u32[]{:S(2)}, u32[]{:S(2)}) collective-permute-start(f32[640,128]{1,0:T(8,128)S(1)} %constant_dynamic-slice_fusion.3), channel_id=1, source_target_pairs={{0,4},{4,0},{8,12},{12,8},{16,20},{20,16},{24,28},{28,24},{1,5},{5... | collective-permute-start | bytes 983048 | tf_op jit(solution)/shard_map/ppermute | solution.py:291
  74.0 1.3 collective-permute-start.12
  76.1 1.8 %collective-permute-start.10 = (f32[160,128]{1,0:T(8,128)}, f32[160,128]{1,0:T(8,128)S(1)}, u32[]{:S(2)}, u32[]{:S(2)}) collective-permute-start(f32[160,128]{1,0:T(8,128)} %get-tuple-element.60), channel_id=1, source_target_pairs={{0,24},{4,28},{8,16},{12,20},{16,8},{20,12},{24,0},{28,4},{1,25},{... | collective-permute-start | bytes 245768 | tf_op jit(solution)/shard_map/ppermute | solution.py:291
  77.8 1.2 collective-permute-start.8
  79.5 2.9 %collective-permute-done.10 = f32[160,128]{1,0:T(8,128)S(1)} collective-permute-done((f32[160,128]{1,0:T(8,128)}, f32[160,128]{1,0:T(8,128)S(1)}, u32[]{:S(2)}, u32[]{:S(2)}) %collective-permute-start.10) | collective-permute-done | bytes 81952 | tf_op jit(solution)/shard_map/ppermute | solution.py:291
  84.7 2.5 %collective-permute-start.11 = (f32[160,128]{1,0:T(8,128)S(1)}, f32[160,128]{1,0:T(8,128)S(1)}, u32[]{:S(2)}, u32[]{:S(2)}) collective-permute-start(f32[160,128]{1,0:T(8,128)S(1)} %add_add_fusion), channel_id=1, source_target_pairs={{0,1},{1,0},{2,3},{3,2},{4,5},{5,4},{6,7},{7,6},{8,9},{9,8},{10,11... | collective-permute-start | bytes 245768 | tf_op jit(solution)/shard_map/ppermute | solution.py:291
  87.2 7.3 %collective-permute-done.11 = f32[160,128]{1,0:T(8,128)S(1)} collective-permute-done((f32[160,128]{1,0:T(8,128)S(1)}, f32[160,128]{1,0:T(8,128)S(1)}, u32[]{:S(2)}, u32[]{:S(2)}) %collective-permute-start.11) | collective-permute-done | bytes 81952 | tf_op jit(solution)/shard_map/ppermute | solution.py:291
  94.6 1.9 %collective-permute-start.13 = (f32[160,128]{1,0:T(8,128)S(1)}, f32[160,128]{1,0:T(8,128)S(1)}, u32[]{:S(2)}, u32[]{:S(2)}) collective-permute-start(f32[160,128]{1,0:T(8,128)S(1)} %add.63), channel_id=1, source_target_pairs={{0,2},{1,3},{2,0},{3,1},{4,6},{5,7},{6,4},{7,5},{8,10},{9,11},{10,... | collective-permute-start | bytes 245768 | tf_op jit(solution)/shard_map/ppermute | solution.py:291
  97.4 1.3 collective-permute-start.18
  98.6 1.3 collective-permute-done.13
  100.0 1.8 %collective-permute-start.14 = (f32[160,128]{1,0:T(8,128)S(1)}, f32[160,128]{1,0:T(8,128)S(1)}, u32[]{:S(2)}, u32[]{:S(2)}) collective-permute-start(f32[160,128]{1,0:T(8,128)S(1)} %add.64), channel_id=1, source_target_pairs={{0,8},{4,12},{8,0},{12,4},{16,24},{20,28},{24,16},{28,20},{1,9},{5... | collective-permute-start | bytes 245768 | tf_op jit(solution)/shard_map/ppermute | solution.py:291
  101.8 1.5 %collective-permute-start.15 = (f32[160,128]{1,0:T(8,128)S(1)}, f32[160,128]{1,0:T(8,128)S(1)}, u32[]{:S(2)}, u32[]{:S(2)}) collective-permute-start(f32[160,128]{1,0:T(8,128)S(1)} %add.64), channel_id=1, source_target_pairs={{0,16},{4,20},{8,24},{12,28},{16,0},{20,4},{24,8},{28,12},{1,17},{... | collective-permute-start | bytes 245768 | tf_op jit(solution)/shard_map/ppermute | solution.py:291
  104.5 2.7 %collective-permute-done.15 = f32[160,128]{1,0:T(8,128)S(1)} collective-permute-done((f32[160,128]{1,0:T(8,128)S(1)}, f32[160,128]{1,0:T(8,128)S(1)}, u32[]{:S(2)}, u32[]{:S(2)}) %collective-permute-start.15) | collective-permute-done | bytes 81952 | tf_op jit(solution)/shard_map/ppermute | solution.py:291
  107.2 1.5 %collective-permute-done.16 = f32[160,128]{1,0:T(8,128)S(1)} collective-permute-done((f32[160,128]{1,0:T(8,128)S(1)}, f32[160,128]{1,0:T(8,128)S(1)}, u32[]{:S(2)}, u32[]{:S(2)}) %collective-permute-start.16) | collective-permute-done | bytes 81952 | tf_op jit(solution)/shard_map/ppermute | solution.py:291
  109.4 1.6 %collective-permute-done.17 = f32[640,128]{1,0:T(8,128)S(1)} collective-permute-done((f32[640,128]{1,0:T(8,128)S(1)}, f32[640,128]{1,0:T(8,128)S(1)}, u32[]{:S(2)}, u32[]{:S(2)}) %collective-permute-start.17) | collective-permute-done | bytes 327712 | tf_op jit(solution)/shard_map/ppermute | solution.py:291
  111.1 4.6 %collective-permute-done.18.refs_6_ = bf16[2592,128]{1,0:T(8,128)(2,1)S(1)} collective-permute-done((bf16[2592,128]{1,0:T(8,128)(2,1)}, bf16[2592,128]{1,0:T(8,128)(2,1)S(1)}, u32[]{:S(2)}, u32[]{:S(2)}) %collective-permute-start.18) | collective-permute-done | bytes 663584 | tf_op jit(solution)/shard_map/ppermute | solution.py:323
  115.7 1.3 collective-permute-start.19
  117.0 20.9 %inverse_factor.1.factor_ref = f32[512,512]{1,0:T(8,128)S(1)} custom-call(f32[1280,128]{1,0:T(8,128)S(1)} %bitcast.12), custom_call_target="tpu_custom_call" | custom-call | bytes 73400320 | tf_op jit(solution)/shard_map/inverse_factor/pallas_call | solution.py:455
  137.9 3.5 %output.1 = f32[3456,128]{1,0:T(8,128)} custom-call(s32[1]{0:T(128)} %bitcast.band, f32[512,512]{1,0:T(8,128)S(1)} %inverse_factor.1.factor_ref, bf16[864,128]{1,0:T(8,128)(2,1)S(1)} %get-tuple-element.50.refs_0_, bf16[864,128]{1,0:T(8,128)(2,1)S(1)} %collective-permute-done.4.refs_1_, bf16[864,128]{1,0:T(8,128)(2,1)S(1)} %collective-permute-done.5.refs_2_, ...), custom_call_target="tpu_custom_call" | custom-call | tf_op jit(solution)/shard_map/output/pallas_call | solution.py:509
  (61 shorter events, 14.5 us)
Async XLA Ops:
  0.0 1.2 copy-start.2
  1.2 0.7 copy-start.6
  1.9 0.7 copy-start.8
  4.0 7.0 %collective-permute-start = (bf16[288,128]{1,0:T(8,128)(2,1)S(1)}, bf16[288,128]{1,0:T(8,128)(2,1)S(1)}, u32[]{:S(2)}, u32[]{:S(2)}) collective-permute-start(bf16[288,128]{1,0:T(8,128)(2,1)S(1)} %get-tuple-element.32), channel_id=1, source_target_pairs={{0,28},{4,0},{8,4},{12,8},{16,12},{20,16},{24,20},{28,24},{1,29},{... | collective-permute-start | bytes 221192 | tf_op jit(solution)/shard_map/ppermute | solution.py:24
  4.0 1.0 copy-start
  5.0 0.7 copy-start.4
  5.7 0.7 copy-start.10
  6.4 4.6 %copy-start.1 = (bf16[343,343]{1,0:T(8,128)(2,1)S(1)}, bf16[343,343]{1,0:T(8,128)(2,1)}, u32[]{:S(2)}) copy-start(bf16[343,343]{1,0:T(8,128)(2,1)} %matrix_ref.7) | copy-start | bytes 705898
  6.4 4.6 %copy-start.5 = (s32[16,343]{1,0:T(8,128)S(1)}, s32[16,343]{1,0:T(8,128)}, u32[]{:S(2)}) copy-start(s32[16,343]{1,0:T(8,128)} %links.11) | copy-start | bytes 65860
  6.4 4.6 %copy-start.11 = (f32[16]{0:T(128)S(1)}, f32[16]{0:T(128)}, u32[]{:S(2)}) copy-start(f32[16]{0:T(128)} %scale.7) | copy-start | bytes 196
  20.2 5.9 %collective-permute-start.1 = (f32[288,128]{1,0:T(8,128)S(1)}, f32[288,128]{1,0:T(8,128)S(1)}, u32[]{:S(2)}, u32[]{:S(2)}) collective-permute-start(f32[288,128]{1,0:T(8,128)S(1)} %get-tuple-element.38), channel_id=1, source_target_pairs={{0,4},{4,8},{8,12},{12,16},{16,20},{20,24},{24,28},{28,0},{1,5},{5... | collective-permute-start | bytes 442376 | tf_op jit(solution)/shard_map/ppermute | solution.py:24
  20.7 5.4 %copy-start.7 = (f32[3456]{0:T(1024)S(1)}, f32[3456]{0:T(1024)}, u32[]{:S(2)}) copy-start(f32[3456]{0:T(1024)} %param.9) | copy-start | bytes 41476
  20.7 5.4 %copy-start.9 = (s32[288]{0:T(512)S(1)}, s32[288]{0:T(512)}, u32[]{:S(2)}) copy-start(s32[288]{0:T(512)} %nodes.5) | copy-start | bytes 3460
  27.9 5.9 %collective-permute-start.2 = (bf16[288,128]{1,0:T(8,128)(2,1)S(1)}, bf16[288,128]{1,0:T(8,128)(2,1)S(1)}, u32[]{:S(2)}, u32[]{:S(2)}) collective-permute-start(bf16[288,128]{1,0:T(8,128)(2,1)S(1)} %get-tuple-element.39), channel_id=1, source_target_pairs={{0,28},{4,0},{8,4},{12,8},{16,12},{20,16},{24,20},{28,24},{1,29},{... | collective-permute-start | bytes 221192 | tf_op jit(solution)/shard_map/ppermute | solution.py:24
  43.0 6.3 %collective-permute-start.3 = (f32[288,128]{1,0:T(8,128)S(1)}, f32[288,128]{1,0:T(8,128)S(1)}, u32[]{:S(2)}, u32[]{:S(2)}) collective-permute-start(f32[288,128]{1,0:T(8,128)S(1)} %get-tuple-element.45), channel_id=1, source_target_pairs={{0,4},{4,8},{8,12},{12,16},{16,20},{20,24},{24,28},{28,0},{1,5},{5... | collective-permute-start | bytes 442376 | tf_op jit(solution)/shard_map/ppermute | solution.py:24
  43.8 5.4 %copy-start.3 = (bf16[3456,128]{1,0:T(8,128)(2,1)S(1)}, bf16[3456,128]{1,0:T(8,128)(2,1)}, u32[]{:S(2)}) copy-start(bf16[3456,128]{1,0:T(8,128)(2,1)} %previous_ref.1) | copy-start | bytes 2654212
  50.7 6.7 %collective-permute-start.4 = (bf16[864,128]{1,0:T(8,128)(2,1)S(1)}, bf16[864,128]{1,0:T(8,128)(2,1)S(1)}, u32[]{:S(2)}, u32[]{:S(2)}) collective-permute-start(bf16[864,128]{1,0:T(8,128)(2,1)S(1)} %get-tuple-element.47), channel_id=1, source_target_pairs={{0,1},{1,2},{2,3},{3,0},{4,5},{5,6},{6,7},{7,4},{8,9},{9,10},{10,1... | collective-permute-start | bytes 663560 | tf_op jit(solution)/shard_map/ppermute | solution.py:24
  50.9 20.5 %collective-permute-start.5 = (bf16[864,128]{1,0:T(8,128)(2,1)S(1)}, bf16[864,128]{1,0:T(8,128)(2,1)S(1)}, u32[]{:S(2)}, u32[]{:S(2)}) collective-permute-start(bf16[864,128]{1,0:T(8,128)(2,1)S(1)} %get-tuple-element.48), channel_id=1, source_target_pairs={{0,2},{1,3},{2,0},{3,1},{4,6},{5,7},{6,4},{7,5},{8,10},{9,11},{10,... | collective-permute-start | bytes 663560 | tf_op jit(solution)/shard_map/ppermute | solution.py:24
  52.6 18.8 %collective-permute-start.6 = (bf16[864,128]{1,0:T(8,128)(2,1)S(1)}, bf16[864,128]{1,0:T(8,128)(2,1)S(1)}, u32[]{:S(2)}, u32[]{:S(2)}) collective-permute-start(bf16[864,128]{1,0:T(8,128)(2,1)S(1)} %get-tuple-element.49), channel_id=1, source_target_pairs={{0,3},{1,0},{2,1},{3,2},{4,7},{5,4},{6,5},{7,6},{8,11},{9,8},{10,9... | collective-permute-start | bytes 663560 | tf_op jit(solution)/shard_map/ppermute | solution.py:24
  72.4 2.9 %collective-permute-start.7 = (f32[640,128]{1,0:T(8,128)S(1)}, f32[640,128]{1,0:T(8,128)S(1)}, u32[]{:S(2)}, u32[]{:S(2)}) collective-permute-start(f32[640,128]{1,0:T(8,128)S(1)} %constant_dynamic-slice_fusion.3), channel_id=1, source_target_pairs={{0,4},{4,0},{8,12},{12,8},{16,20},{20,16},{24,28},{28,24},{1,5},{5... | collective-permute-start | bytes 983048 | tf_op jit(solution)/shard_map/ppermute | solution.py:291
  74.0 20.5 %collective-permute-start.12 = (bf16[2592,128]{1,0:T(8,128)(2,1)S(1)}, bf16[2592,128]{1,0:T(8,128)(2,1)S(1)}, u32[]{:S(2)}, u32[]{:S(2)}) collective-permute-start(bf16[2592,128]{1,0:T(8,128)(2,1)S(1)} %pad_maximum_fusion), channel_id=1, source_target_pairs={{0,1},{1,2},{2,3},{4,5},{5,6},{6,7},{8,9},{9,10},{10,11},{12,13},{... | collective-permute-start | bytes 1990664 | tf_op jit(solution)/shard_map/ppermute | solution.py:323
  76.1 6.4 %collective-permute-start.10 = (f32[160,128]{1,0:T(8,128)}, f32[160,128]{1,0:T(8,128)S(1)}, u32[]{:S(2)}, u32[]{:S(2)}) collective-permute-start(f32[160,128]{1,0:T(8,128)} %get-tuple-element.60), channel_id=1, source_target_pairs={{0,24},{4,28},{8,16},{12,20},{16,8},{20,12},{24,0},{28,4},{1,25},{... | collective-permute-start | bytes 245768 | tf_op jit(solution)/shard_map/ppermute | solution.py:291
  77.8 5.8 %collective-permute-start.8 = (f32[160,128]{1,0:T(8,128)S(1)}, f32[160,128]{1,0:T(8,128)S(1)}, u32[]{:S(2)}, u32[]{:S(2)}) collective-permute-start(f32[160,128]{1,0:T(8,128)S(1)} %get-tuple-element.59), channel_id=1, source_target_pairs={{0,8},{4,12},{8,0},{12,4},{16,24},{20,28},{24,16},{28,20},{1,9},{5... | collective-permute-start | bytes 245768 | tf_op jit(solution)/shard_map/ppermute | solution.py:291
  79.0 4.7 %collective-permute-start.9 = (f32[160,128]{1,0:T(8,128)S(1)}, f32[160,128]{1,0:T(8,128)}, u32[]{:S(2)}, u32[]{:S(2)}) collective-permute-start(f32[160,128]{1,0:T(8,128)S(1)} %get-tuple-element.61), channel_id=1, source_target_pairs={{0,16},{4,20},{8,24},{12,28},{16,0},{20,4},{24,8},{28,12},{1,17},{... | collective-permute-start | bytes 245768 | tf_op jit(solution)/shard_map/ppermute | solution.py:291
  84.7 9.9 %collective-permute-start.11 = (f32[160,128]{1,0:T(8,128)S(1)}, f32[160,128]{1,0:T(8,128)S(1)}, u32[]{:S(2)}, u32[]{:S(2)}) collective-permute-start(f32[160,128]{1,0:T(8,128)S(1)} %add_add_fusion), channel_id=1, source_target_pairs={{0,1},{1,0},{2,3},{3,2},{4,5},{5,4},{6,7},{7,6},{8,9},{9,8},{10,11... | collective-permute-start | bytes 245768 | tf_op jit(solution)/shard_map/ppermute | solution.py:291
  94.6 5.4 %collective-permute-start.13 = (f32[160,128]{1,0:T(8,128)S(1)}, f32[160,128]{1,0:T(8,128)S(1)}, u32[]{:S(2)}, u32[]{:S(2)}) collective-permute-start(f32[160,128]{1,0:T(8,128)S(1)} %add.63), channel_id=1, source_target_pairs={{0,2},{1,3},{2,0},{3,1},{4,6},{5,7},{6,4},{7,5},{8,10},{9,11},{10,... | collective-permute-start | bytes 245768 | tf_op jit(solution)/shard_map/ppermute | solution.py:291
  97.4 18.3 %collective-permute-start.18 = (bf16[2592,128]{1,0:T(8,128)(2,1)}, bf16[2592,128]{1,0:T(8,128)(2,1)S(1)}, u32[]{:S(2)}, u32[]{:S(2)}) collective-permute-start(bf16[2592,128]{1,0:T(8,128)(2,1)} %pad_maximum_fusion.1), channel_id=1, source_target_pairs={{1,2},{2,3},{5,6},{6,7},{9,10},{10,11},{13,14},{14,15},{17,18},{18... | collective-permute-start | bytes 1990664 | tf_op jit(solution)/shard_map/ppermute | solution.py:323
  100.0 4.5 %collective-permute-start.14 = (f32[160,128]{1,0:T(8,128)S(1)}, f32[160,128]{1,0:T(8,128)S(1)}, u32[]{:S(2)}, u32[]{:S(2)}) collective-permute-start(f32[160,128]{1,0:T(8,128)S(1)} %add.64), channel_id=1, source_target_pairs={{0,8},{4,12},{8,0},{12,4},{16,24},{20,28},{24,16},{28,20},{1,9},{5... | collective-permute-start | bytes 245768 | tf_op jit(solution)/shard_map/ppermute | solution.py:291
  101.8 5.3 %collective-permute-start.15 = (f32[160,128]{1,0:T(8,128)S(1)}, f32[160,128]{1,0:T(8,128)S(1)}, u32[]{:S(2)}, u32[]{:S(2)}) collective-permute-start(f32[160,128]{1,0:T(8,128)S(1)} %add.64), channel_id=1, source_target_pairs={{0,16},{4,20},{8,24},{12,28},{16,0},{20,4},{24,8},{28,12},{1,17},{... | collective-permute-start | bytes 245768 | tf_op jit(solution)/shard_map/ppermute | solution.py:291
  103.4 5.3 %collective-permute-start.16 = (f32[160,128]{1,0:T(8,128)S(1)}, f32[160,128]{1,0:T(8,128)S(1)}, u32[]{:S(2)}, u32[]{:S(2)}) collective-permute-start(f32[160,128]{1,0:T(8,128)S(1)} %add.64), channel_id=1, source_target_pairs={{0,24},{4,28},{8,16},{12,20},{16,8},{20,12},{24,0},{28,4},{1,25},{... | collective-permute-start | bytes 245768 | tf_op jit(solution)/shard_map/ppermute | solution.py:291
  109.3 1.7 %collective-permute-start.17 = (f32[640,128]{1,0:T(8,128)S(1)}, f32[640,128]{1,0:T(8,128)S(1)}, u32[]{:S(2)}, u32[]{:S(2)}) collective-permute-start(f32[640,128]{1,0:T(8,128)S(1)} %bitcast.15), channel_id=1, source_target_pairs={{0,4},{4,0},{8,12},{12,8},{16,20},{20,16},{24,28},{28,24},{1,5},{5... | collective-permute-start | bytes 983048 | tf_op jit(solution)/shard_map/ppermute | solution.py:291
  115.7 22.2 %collective-permute-start.19 = (bf16[2592,128]{1,0:T(8,128)(2,1)S(1)}, bf16[2592,128]{1,0:T(8,128)(2,1)S(1)}, u32[]{:S(2)}, u32[]{:S(2)}) collective-permute-start(bf16[2592,128]{1,0:T(8,128)(2,1)S(1)} %pad_maximum_fusion.2), channel_id=1, source_target_pairs={{2,3},{6,7},{10,11},{14,15},{18,19},{22,23},{26,27},{30,31}} | collective-permute-start | bytes 1990664 | tf_op jit(solution)/shard_map/ppermute | solution.py:323

commit v4 on v3

--- a/solution.py
+++ b/solution.py
@@ -10,13 +10,19 @@
 CENTER = 1.5
 HALF_WIDTH = 1.25
 LANES = 128
-CHAINS = 4
-EXACT = lax.Precision.HIGHEST
+CHAINS = 6
 F32 = jnp.float32
 BF16 = jnp.bfloat16
 VM = pl.BlockSpec(memory_space=pltpu.VMEM)
 SM = pl.BlockSpec(memory_space=pltpu.SMEM)
-PARAMS = pltpu.CompilerParams(vmem_limit_bytes=48 << 20)
+
+
+def params(mebibytes):
+    return pltpu.CompilerParams(vmem_limit_bytes=mebibytes << 20)
+
+
+def cost(flops, moved):
+    return pl.CostEstimate(flops=flops, bytes_accessed=moved, transcendentals=0)
 
 
 def shifted(value, axis, steps):
@@ -37,9 +43,9 @@
     base_ref[owned:, :] = jnp.zeros_like(base_ref[owned:, :])
 
 
-def prepare_kernel(nodes, rows_ref, potential_ref, base_ref, ext_ref, edge_ref, picked):
+def prepare_kernel(nodes, rows_ref, ext_ref, edge_ref, picked):
     owned = rows_ref.shape[0]
-    rows_out(lambda here: rows_ref[here, :].astype(F32), potential_ref, owned, base_ref, ext_ref)
+    ext_ref[0:owned, :] = rows_ref[...].astype(F32)
 
     def body(step, _):
         for k in range(16):
@@ -51,36 +57,32 @@
     edge_ref[...] = picked[...].astype(BF16)
 
 
-def prepared_shapes(owned, plane):
-    return (
-        jax.ShapeDtypeStruct((owned + plane, LANES), F32),
-        jax.ShapeDtypeStruct((owned + plane, LANES), F32),
-        jax.ShapeDtypeStruct((plane, LANES), BF16),
-    )
-
-
-def prepare(nodes, rows, potential):
+def prepare(nodes, rows):
     owned, plane = rows.shape[0], nodes.shape[0]
-    return pl.pallas_call(
+    ext, edge = pl.pallas_call(
         prepare_kernel,
-        out_shape=prepared_shapes(owned, plane),
-        in_specs=[SM, VM, VM],
-        out_specs=(VM, VM, VM),
+        out_shape=(
+            jax.ShapeDtypeStruct((owned + plane, LANES), F32),
+            jax.ShapeDtypeStruct((plane, LANES), BF16),
+        ),
+        in_specs=[SM, VM],
+        out_specs=(VM, VM),
         scratch_shapes=[pltpu.VMEM((plane, LANES), F32)],
-        compiler_params=PARAMS,
+        compiler_params=params(8),
+        cost_estimate=cost(0, 12 << 20),
         name="prepare",
-    )(nodes, rows, potential)
-
-
-def gather_cells(links, ext_ref, gathered, first):
-    cells, npc = gathered.shape[0], links.shape[1]
-
+    )(nodes, rows)
+    return ext, ext, edge
+
+
+def gather_cells(links, npc, ext_ref, gathered, first):
     def cell(c, _):
+        base = (first + c) * npc
         for r in range(npc):
-            gathered[c, r : r + 1, :] = ext_ref[pl.ds(links[first + c, r], 1), :]
+            gathered[c, r : r + 1, :] = ext_ref[pl.ds(links[base + r], 1), :]
         return 0
 
-    lax.fori_loop(0, cells, cell, 0)
+    lax.fori_loop(0, gathered.shape[0], cell, 0)
 
 
 def multiply_cells(scale, matrix_ref, gathered, products, first):
@@ -96,61 +98,61 @@
             )
 
 
-def scatter_cells(links, products, sums, first):
-    cells, npc = products.shape[0], links.shape[1]
+def scatter_cells(links, npc, products, sums, first):
     chains = len(sums)
 
     def cell(c, _):
+        base = (first + c) * npc
         for r in range(npc):
             total = sums[r % chains]
-            row = pl.ds(links[first + c, r], 1)
+            row = pl.ds(links[base + r], 1)
             total[row, :] = total[row, :] + products[c, r : r + 1, :]
         return 0
 
-    lax.fori_loop(0, cells, cell, 0)
+    lax.fori_loop(0, products.shape[0], cell, 0)
 
 
 def near_products_kernel(links, scale, ext_ref, matrix_ref, out_ref, gathered):
-    gather_cells(links, ext_ref, gathered, 0)
+    gather_cells(links, matrix_ref.shape[0], ext_ref, gathered, 0)
     multiply_cells(scale, matrix_ref, gathered, out_ref, 0)
 
 
 def far_cells_kernel(
-    links, scale, ext_ref, ghost_ref, matrix_ref, base_ref, out_ref, back_ref, ext, gathered,
+    links, scale, ext_ref, ghost_ref, matrix_ref, wide_ref, potential_ref, out_ref, back_ref, ext, gathered,
     products, *sums
 ):
     owned = out_ref.shape[0]
     half = gathered.shape[0]
     ext[0:owned, :] = ext_ref[0:owned, :]
     ext[owned:, :] = ghost_ref[...].astype(F32)
-    sums[0][...] = base_ref[...]
+    for block in range(owned // LANES):
+        here = slice(block * LANES, (block + 1) * LANES)
+        sums[0][here, :] = spread_levels(potential_ref, block) * wide_ref[here, :]
+    sums[0][owned:, :] = jnp.zeros_like(sums[0][owned:, :])
     for total in sums[1:]:
         total[...] = jnp.zeros_like(total)
-    gather_cells(links, ext, gathered, half)
+    npc = matrix_ref.shape[0]
+    gather_cells(links, npc, ext, gathered, half)
     multiply_cells(scale, matrix_ref, gathered, products, half)
-    scatter_cells(links, products, sums, half)
+    scatter_cells(links, npc, products, sums, half)
     back_ref[...] = sum(total[owned:, :] for total in sums)
     out_ref[...] = sum(total[0:owned, :] for total in sums)
 
 
-def near_sums_kernel(links, products_ref, start_ref, out_ref, *sums):
+def near_sums_kernel(npc, links, products_ref, start_ref, out_ref, *sums):
     sums = (out_ref,) + sums
     out_ref[...] = start_ref[...]
     for total in sums[1:]:
         total[...] = jnp.zeros_like(total)
-    scatter_cells(links, products_ref, sums, 0)
+    scatter_cells(links, npc, products_ref, sums, 0)
     out_ref[...] = sum(total[...] for total in sums)
 
 
-def cost(flops, moved):
-    return pl.CostEstimate(flops=flops, bytes_accessed=moved, transcendentals=0)
-
-
-def apply_operator(links, scale, matrix, base, ext, edge):
-    cells, npc = links.shape
+def apply_operator(links, scale, matrix, potential, wide, ext, edge):
+    cells, npc = scale.shape[0], matrix.shape[0]
     half, padded = cells // 2, (npc + 7) // 8 * 8
     plane = edge.shape[0]
-    whole = base.shape
+    whole = ext.shape
     owned = whole[0] - plane
     held = (half, padded, LANES)
     ghost = shifted(edge, "domain", -1)
@@ -160,7 +162,7 @@
         in_specs=[SM, SM, VM, VM],
         out_specs=VM,
         scratch_shapes=[pltpu.VMEM(held, F32)],
-        compiler_params=PARAMS,
+        compiler_params=params(16),
         cost_estimate=cost(0, 14 << 20),
         name="near_products",
     )(links, scale, ext, matrix)
@@ -171,22 +173,22 @@
             jax.ShapeDtypeStruct((owned, LANES), F32),
             jax.ShapeDtypeStruct((plane, LANES), F32),
         ),
-        in_specs=[SM, SM, VM, VM, VM, VM],
+        in_specs=[SM, SM, VM, VM, VM, VM, VM],
         out_specs=(VM, VM),
         scratch_shapes=[pltpu.VMEM(whole, F32), pltpu.VMEM(held, F32), pltpu.VMEM(held, F32)]
         + [pltpu.VMEM(whole, F32)] * CHAINS,
-        compiler_params=PARAMS,
+        compiler_params=params(22),
         cost_estimate=cost(0, 28 << 20),
         name="far_cells",
-    )(links, scale, ext, ghost, matrix, base)
+    )(links, scale, ext, ghost, matrix, wide, potential)
     back = shifted(back, "domain", 1)
     sums = pl.pallas_call(
-        near_sums_kernel,
+        functools.partial(near_sums_kernel, npc),
         out_shape=jax.ShapeDtypeStruct((owned, LANES), F32),
         in_specs=[SM, VM, VM],
         out_specs=VM,
         scratch_shapes=[pltpu.VMEM((owned, LANES), F32)] * (CHAINS - 1),
-        compiler_params=PARAMS,
+        compiler_params=params(16),
         cost_estimate=cost(0, 14 << 20),
         name="near_sums",
     )(links, products, sums)
@@ -207,25 +209,30 @@
     lax.fori_loop(0, nodes.shape[0] // 16, body, 0)
 
 
-def first_kernel(nodes, sums_ref, back_ref, potential_ref, base_ref, ext_ref, edge_ref, picked, term):
+def first_kernel(nodes, sums_ref, back_ref, term_ref, ext_ref, edge_ref, picked):
     owned = sums_ref.shape[0]
-    term[...] = sums_ref[...] * (1.0 / HALF_WIDTH)
-    add_back(nodes, term, back_ref, 1.0 / HALF_WIDTH, picked)
+    term_ref[...] = sums_ref[...] * (1.0 / HALF_WIDTH)
+    add_back(nodes, term_ref, back_ref, 1.0 / HALF_WIDTH, picked)
     edge_ref[...] = picked[...].astype(BF16)
-    rows_out(lambda here: term[here, :], potential_ref, owned, base_ref, ext_ref)
-
-
-def first_term(nodes, sums, back, potential):
+    ext_ref[0:owned, :] = term_ref[...].astype(BF16).astype(F32)
+
+
+def first_term(nodes, sums, back):
     owned, plane = sums.shape[0], nodes.shape[0]
     return pl.pallas_call(
         first_kernel,
-        out_shape=prepared_shapes(owned, plane),
-        in_specs=[SM, VM, VM, VM],
+        out_shape=(
+            jax.ShapeDtypeStruct((owned, LANES), F32),
+            jax.ShapeDtypeStruct((owned + plane, LANES), F32),
+            jax.ShapeDtypeStruct((plane, LANES), BF16),
+        ),
+        in_specs=[SM, VM, VM],
         out_specs=(VM, VM, VM),
-        scratch_shapes=[pltpu.VMEM((plane, LANES), F32), pltpu.VMEM(sums.shape, F32)],
-        compiler_params=PARAMS,
+        scratch_shapes=[pltpu.VMEM((plane, LANES), F32)],
+        compiler_params=params(16),
+        cost_estimate=cost(0, 8 << 20),
         name="first_term",
-    )(nodes, sums, back, potential)
+    )(nodes, sums, back)
 
 
 def second_kernel(band, nodes, sums_ref, back_ref, previous_ref, *refs):
@@ -252,7 +259,8 @@
         in_specs=[SM, SM, VM, VM, VM],
         out_specs=[VM] * (count + 1),
         scratch_shapes=[pltpu.VMEM(sums.shape, F32)],
-        compiler_params=PARAMS,
+        compiler_params=params(16),
+        cost_estimate=cost(0, 6 << 20),
         name="second_term",
     )(band, nodes, sums, back, previous)
     return made[:count], made[count]
@@ -281,7 +289,8 @@
         in_specs=[SM] + [VM] * count,
         out_specs=VM,
         scratch_shapes=[pltpu.VMEM((count,) + pieces[0].shape, BF16)],
-        compiler_params=PARAMS,
+        compiler_params=params(16),
+        cost_estimate=cost(0, 4 << 20),
         name="partial_gram",
     )(band, *pieces)
 
@@ -345,45 +354,64 @@
     return total
 
 
+def split_dot(a, b, dims=(((1,), (0,)), ((), ()))):
+    def parts(x):
+        high = x.astype(BF16)
+        return high, (x - high.astype(F32)).astype(BF16)
+
+    def dot(x, y):
+        return lax.dot_general(x, y, dims, preferred_element_type=F32)
+
+    (a_high, a_low), (b_high, b_low) = parts(a), parts(b)
+    return dot(a_high, b_high) + (dot(a_high, b_low) + dot(a_low, b_high))
+
+
 def small_inverse(tiles, lane):
     count, tiles, done = len(tiles), list(tiles), []
-    sub = lax.broadcasted_iota(jnp.int32, tiles[0].shape, 0)
+    shape = tiles[0].shape
+    sub = lax.broadcasted_iota(jnp.int32, shape, 0)
 
     def along_lanes(tile, column):
-        return jnp.broadcast_to(tile[:, column : column + 1], tile.shape)
+        return jnp.broadcast_to(tile[:, column : column + 1], shape)
 
     def along_rows(tile, row):
-        return jnp.broadcast_to(tile[row : row + 1, :], tile.shape)
-
+        return jnp.broadcast_to(tile[row : row + 1, :], shape)
+
+    def stacked(rows):
+        tile = rows[0]
+        for i in range(1, 8):
+            tile = jnp.where(sub == i, rows[i], tile)
+        return tile
+
+    columns = [along_lanes(tiles[0], m) for m in range(8)]
     for p in range(count):
         base = 8 * p
         group = (lane >= base) & (lane < base + 8)
-        columns = [along_lanes(tiles[p], base + m) for m in range(8)]
         entry = {(i, j): along_rows(columns[j], i) for j in range(8) for i in range(j, 8)}
         start = jnp.where(group, (lane - base == sub).astype(F32), tiles[p])
         solved = [along_rows(start, i) for i in range(8)]
         following = None
         if p + 1 < count:
             ahead = [along_lanes(tiles[p + 1], base + m) for m in range(8)]
+            columns = [along_lanes(tiles[p + 1], base + 8 + m) for m in range(8)]
             following = jnp.where(group, 0.0, tiles[p + 1])
         inverse, factor = [], {}
         for j in range(8):
             pivot = 1.0 / entry[j, j]
             inverse.append(pivot)
+            if following is not None:
+                scaled = ahead[j] * pivot
+                columns = [c - scaled * along_rows(ahead[j], m) for m, c in enumerate(columns)]
+                following = following - scaled * solved[j]
+                for m in range(j + 1, 8):
+                    ahead[m] = ahead[m] - scaled * entry[m, j]
             for i in range(j + 1, 8):
                 factor[i, j] = entry[i, j] * pivot
             for i in range(j + 1, 8):
                 for k in range(j + 1, i + 1):
                     entry[i, k] = entry[i, k] - factor[i, j] * entry[k, j]
                 solved[i] = solved[i] - factor[i, j] * solved[j]
-            if following is not None:
-                scaled = ahead[j] * pivot
-                following = following - scaled * solved[j]
-                for m in range(j + 1, 8):
-                    ahead[m] = ahead[m] - scaled * entry[m, j]
-        result = solved[0] * lax.rsqrt(entry[0, 0])
-        for i in range(1, 8):
-            result = jnp.where(sub == i, solved[i] * lax.rsqrt(entry[i, i]), result)
+        result = stacked([solved[i] * lax.rsqrt(entry[i, i]) for i in range(8)])
         done.append(jnp.where(lane <= base + sub, result, 0.0))
         if p + 2 < count:
             back = [None] * 8
@@ -392,18 +420,23 @@
                 for k in range(i + 1, 8):
                     value = value - factor[k, i] * back[k]
                 back[i] = value
-            for i in range(p + 2, count):
-                value = jnp.where(group, 0.0, tiles[i])
-                for m in range(8):
-                    value = value - along_lanes(tiles[i], base + m) * back[m]
-                tiles[i] = value
+            value = jnp.where(group, 0.0, tiles[p + 2])
+            for m in range(8):
+                value = value - along_lanes(tiles[p + 2], base + m) * back[m]
+            tiles[p + 2] = value
+            if p + 3 < count:
+                spread = [stacked(back), jnp.zeros((LANES - 8 - base, LANES), F32)]
+                if base:
+                    spread = [jnp.zeros((base, LANES), F32)] + spread
+                made = split_dot(
+                    jnp.concatenate(tiles[p + 3 :], axis=0), jnp.concatenate(spread, axis=0)
+                )
+                for i in range(p + 3, count):
+                    row = 8 * (i - p - 3)
+                    tiles[i] = jnp.where(group, 0.0, tiles[i]) - made[row : row + 8, :]
         if following is not None:
             tiles[p + 1] = following
     return done
-
-
-def exact_dot(a, b, dims=(((1,), (0,)), ((), ()))):
-    return lax.dot_general(a, b, dims, precision=EXACT, preferred_element_type=F32)
 
 
 def inverse_kernel(over, packed_ref, out_ref, work, small):
@@ -436,15 +469,15 @@
                 diagonal = small[...]
                 out_ref[a:b, a:b] = diagonal
                 if which:
-                    left = exact_dot(diagonal, work[a:b, 0:a])
+                    left = split_dot(diagonal, work[a:b, 0:a])
                     out_ref[a:b, 0:a] = left
                 if b < size:
-                    right = exact_dot(diagonal, work[a:b, b:size])
-                    column = exact_dot(work[b:size, a:b], diagonal, (((1,), (1,)), ((), ())))
-                    work[b:size, b:size] = work[b:size, b:size] - exact_dot(column, right)
-                    work[b:size, a:b] = -exact_dot(column, diagonal)
+                    right = split_dot(diagonal, work[a:b, b:size])
+                    column = split_dot(work[b:size, a:b], diagonal, (((1,), (1,)), ((), ())))
+                    work[b:size, b:size] = work[b:size, b:size] - split_dot(column, right)
+                    work[b:size, a:b] = -split_dot(column, diagonal)
                     if which:
-                        work[b:size, 0:a] = work[b:size, 0:a] - exact_dot(column, left)
+                        work[b:size, 0:a] = work[b:size, 0:a] - split_dot(column, left)
 
         return 0
 
@@ -458,38 +491,34 @@
         in_specs=[VM],
         out_specs=VM,
         scratch_shapes=[pltpu.VMEM((size, size), F32), pltpu.VMEM((LANES, LANES), F32)],
-        compiler_params=PARAMS,
+        compiler_params=params(16),
         cost_estimate=cost(0, 70 << 20),
         name="inverse_factor",
     )(packed)
 
 
 def output_kernel(band, factor_ref, *refs):
-    out_ref, high_ref, low_ref = refs[-3:]
+    out_ref, blocks_ref = refs[-2:]
     count = factor_ref.shape[0] // LANES
-    firsts, rests = refs[:count], refs[count:-3]
+    firsts, rests = refs[:count], refs[count:-2]
     j = pl.program_id(0)
 
     @pl.when(j == 0)
     def _():
+        row = pl.ds(pl.multiple_of(band[0] * LANES, LANES), LANES)
         for s in range(count):
             source = band[0] - s
-            column = pl.multiple_of(jnp.maximum(source, 0) * LANES, LANES)
-            row = pl.multiple_of(band[0] * LANES, LANES)
-            block = factor_ref[pl.ds(row, LANES), pl.ds(column, LANES)]
-            block = jnp.where(source >= 0, block, 0.0)
+            column = pl.ds(pl.multiple_of(jnp.maximum(source, 0) * LANES, LANES), LANES)
+            block = jnp.where(source >= 0, factor_ref[row, column], 0.0).T
             high = block.astype(BF16)
-            high_ref[s] = high
-            low_ref[s] = (block - high.astype(F32)).astype(BF16)
+            here = slice(s * LANES, (s + 1) * LANES)
+            blocks_ref[here, 0:LANES] = high
+            blocks_ref[here, LANES:] = (block - high.astype(F32)).astype(BF16)
 
     def put(pieces):
-        total = None
-        dims = (((1,), (1,)), ((), ()))
-        for s, piece in enumerate(pieces):
-            for factor in (high_ref, low_ref):
-                part = lax.dot_general(piece, factor[s], dims, preferred_element_type=F32)
-                total = part if total is None else total + part
-        out_ref[...] = total
+        rows = jnp.concatenate(pieces, axis=1)
+        made = jnp.dot(rows, blocks_ref[...], preferred_element_type=F32)
+        out_ref[...] = made[:, 0:LANES] + made[:, LANES:]
 
     rows = out_ref.shape[0]
 
@@ -514,9 +543,10 @@
             grid=(count,),
             in_specs=[VM] * (1 + 2 * count),
             out_specs=pl.BlockSpec((rows, LANES), lambda j, band: (lax.rem(band[0] + j, count), 0)),
-            scratch_shapes=[pltpu.VMEM((count, LANES, LANES), BF16)] * 2,
+            scratch_shapes=[pltpu.VMEM((count * LANES, 2 * LANES), BF16)],
         ),
-        compiler_params=PARAMS,
+        compiler_params=params(24),
+        cost_estimate=cost(0, 10 << 20),
         name="output",
     )(band, factor, *firsts, *rests)
 
@@ -527,9 +557,11 @@
     band = lax.axis_index("band").astype(jnp.int32).reshape(1)
     levels = potential.reshape(owned // LANES, LANES)
 
-    operator = functools.partial(apply_operator, connectivity, cell_scale, cell_matrix)
-    sums, back = operator(*prepare(boundary_nodes, states_block, levels))
-    sums, back = operator(*first_term(boundary_nodes, sums, back, levels))
+    operator = functools.partial(
+        apply_operator, connectivity.reshape(-1), cell_scale, cell_matrix, levels
+    )
+    sums, back = operator(*prepare(boundary_nodes, states_block))
+    sums, back = operator(*first_term(boundary_nodes, sums, back))
     pieces, rest = second_term(band, boundary_nodes, sums, back, states_block, count)
 
     firsts = [pieces[0]] + [shifted(pieces[s], "band", s) for s in range(1, count)]

time: 144 us -> 129 us (0.90); the launches traced: 141 us -> 129 us
  Pallas kernels: 68.1 us -> 53 us
  waiting for transfers between devices: 42.5 us -> 45.9 us
    pallas_call x1, Pallas kernels: 20.9 us -> 13.4 us  [inverse_factor(): pl.pallas_call(functools.partial(inverse_kernel, over), out_shape=jax.Sha...]
    ppermute x3, waiting for transfers between devices: 4.57 us -> 7.84 us  [passed_up(): lax.ppermute(onward, 'band', [(i, i + 1) for i in range(held, count - 1)])]
    pallas_call x2, Pallas kernels: 18.3 us -> 15.6 us  [apply_operator(): pl.pallas_call(far_cells_kernel, out_shape=(jax.ShapeDtypeStruct((owned,...]
    pallas_call x4, Pallas kernels: 13.9 us -> 11.5 us  [the longest x2 8.98 us: apply_operator(): pl.pallas_call(functools.partial(near_sums_kernel, npc), out_shape=jax.Sh...]
    pallas_call x2, Pallas kernels: 9.12 us -> 7.27 us  [apply_operator(): pl.pallas_call(near_products_kernel, out_shape=jax.ShapeDtypeStruct(held,...]
    unnamed x24 -> x16, local copies, waits for them, and re-layouts: 4.92 us -> 3.46 us
  transfers between devices with their start and end apart: 20 -> 20, of which waited for: 12 -> 13; matrix products, arithmetic and copies ran while one was open for 2% -> 3% of each run, Pallas kernels for 29% -> 23%
where the time goes in v4:
time: 129 us
  Pallas kernels  53 us (41%)
  waiting for transfers between devices  45.9 us (36%)
  starting transfers between devices  22 us (17%)
  local copies, waits for them, and re-layouts  5.65 us (4%)
  other arithmetic  2.03 us (2%)
    ppermute x7, waiting for transfers between devices, shifted(): lax.ppermute(value, axis, [(i, (i + steps) % count) for i in range(count)])  19.4 us
    ppermute x10, waiting for transfers between devices, paired(): return lax.ppermute(value, axis, [(i, i ^ mask) for i in range(count)])  18.7 us
    pallas_call x2, Pallas kernels, apply_operator(): pl.pallas_call(far_cells_kernel, out_shape=(jax.ShapeDtypeStruct((owned,...  15.6 us
    pallas_call x1, Pallas kernels, inverse_factor(): pl.pallas_call(functools.partial(inverse_kernel, over), out_shape=jax.Sha...  13.4 us
    ppermute x10, starting transfers between devices, paired(): return lax.ppermute(value, axis, [(i, i ^ mask) for i in range(count)])  12.1 us
    pallas_call x2, Pallas kernels, apply_operator(): pl.pallas_call(functools.partial(near_sums_kernel, npc), out_shape=jax.Sh...  8.98 us
    ppermute x3, waiting for transfers between devices, passed_up(): lax.ppermute(onward, 'band', [(i, i + 1) for i in range(held, count - 1)])  7.84 us
    pallas_call x2, Pallas kernels, apply_operator(): pl.pallas_call(near_products_kernel, out_shape=jax.ShapeDtypeStruct(held,...  7.27 us
  transfers between devices with their start and end apart: 20, of which 13 were waited for; matrix products, arithmetic and copies ran while one was open for 3% of the time, Pallas kernels for 23%

profile of v4, /device:TPU:26, one launch (start us, length us, event | category | flops | bytes accessed | tf_op | source)
XLA Modules:
  0.0 128.9 jit_solution(12258987998614372864)
XLA Ops:
  0.0 1.2 copy-done.2
  5.4 3.6 %near_products.2.products_ref = f32[8,344,128]{2,1,0:T(8,128)S(1)} custom-call(s32[5488]{0:T(1024)S(1)} %reshape.34.links, f32[16]{0:T(128)S(1)} %copy-done.7, f32[3744,128]{1,0:T(8,128)S(1)} %get-tuple-element.32.ext_ref.wide_ref, bf16[343,343]{1,0:T(8,128)(2,1)S(1)} %copy-done), custom_call_target="tpu_custom_call" | custom-call | bytes 14680064 | tf_op jit(solution)/shard_map/near_products/pallas_call | solution.py:159
  9.0 7.8 %far_cells.2 = (f32[3456,128]{1,0:T(8,128)S(1)}, f32[288,128]{1,0:T(8,128)S(1)}) custom-call(s32[5488]{0:T(1024)S(1)} %reshape.34.links, f32[16]{0:T(128)S(1)} %copy-done.7, f32[3744,128]{1,0:T(8,128)S(1)} %get-tuple-element.32.ext_ref.wide_ref, bf16[288,128]{1,0:T(8,128)(2,1)S(1)} %collective-permute-done.ghost_ref, bf16[343,343]{1,0:T(8,128)(2,1)S(1)} %copy-done.1, ...), custom_call_target="tpu_custom_call" | custom-call | bytes 29360128 | tf_op jit(solution)/shard_map/far_cells/pallas_call | solution.py:170
  17.4 4.5 %near_sums.2.sums_ref = f32[3456,128]{1,0:T(8,128)S(1)} custom-call(s32[5488]{0:T(1024)S(1)} %reshape.34.links, f32[8,344,128]{2,1,0:T(8,128)S(1)} %near_products.2.products_ref, f32[3456,128]{1,0:T(8,128)S(1)} %get-tuple-element.35.start_ref), custom_call_target="tpu_custom_call" | custom-call | bytes 14680064 | tf_op jit(solution)/shard_map/near_sums/pallas_call | solution.py:185
  21.9 1.5 %first_term.1 = (f32[3456,128]{1,0:T(8,128)S(1)}, f32[3744,128]{1,0:T(8,128)S(1)}, bf16[288,128]{1,0:T(8,128)(2,1)S(1)}) custom-call(s32[288]{0:T(512)S(1)} %copy-done.6, f32[3456,128]{1,0:T(8,128)S(1)} %near_sums.2.sums_ref, f32[288,128]{1,0:T(8,128)S(1)} %collective-permute-done.1.back_ref), custom_call_target="tpu_custom_call" | custom-call | bytes 8388608 | tf_op jit(solution)/shard_map/first_term/pallas_call | solution.py:222
  23.4 1.3 %collective-permute-start.2 = (bf16[288,128]{1,0:T(8,128)(2,1)S(1)}, bf16[288,128]{1,0:T(8,128)(2,1)S(1)}, u32[]{:S(2)}, u32[]{:S(2)}) collective-permute-start(bf16[288,128]{1,0:T(8,128)(2,1)S(1)} %get-tuple-element.37), channel_id=1, source_target_pairs={{0,28},{4,0},{8,4},{12,8},{16,12},{20,16},{24,20},{28,24},{1,29},{... | collective-permute-start | bytes 221192 | tf_op jit(solution)/shard_map/ppermute | solution.py:30
  24.7 3.6 %near_products.3.products_ref = f32[8,344,128]{2,1,0:T(8,128)S(1)} custom-call(s32[5488]{0:T(1024)S(1)} %reshape.34.links, f32[16]{0:T(128)S(1)} %copy-done.7, f32[3744,128]{1,0:T(8,128)S(1)} %get-tuple-element.38.ext_ref, bf16[343,343]{1,0:T(8,128)(2,1)S(1)} %copy-done.1), custom_call_target="tpu_custom_call" | custom-call | bytes 14680064 | tf_op jit(solution)/shard_map/near_products/pallas_call | solution.py:159
  28.4 7.8 %far_cells.3 = (f32[3456,128]{1,0:T(8,128)S(1)}, f32[288,128]{1,0:T(8,128)S(1)}) custom-call(s32[5488]{0:T(1024)S(1)} %reshape.34.links, f32[16]{0:T(128)S(1)} %copy-done.7, f32[3744,128]{1,0:T(8,128)S(1)} %get-tuple-element.38.ext_ref, bf16[288,128]{1,0:T(8,128)(2,1)S(1)} %collective-permute-done.2.ghost_ref, bf16[343,343]{1,0:T(8,128)(2,1)S(1)} %copy-done.1, ...), custom_call_target="tpu_custom_call" | custom-call | bytes 29360128 | tf_op jit(solution)/shard_map/far_cells/pallas_call | solution.py:170
  36.2 1.8 %collective-permute-start.3 = (f32[288,128]{1,0:T(8,128)S(1)}, f32[288,128]{1,0:T(8,128)S(1)}, u32[]{:S(2)}, u32[]{:S(2)}) collective-permute-start(f32[288,128]{1,0:T(8,128)S(1)} %get-tuple-element.43), channel_id=1, source_target_pairs={{0,4},{4,8},{8,12},{12,16},{16,20},{20,24},{24,28},{28,0},{1,5},{5... | collective-permute-start | bytes 442376 | tf_op jit(solution)/shard_map/ppermute | solution.py:30
  38.0 4.5 %near_sums.3.sums_ref = f32[3456,128]{1,0:T(8,128)S(1)} custom-call(s32[5488]{0:T(1024)S(1)} %reshape.34.links, f32[8,344,128]{2,1,0:T(8,128)S(1)} %near_products.3.products_ref, f32[3456,128]{1,0:T(8,128)S(1)} %get-tuple-element.42.start_ref), custom_call_target="tpu_custom_call" | custom-call | bytes 14680064 | tf_op jit(solution)/shard_map/near_sums/pallas_call | solution.py:185
  42.5 1.4 %second_term.1 = (bf16[864,128]{1,0:T(8,128)(2,1)S(1)}, bf16[864,128]{1,0:T(8,128)(2,1)S(1)}, bf16[864,128]{1,0:T(8,128)(2,1)S(1)}, bf16[864,128]{1,0:T(8,128)(2,1)S(1)}, bf16[2592,128]{1,0:T(8,128)(2,1)S(1)}) custom-call(s32[1]{0:T(128)} %bitcast.band, s32[288]{0:T(512)S(1)} %copy-done.6, f32[3456,128]{1,0:T(8,128)S(1)} %near_sums.3.sums_ref, ...), custom_call_target="tpu_custom_call" | custom-call | bytes 6291456 | tf_op jit(solution)/shard_map/second_term/pallas_call | solution.py:255
  44.2 1.7 %collective-permute-start.5 = (bf16[864,128]{1,0:T(8,128)(2,1)S(1)}, bf16[864,128]{1,0:T(8,128)(2,1)S(1)}, u32[]{:S(2)}, u32[]{:S(2)}) collective-permute-start(bf16[864,128]{1,0:T(8,128)(2,1)S(1)} %get-tuple-element.46), channel_id=1, source_target_pairs={{0,2},{1,3},{2,0},{3,1},{4,6},{5,7},{6,4},{7,5},{8,10},{9,11},{10,... | collective-permute-start | bytes 663560 | tf_op jit(solution)/shard_map/ppermute | solution.py:30
  46.4 5.3 %collective-permute-done.4.refs_1_ = bf16[864,128]{1,0:T(8,128)(2,1)S(1)} collective-permute-done((bf16[864,128]{1,0:T(8,128)(2,1)S(1)}, bf16[864,128]{1,0:T(8,128)(2,1)S(1)}, u32[]{:S(2)}, u32[]{:S(2)}) %collective-permute-start.4) | collective-permute-done | bytes 221216 | tf_op jit(solution)/shard_map/ppermute | solution.py:30
  51.7 14.1 %collective-permute-done.5.refs_2_ = bf16[864,128]{1,0:T(8,128)(2,1)S(1)} collective-permute-done((bf16[864,128]{1,0:T(8,128)(2,1)S(1)}, bf16[864,128]{1,0:T(8,128)(2,1)S(1)}, u32[]{:S(2)}, u32[]{:S(2)}) %collective-permute-start.5) | collective-permute-done | bytes 221216 | tf_op jit(solution)/shard_map/ppermute | solution.py:30
  67.3 1.3 %collective-permute-start.12 = (bf16[2592,128]{1,0:T(8,128)(2,1)S(1)}, bf16[2592,128]{1,0:T(8,128)(2,1)S(1)}, u32[]{:S(2)}, u32[]{:S(2)}) collective-permute-start(bf16[2592,128]{1,0:T(8,128)(2,1)S(1)} %pad_maximum_fusion), channel_id=1, source_target_pairs={{0,1},{1,2},{2,3},{4,5},{5,6},{6,7},{8,9},{9,10},{10,11},{12,13},{... | collective-permute-start | bytes 1990664 | tf_op jit(solution)/shard_map/ppermute | solution.py:332
  70.2 2.1 %collective-permute-start.8 = (f32[160,128]{1,0:T(8,128)S(1)}, f32[160,128]{1,0:T(8,128)S(1)}, u32[]{:S(2)}, u32[]{:S(2)}) collective-permute-start(f32[160,128]{1,0:T(8,128)S(1)} %get-tuple-element.57), channel_id=1, source_target_pairs={{0,8},{4,12},{8,0},{12,4},{16,24},{20,28},{24,16},{28,20},{1,9},{5... | collective-permute-start | bytes 245768 | tf_op jit(solution)/shard_map/ppermute | solution.py:300
  72.8 2.9 %collective-permute-done.10 = f32[160,128]{1,0:T(8,128)S(1)} collective-permute-done((f32[160,128]{1,0:T(8,128)}, f32[160,128]{1,0:T(8,128)S(1)}, u32[]{:S(2)}, u32[]{:S(2)}) %collective-permute-start.10) | collective-permute-done | bytes 81952 | tf_op jit(solution)/shard_map/ppermute | solution.py:300
  77.9 2.5 %collective-permute-start.11 = (f32[160,128]{1,0:T(8,128)S(1)}, f32[160,128]{1,0:T(8,128)S(1)}, u32[]{:S(2)}, u32[]{:S(2)}) collective-permute-start(f32[160,128]{1,0:T(8,128)S(1)} %add_add_fusion), channel_id=1, source_target_pairs={{0,1},{1,0},{2,3},{3,2},{4,5},{5,4},{6,7},{7,6},{8,9},{9,8},{10,11... | collective-permute-start | bytes 245768 | tf_op jit(solution)/shard_map/ppermute | solution.py:300
  80.5 7.4 %collective-permute-done.11 = f32[160,128]{1,0:T(8,128)S(1)} collective-permute-done((f32[160,128]{1,0:T(8,128)S(1)}, f32[160,128]{1,0:T(8,128)S(1)}, u32[]{:S(2)}, u32[]{:S(2)}) %collective-permute-start.11) | collective-permute-done | bytes 81952 | tf_op jit(solution)/shard_map/ppermute | solution.py:300
  87.9 1.9 %collective-permute-start.13 = (f32[160,128]{1,0:T(8,128)S(1)}, f32[160,128]{1,0:T(8,128)S(1)}, u32[]{:S(2)}, u32[]{:S(2)}) collective-permute-start(f32[160,128]{1,0:T(8,128)S(1)} %add.63), channel_id=1, source_target_pairs={{0,2},{1,3},{2,0},{3,1},{4,6},{5,7},{6,4},{7,5},{8,10},{9,11},{10,... | collective-permute-start | bytes 245768 | tf_op jit(solution)/shard_map/ppermute | solution.py:300
  90.7 1.3 collective-permute-start.18
  92.0 1.3 %collective-permute-done.13 = f32[160,128]{1,0:T(8,128)S(1)} collective-permute-done((f32[160,128]{1,0:T(8,128)S(1)}, f32[160,128]{1,0:T(8,128)S(1)}, u32[]{:S(2)}, u32[]{:S(2)}) %collective-permute-start.13) | collective-permute-done | bytes 81952 | tf_op jit(solution)/shard_map/ppermute | solution.py:300
  94.2 1.5 %collective-permute-start.15 = (f32[160,128]{1,0:T(8,128)S(1)}, f32[160,128]{1,0:T(8,128)S(1)}, u32[]{:S(2)}, u32[]{:S(2)}) collective-permute-start(f32[160,128]{1,0:T(8,128)S(1)} %add.64), channel_id=1, source_target_pairs={{0,16},{4,20},{8,24},{12,28},{16,0},{20,4},{24,8},{28,12},{1,17},{... | collective-permute-start | bytes 245768 | tf_op jit(solution)/shard_map/ppermute | solution.py:300
  95.7 1.2 collective-permute-start.16
  96.9 1.6 %collective-permute-done.14 = f32[160,128]{1,0:T(8,128)S(1)} collective-permute-done((f32[160,128]{1,0:T(8,128)S(1)}, f32[160,128]{1,0:T(8,128)S(1)}, u32[]{:S(2)}, u32[]{:S(2)}) %collective-permute-start.14) | collective-permute-done | bytes 81952 | tf_op jit(solution)/shard_map/ppermute | solution.py:300
  99.2 1.9 %collective-permute-done.16 = f32[160,128]{1,0:T(8,128)S(1)} collective-permute-done((f32[160,128]{1,0:T(8,128)S(1)}, f32[160,128]{1,0:T(8,128)S(1)}, u32[]{:S(2)}, u32[]{:S(2)}) %collective-permute-start.16) | collective-permute-done | bytes 81952 | tf_op jit(solution)/shard_map/ppermute | solution.py:300
  101.8 1.6 %collective-permute-done.17 = f32[640,128]{1,0:T(8,128)S(1)} collective-permute-done((f32[640,128]{1,0:T(8,128)S(1)}, f32[640,128]{1,0:T(8,128)S(1)}, u32[]{:S(2)}, u32[]{:S(2)}) %collective-permute-start.17) | collective-permute-done | bytes 327712 | tf_op jit(solution)/shard_map/ppermute | solution.py:300
  103.4 5.5 %collective-permute-done.18.refs_6_ = bf16[2592,128]{1,0:T(8,128)(2,1)S(1)} collective-permute-done((bf16[2592,128]{1,0:T(8,128)(2,1)}, bf16[2592,128]{1,0:T(8,128)(2,1)S(1)}, u32[]{:S(2)}, u32[]{:S(2)}) %collective-permute-start.18) | collective-permute-done | bytes 663584 | tf_op jit(solution)/shard_map/ppermute | solution.py:332
  109.0 1.3 %collective-permute-start.19 = (bf16[2592,128]{1,0:T(8,128)(2,1)S(1)}, bf16[2592,128]{1,0:T(8,128)(2,1)S(1)}, u32[]{:S(2)}, u32[]{:S(2)}) collective-permute-start(bf16[2592,128]{1,0:T(8,128)(2,1)S(1)} %pad_maximum_fusion.2), channel_id=1, source_target_pairs={{2,3},{6,7},{10,11},{14,15},{18,19},{22,23},{26,27},{30,31}} | collective-permute-start | bytes 1990664 | tf_op jit(solution)/shard_map/ppermute | solution.py:332
  110.3 13.4 %inverse_factor.1.factor_ref = f32[512,512]{1,0:T(8,128)S(1)} custom-call(f32[1280,128]{1,0:T(8,128)S(1)} %bitcast.12), custom_call_target="tpu_custom_call" | custom-call | bytes 73400320 | tf_op jit(solution)/shard_map/inverse_factor/pallas_call | solution.py:488
  123.7 2.4 %collective-permute-done.19.refs_7_ = bf16[2592,128]{1,0:T(8,128)(2,1)S(1)} collective-permute-done((bf16[2592,128]{1,0:T(8,128)(2,1)S(1)}, bf16[2592,128]{1,0:T(8,128)(2,1)S(1)}, u32[]{:S(2)}, u32[]{:S(2)}) %collective-permute-start.19) | collective-permute-done | bytes 663584 | tf_op jit(solution)/shard_map/ppermute | solution.py:332
  126.0 2.9 %output.1 = f32[3456,128]{1,0:T(8,128)} custom-call(s32[1]{0:T(128)} %bitcast.band, f32[512,512]{1,0:T(8,128)S(1)} %inverse_factor.1.factor_ref, bf16[864,128]{1,0:T(8,128)(2,1)S(1)} %get-tuple-element.48.refs_0_, bf16[864,128]{1,0:T(8,128)(2,1)S(1)} %collective-permute-done.4.refs_1_, bf16[864,128]{1,0:T(8,128)(2,1)S(1)} %collective-permute-done.5.refs_2_, ...), custom_call_target="tpu_custom_call" | custom-call | bytes 10485760 | tf_op jit(solution)/shard_map/output/pallas_call | solution.py:538
  (54 shorter events, 14.5 us)
Async XLA Ops:
  0.0 1.2 copy-start.2
  1.2 0.7 copy-start.5
  2.8 6.2 %collective-permute-start = (bf16[288,128]{1,0:T(8,128)(2,1)S(1)}, bf16[288,128]{1,0:T(8,128)(2,1)S(1)}, u32[]{:S(2)}, u32[]{:S(2)}) collective-permute-start(bf16[288,128]{1,0:T(8,128)(2,1)S(1)} %get-tuple-element.31), channel_id=1, source_target_pairs={{0,28},{4,0},{8,4},{12,8},{16,12},{20,16},{24,20},{28,24},{1,29},{... | collective-permute-start | bytes 221192 | tf_op jit(solution)/shard_map/ppermute | solution.py:30
  3.7 1.0 copy-start
  4.7 0.7 copy-start.7
  5.4 3.7 %copy-start.1 = (bf16[343,343]{1,0:T(8,128)(2,1)S(1)}, bf16[343,343]{1,0:T(8,128)(2,1)}, u32[]{:S(2)}) copy-start(bf16[343,343]{1,0:T(8,128)(2,1)} %matrix_ref.7) | copy-start | bytes 705898
  5.4 3.7 %copy-start.4 = (f32[3456]{0:T(1024)S(1)}, f32[3456]{0:T(1024)}, u32[]{:S(2)}) copy-start(f32[3456]{0:T(1024)} %param.9) | copy-start | bytes 41476
  16.8 5.1 %collective-permute-start.1 = (f32[288,128]{1,0:T(8,128)S(1)}, f32[288,128]{1,0:T(8,128)S(1)}, u32[]{:S(2)}, u32[]{:S(2)}) collective-permute-start(f32[288,128]{1,0:T(8,128)S(1)} %get-tuple-element.36), channel_id=1, source_target_pairs={{0,4},{4,8},{8,12},{12,16},{16,20},{20,24},{24,28},{28,0},{1,5},{5... | collective-permute-start | bytes 442376 | tf_op jit(solution)/shard_map/ppermute | solution.py:30
  17.4 4.5 %copy-start.6 = (s32[288]{0:T(512)S(1)}, s32[288]{0:T(512)}, u32[]{:S(2)}) copy-start(s32[288]{0:T(512)} %nodes.5) | copy-start | bytes 3460
  23.4 4.9 %collective-permute-start.2 = (bf16[288,128]{1,0:T(8,128)(2,1)S(1)}, bf16[288,128]{1,0:T(8,128)(2,1)S(1)}, u32[]{:S(2)}, u32[]{:S(2)}) collective-permute-start(bf16[288,128]{1,0:T(8,128)(2,1)S(1)} %get-tuple-element.37), channel_id=1, source_target_pairs={{0,28},{4,0},{8,4},{12,8},{16,12},{20,16},{24,20},{28,24},{1,29},{... | collective-permute-start | bytes 221192 | tf_op jit(solution)/shard_map/ppermute | solution.py:30
  36.2 6.3 %collective-permute-start.3 = (f32[288,128]{1,0:T(8,128)S(1)}, f32[288,128]{1,0:T(8,128)S(1)}, u32[]{:S(2)}, u32[]{:S(2)}) collective-permute-start(f32[288,128]{1,0:T(8,128)S(1)} %get-tuple-element.43), channel_id=1, source_target_pairs={{0,4},{4,8},{8,12},{12,16},{16,20},{20,24},{24,28},{28,0},{1,5},{5... | collective-permute-start | bytes 442376 | tf_op jit(solution)/shard_map/ppermute | solution.py:30
  38.0 4.5 %copy-start.3 = (bf16[3456,128]{1,0:T(8,128)(2,1)S(1)}, bf16[3456,128]{1,0:T(8,128)(2,1)}, u32[]{:S(2)}) copy-start(bf16[3456,128]{1,0:T(8,128)(2,1)} %previous_ref.1) | copy-start | bytes 2654212
  43.9 7.7 %collective-permute-start.4 = (bf16[864,128]{1,0:T(8,128)(2,1)S(1)}, bf16[864,128]{1,0:T(8,128)(2,1)S(1)}, u32[]{:S(2)}, u32[]{:S(2)}) collective-permute-start(bf16[864,128]{1,0:T(8,128)(2,1)S(1)} %get-tuple-element.45), channel_id=1, source_target_pairs={{0,1},{1,2},{2,3},{3,0},{4,5},{5,6},{6,7},{7,4},{8,9},{9,10},{10,1... | collective-permute-start | bytes 663560 | tf_op jit(solution)/shard_map/ppermute | solution.py:30
  44.2 21.6 %collective-permute-start.5 = (bf16[864,128]{1,0:T(8,128)(2,1)S(1)}, bf16[864,128]{1,0:T(8,128)(2,1)S(1)}, u32[]{:S(2)}, u32[]{:S(2)}) collective-permute-start(bf16[864,128]{1,0:T(8,128)(2,1)S(1)} %get-tuple-element.46), channel_id=1, source_target_pairs={{0,2},{1,3},{2,0},{3,1},{4,6},{5,7},{6,4},{7,5},{8,10},{9,11},{10,... | collective-permute-start | bytes 663560 | tf_op jit(solution)/shard_map/ppermute | solution.py:30
  45.9 19.9 %collective-permute-start.6 = (bf16[864,128]{1,0:T(8,128)(2,1)S(1)}, bf16[864,128]{1,0:T(8,128)(2,1)S(1)}, u32[]{:S(2)}, u32[]{:S(2)}) collective-permute-start(bf16[864,128]{1,0:T(8,128)(2,1)S(1)} %get-tuple-element.47), channel_id=1, source_target_pairs={{0,3},{1,0},{2,1},{3,2},{4,7},{5,4},{6,5},{7,6},{8,11},{9,8},{10,9... | collective-permute-start | bytes 663560 | tf_op jit(solution)/shard_map/ppermute | solution.py:30
  66.8 1.9 %collective-permute-start.7 = (f32[640,128]{1,0:T(8,128)S(1)}, f32[640,128]{1,0:T(8,128)S(1)}, u32[]{:S(2)}, u32[]{:S(2)}) collective-permute-start(f32[640,128]{1,0:T(8,128)S(1)} %constant_dynamic-slice_fusion.3), channel_id=1, source_target_pairs={{0,4},{4,0},{8,12},{12,8},{16,20},{20,16},{24,28},{28,24},{1,5},{5... | collective-permute-start | bytes 983048 | tf_op jit(solution)/shard_map/ppermute | solution.py:300
  67.3 20.6 %collective-permute-start.12 = (bf16[2592,128]{1,0:T(8,128)(2,1)S(1)}, bf16[2592,128]{1,0:T(8,128)(2,1)S(1)}, u32[]{:S(2)}, u32[]{:S(2)}) collective-permute-start(bf16[2592,128]{1,0:T(8,128)(2,1)S(1)} %pad_maximum_fusion), channel_id=1, source_target_pairs={{0,1},{1,2},{2,3},{4,5},{5,6},{6,7},{8,9},{9,10},{10,11},{12,13},{... | collective-permute-start | bytes 1990664 | tf_op jit(solution)/shard_map/ppermute | solution.py:332
  69.3 6.4 %collective-permute-start.10 = (f32[160,128]{1,0:T(8,128)}, f32[160,128]{1,0:T(8,128)S(1)}, u32[]{:S(2)}, u32[]{:S(2)}) collective-permute-start(f32[160,128]{1,0:T(8,128)} %get-tuple-element.58), channel_id=1, source_target_pairs={{0,24},{4,28},{8,16},{12,20},{16,8},{20,12},{24,0},{28,4},{1,25},{... | collective-permute-start | bytes 245768 | tf_op jit(solution)/shard_map/ppermute | solution.py:300
  70.2 6.7 %collective-permute-start.8 = (f32[160,128]{1,0:T(8,128)S(1)}, f32[160,128]{1,0:T(8,128)S(1)}, u32[]{:S(2)}, u32[]{:S(2)}) collective-permute-start(f32[160,128]{1,0:T(8,128)S(1)} %get-tuple-element.57), channel_id=1, source_target_pairs={{0,8},{4,12},{8,0},{12,4},{16,24},{20,28},{24,16},{28,20},{1,9},{5... | collective-permute-start | bytes 245768 | tf_op jit(solution)/shard_map/ppermute | solution.py:300
  72.3 4.7 %collective-permute-start.9 = (f32[160,128]{1,0:T(8,128)S(1)}, f32[160,128]{1,0:T(8,128)}, u32[]{:S(2)}, u32[]{:S(2)}) collective-permute-start(f32[160,128]{1,0:T(8,128)S(1)} %get-tuple-element.59), channel_id=1, source_target_pairs={{0,16},{4,20},{8,24},{12,28},{16,0},{20,4},{24,8},{28,12},{1,17},{... | collective-permute-start | bytes 245768 | tf_op jit(solution)/shard_map/ppermute | solution.py:300
  77.9 9.9 %collective-permute-start.11 = (f32[160,128]{1,0:T(8,128)S(1)}, f32[160,128]{1,0:T(8,128)S(1)}, u32[]{:S(2)}, u32[]{:S(2)}) collective-permute-start(f32[160,128]{1,0:T(8,128)S(1)} %add_add_fusion), channel_id=1, source_target_pairs={{0,1},{1,0},{2,3},{3,2},{4,5},{5,4},{6,7},{7,6},{8,9},{9,8},{10,11... | collective-permute-start | bytes 245768 | tf_op jit(solution)/shard_map/ppermute | solution.py:300
  87.9 5.4 %collective-permute-start.13 = (f32[160,128]{1,0:T(8,128)S(1)}, f32[160,128]{1,0:T(8,128)S(1)}, u32[]{:S(2)}, u32[]{:S(2)}) collective-permute-start(f32[160,128]{1,0:T(8,128)S(1)} %add.63), channel_id=1, source_target_pairs={{0,2},{1,3},{2,0},{3,1},{4,6},{5,7},{6,4},{7,5},{8,10},{9,11},{10,... | collective-permute-start | bytes 245768 | tf_op jit(solution)/shard_map/ppermute | solution.py:300
  90.7 18.2 %collective-permute-start.18 = (bf16[2592,128]{1,0:T(8,128)(2,1)}, bf16[2592,128]{1,0:T(8,128)(2,1)S(1)}, u32[]{:S(2)}, u32[]{:S(2)}) collective-permute-start(bf16[2592,128]{1,0:T(8,128)(2,1)} %pad_maximum_fusion.1), channel_id=1, source_target_pairs={{1,2},{2,3},{5,6},{6,7},{9,10},{10,11},{13,14},{14,15},{17,18},{18... | collective-permute-start | bytes 1990664 | tf_op jit(solution)/shard_map/ppermute | solution.py:332
  93.4 5.2 %collective-permute-start.14 = (f32[160,128]{1,0:T(8,128)S(1)}, f32[160,128]{1,0:T(8,128)S(1)}, u32[]{:S(2)}, u32[]{:S(2)}) collective-permute-start(f32[160,128]{1,0:T(8,128)S(1)} %add.64), channel_id=1, source_target_pairs={{0,8},{4,12},{8,0},{12,4},{16,24},{20,28},{24,16},{28,20},{1,9},{5... | collective-permute-start | bytes 245768 | tf_op jit(solution)/shard_map/ppermute | solution.py:300
  94.2 5.0 %collective-permute-start.15 = (f32[160,128]{1,0:T(8,128)S(1)}, f32[160,128]{1,0:T(8,128)S(1)}, u32[]{:S(2)}, u32[]{:S(2)}) collective-permute-start(f32[160,128]{1,0:T(8,128)S(1)} %add.64), channel_id=1, source_target_pairs={{0,16},{4,20},{8,24},{12,28},{16,0},{20,4},{24,8},{28,12},{1,17},{... | collective-permute-start | bytes 245768 | tf_op jit(solution)/shard_map/ppermute | solution.py:300
  95.7 5.3 %collective-permute-start.16 = (f32[160,128]{1,0:T(8,128)S(1)}, f32[160,128]{1,0:T(8,128)S(1)}, u32[]{:S(2)}, u32[]{:S(2)}) collective-permute-start(f32[160,128]{1,0:T(8,128)S(1)} %add.64), channel_id=1, source_target_pairs={{0,24},{4,28},{8,16},{12,20},{16,8},{20,12},{24,0},{28,4},{1,25},{... | collective-permute-start | bytes 245768 | tf_op jit(solution)/shard_map/ppermute | solution.py:300
  101.7 1.7 %collective-permute-start.17 = (f32[640,128]{1,0:T(8,128)S(1)}, f32[640,128]{1,0:T(8,128)S(1)}, u32[]{:S(2)}, u32[]{:S(2)}) collective-permute-start(f32[640,128]{1,0:T(8,128)S(1)} %bitcast.15), channel_id=1, source_target_pairs={{0,4},{4,0},{8,12},{12,8},{16,20},{20,16},{24,28},{28,24},{1,5},{5... | collective-permute-start | bytes 983048 | tf_op jit(solution)/shard_map/ppermute | solution.py:300
  109.0 17.1 %collective-permute-start.19 = (bf16[2592,128]{1,0:T(8,128)(2,1)S(1)}, bf16[2592,128]{1,0:T(8,128)(2,1)S(1)}, u32[]{:S(2)}, u32[]{:S(2)}) collective-permute-start(bf16[2592,128]{1,0:T(8,128)(2,1)S(1)} %pad_maximum_fusion.2), channel_id=1, source_target_pairs={{2,3},{6,7},{10,11},{14,15},{18,19},{22,23},{26,27},{30,31}} | collective-permute-start | bytes 1990664 | tf_op jit(solution)/shard_map/ppermute | solution.py:332

commit v5 on v4

--- a/solution.py
+++ b/solution.py
@@ -75,11 +75,28 @@
     return ext, ext, edge
 
 
-def gather_cells(links, npc, ext_ref, gathered, first):
+def packed_links(links):
+    npc = links.shape[1]
+    half = (npc + 1) // 2
+    later = jnp.pad(links[:, half:], ((0, 0), (0, 2 * half - npc)))
+    return (links[:, :half] | (later << 16)).reshape(-1)
+
+
+def each_row(words, npc, cell, visit):
+    half = (npc + 1) // 2
+    for r in range(half):
+        word = words[cell * half + r]
+        visit(r, pl.ds(word & 0xFFFF, 1))
+        if r + half < npc:
+            visit(r + half, pl.ds(word >> 16, 1))
+
+
+def gather_cells(words, npc, ext_ref, gathered, first):
     def cell(c, _):
-        base = (first + c) * npc
-        for r in range(npc):
-            gathered[c, r : r + 1, :] = ext_ref[pl.ds(links[base + r], 1), :]
+        def visit(r, row):
+            gathered[c, r : r + 1, :] = ext_ref[row, :]
+
+        each_row(words, npc, first + c, visit)
         return 0
 
     lax.fori_loop(0, gathered.shape[0], cell, 0)
@@ -98,15 +115,16 @@
             )
 
 
-def scatter_cells(links, npc, products, sums, first):
-    chains = len(sums)
-
+def scatter_cells(words, npc, products, sums, first):
     def cell(c, _):
-        base = (first + c) * npc
-        for r in range(npc):
-            total = sums[r % chains]
-            row = pl.ds(links[base + r], 1)
+        seen = []
+
+        def visit(r, row):
+            total = sums[len(seen) % len(sums)]
+            seen.append(r)
             total[row, :] = total[row, :] + products[c, r : r + 1, :]
+
+        each_row(words, npc, first + c, visit)
         return 0
 
     lax.fori_loop(0, products.shape[0], cell, 0)
@@ -266,63 +284,87 @@
     return made[:count], made[count]
 
 
-def gram_kernel(band, *refs):
-    pieces, out_ref, held = refs[:-2], refs[-2], refs[-1]
+def gram_kernel(place, *refs):
+    pieces, (keep_ref, send_ref, held, whole) = refs[:-4], refs[-4:]
     count = len(pieces)
     for s, piece in enumerate(pieces):
-        held[lax.rem(band[0] + (count - s), count)] = piece[...]
+        held[lax.rem(place[0] + (count - s), count)] = piece[...]
     at = 0
     for i in range(count):
         for j in range(i + 1):
-            out_ref[at : at + LANES, :] = lax.dot_general(
+            whole[at : at + LANES, :] = lax.dot_general(
                 held[i], held[j], (((0,), (0,)), ((), ())), preferred_element_type=F32
             )
             at += LANES
-
-
-def partial_gram(band, pieces):
+    half = at // 2
+    mine = pl.multiple_of(place[1] * half, half)
+    keep_ref[...] = whole[pl.ds(mine, half), :]
+    send_ref[...] = whole[pl.ds(half - mine, half), :]
+
+
+def partial_gram(place, pieces):
     count = len(pieces)
-    blocks = count * (count + 1) // 2
+    rows = count * (count + 1) // 2 * LANES
     return pl.pallas_call(
         gram_kernel,
-        out_shape=jax.ShapeDtypeStruct((blocks * LANES, LANES), F32),
+        out_shape=[jax.ShapeDtypeStruct((rows // 2, LANES), F32)] * 2,
         in_specs=[SM] + [VM] * count,
-        out_specs=VM,
-        scratch_shapes=[pltpu.VMEM((count,) + pieces[0].shape, BF16)],
+        out_specs=[VM] * 2,
+        scratch_shapes=[
+            pltpu.VMEM((count,) + pieces[0].shape, BF16),
+            pltpu.VMEM((rows, LANES), F32),
+        ],
         compiler_params=params(16),
         cost_estimate=cost(0, 4 << 20),
         name="partial_gram",
-    )(band, *pieces)
+    )(place, *pieces)
+
+
+def quarters_kernel(place, a_ref, b_ref, *refs):
+    outs, total = refs[:-1], refs[-1]
+    total[...] = a_ref[...] + b_ref[...]
+    rows = outs[0].shape[0]
+    for m, out in enumerate(outs):
+        out[...] = total[pl.ds(pl.multiple_of((place[2] ^ m) * rows, rows), rows), :]
+
+
+def quarters(place, a, b, count):
+    rows = a.shape[0] // count
+    return pl.pallas_call(
+        quarters_kernel,
+        out_shape=[jax.ShapeDtypeStruct((rows, LANES), F32)] * count,
+        in_specs=[SM, VM, VM],
+        out_specs=[VM] * count,
+        scratch_shapes=[pltpu.VMEM(a.shape, F32)],
+        compiler_params=params(4),
+        cost_estimate=cost(0, 1 << 20),
+        name="quarters",
+    )(place, a, b)
+
+
+def joined_kernel(place, *refs):
+    parts, out_ref = refs[:-1], refs[-1]
+    rows = parts[0].shape[0]
+    for m, part in enumerate(parts):
+        out_ref[pl.ds(pl.multiple_of((place[2] ^ m) * rows, rows), rows), :] = part[...]
+
+
+def joined(place, parts):
+    rows = parts[0].shape[0] * len(parts)
+    return pl.pallas_call(
+        joined_kernel,
+        out_shape=jax.ShapeDtypeStruct((rows, LANES), F32),
+        in_specs=[SM] + [VM] * len(parts),
+        out_specs=VM,
+        compiler_params=params(4),
+        cost_estimate=cost(0, 1 << 20),
+        name="joined",
+    )(place, *parts)
 
 
 def paired(value, axis, mask):
     count = lax.axis_size(axis)
     return lax.ppermute(value, axis, [(i, i ^ mask) for i in range(count)])
-
-
-def chunk(value, count, index):
-    rows = value.shape[0] // count
-    return lax.dynamic_slice_in_dim(value, index * rows, rows, 0)
-
-
-def reduced(value):
-    me = lax.axis_index("domain")
-    side, place = me % 2, me // 2
-    half = chunk(value, 2, side) + paired(chunk(value, 2, 1 - side), "domain", 1)
-    total = chunk(half, 4, place)
-    for part in [paired(chunk(half, 4, place ^ m), "domain", 2 * m) for m in (1, 2, 3)]:
-        total = total + part
-    return total
-
-
-def gathered_back(total):
-    me = lax.axis_index("domain")
-    side, place = me % 2, me // 2
-    parts = jnp.stack([total] + [paired(total, "domain", 2 * m) for m in (1, 2, 3)])
-    half = parts[place ^ jnp.arange(4)].reshape(-1, LANES)
-    other = paired(half, "domain", 1)
-    pair = jnp.where(side == 0, jnp.stack([half, other]), jnp.stack([other, half]))
-    return pair.reshape(-1, LANES)
 
 
 def passed_up(rests, firsts, held):
@@ -336,22 +378,29 @@
     return lax.optimization_barrier(values)
 
 
-def summed_beside(gram, rests, firsts):
+def summed_beside(place, keep, send, rests, firsts):
     count = lax.axis_size("band")
+    half = keep + paired(send, "domain", 1)
     if lax.axis_size("domain") != 8 or count != 4:
         for held in range(count - 1):
             rests.append(passed_up(rests, firsts, held))
-        return lax.psum(gram, ("domain", "band"))
+        side = lax.axis_index("domain") % 2
+        both = jnp.stack([half, jnp.zeros_like(half)])
+        both = lax.psum(jnp.where(side == 0, both, both[::-1]) * 1.0, ("domain", "band"))
+        return both[side], both[1 - side]
     rests.append(passed_up(rests, firsts, 0))
-    total = reduced(gram)
-    total = total + paired(total, "band", 1)
-    total, rests[1] = ordered(total, rests[1])
+    total, *others = quarters(place, keep, paired(send, "domain", 1), 4)
+    for part in [paired(other, "domain", 2 * m) for m, other in enumerate(others, 1)]:
+        total = total + part
+    parts = [total] + [shifted(total, "band", s) for s in range(1, count)]
+    parts[1], rests[1] = ordered(parts[1], rests[1])
     rests.append(passed_up(rests, firsts, 1))
-    total = total + paired(total, "band", 2)
-    total = gathered_back(total)
-    total, rests[2] = ordered(total, rests[2])
-    rests.append(passed_up(rests, firsts, 2))
-    return total
+    rows = firsts[1].shape[0]
+    skipping = jnp.concatenate([rests[1][2 * rows :], firsts[1], rests[1][:rows]])
+    rests.append(lax.ppermute(skipping, "band", [(1, 3)]))
+    total = sum(parts[1:], parts[0])
+    half = joined(place, [total] + [paired(total, "domain", 2 * m) for m in (1, 2, 3)])
+    return half, paired(half, "domain", 1)
 
 
 def split_dot(a, b, dims=(((1,), (0,)), ((), ()))):
@@ -439,7 +488,11 @@
     return done
 
 
-def inverse_kernel(over, packed_ref, out_ref, work, small):
+def inverse_kernel(over, place, mine_ref, other_ref, out_ref, packed_ref, work, small):
+    half = mine_ref.shape[0]
+    mine = pl.multiple_of(place[1] * half, half)
+    packed_ref[pl.ds(mine, half), :] = mine_ref[...]
+    packed_ref[pl.ds(half - mine, half), :] = other_ref[...]
     size = work.shape[0]
     blocks = size // LANES
     at = 0
@@ -484,17 +537,21 @@
     lax.fori_loop(0, blocks, step, 0)
 
 
-def inverse_factor(packed, size, over):
+def inverse_factor(place, mine, other, size, over):
     return pl.pallas_call(
         functools.partial(inverse_kernel, over),
         out_shape=jax.ShapeDtypeStruct((size, size), F32),
-        in_specs=[VM],
+        in_specs=[SM, VM, VM],
         out_specs=VM,
-        scratch_shapes=[pltpu.VMEM((size, size), F32), pltpu.VMEM((LANES, LANES), F32)],
+        scratch_shapes=[
+            pltpu.VMEM((2 * mine.shape[0], LANES), F32),
+            pltpu.VMEM((size, size), F32),
+            pltpu.VMEM((LANES, LANES), F32),
+        ],
         compiler_params=params(16),
         cost_estimate=cost(0, 70 << 20),
         name="inverse_factor",
-    )(packed)
+    )(place, mine, other)
 
 
 def output_kernel(band, factor_ref, *refs):
@@ -558,7 +615,7 @@
     levels = potential.reshape(owned // LANES, LANES)
 
     operator = functools.partial(
-        apply_operator, connectivity.reshape(-1), cell_scale, cell_matrix, levels
+        apply_operator, packed_links(connectivity), cell_scale, cell_matrix, levels
     )
     sums, back = operator(*prepare(boundary_nodes, states_block))
     sums, back = operator(*first_term(boundary_nodes, sums, back))
@@ -567,8 +624,12 @@
     firsts = [pieces[0]] + [shifted(pieces[s], "band", s) for s in range(1, count)]
     firsts = list(ordered(*firsts))
     rests = [rest]
-    packed = summed_beside(partial_gram(band, firsts), rests, firsts)
-    factor = inverse_factor(packed, count * LANES, 1.0 / (owned * lax.axis_size("domain")))
+    domain = lax.axis_index("domain")
+    place = jnp.stack([lax.axis_index("band"), domain % 2, domain // 2]).astype(jnp.int32)
+    keep, send = partial_gram(place, firsts)
+    mine, other = summed_beside(place, keep, send, rests, firsts)
+    over = 1.0 / (owned * lax.axis_size("domain"))
+    factor = inverse_factor(place, mine, other, count * LANES, over)
     return output(band, factor, firsts, rests)
 
 

time: 129 us -> 125 us (0.969)
  waiting for transfers between devices: 45.9 us -> 43.1 us
  Pallas kernels: 53 us -> 54.3 us
    ppermute x7 -> x10, waiting for transfers between devices: 19.4 us -> 29.2 us  [shifted(): lax.ppermute(value, axis, [(i, (i + steps) % count) for i in range(count)])]
    ppermute x10 -> x8, waiting for transfers between devices: 18.7 us -> 9.1 us  [paired(): return lax.ppermute(value, axis, [(i, i ^ mask) for i in range(count)])]
    ppermute x3 -> x2, waiting for transfers between devices: 7.84 us -> 0.01 us  [passed_up(): lax.ppermute(onward, 'band', [(i, i + 1) for i in range(held, count - 1)])]
    ppermute x0 -> x1, waiting for transfers between devices: none -> 4.82 us  [summed_beside(): rests.append(lax.ppermute(skipping, 'band', [(1, 3)]))]
    ppermute x10 -> x8, starting transfers between devices: 12.1 us -> 7.49 us  [paired(): return lax.ppermute(value, axis, [(i, i ^ mask) for i in range(count)])]
    ppermute x7 -> x10, starting transfers between devices: 6.11 us -> 10.6 us  [shifted(): lax.ppermute(value, axis, [(i, (i + steps) % count) for i in range(count)])]
    pallas_call x1 -> x3, Pallas kernels: 0.93 us -> 2.69 us  [the longest x1 1.52 us: partial_gram(): pl.pallas_call(gram_kernel, out_shape=[jax.ShapeDtypeStruct((rows // 2, L...]
    ppermute x0 -> x1, starting transfers between devices: none -> 1.29 us  [summed_beside(): rests.append(lax.ppermute(skipping, 'band', [(1, 3)]))]
  transfers between devices with their start and end apart: 20 -> 21, of which waited for: 13 -> 11; matrix products, arithmetic and copies ran while one was open for 3% -> 2% of each run, Pallas kernels for 23% -> 25%
where the time goes in v5:
time: 125 us
  Pallas kernels  54.3 us (43%)
  waiting for transfers between devices  43.1 us (34%)
  starting transfers between devices  22 us (18%)
  local copies, waits for them, and re-layouts  4.45 us (4%)
    ppermute x10, waiting for transfers between devices, shifted(): lax.ppermute(value, axis, [(i, (i + steps) % count) for i in range(count)])  29.2 us
    pallas_call x2, Pallas kernels, apply_operator(): pl.pallas_call(far_cells_kernel, out_shape=(jax.ShapeDtypeStruct((owned,...  15.3 us
    pallas_call x1, Pallas kernels, inverse_factor(): pl.pallas_call(functools.partial(inverse_kernel, over), out_shape=jax.Sha...  14 us
    ppermute x10, starting transfers between devices, shifted(): lax.ppermute(value, axis, [(i, (i + steps) % count) for i in range(count)])  10.6 us
    ppermute x8, waiting for transfers between devices, paired(): return lax.ppermute(value, axis, [(i, i ^ mask) for i in range(count)])  9.1 us
    pallas_call x2, Pallas kernels, apply_operator(): pl.pallas_call(functools.partial(near_sums_kernel, npc), out_shape=jax.Sh...  8.62 us
    ppermute x8, starting transfers between devices, paired(): return lax.ppermute(value, axis, [(i, i ^ mask) for i in range(count)])  7.49 us
    pallas_call x2, Pallas kernels, apply_operator(): pl.pallas_call(near_products_kernel, out_shape=jax.ShapeDtypeStruct(held,...  6.94 us
  transfers between devices with their start and end apart: 21, of which 11 were waited for; matrix products, arithmetic and copies ran while one was open for 2% of the time, Pallas kernels for 25%

profile of v5, /device:TPU:26, one launch (start us, length us, event | category | flops | bytes accessed | tf_op | source)
XLA Modules:
  0.0 125.0 jit_solution(17556466338996080001)
XLA Ops:
  0.0 1.2 copy-done.2
  6.1 3.5 %near_products.2.products_ref = f32[8,344,128]{2,1,0:T(8,128)S(1)} custom-call(s32[2752]{0:T(1024)S(1)} %reshape.10.links, f32[16]{0:T(128)S(1)} %copy-done.7, f32[3744,128]{1,0:T(8,128)S(1)} %get-tuple-element.36.ext_ref.wide_ref, bf16[343,343]{1,0:T(8,128)(2,1)S(1)} %copy-done), custom_call_target="tpu_custom_call" | custom-call | bytes 14680064 | tf_op jit(solution)/shard_map/near_products/pallas_call | solution.py:177
  9.7 7.7 %far_cells.2 = (f32[3456,128]{1,0:T(8,128)S(1)}, f32[288,128]{1,0:T(8,128)S(1)}) custom-call(s32[2752]{0:T(1024)S(1)} %reshape.10.links, f32[16]{0:T(128)S(1)} %copy-done.7, f32[3744,128]{1,0:T(8,128)S(1)} %get-tuple-element.36.ext_ref.wide_ref, bf16[288,128]{1,0:T(8,128)(2,1)S(1)} %collective-permute-done.ghost_ref, bf16[343,343]{1,0:T(8,128)(2,1)S(1)} %copy-done.1, ...), custom_call_target="tpu_custom_call" | custom-call | bytes 29360128 | tf_op jit(solution)/shard_map/far_cells/pallas_call | solution.py:188
  17.9 4.3 %near_sums.2.sums_ref = f32[3456,128]{1,0:T(8,128)S(1)} custom-call(s32[2752]{0:T(1024)S(1)} %reshape.10.links, f32[8,344,128]{2,1,0:T(8,128)S(1)} %near_products.2.products_ref, f32[3456,128]{1,0:T(8,128)S(1)} %get-tuple-element.39.start_ref), custom_call_target="tpu_custom_call" | custom-call | bytes 14680064 | tf_op jit(solution)/shard_map/near_sums/pallas_call | solution.py:203
  22.2 1.5 %first_term.1 = (f32[3456,128]{1,0:T(8,128)S(1)}, f32[3744,128]{1,0:T(8,128)S(1)}, bf16[288,128]{1,0:T(8,128)(2,1)S(1)}) custom-call(s32[288]{0:T(512)S(1)} %copy-done.6, f32[3456,128]{1,0:T(8,128)S(1)} %near_sums.2.sums_ref, f32[288,128]{1,0:T(8,128)S(1)} %collective-permute-done.1.back_ref), custom_call_target="tpu_custom_call" | custom-call | bytes 8388608 | tf_op jit(solution)/shard_map/first_term/pallas_call | solution.py:240
  23.7 1.3 %collective-permute-start.2 = (bf16[288,128]{1,0:T(8,128)(2,1)S(1)}, bf16[288,128]{1,0:T(8,128)(2,1)S(1)}, u32[]{:S(2)}, u32[]{:S(2)}) collective-permute-start(bf16[288,128]{1,0:T(8,128)(2,1)S(1)} %get-tuple-element.41), channel_id=1, source_target_pairs={{0,28},{4,0},{8,4},{12,8},{16,12},{20,16},{24,20},{28,24},{1,29},{... | collective-permute-start | bytes 221192 | tf_op jit(solution)/shard_map/ppermute | solution.py:30
  25.0 3.5 %near_products.3.products_ref = f32[8,344,128]{2,1,0:T(8,128)S(1)} custom-call(s32[2752]{0:T(1024)S(1)} %reshape.10.links, f32[16]{0:T(128)S(1)} %copy-done.8, f32[3744,128]{1,0:T(8,128)S(1)} %get-tuple-element.42.ext_ref, bf16[343,343]{1,0:T(8,128)(2,1)S(1)} %copy-done.1), custom_call_target="tpu_custom_call" | custom-call | bytes 14680064 | tf_op jit(solution)/shard_map/near_products/pallas_call | solution.py:177
  28.5 7.7 %far_cells.3 = (f32[3456,128]{1,0:T(8,128)S(1)}, f32[288,128]{1,0:T(8,128)S(1)}) custom-call(s32[2752]{0:T(1024)S(1)} %reshape.10.links, f32[16]{0:T(128)S(1)} %copy-done.8, f32[3744,128]{1,0:T(8,128)S(1)} %get-tuple-element.42.ext_ref, bf16[288,128]{1,0:T(8,128)(2,1)S(1)} %collective-permute-done.2.ghost_ref, bf16[343,343]{1,0:T(8,128)(2,1)S(1)} %copy-done.1, ...), custom_call_target="tpu_custom_call" | custom-call | bytes 29360128 | tf_op jit(solution)/shard_map/far_cells/pallas_call | solution.py:188
  36.2 1.9 %collective-permute-start.3 = (f32[288,128]{1,0:T(8,128)S(1)}, f32[288,128]{1,0:T(8,128)S(1)}, u32[]{:S(2)}, u32[]{:S(2)}) collective-permute-start(f32[288,128]{1,0:T(8,128)S(1)} %get-tuple-element.47), channel_id=1, source_target_pairs={{0,4},{4,8},{8,12},{12,16},{16,20},{20,24},{24,28},{28,0},{1,5},{5... | collective-permute-start | bytes 442376 | tf_op jit(solution)/shard_map/ppermute | solution.py:30
  38.2 4.3 %near_sums.3.sums_ref = f32[3456,128]{1,0:T(8,128)S(1)} custom-call(s32[2752]{0:T(1024)S(1)} %reshape.10.links, f32[8,344,128]{2,1,0:T(8,128)S(1)} %near_products.3.products_ref, f32[3456,128]{1,0:T(8,128)S(1)} %get-tuple-element.46.start_ref), custom_call_target="tpu_custom_call" | custom-call | bytes 14680064 | tf_op jit(solution)/shard_map/near_sums/pallas_call | solution.py:203
  42.5 1.4 %second_term.1 = (bf16[864,128]{1,0:T(8,128)(2,1)S(1)}, bf16[864,128]{1,0:T(8,128)(2,1)S(1)}, bf16[864,128]{1,0:T(8,128)(2,1)S(1)}, bf16[864,128]{1,0:T(8,128)(2,1)S(1)}, bf16[2592,128]{1,0:T(8,128)(2,1)S(1)}) custom-call(s32[1]{0:T(128)} %bitcast.band, s32[288]{0:T(512)S(1)} %copy-done.6, f32[3456,128]{1,0:T(8,128)S(1)} %near_sums.3.sums_ref, ...), custom_call_target="tpu_custom_call" | custom-call | bytes 6291456 | tf_op jit(solution)/shard_map/second_term/pallas_call | solution.py:273
  44.1 1.7 %collective-permute-start.5 = (bf16[864,128]{1,0:T(8,128)(2,1)S(1)}, bf16[864,128]{1,0:T(8,128)(2,1)S(1)}, u32[]{:S(2)}, u32[]{:S(2)}) collective-permute-start(bf16[864,128]{1,0:T(8,128)(2,1)S(1)} %get-tuple-element.50), channel_id=1, source_target_pairs={{0,2},{1,3},{2,0},{3,1},{4,6},{5,7},{6,4},{7,5},{8,10},{9,11},{10,... | collective-permute-start | bytes 663560 | tf_op jit(solution)/shard_map/ppermute | solution.py:30
  46.4 5.4 %collective-permute-done.4.refs_1_ = bf16[864,128]{1,0:T(8,128)(2,1)S(1)} collective-permute-done((bf16[864,128]{1,0:T(8,128)(2,1)S(1)}, bf16[864,128]{1,0:T(8,128)(2,1)S(1)}, u32[]{:S(2)}, u32[]{:S(2)}) %collective-permute-start.4) | collective-permute-done | bytes 221216 | tf_op jit(solution)/shard_map/ppermute | solution.py:30
  51.8 14.1 %collective-permute-done.5.refs_2_ = bf16[864,128]{1,0:T(8,128)(2,1)S(1)} collective-permute-done((bf16[864,128]{1,0:T(8,128)(2,1)S(1)}, bf16[864,128]{1,0:T(8,128)(2,1)S(1)}, u32[]{:S(2)}, u32[]{:S(2)}) %collective-permute-start.5) | collective-permute-done | bytes 221216 | tf_op jit(solution)/shard_map/ppermute | solution.py:30
  65.9 1.5 %partial_gram.1 = (f32[640,128]{1,0:T(8,128)S(1)}, f32[640,128]{1,0:T(8,128)S(1)}) custom-call(s32[3]{0:T(128)S(1)} %pad_add_fusion.place, bf16[864,128]{1,0:T(8,128)(2,1)S(1)} %get-tuple-element.52.refs_0_, bf16[864,128]{1,0:T(8,128)(2,1)S(1)} %collective-permute-done.4.refs_1_, bf16[864,128]{1,0:T(8,128)(2,1)S(1)} %collective-permute-done.5.refs_2_, ...), custom_call_target="tpu_custom_call" | custom-call | bytes 4194304 | tf_op jit(solution)/shard_map/partial_gram/pallas_call | solution.py:308
  67.8 1.3 %collective-permute-start.12 = (bf16[2592,128]{1,0:T(8,128)(2,1)S(1)}, bf16[2592,128]{1,0:T(8,128)(2,1)S(1)}, u32[]{:S(2)}, u32[]{:S(2)}) collective-permute-start(bf16[2592,128]{1,0:T(8,128)(2,1)S(1)} %pad_maximum_fusion), channel_id=1, source_target_pairs={{0,1},{1,2},{2,3},{4,5},{5,6},{6,7},{8,9},{9,10},{10,11},{12,13},{... | collective-permute-start | bytes 1990664 | tf_op jit(solution)/shard_map/ppermute | solution.py:374
  70.4 2.3 %collective-permute-start.8 = (f32[160,128]{1,0:T(8,128)S(1)}, f32[160,128]{1,0:T(8,128)S(1)}, u32[]{:S(2)}, u32[]{:S(2)}) collective-permute-start(f32[160,128]{1,0:T(8,128)S(1)} %get-tuple-element.59), channel_id=1, source_target_pairs={{0,8},{4,12},{8,0},{12,4},{16,24},{20,28},{24,16},{28,20},{1,9},{5... | collective-permute-start | bytes 245768 | tf_op jit(solution)/shard_map/ppermute | solution.py:367
  73.3 2.7 %collective-permute-done.10 = f32[160,128]{1,0:T(8,128)S(1)} collective-permute-done((f32[160,128]{1,0:T(8,128)S(1)}, f32[160,128]{1,0:T(8,128)S(1)}, u32[]{:S(2)}, u32[]{:S(2)}) %collective-permute-start.10) | collective-permute-done | bytes 81952 | tf_op jit(solution)/shard_map/ppermute | solution.py:367
  76.0 1.1 collective-permute-done.8
  77.3 3.7 %collective-permute-start.11 = (f32[160,128]{1,0:T(8,128)S(1)}, f32[160,128]{1,0:T(8,128)S(1)}, u32[]{:S(2)}, u32[]{:S(2)}) collective-permute-start(f32[160,128]{1,0:T(8,128)S(1)} %add_add_fusion.1), channel_id=1, source_target_pairs={{0,1},{1,2},{2,3},{3,0},{4,5},{5,6},{6,7},{7,4},{8,9},{9,10},{10,1... | collective-permute-start | bytes 245768 | tf_op jit(solution)/shard_map/ppermute | solution.py:30
  81.6 7.2 %collective-permute-done.11 = f32[160,128]{1,0:T(8,128)S(1)} collective-permute-done((f32[160,128]{1,0:T(8,128)S(1)}, f32[160,128]{1,0:T(8,128)S(1)}, u32[]{:S(2)}, u32[]{:S(2)}) %collective-permute-start.11) | collective-permute-done | bytes 81952 | tf_op jit(solution)/shard_map/ppermute | solution.py:30
  89.0 1.3 %collective-permute-start.19 = (bf16[2592,128]{1,0:T(8,128)(2,1)S(1)}, bf16[2592,128]{1,0:T(8,128)(2,1)S(1)}, u32[]{:S(2)}, u32[]{:S(2)}) collective-permute-start(bf16[2592,128]{1,0:T(8,128)(2,1)S(1)} %get-tuple-element.68), channel_id=1, source_target_pairs={{1,2},{2,3},{5,6},{6,7},{9,10},{10,11},{13,14},{14,15},{17,18},{18... | collective-permute-start | bytes 1990664 | tf_op jit(solution)/shard_map/ppermute | solution.py:374
  90.3 1.3 %collective-permute-start.20 = (bf16[2592,128]{1,0:T(8,128)(2,1)S(1)}, bf16[2592,128]{1,0:T(8,128)(2,1)S(1)}, u32[]{:S(2)}, u32[]{:S(2)}) collective-permute-start(bf16[2592,128]{1,0:T(8,128)(2,1)S(1)} %get-tuple-element.67), channel_id=1, source_target_pairs={{1,3},{5,7},{9,11},{13,15},{17,19},{21,23},{25,27},{29,31}} | collective-permute-start | bytes 1990664 | tf_op jit(solution)/shard_map/ppermute | solution.py:400
  91.6 2.4 %collective-permute-done.13 = f32[160,128]{1,0:T(8,128)S(1)} collective-permute-done((f32[160,128]{1,0:T(8,128)S(1)}, f32[160,128]{1,0:T(8,128)S(1)}, u32[]{:S(2)}, u32[]{:S(2)}) %collective-permute-start.13) | collective-permute-done | bytes 81952 | tf_op jit(solution)/shard_map/ppermute | solution.py:30
  94.1 1.6 %collective-permute-start.16 = (f32[160,128]{1,0:T(8,128)S(1)}, f32[160,128]{1,0:T(8,128)S(1)}, u32[]{:S(2)}, u32[]{:S(2)}) collective-permute-start(f32[160,128]{1,0:T(8,128)S(1)} %add_add_fusion.refs_0_), channel_id=1, source_target_pairs={{0,16},{4,20},{8,24},{12,28},{16,0},{20,4},{24,8},{28,12},{1,17},{... | collective-permute-start | bytes 245768 | tf_op jit(solution)/shard_map/ppermute | solution.py:367
  95.7 1.9 %collective-permute-start.17 = (f32[160,128]{1,0:T(8,128)S(1)}, f32[160,128]{1,0:T(8,128)S(1)}, u32[]{:S(2)}, u32[]{:S(2)}) collective-permute-start(f32[160,128]{1,0:T(8,128)S(1)} %add_add_fusion.refs_0_), channel_id=1, source_target_pairs={{0,24},{4,28},{8,16},{12,20},{16,8},{20,12},{24,0},{28,4},{1,25},{... | collective-permute-start | bytes 245768 | tf_op jit(solution)/shard_map/ppermute | solution.py:367
  97.6 1.6 %collective-permute-done.15.refs_1_ = f32[160,128]{1,0:T(8,128)S(1)} collective-permute-done((f32[160,128]{1,0:T(8,128)S(1)}, f32[160,128]{1,0:T(8,128)S(1)}, u32[]{:S(2)}, u32[]{:S(2)}) %collective-permute-start.15) | collective-permute-done | bytes 81952 | tf_op jit(solution)/shard_map/ppermute | solution.py:367
  99.2 1.8 %collective-permute-done.17.refs_3_ = f32[160,128]{1,0:T(8,128)S(1)} collective-permute-done((f32[160,128]{1,0:T(8,128)S(1)}, f32[160,128]{1,0:T(8,128)S(1)}, u32[]{:S(2)}, u32[]{:S(2)}) %collective-permute-start.17) | collective-permute-done | bytes 81952 | tf_op jit(solution)/shard_map/ppermute | solution.py:367
  101.7 1.6 %collective-permute-done.18.other_ref = f32[640,128]{1,0:T(8,128)S(1)} collective-permute-done((f32[640,128]{1,0:T(8,128)S(1)}, f32[640,128]{1,0:T(8,128)S(1)}, u32[]{:S(2)}, u32[]{:S(2)}) %collective-permute-start.18) | collective-permute-done | bytes 327712 | tf_op jit(solution)/shard_map/ppermute | solution.py:367
  103.3 14.0 %inverse_factor.1.factor_ref = f32[512,512]{1,0:T(8,128)S(1)} custom-call(s32[3]{0:T(128)S(1)} %pad_add_fusion.place, f32[640,128]{1,0:T(8,128)S(1)} %joined.1.mine_ref, f32[640,128]{1,0:T(8,128)S(1)} %collective-permute-done.18.other_ref), custom_call_target="tpu_custom_call" | custom-call | bytes 73400320 | tf_op jit(solution)/shard_map/inverse_factor/pallas_call | solution.py:541
  117.3 4.8 %collective-permute-done.20.refs_7_ = bf16[2592,128]{1,0:T(8,128)(2,1)S(1)} collective-permute-done((bf16[2592,128]{1,0:T(8,128)(2,1)S(1)}, bf16[2592,128]{1,0:T(8,128)(2,1)S(1)}, u32[]{:S(2)}, u32[]{:S(2)}) %collective-permute-start.20) | collective-permute-done | bytes 663584 | tf_op jit(solution)/shard_map/ppermute | solution.py:400
  122.1 2.9 %output.1 = f32[3456,128]{1,0:T(8,128)} custom-call(s32[1]{0:T(128)} %bitcast.band, f32[512,512]{1,0:T(8,128)S(1)} %inverse_factor.1.factor_ref, bf16[864,128]{1,0:T(8,128)(2,1)S(1)} %get-tuple-element.52.refs_0_, bf16[864,128]{1,0:T(8,128)(2,1)S(1)} %collective-permute-done.4.refs_1_, bf16[864,128]{1,0:T(8,128)(2,1)S(1)} %collective-permute-done.5.refs_2_, ...), custom_call_target="tpu_custom_call" | custom-call | bytes 10485760 | tf_op jit(solution)/shard_map/output/pallas_call | solution.py:595
  (53 shorter events, 10.3 us)
Async XLA Ops:
  0.0 1.2 copy-start.2
  1.2 0.7 copy-start.5
  2.8 6.8 %collective-permute-start = (bf16[288,128]{1,0:T(8,128)(2,1)S(1)}, bf16[288,128]{1,0:T(8,128)(2,1)S(1)}, u32[]{:S(2)}, u32[]{:S(2)}) collective-permute-start(bf16[288,128]{1,0:T(8,128)(2,1)S(1)} %get-tuple-element.35), channel_id=1, source_target_pairs={{0,28},{4,0},{8,4},{12,8},{16,12},{20,16},{24,20},{28,24},{1,29},{... | collective-permute-start | bytes 221192 | tf_op jit(solution)/shard_map/ppermute | solution.py:30
  4.5 1.0 copy-start
  5.5 0.7 copy-start.7
  6.1 3.5 %copy-start.1 = (bf16[343,343]{1,0:T(8,128)(2,1)S(1)}, bf16[343,343]{1,0:T(8,128)(2,1)}, u32[]{:S(2)}) copy-start(bf16[343,343]{1,0:T(8,128)(2,1)} %matrix_ref.7) | copy-start | bytes 705898
  6.1 3.5 %copy-start.4 = (f32[3456]{0:T(1024)S(1)}, f32[3456]{0:T(1024)}, u32[]{:S(2)}) copy-start(f32[3456]{0:T(1024)} %param.9) | copy-start | bytes 41476
  17.3 4.9 %collective-permute-start.1 = (f32[288,128]{1,0:T(8,128)S(1)}, f32[288,128]{1,0:T(8,128)S(1)}, u32[]{:S(2)}, u32[]{:S(2)}) collective-permute-start(f32[288,128]{1,0:T(8,128)S(1)} %get-tuple-element.40), channel_id=1, source_target_pairs={{0,4},{4,8},{8,12},{12,16},{16,20},{20,24},{24,28},{28,0},{1,5},{5... | collective-permute-start | bytes 442376 | tf_op jit(solution)/shard_map/ppermute | solution.py:30
  17.9 4.3 %copy-start.6 = (s32[288]{0:T(512)S(1)}, s32[288]{0:T(512)}, u32[]{:S(2)}) copy-start(s32[288]{0:T(512)} %nodes.5) | copy-start | bytes 3460
  22.2 2.9 %copy-start.8 = (f32[16]{0:T(128)S(1)}, f32[16]{0:T(128)}, u32[]{:S(2)}) copy-start(f32[16]{0:T(128)} %scale.7) | copy-start | bytes 196
  23.7 4.8 %collective-permute-start.2 = (bf16[288,128]{1,0:T(8,128)(2,1)S(1)}, bf16[288,128]{1,0:T(8,128)(2,1)S(1)}, u32[]{:S(2)}, u32[]{:S(2)}) collective-permute-start(bf16[288,128]{1,0:T(8,128)(2,1)S(1)} %get-tuple-element.41), channel_id=1, source_target_pairs={{0,28},{4,0},{8,4},{12,8},{16,12},{20,16},{24,20},{28,24},{1,29},{... | collective-permute-start | bytes 221192 | tf_op jit(solution)/shard_map/ppermute | solution.py:30
  36.2 6.3 %collective-permute-start.3 = (f32[288,128]{1,0:T(8,128)S(1)}, f32[288,128]{1,0:T(8,128)S(1)}, u32[]{:S(2)}, u32[]{:S(2)}) collective-permute-start(f32[288,128]{1,0:T(8,128)S(1)} %get-tuple-element.47), channel_id=1, source_target_pairs={{0,4},{4,8},{8,12},{12,16},{16,20},{20,24},{24,28},{28,0},{1,5},{5... | collective-permute-start | bytes 442376 | tf_op jit(solution)/shard_map/ppermute | solution.py:30
  38.2 4.3 %copy-start.3 = (bf16[3456,128]{1,0:T(8,128)(2,1)S(1)}, bf16[3456,128]{1,0:T(8,128)(2,1)}, u32[]{:S(2)}) copy-start(bf16[3456,128]{1,0:T(8,128)(2,1)} %previous_ref.1) | copy-start | bytes 2654212
  43.9 7.9 %collective-permute-start.4 = (bf16[864,128]{1,0:T(8,128)(2,1)S(1)}, bf16[864,128]{1,0:T(8,128)(2,1)S(1)}, u32[]{:S(2)}, u32[]{:S(2)}) collective-permute-start(bf16[864,128]{1,0:T(8,128)(2,1)S(1)} %get-tuple-element.49), channel_id=1, source_target_pairs={{0,1},{1,2},{2,3},{3,0},{4,5},{5,6},{6,7},{7,4},{8,9},{9,10},{10,1... | collective-permute-start | bytes 663560 | tf_op jit(solution)/shard_map/ppermute | solution.py:30
  44.1 21.8 %collective-permute-start.5 = (bf16[864,128]{1,0:T(8,128)(2,1)S(1)}, bf16[864,128]{1,0:T(8,128)(2,1)S(1)}, u32[]{:S(2)}, u32[]{:S(2)}) collective-permute-start(bf16[864,128]{1,0:T(8,128)(2,1)S(1)} %get-tuple-element.50), channel_id=1, source_target_pairs={{0,2},{1,3},{2,0},{3,1},{4,6},{5,7},{6,4},{7,5},{8,10},{9,11},{10,... | collective-permute-start | bytes 663560 | tf_op jit(solution)/shard_map/ppermute | solution.py:30
  45.8 20.1 %collective-permute-start.6 = (bf16[864,128]{1,0:T(8,128)(2,1)S(1)}, bf16[864,128]{1,0:T(8,128)(2,1)S(1)}, u32[]{:S(2)}, u32[]{:S(2)}) collective-permute-start(bf16[864,128]{1,0:T(8,128)(2,1)S(1)} %get-tuple-element.51), channel_id=1, source_target_pairs={{0,3},{1,0},{2,1},{3,2},{4,7},{5,4},{6,5},{7,6},{8,11},{9,8},{10,9... | collective-permute-start | bytes 663560 | tf_op jit(solution)/shard_map/ppermute | solution.py:30
  67.4 1.7 %collective-permute-start.7 = (f32[640,128]{1,0:T(8,128)S(1)}, f32[640,128]{1,0:T(8,128)S(1)}, u32[]{:S(2)}, u32[]{:S(2)}) collective-permute-start(f32[640,128]{1,0:T(8,128)S(1)} %get-tuple-element.57), channel_id=1, source_target_pairs={{0,4},{4,0},{8,12},{12,8},{16,20},{20,16},{24,28},{28,24},{1,5},{5... | collective-permute-start | bytes 983048 | tf_op jit(solution)/shard_map/ppermute | solution.py:367
  67.8 21.0 %collective-permute-start.12 = (bf16[2592,128]{1,0:T(8,128)(2,1)S(1)}, bf16[2592,128]{1,0:T(8,128)(2,1)S(1)}, u32[]{:S(2)}, u32[]{:S(2)}) collective-permute-start(bf16[2592,128]{1,0:T(8,128)(2,1)S(1)} %pad_maximum_fusion), channel_id=1, source_target_pairs={{0,1},{1,2},{2,3},{4,5},{5,6},{6,7},{8,9},{9,10},{10,11},{12,13},{... | collective-permute-start | bytes 1990664 | tf_op jit(solution)/shard_map/ppermute | solution.py:374
  69.7 6.2 %collective-permute-start.10 = (f32[160,128]{1,0:T(8,128)S(1)}, f32[160,128]{1,0:T(8,128)S(1)}, u32[]{:S(2)}, u32[]{:S(2)}) collective-permute-start(f32[160,128]{1,0:T(8,128)S(1)} %get-tuple-element.61), channel_id=1, source_target_pairs={{0,24},{4,28},{8,16},{12,20},{16,8},{20,12},{24,0},{28,4},{1,25},{... | collective-permute-start | bytes 245768 | tf_op jit(solution)/shard_map/ppermute | solution.py:367
  70.4 6.6 %collective-permute-start.8 = (f32[160,128]{1,0:T(8,128)S(1)}, f32[160,128]{1,0:T(8,128)S(1)}, u32[]{:S(2)}, u32[]{:S(2)}) collective-permute-start(f32[160,128]{1,0:T(8,128)S(1)} %get-tuple-element.59), channel_id=1, source_target_pairs={{0,8},{4,12},{8,0},{12,4},{16,24},{20,28},{24,16},{28,20},{1,9},{5... | collective-permute-start | bytes 245768 | tf_op jit(solution)/shard_map/ppermute | solution.py:367
  72.8 4.5 %collective-permute-start.9 = (f32[160,128]{1,0:T(8,128)S(1)}, f32[160,128]{1,0:T(8,128)S(1)}, u32[]{:S(2)}, u32[]{:S(2)}) collective-permute-start(f32[160,128]{1,0:T(8,128)S(1)} %get-tuple-element.60), channel_id=1, source_target_pairs={{0,16},{4,20},{8,24},{12,28},{16,0},{20,4},{24,8},{28,12},{1,17},{... | collective-permute-start | bytes 245768 | tf_op jit(solution)/shard_map/ppermute | solution.py:367
  77.3 11.5 %collective-permute-start.11 = (f32[160,128]{1,0:T(8,128)S(1)}, f32[160,128]{1,0:T(8,128)S(1)}, u32[]{:S(2)}, u32[]{:S(2)}) collective-permute-start(f32[160,128]{1,0:T(8,128)S(1)} %add_add_fusion.1), channel_id=1, source_target_pairs={{0,1},{1,2},{2,3},{3,0},{4,5},{5,6},{6,7},{7,4},{8,9},{9,10},{10,1... | collective-permute-start | bytes 245768 | tf_op jit(solution)/shard_map/ppermute | solution.py:30
  81.0 13.0 %collective-permute-start.13 = (f32[160,128]{1,0:T(8,128)S(1)}, f32[160,128]{1,0:T(8,128)S(1)}, u32[]{:S(2)}, u32[]{:S(2)}) collective-permute-start(f32[160,128]{1,0:T(8,128)S(1)} %add_add_fusion.1), channel_id=1, source_target_pairs={{0,2},{1,3},{2,0},{3,1},{4,6},{5,7},{6,4},{7,5},{8,10},{9,11},{10,... | collective-permute-start | bytes 245768 | tf_op jit(solution)/shard_map/ppermute | solution.py:30
  81.4 12.6 %collective-permute-start.14 = (f32[160,128]{1,0:T(8,128)S(1)}, f32[160,128]{1,0:T(8,128)S(1)}, u32[]{:S(2)}, u32[]{:S(2)}) collective-permute-start(f32[160,128]{1,0:T(8,128)S(1)} %add_add_fusion.1), channel_id=1, source_target_pairs={{0,3},{1,0},{2,1},{3,2},{4,7},{5,4},{6,5},{7,6},{8,11},{9,8},{10,9... | collective-permute-start | bytes 245768 | tf_op jit(solution)/shard_map/ppermute | solution.py:30
  89.0 28.3 %collective-permute-start.19 = (bf16[2592,128]{1,0:T(8,128)(2,1)S(1)}, bf16[2592,128]{1,0:T(8,128)(2,1)S(1)}, u32[]{:S(2)}, u32[]{:S(2)}) collective-permute-start(bf16[2592,128]{1,0:T(8,128)(2,1)S(1)} %get-tuple-element.68), channel_id=1, source_target_pairs={{1,2},{2,3},{5,6},{6,7},{9,10},{10,11},{13,14},{14,15},{17,18},{18... | collective-permute-start | bytes 1990664 | tf_op jit(solution)/shard_map/ppermute | solution.py:374
  90.3 31.9 %collective-permute-start.20 = (bf16[2592,128]{1,0:T(8,128)(2,1)S(1)}, bf16[2592,128]{1,0:T(8,128)(2,1)S(1)}, u32[]{:S(2)}, u32[]{:S(2)}) collective-permute-start(bf16[2592,128]{1,0:T(8,128)(2,1)S(1)} %get-tuple-element.67), channel_id=1, source_target_pairs={{1,3},{5,7},{9,11},{13,15},{17,19},{21,23},{25,27},{29,31}} | collective-permute-start | bytes 1990664 | tf_op jit(solution)/shard_map/ppermute | solution.py:400
  94.0 5.2 %collective-permute-start.15 = (f32[160,128]{1,0:T(8,128)S(1)}, f32[160,128]{1,0:T(8,128)S(1)}, u32[]{:S(2)}, u32[]{:S(2)}) collective-permute-start(f32[160,128]{1,0:T(8,128)S(1)} %add_add_fusion.refs_0_), channel_id=1, source_target_pairs={{0,8},{4,12},{8,0},{12,4},{16,24},{20,28},{24,16},{28,20},{1,9},{5... | collective-permute-start | bytes 245768 | tf_op jit(solution)/shard_map/ppermute | solution.py:367
  94.1 5.1 %collective-permute-start.16 = (f32[160,128]{1,0:T(8,128)S(1)}, f32[160,128]{1,0:T(8,128)S(1)}, u32[]{:S(2)}, u32[]{:S(2)}) collective-permute-start(f32[160,128]{1,0:T(8,128)S(1)} %add_add_fusion.refs_0_), channel_id=1, source_target_pairs={{0,16},{4,20},{8,24},{12,28},{16,0},{20,4},{24,8},{28,12},{1,17},{... | collective-permute-start | bytes 245768 | tf_op jit(solution)/shard_map/ppermute | solution.py:367
  95.7 5.4 %collective-permute-start.17 = (f32[160,128]{1,0:T(8,128)S(1)}, f32[160,128]{1,0:T(8,128)S(1)}, u32[]{:S(2)}, u32[]{:S(2)}) collective-permute-start(f32[160,128]{1,0:T(8,128)S(1)} %add_add_fusion.refs_0_), channel_id=1, source_target_pairs={{0,24},{4,28},{8,16},{12,20},{16,8},{20,12},{24,0},{28,4},{1,25},{... | collective-permute-start | bytes 245768 | tf_op jit(solution)/shard_map/ppermute | solution.py:367
  101.6 1.7 %collective-permute-start.18 = (f32[640,128]{1,0:T(8,128)S(1)}, f32[640,128]{1,0:T(8,128)S(1)}, u32[]{:S(2)}, u32[]{:S(2)}) collective-permute-start(f32[640,128]{1,0:T(8,128)S(1)} %joined.1.mine_ref), channel_id=1, source_target_pairs={{0,4},{4,0},{8,12},{12,8},{16,20},{20,16},{24,28},{28,24},{1,5},{5... | collective-permute-start | bytes 983048 | tf_op jit(solution)/shard_map/ppermute | solution.py:367

commit v6 on v5

--- a/solution.py
+++ b/solution.py
@@ -43,9 +43,10 @@
     base_ref[owned:, :] = jnp.zeros_like(base_ref[owned:, :])
 
 
-def prepare_kernel(nodes, rows_ref, ext_ref, edge_ref, picked):
+def prepare_kernel(nodes, rows_ref, links_ref, ext_ref, edge_ref, words_ref, picked):
     owned = rows_ref.shape[0]
     ext_ref[0:owned, :] = rows_ref[...].astype(F32)
+    pack_links(links_ref, words_ref)
 
     def body(step, _):
         for k in range(16):
@@ -57,46 +58,56 @@
     edge_ref[...] = picked[...].astype(BF16)
 
 
-def prepare(nodes, rows):
+def prepare(nodes, rows, links):
     owned, plane = rows.shape[0], nodes.shape[0]
-    ext, edge = pl.pallas_call(
+    cells, npc = links.shape
+    groups = ((npc + 1) // 2 + LANES - 1) // LANES
+    ext, edge, words = pl.pallas_call(
         prepare_kernel,
         out_shape=(
             jax.ShapeDtypeStruct((owned + plane, LANES), F32),
             jax.ShapeDtypeStruct((plane, LANES), BF16),
+            jax.ShapeDtypeStruct((groups * cells, LANES), jnp.int32),
         ),
-        in_specs=[SM, VM],
-        out_specs=(VM, VM),
+        in_specs=[SM, VM, VM],
+        out_specs=(VM, VM, VM),
         scratch_shapes=[pltpu.VMEM((plane, LANES), F32)],
         compiler_params=params(8),
         cost_estimate=cost(0, 12 << 20),
         name="prepare",
-    )(nodes, rows)
-    return ext, ext, edge
-
-
-def packed_links(links):
-    npc = links.shape[1]
+    )(nodes, rows, links)
+    return (ext, ext, edge), words.reshape(-1)
+
+
+def pack_links(links_ref, words_ref):
+    cells, npc = links_ref.shape
     half = (npc + 1) // 2
-    later = jnp.pad(links[:, half:], ((0, 0), (0, 2 * half - npc)))
-    return (links[:, :half] | (later << 16)).reshape(-1)
-
-
-def each_row(words, npc, cell, visit):
+    early = links_ref[:, 0:half]
+    late = jnp.concatenate(
+        [links_ref[:, half:npc], jnp.zeros((cells, 2 * half - npc), jnp.int32)], axis=1
+    )
+    words = early | (late << 16)
+    for k in range(0, half, LANES):
+        width = min(LANES, half - k)
+        words_ref[k // LANES * cells : (k // LANES + 1) * cells, 0:width] = words[:, k : k + width]
+
+
+def each_row(words, cells, npc, cell, visit):
     half = (npc + 1) // 2
+    base = cell * LANES
     for r in range(half):
-        word = words[cell * half + r]
+        word = words[base + (r // LANES * cells * LANES + r % LANES)]
         visit(r, pl.ds(word & 0xFFFF, 1))
         if r + half < npc:
             visit(r + half, pl.ds(word >> 16, 1))
 
 
-def gather_cells(words, npc, ext_ref, gathered, first):
+def gather_cells(words, cells, npc, ext_ref, gathered, first):
     def cell(c, _):
         def visit(r, row):
             gathered[c, r : r + 1, :] = ext_ref[row, :]
 
-        each_row(words, npc, first + c, visit)
+        each_row(words, cells, npc, first + c, visit)
         return 0
 
     lax.fori_loop(0, gathered.shape[0], cell, 0)
@@ -115,7 +126,7 @@
             )
 
 
-def scatter_cells(words, npc, products, sums, first):
+def scatter_cells(words, cells, npc, products, sums, first):
     def cell(c, _):
         seen = []
 
@@ -124,23 +135,25 @@
             seen.append(r)
             total[row, :] = total[row, :] + products[c, r : r + 1, :]
 
-        each_row(words, npc, first + c, visit)
+        each_row(words, cells, npc, first + c, visit)
         return 0
 
     lax.fori_loop(0, products.shape[0], cell, 0)
 
 
-def near_products_kernel(links, scale, ext_ref, matrix_ref, out_ref, gathered):
-    gather_cells(links, matrix_ref.shape[0], ext_ref, gathered, 0)
+def near_products_kernel(words, scale, ext_ref, matrix_ref, out_ref, gathered):
+    gather_cells(words, 2 * gathered.shape[0], matrix_ref.shape[0], ext_ref, gathered, 0)
     multiply_cells(scale, matrix_ref, gathered, out_ref, 0)
 
 
 def far_cells_kernel(
-    links, scale, ext_ref, ghost_ref, matrix_ref, wide_ref, potential_ref, out_ref, back_ref, ext, gathered,
-    products, *sums
+    words_ref, scale, ext_ref, ghost_ref, matrix_ref, wide_ref, potential_ref, out_ref, back_ref,
+    ext, gathered, products, words, sem, *sums
 ):
+    copy = pltpu.make_async_copy(words_ref, words, sem)
+    copy.start()
     owned = out_ref.shape[0]
-    half = gathered.shape[0]
+    half, npc = gathered.shape[0], matrix_ref.shape[0]
     ext[0:owned, :] = ext_ref[0:owned, :]
     ext[owned:, :] = ghost_ref[...].astype(F32)
     for block in range(owned // LANES):
@@ -149,20 +162,23 @@
     sums[0][owned:, :] = jnp.zeros_like(sums[0][owned:, :])
     for total in sums[1:]:
         total[...] = jnp.zeros_like(total)
-    npc = matrix_ref.shape[0]
-    gather_cells(links, npc, ext, gathered, half)
+    copy.wait()
+    gather_cells(words, 2 * half, npc, ext, gathered, half)
     multiply_cells(scale, matrix_ref, gathered, products, half)
-    scatter_cells(links, npc, products, sums, half)
+    scatter_cells(words, 2 * half, npc, products, sums, half)
     back_ref[...] = sum(total[owned:, :] for total in sums)
     out_ref[...] = sum(total[0:owned, :] for total in sums)
 
 
-def near_sums_kernel(npc, links, products_ref, start_ref, out_ref, *sums):
+def near_sums_kernel(npc, words_ref, products_ref, start_ref, out_ref, words, sem, *sums):
+    copy = pltpu.make_async_copy(words_ref, words, sem)
+    copy.start()
     sums = (out_ref,) + sums
     out_ref[...] = start_ref[...]
     for total in sums[1:]:
         total[...] = jnp.zeros_like(total)
-    scatter_cells(links, npc, products_ref, sums, 0)
+    copy.wait()
+    scatter_cells(words, 2 * products_ref.shape[0], npc, products_ref, sums, 0)
     out_ref[...] = sum(total[...] for total in sums)
 
 
@@ -174,6 +190,7 @@
     owned = whole[0] - plane
     held = (half, padded, LANES)
     ghost = shifted(edge, "domain", -1)
+    index = [pltpu.SMEM(links.shape, jnp.int32), pltpu.SemaphoreType.DMA]
     products = pl.pallas_call(
         near_products_kernel,
         out_shape=jax.ShapeDtypeStruct(held, F32),
@@ -191,9 +208,10 @@
             jax.ShapeDtypeStruct((owned, LANES), F32),
             jax.ShapeDtypeStruct((plane, LANES), F32),
         ),
-        in_specs=[SM, SM, VM, VM, VM, VM, VM],
+        in_specs=[VM, SM, VM, VM, VM, VM, VM],
         out_specs=(VM, VM),
         scratch_shapes=[pltpu.VMEM(whole, F32), pltpu.VMEM(held, F32), pltpu.VMEM(held, F32)]
+        + index
         + [pltpu.VMEM(whole, F32)] * CHAINS,
         compiler_params=params(22),
         cost_estimate=cost(0, 28 << 20),
@@ -203,9 +221,9 @@
     sums = pl.pallas_call(
         functools.partial(near_sums_kernel, npc),
         out_shape=jax.ShapeDtypeStruct((owned, LANES), F32),
-        in_specs=[SM, VM, VM],
+        in_specs=[VM] * 3,
         out_specs=VM,
-        scratch_shapes=[pltpu.VMEM((owned, LANES), F32)] * (CHAINS - 1),
+        scratch_shapes=index + [pltpu.VMEM((owned, LANES), F32)] * (CHAINS - 1),
         compiler_params=params(16),
         cost_estimate=cost(0, 14 << 20),
         name="near_sums",
@@ -614,10 +632,9 @@
     band = lax.axis_index("band").astype(jnp.int32).reshape(1)
     levels = potential.reshape(owned // LANES, LANES)
 
-    operator = functools.partial(
-        apply_operator, packed_links(connectivity), cell_scale, cell_matrix, levels
-    )
-    sums, back = operator(*prepare(boundary_nodes, states_block))
+    start, words = prepare(boundary_nodes, states_block, connectivity)
+    operator = functools.partial(apply_operator, words, cell_scale, cell_matrix, levels)
+    sums, back = operator(*start)
     sums, back = operator(*first_term(boundary_nodes, sums, back))
     pieces, rest = second_term(band, boundary_nodes, sums, back, states_block, count)
 

time: 125 us -> 123 us (0.984)
  Pallas kernels: 54.3 us -> 52.9 us
  transfers between devices with their start and end apart: 21 -> 21, of which waited for: 11 -> 12; matrix products, arithmetic and copies ran while one was open for 2% -> 0% of each run, Pallas kernels for 25% -> 24%
where the time goes in v6:
time: 123 us
  Pallas kernels  52.9 us (43%)
  waiting for transfers between devices  43.3 us (35%)
  starting transfers between devices  21.6 us (18%)
  local copies, waits for them, and re-layouts  4.29 us (3%)
    ppermute x10, waiting for transfers between devices, shifted(): lax.ppermute(value, axis, [(i, (i + steps) % count) for i in range(count)])  29.4 us
    pallas_call x2, Pallas kernels, apply_operator(): pl.pallas_call(far_cells_kernel, out_shape=(jax.ShapeDtypeStruct((owned,...  15 us
    pallas_call x1, Pallas kernels, inverse_factor(): pl.pallas_call(functools.partial(inverse_kernel, over), out_shape=jax.Sha...  14 us
    ppermute x10, starting transfers between devices, shifted(): lax.ppermute(value, axis, [(i, (i + steps) % count) for i in range(count)])  10.2 us
    ppermute x8, waiting for transfers between devices, paired(): return lax.ppermute(value, axis, [(i, i ^ mask) for i in range(count)])  9.09 us
    ppermute x8, starting transfers between devices, paired(): return lax.ppermute(value, axis, [(i, i ^ mask) for i in range(count)])  7.57 us
    pallas_call x2, Pallas kernels, apply_operator(): pl.pallas_call(functools.partial(near_sums_kernel, npc), out_shape=jax.Sh...  7.43 us
    pallas_call x2, Pallas kernels, apply_operator(): pl.pallas_call(near_products_kernel, out_shape=jax.ShapeDtypeStruct(held,...  7.1 us
  transfers between devices with their start and end apart: 21, of which 12 were waited for; matrix products, arithmetic and copies ran while one was open for 0% of the time, Pallas kernels for 24%

profile of v6, /device:TPU:26, one launch (start us, length us, event | category | flops | bytes accessed | tf_op | source)
XLA Modules:
  0.0 122.7 jit_solution(2536557911703372588)
XLA Ops:
  0.0 1.2 copy-done.2
  2.6 1.0 prepare.1
  5.3 3.6 %near_products.2.products_ref = f32[8,344,128]{2,1,0:T(8,128)S(1)} custom-call(s32[4096]{0:T(1024)S(1)} %bitcast.5, f32[16]{0:T(128)S(1)} %copy-done.8, f32[3744,128]{1,0:T(8,128)S(1)} %get-tuple-element.38.ext_ref.wide_ref, bf16[343,343]{1,0:T(8,128)(2,1)S(1)} %copy-done), custom_call_target="tpu_custom_call" | custom-call | bytes 14680064 | tf_op jit(solution)/shard_map/near_products/pallas_call | solution.py:194
  8.9 7.5 %far_cells.2 = (f32[3456,128]{1,0:T(8,128)S(1)}, f32[288,128]{1,0:T(8,128)S(1)}) custom-call(s32[4096]{0:T(1024)S(1)} %bitcast.6, f32[16]{0:T(128)S(1)} %copy-done.8, f32[3744,128]{1,0:T(8,128)S(1)} %get-tuple-element.38.ext_ref.wide_ref, bf16[288,128]{1,0:T(8,128)(2,1)S(1)} %collective-permute-done.ghost_ref, bf16[343,343]{1,0:T(8,128)(2,1)S(1)} %copy-done.1, ...), custom_call_target="tpu_custom_call" | custom-call | bytes 29360128 | tf_op jit(solution)/shard_map/far_cells/pallas_call | solution.py:205
  16.9 3.7 %near_sums.2.sums_ref = f32[3456,128]{1,0:T(8,128)S(1)} custom-call(s32[4096]{0:T(1024)S(1)} %bitcast.7, f32[8,344,128]{2,1,0:T(8,128)S(1)} %near_products.2.products_ref, f32[3456,128]{1,0:T(8,128)S(1)} %get-tuple-element.41.start_ref), custom_call_target="tpu_custom_call" | custom-call | bytes 14680064 | tf_op jit(solution)/shard_map/near_sums/pallas_call | solution.py:221
  21.0 1.5 %first_term.1 = (f32[3456,128]{1,0:T(8,128)S(1)}, f32[3744,128]{1,0:T(8,128)S(1)}, bf16[288,128]{1,0:T(8,128)(2,1)S(1)}) custom-call(s32[288]{0:T(512)S(1)} %copy-done.7, f32[3456,128]{1,0:T(8,128)S(1)} %near_sums.2.sums_ref, f32[288,128]{1,0:T(8,128)S(1)} %collective-permute-done.1.back_ref), custom_call_target="tpu_custom_call" | custom-call | bytes 8388608 | tf_op jit(solution)/shard_map/first_term/pallas_call | solution.py:258
  23.5 3.6 %near_products.3.products_ref = f32[8,344,128]{2,1,0:T(8,128)S(1)} custom-call(s32[4096]{0:T(1024)S(1)} %bitcast.8, f32[16]{0:T(128)S(1)} %copy-done.8, f32[3744,128]{1,0:T(8,128)S(1)} %get-tuple-element.44.ext_ref, bf16[343,343]{1,0:T(8,128)(2,1)S(1)} %copy-done.1), custom_call_target="tpu_custom_call" | custom-call | bytes 14680064 | tf_op jit(solution)/shard_map/near_products/pallas_call | solution.py:194
  27.0 7.5 %far_cells.3 = (f32[3456,128]{1,0:T(8,128)S(1)}, f32[288,128]{1,0:T(8,128)S(1)}) custom-call(s32[4096]{0:T(1024)S(1)} %bitcast.9, f32[16]{0:T(128)S(1)} %copy-done.8, f32[3744,128]{1,0:T(8,128)S(1)} %get-tuple-element.44.ext_ref, bf16[288,128]{1,0:T(8,128)(2,1)S(1)} %collective-permute-done.2.ghost_ref, bf16[343,343]{1,0:T(8,128)(2,1)S(1)} %copy-done.1, ...), custom_call_target="tpu_custom_call" | custom-call | bytes 29360128 | tf_op jit(solution)/shard_map/far_cells/pallas_call | solution.py:205
  34.5 1.9 %collective-permute-start.3 = (f32[288,128]{1,0:T(8,128)S(1)}, f32[288,128]{1,0:T(8,128)S(1)}, u32[]{:S(2)}, u32[]{:S(2)}) collective-permute-start(f32[288,128]{1,0:T(8,128)S(1)} %get-tuple-element.49), channel_id=1, source_target_pairs={{0,4},{4,8},{8,12},{12,16},{16,20},{20,24},{24,28},{28,0},{1,5},{5... | collective-permute-start | bytes 442376 | tf_op jit(solution)/shard_map/ppermute | solution.py:30
  36.4 3.7 %near_sums.3.sums_ref = f32[3456,128]{1,0:T(8,128)S(1)} custom-call(s32[4096]{0:T(1024)S(1)} %bitcast.10, f32[8,344,128]{2,1,0:T(8,128)S(1)} %near_products.3.products_ref, f32[3456,128]{1,0:T(8,128)S(1)} %get-tuple-element.48.start_ref), custom_call_target="tpu_custom_call" | custom-call | bytes 14680064 | tf_op jit(solution)/shard_map/near_sums/pallas_call | solution.py:221
  40.2 1.3 %second_term.1 = (bf16[864,128]{1,0:T(8,128)(2,1)S(1)}, bf16[864,128]{1,0:T(8,128)(2,1)S(1)}, bf16[864,128]{1,0:T(8,128)(2,1)S(1)}, bf16[864,128]{1,0:T(8,128)(2,1)S(1)}, bf16[2592,128]{1,0:T(8,128)(2,1)S(1)}) custom-call(s32[1]{0:T(128)} %bitcast.band, s32[288]{0:T(512)S(1)} %copy-done.7, f32[3456,128]{1,0:T(8,128)S(1)} %near_sums.3.sums_ref, ...), custom_call_target="tpu_custom_call" | custom-call | bytes 6291456 | tf_op jit(solution)/shard_map/second_term/pallas_call | solution.py:291
  41.8 1.7 %collective-permute-start.5 = (bf16[864,128]{1,0:T(8,128)(2,1)S(1)}, bf16[864,128]{1,0:T(8,128)(2,1)S(1)}, u32[]{:S(2)}, u32[]{:S(2)}) collective-permute-start(bf16[864,128]{1,0:T(8,128)(2,1)S(1)} %get-tuple-element.52), channel_id=1, source_target_pairs={{0,2},{1,3},{2,0},{3,1},{4,6},{5,7},{6,4},{7,5},{8,10},{9,11},{10,... | collective-permute-start | bytes 663560 | tf_op jit(solution)/shard_map/ppermute | solution.py:30
  44.0 5.3 %collective-permute-done.4.refs_1_ = bf16[864,128]{1,0:T(8,128)(2,1)S(1)} collective-permute-done((bf16[864,128]{1,0:T(8,128)(2,1)S(1)}, bf16[864,128]{1,0:T(8,128)(2,1)S(1)}, u32[]{:S(2)}, u32[]{:S(2)}) %collective-permute-start.4) | collective-permute-done | bytes 221216 | tf_op jit(solution)/shard_map/ppermute | solution.py:30
  49.3 14.1 %collective-permute-done.5.refs_2_ = bf16[864,128]{1,0:T(8,128)(2,1)S(1)} collective-permute-done((bf16[864,128]{1,0:T(8,128)(2,1)S(1)}, bf16[864,128]{1,0:T(8,128)(2,1)S(1)}, u32[]{:S(2)}, u32[]{:S(2)}) %collective-permute-start.5) | collective-permute-done | bytes 221216 | tf_op jit(solution)/shard_map/ppermute | solution.py:30
  63.5 1.5 %partial_gram.1 = (f32[640,128]{1,0:T(8,128)S(1)}, f32[640,128]{1,0:T(8,128)S(1)}) custom-call(s32[3]{0:T(128)S(1)} %pad_add_fusion.place, bf16[864,128]{1,0:T(8,128)(2,1)S(1)} %get-tuple-element.54.refs_0_, bf16[864,128]{1,0:T(8,128)(2,1)S(1)} %collective-permute-done.4.refs_1_, bf16[864,128]{1,0:T(8,128)(2,1)S(1)} %collective-permute-done.5.refs_2_, ...), custom_call_target="tpu_custom_call" | custom-call | bytes 4194304 | tf_op jit(solution)/shard_map/partial_gram/pallas_call | solution.py:326
  65.4 1.3 %collective-permute-start.12 = (bf16[2592,128]{1,0:T(8,128)(2,1)S(1)}, bf16[2592,128]{1,0:T(8,128)(2,1)S(1)}, u32[]{:S(2)}, u32[]{:S(2)}) collective-permute-start(bf16[2592,128]{1,0:T(8,128)(2,1)S(1)} %pad_maximum_fusion), channel_id=1, source_target_pairs={{0,1},{1,2},{2,3},{4,5},{5,6},{6,7},{8,9},{9,10},{10,11},{12,13},{... | collective-permute-start | bytes 1990664 | tf_op jit(solution)/shard_map/ppermute | solution.py:392
  68.2 2.2 %collective-permute-start.8 = (f32[160,128]{1,0:T(8,128)S(1)}, f32[160,128]{1,0:T(8,128)S(1)}, u32[]{:S(2)}, u32[]{:S(2)}) collective-permute-start(f32[160,128]{1,0:T(8,128)S(1)} %get-tuple-element.61), channel_id=1, source_target_pairs={{0,8},{4,12},{8,0},{12,4},{16,24},{20,28},{24,16},{28,20},{1,9},{5... | collective-permute-start | bytes 245768 | tf_op jit(solution)/shard_map/ppermute | solution.py:385
  70.9 2.7 %collective-permute-done.10 = f32[160,128]{1,0:T(8,128)S(1)} collective-permute-done((f32[160,128]{1,0:T(8,128)S(1)}, f32[160,128]{1,0:T(8,128)S(1)}, u32[]{:S(2)}, u32[]{:S(2)}) %collective-permute-start.10) | collective-permute-done | bytes 81952 | tf_op jit(solution)/shard_map/ppermute | solution.py:385
  73.6 1.2 collective-permute-done.8
  74.9 3.7 %collective-permute-start.11 = (f32[160,128]{1,0:T(8,128)S(1)}, f32[160,128]{1,0:T(8,128)S(1)}, u32[]{:S(2)}, u32[]{:S(2)}) collective-permute-start(f32[160,128]{1,0:T(8,128)S(1)} %add_add_fusion.1), channel_id=1, source_target_pairs={{0,1},{1,2},{2,3},{3,0},{4,5},{5,6},{6,7},{7,4},{8,9},{9,10},{10,1... | collective-permute-start | bytes 245768 | tf_op jit(solution)/shard_map/ppermute | solution.py:30
  79.2 7.1 %collective-permute-done.11 = f32[160,128]{1,0:T(8,128)S(1)} collective-permute-done((f32[160,128]{1,0:T(8,128)S(1)}, f32[160,128]{1,0:T(8,128)S(1)}, u32[]{:S(2)}, u32[]{:S(2)}) %collective-permute-start.11) | collective-permute-done | bytes 81952 | tf_op jit(solution)/shard_map/ppermute | solution.py:30
  86.5 1.3 %collective-permute-start.19 = (bf16[2592,128]{1,0:T(8,128)(2,1)S(1)}, bf16[2592,128]{1,0:T(8,128)(2,1)S(1)}, u32[]{:S(2)}, u32[]{:S(2)}) collective-permute-start(bf16[2592,128]{1,0:T(8,128)(2,1)S(1)} %get-tuple-element.70), channel_id=1, source_target_pairs={{1,2},{2,3},{5,6},{6,7},{9,10},{10,11},{13,14},{14,15},{17,18},{18... | collective-permute-start | bytes 1990664 | tf_op jit(solution)/shard_map/ppermute | solution.py:392
  87.8 1.3 %collective-permute-start.20 = (bf16[2592,128]{1,0:T(8,128)(2,1)S(1)}, bf16[2592,128]{1,0:T(8,128)(2,1)S(1)}, u32[]{:S(2)}, u32[]{:S(2)}) collective-permute-start(bf16[2592,128]{1,0:T(8,128)(2,1)S(1)} %get-tuple-element.69), channel_id=1, source_target_pairs={{1,3},{5,7},{9,11},{13,15},{17,19},{21,23},{25,27},{29,31}} | collective-permute-start | bytes 1990664 | tf_op jit(solution)/shard_map/ppermute | solution.py:418
  89.1 2.5 %collective-permute-done.13 = f32[160,128]{1,0:T(8,128)S(1)} collective-permute-done((f32[160,128]{1,0:T(8,128)S(1)}, f32[160,128]{1,0:T(8,128)S(1)}, u32[]{:S(2)}, u32[]{:S(2)}) %collective-permute-start.13) | collective-permute-done | bytes 81952 | tf_op jit(solution)/shard_map/ppermute | solution.py:30
  91.9 1.5 %collective-permute-start.16 = (f32[160,128]{1,0:T(8,128)S(1)}, f32[160,128]{1,0:T(8,128)S(1)}, u32[]{:S(2)}, u32[]{:S(2)}) collective-permute-start(f32[160,128]{1,0:T(8,128)S(1)} %add_add_fusion.refs_0_), channel_id=1, source_target_pairs={{0,16},{4,20},{8,24},{12,28},{16,0},{20,4},{24,8},{28,12},{1,17},{... | collective-permute-start | bytes 245768 | tf_op jit(solution)/shard_map/ppermute | solution.py:385
  93.3 1.9 %collective-permute-start.17 = (f32[160,128]{1,0:T(8,128)S(1)}, f32[160,128]{1,0:T(8,128)S(1)}, u32[]{:S(2)}, u32[]{:S(2)}) collective-permute-start(f32[160,128]{1,0:T(8,128)S(1)} %add_add_fusion.refs_0_), channel_id=1, source_target_pairs={{0,24},{4,28},{8,16},{12,20},{16,8},{20,12},{24,0},{28,4},{1,25},{... | collective-permute-start | bytes 245768 | tf_op jit(solution)/shard_map/ppermute | solution.py:385
  95.2 1.6 %collective-permute-done.15.refs_1_ = f32[160,128]{1,0:T(8,128)S(1)} collective-permute-done((f32[160,128]{1,0:T(8,128)S(1)}, f32[160,128]{1,0:T(8,128)S(1)}, u32[]{:S(2)}, u32[]{:S(2)}) %collective-permute-start.15) | collective-permute-done | bytes 81952 | tf_op jit(solution)/shard_map/ppermute | solution.py:385
  96.9 1.8 %collective-permute-done.17.refs_3_ = f32[160,128]{1,0:T(8,128)S(1)} collective-permute-done((f32[160,128]{1,0:T(8,128)S(1)}, f32[160,128]{1,0:T(8,128)S(1)}, u32[]{:S(2)}, u32[]{:S(2)}) %collective-permute-start.17) | collective-permute-done | bytes 81952 | tf_op jit(solution)/shard_map/ppermute | solution.py:385
  99.4 1.6 %collective-permute-done.18.other_ref = f32[640,128]{1,0:T(8,128)S(1)} collective-permute-done((f32[640,128]{1,0:T(8,128)S(1)}, f32[640,128]{1,0:T(8,128)S(1)}, u32[]{:S(2)}, u32[]{:S(2)}) %collective-permute-start.18) | collective-permute-done | bytes 327712 | tf_op jit(solution)/shard_map/ppermute | solution.py:385
  101.0 14.0 %inverse_factor.1.factor_ref = f32[512,512]{1,0:T(8,128)S(1)} custom-call(s32[3]{0:T(128)S(1)} %pad_add_fusion.place, f32[640,128]{1,0:T(8,128)S(1)} %joined.1.mine_ref, f32[640,128]{1,0:T(8,128)S(1)} %collective-permute-done.18.other_ref), custom_call_target="tpu_custom_call" | custom-call | bytes 73400320 | tf_op jit(solution)/shard_map/inverse_factor/pallas_call | solution.py:559
  115.0 4.8 %collective-permute-done.20.refs_7_ = bf16[2592,128]{1,0:T(8,128)(2,1)S(1)} collective-permute-done((bf16[2592,128]{1,0:T(8,128)(2,1)S(1)}, bf16[2592,128]{1,0:T(8,128)(2,1)S(1)}, u32[]{:S(2)}, u32[]{:S(2)}) %collective-permute-start.20) | collective-permute-done | bytes 663584 | tf_op jit(solution)/shard_map/ppermute | solution.py:418
  119.8 2.9 %output.1 = f32[3456,128]{1,0:T(8,128)} custom-call(s32[1]{0:T(128)} %bitcast.band, f32[512,512]{1,0:T(8,128)S(1)} %inverse_factor.1.factor_ref, bf16[864,128]{1,0:T(8,128)(2,1)S(1)} %get-tuple-element.54.refs_0_, bf16[864,128]{1,0:T(8,128)(2,1)S(1)} %collective-permute-done.4.refs_1_, bf16[864,128]{1,0:T(8,128)(2,1)S(1)} %collective-permute-done.5.refs_2_, ...), custom_call_target="tpu_custom_call" | custom-call | bytes 10485760 | tf_op jit(solution)/shard_map/output/pallas_call | solution.py:613
  (50 shorter events, 10.0 us)
Async XLA Ops:
  0.0 1.2 copy-start.2
  1.2 0.7 copy-start.5
  1.9 0.7 copy-start.6
  3.6 5.2 %collective-permute-start = (bf16[288,128]{1,0:T(8,128)(2,1)S(1)}, bf16[288,128]{1,0:T(8,128)(2,1)S(1)}, u32[]{:S(2)}, u32[]{:S(2)}) collective-permute-start(bf16[288,128]{1,0:T(8,128)(2,1)S(1)} %get-tuple-element.37), channel_id=1, source_target_pairs={{0,28},{4,0},{8,4},{12,8},{16,12},{20,16},{24,20},{28,24},{1,29},{... | collective-permute-start | bytes 221192 | tf_op jit(solution)/shard_map/ppermute | solution.py:30
  3.6 1.0 copy-start
  4.6 0.7 copy-start.8
  5.3 3.6 %copy-start.1 = (bf16[343,343]{1,0:T(8,128)(2,1)S(1)}, bf16[343,343]{1,0:T(8,128)(2,1)}, u32[]{:S(2)}) copy-start(bf16[343,343]{1,0:T(8,128)(2,1)} %matrix_ref.7) | copy-start | bytes 705898
  5.3 3.6 %copy-start.4 = (f32[3456]{0:T(1024)S(1)}, f32[3456]{0:T(1024)}, u32[]{:S(2)}) copy-start(f32[3456]{0:T(1024)} %param.9) | copy-start | bytes 41476
  16.4 4.6 %collective-permute-start.1 = (f32[288,128]{1,0:T(8,128)S(1)}, f32[288,128]{1,0:T(8,128)S(1)}, u32[]{:S(2)}, u32[]{:S(2)}) collective-permute-start(f32[288,128]{1,0:T(8,128)S(1)} %get-tuple-element.42), channel_id=1, source_target_pairs={{0,4},{4,8},{8,12},{12,16},{16,20},{20,24},{24,28},{28,0},{1,5},{5... | collective-permute-start | bytes 442376 | tf_op jit(solution)/shard_map/ppermute | solution.py:30
  16.9 4.1 %copy-start.7 = (s32[288]{0:T(512)S(1)}, s32[288]{0:T(512)}, u32[]{:S(2)}) copy-start(s32[288]{0:T(512)} %nodes.5) | copy-start | bytes 3460
  22.5 4.5 %collective-permute-start.2 = (bf16[288,128]{1,0:T(8,128)(2,1)S(1)}, bf16[288,128]{1,0:T(8,128)(2,1)S(1)}, u32[]{:S(2)}, u32[]{:S(2)}) collective-permute-start(bf16[288,128]{1,0:T(8,128)(2,1)S(1)} %get-tuple-element.43), channel_id=1, source_target_pairs={{0,28},{4,0},{8,4},{12,8},{16,12},{20,16},{24,20},{28,24},{1,29},{... | collective-permute-start | bytes 221192 | tf_op jit(solution)/shard_map/ppermute | solution.py:30
  34.5 5.6 %collective-permute-start.3 = (f32[288,128]{1,0:T(8,128)S(1)}, f32[288,128]{1,0:T(8,128)S(1)}, u32[]{:S(2)}, u32[]{:S(2)}) collective-permute-start(f32[288,128]{1,0:T(8,128)S(1)} %get-tuple-element.49), channel_id=1, source_target_pairs={{0,4},{4,8},{8,12},{12,16},{16,20},{20,24},{24,28},{28,0},{1,5},{5... | collective-permute-start | bytes 442376 | tf_op jit(solution)/shard_map/ppermute | solution.py:30
  36.4 3.7 %copy-start.3 = (bf16[3456,128]{1,0:T(8,128)(2,1)S(1)}, bf16[3456,128]{1,0:T(8,128)(2,1)}, u32[]{:S(2)}) copy-start(bf16[3456,128]{1,0:T(8,128)(2,1)} %previous_ref.1) | copy-start | bytes 2654212
  41.5 7.8 %collective-permute-start.4 = (bf16[864,128]{1,0:T(8,128)(2,1)S(1)}, bf16[864,128]{1,0:T(8,128)(2,1)S(1)}, u32[]{:S(2)}, u32[]{:S(2)}) collective-permute-start(bf16[864,128]{1,0:T(8,128)(2,1)S(1)} %get-tuple-element.51), channel_id=1, source_target_pairs={{0,1},{1,2},{2,3},{3,0},{4,5},{5,6},{6,7},{7,4},{8,9},{9,10},{10,1... | collective-permute-start | bytes 663560 | tf_op jit(solution)/shard_map/ppermute | solution.py:30
  41.8 21.7 %collective-permute-start.5 = (bf16[864,128]{1,0:T(8,128)(2,1)S(1)}, bf16[864,128]{1,0:T(8,128)(2,1)S(1)}, u32[]{:S(2)}, u32[]{:S(2)}) collective-permute-start(bf16[864,128]{1,0:T(8,128)(2,1)S(1)} %get-tuple-element.52), channel_id=1, source_target_pairs={{0,2},{1,3},{2,0},{3,1},{4,6},{5,7},{6,4},{7,5},{8,10},{9,11},{10,... | collective-permute-start | bytes 663560 | tf_op jit(solution)/shard_map/ppermute | solution.py:30
  43.5 20.0 %collective-permute-start.6 = (bf16[864,128]{1,0:T(8,128)(2,1)S(1)}, bf16[864,128]{1,0:T(8,128)(2,1)S(1)}, u32[]{:S(2)}, u32[]{:S(2)}) collective-permute-start(bf16[864,128]{1,0:T(8,128)(2,1)S(1)} %get-tuple-element.53), channel_id=1, source_target_pairs={{0,3},{1,0},{2,1},{3,2},{4,7},{5,4},{6,5},{7,6},{8,11},{9,8},{10,9... | collective-permute-start | bytes 663560 | tf_op jit(solution)/shard_map/ppermute | solution.py:30
  65.0 1.7 %collective-permute-start.7 = (f32[640,128]{1,0:T(8,128)S(1)}, f32[640,128]{1,0:T(8,128)S(1)}, u32[]{:S(2)}, u32[]{:S(2)}) collective-permute-start(f32[640,128]{1,0:T(8,128)S(1)} %get-tuple-element.59), channel_id=1, source_target_pairs={{0,4},{4,0},{8,12},{12,8},{16,20},{20,16},{24,28},{28,24},{1,5},{5... | collective-permute-start | bytes 983048 | tf_op jit(solution)/shard_map/ppermute | solution.py:385
  65.4 20.9 %collective-permute-start.12 = (bf16[2592,128]{1,0:T(8,128)(2,1)S(1)}, bf16[2592,128]{1,0:T(8,128)(2,1)S(1)}, u32[]{:S(2)}, u32[]{:S(2)}) collective-permute-start(bf16[2592,128]{1,0:T(8,128)(2,1)S(1)} %pad_maximum_fusion), channel_id=1, source_target_pairs={{0,1},{1,2},{2,3},{4,5},{5,6},{6,7},{8,9},{9,10},{10,11},{12,13},{... | collective-permute-start | bytes 1990664 | tf_op jit(solution)/shard_map/ppermute | solution.py:392
  67.3 6.2 %collective-permute-start.10 = (f32[160,128]{1,0:T(8,128)S(1)}, f32[160,128]{1,0:T(8,128)S(1)}, u32[]{:S(2)}, u32[]{:S(2)}) collective-permute-start(f32[160,128]{1,0:T(8,128)S(1)} %get-tuple-element.63), channel_id=1, source_target_pairs={{0,24},{4,28},{8,16},{12,20},{16,8},{20,12},{24,0},{28,4},{1,25},{... | collective-permute-start | bytes 245768 | tf_op jit(solution)/shard_map/ppermute | solution.py:385
  68.2 6.6 %collective-permute-start.8 = (f32[160,128]{1,0:T(8,128)S(1)}, f32[160,128]{1,0:T(8,128)S(1)}, u32[]{:S(2)}, u32[]{:S(2)}) collective-permute-start(f32[160,128]{1,0:T(8,128)S(1)} %get-tuple-element.61), channel_id=1, source_target_pairs={{0,8},{4,12},{8,0},{12,4},{16,24},{20,28},{24,16},{28,20},{1,9},{5... | collective-permute-start | bytes 245768 | tf_op jit(solution)/shard_map/ppermute | solution.py:385
  70.4 4.5 %collective-permute-start.9 = (f32[160,128]{1,0:T(8,128)S(1)}, f32[160,128]{1,0:T(8,128)S(1)}, u32[]{:S(2)}, u32[]{:S(2)}) collective-permute-start(f32[160,128]{1,0:T(8,128)S(1)} %get-tuple-element.62), channel_id=1, source_target_pairs={{0,16},{4,20},{8,24},{12,28},{16,0},{20,4},{24,8},{28,12},{1,17},{... | collective-permute-start | bytes 245768 | tf_op jit(solution)/shard_map/ppermute | solution.py:385
  74.9 11.4 %collective-permute-start.11 = (f32[160,128]{1,0:T(8,128)S(1)}, f32[160,128]{1,0:T(8,128)S(1)}, u32[]{:S(2)}, u32[]{:S(2)}) collective-permute-start(f32[160,128]{1,0:T(8,128)S(1)} %add_add_fusion.1), channel_id=1, source_target_pairs={{0,1},{1,2},{2,3},{3,0},{4,5},{5,6},{6,7},{7,4},{8,9},{9,10},{10,1... | collective-permute-start | bytes 245768 | tf_op jit(solution)/shard_map/ppermute | solution.py:30
  78.6 13.0 %collective-permute-start.13 = (f32[160,128]{1,0:T(8,128)S(1)}, f32[160,128]{1,0:T(8,128)S(1)}, u32[]{:S(2)}, u32[]{:S(2)}) collective-permute-start(f32[160,128]{1,0:T(8,128)S(1)} %add_add_fusion.1), channel_id=1, source_target_pairs={{0,2},{1,3},{2,0},{3,1},{4,6},{5,7},{6,4},{7,5},{8,10},{9,11},{10,... | collective-permute-start | bytes 245768 | tf_op jit(solution)/shard_map/ppermute | solution.py:30
  79.0 12.6 %collective-permute-start.14 = (f32[160,128]{1,0:T(8,128)S(1)}, f32[160,128]{1,0:T(8,128)S(1)}, u32[]{:S(2)}, u32[]{:S(2)}) collective-permute-start(f32[160,128]{1,0:T(8,128)S(1)} %add_add_fusion.1), channel_id=1, source_target_pairs={{0,3},{1,0},{2,1},{3,2},{4,7},{5,4},{6,5},{7,6},{8,11},{9,8},{10,9... | collective-permute-start | bytes 245768 | tf_op jit(solution)/shard_map/ppermute | solution.py:30
  86.5 28.5 %collective-permute-start.19 = (bf16[2592,128]{1,0:T(8,128)(2,1)S(1)}, bf16[2592,128]{1,0:T(8,128)(2,1)S(1)}, u32[]{:S(2)}, u32[]{:S(2)}) collective-permute-start(bf16[2592,128]{1,0:T(8,128)(2,1)S(1)} %get-tuple-element.70), channel_id=1, source_target_pairs={{1,2},{2,3},{5,6},{6,7},{9,10},{10,11},{13,14},{14,15},{17,18},{18... | collective-permute-start | bytes 1990664 | tf_op jit(solution)/shard_map/ppermute | solution.py:392
  87.8 32.0 %collective-permute-start.20 = (bf16[2592,128]{1,0:T(8,128)(2,1)S(1)}, bf16[2592,128]{1,0:T(8,128)(2,1)S(1)}, u32[]{:S(2)}, u32[]{:S(2)}) collective-permute-start(bf16[2592,128]{1,0:T(8,128)(2,1)S(1)} %get-tuple-element.69), channel_id=1, source_target_pairs={{1,3},{5,7},{9,11},{13,15},{17,19},{21,23},{25,27},{29,31}} | collective-permute-start | bytes 1990664 | tf_op jit(solution)/shard_map/ppermute | solution.py:418
  91.7 5.2 %collective-permute-start.15 = (f32[160,128]{1,0:T(8,128)S(1)}, f32[160,128]{1,0:T(8,128)S(1)}, u32[]{:S(2)}, u32[]{:S(2)}) collective-permute-start(f32[160,128]{1,0:T(8,128)S(1)} %add_add_fusion.refs_0_), channel_id=1, source_target_pairs={{0,8},{4,12},{8,0},{12,4},{16,24},{20,28},{24,16},{28,20},{1,9},{5... | collective-permute-start | bytes 245768 | tf_op jit(solution)/shard_map/ppermute | solution.py:385
  91.9 5.0 %collective-permute-start.16 = (f32[160,128]{1,0:T(8,128)S(1)}, f32[160,128]{1,0:T(8,128)S(1)}, u32[]{:S(2)}, u32[]{:S(2)}) collective-permute-start(f32[160,128]{1,0:T(8,128)S(1)} %add_add_fusion.refs_0_), channel_id=1, source_target_pairs={{0,16},{4,20},{8,24},{12,28},{16,0},{20,4},{24,8},{28,12},{1,17},{... | collective-permute-start | bytes 245768 | tf_op jit(solution)/shard_map/ppermute | solution.py:385
  93.3 5.4 %collective-permute-start.17 = (f32[160,128]{1,0:T(8,128)S(1)}, f32[160,128]{1,0:T(8,128)S(1)}, u32[]{:S(2)}, u32[]{:S(2)}) collective-permute-start(f32[160,128]{1,0:T(8,128)S(1)} %add_add_fusion.refs_0_), channel_id=1, source_target_pairs={{0,24},{4,28},{8,16},{12,20},{16,8},{20,12},{24,0},{28,4},{1,25},{... | collective-permute-start | bytes 245768 | tf_op jit(solution)/shard_map/ppermute | solution.py:385
  99.3 1.7 %collective-permute-start.18 = (f32[640,128]{1,0:T(8,128)S(1)}, f32[640,128]{1,0:T(8,128)S(1)}, u32[]{:S(2)}, u32[]{:S(2)}) collective-permute-start(f32[640,128]{1,0:T(8,128)S(1)} %joined.1.mine_ref), channel_id=1, source_target_pairs={{0,4},{4,0},{8,12},{12,8},{16,20},{20,16},{24,28},{28,24},{1,5},{5... | collective-permute-start | bytes 983048 | tf_op jit(solution)/shard_map/ppermute | solution.py:385

commit v7 on v6

--- a/solution.py
+++ b/solution.py
@@ -166,7 +166,7 @@
     gather_cells(words, 2 * half, npc, ext, gathered, half)
     multiply_cells(scale, matrix_ref, gathered, products, half)
     scatter_cells(words, 2 * half, npc, products, sums, half)
-    back_ref[...] = sum(total[owned:, :] for total in sums)
+    back_ref[...] = sum(total[owned:, :] for total in sums).astype(BF16)
     out_ref[...] = sum(total[0:owned, :] for total in sums)
 
 
@@ -206,7 +206,7 @@
         far_cells_kernel,
         out_shape=(
             jax.ShapeDtypeStruct((owned, LANES), F32),
-            jax.ShapeDtypeStruct((plane, LANES), F32),
+            jax.ShapeDtypeStruct((plane, LANES), BF16),
         ),
         in_specs=[VM, SM, VM, VM, VM, VM, VM],
         out_specs=(VM, VM),
@@ -231,11 +231,13 @@
     return sums, back
 
 
-def add_back(nodes, target, back_ref, factor, picked=None):
+def add_back(nodes, target, back_ref, factor, scaled, picked=None):
+    scaled[...] = back_ref[...].astype(F32) * factor
+
     def body(step, _):
         at = [step * 16 + k for k in range(16)]
         rows = [pl.ds(nodes[i], 1) for i in at]
-        new = [target[r, :] + factor * back_ref[pl.ds(i, 1), :] for i, r in zip(at, rows)]
+        new = [target[r, :] + scaled[pl.ds(i, 1), :] for i, r in zip(at, rows)]
         for i, r, value in zip(at, rows, new):
             target[r, :] = value
             if picked is not None:
@@ -245,10 +247,10 @@
     lax.fori_loop(0, nodes.shape[0] // 16, body, 0)
 
 
-def first_kernel(nodes, sums_ref, back_ref, term_ref, ext_ref, edge_ref, picked):
+def first_kernel(nodes, sums_ref, back_ref, term_ref, ext_ref, edge_ref, scaled, picked):
     owned = sums_ref.shape[0]
     term_ref[...] = sums_ref[...] * (1.0 / HALF_WIDTH)
-    add_back(nodes, term_ref, back_ref, 1.0 / HALF_WIDTH, picked)
+    add_back(nodes, term_ref, back_ref, 1.0 / HALF_WIDTH, scaled, picked)
     edge_ref[...] = picked[...].astype(BF16)
     ext_ref[0:owned, :] = term_ref[...].astype(BF16).astype(F32)
 
@@ -264,120 +266,122 @@
         ),
         in_specs=[SM, VM, VM],
         out_specs=(VM, VM, VM),
-        scratch_shapes=[pltpu.VMEM((plane, LANES), F32)],
+        scratch_shapes=[pltpu.VMEM((plane, LANES), F32)] * 2,
         compiler_params=params(16),
         cost_estimate=cost(0, 8 << 20),
         name="first_term",
     )(nodes, sums, back)
 
 
-def second_kernel(band, nodes, sums_ref, back_ref, previous_ref, *refs):
-    pieces, rest_ref, total = refs[:-2], refs[-2], refs[-1]
+def second_kernel(nodes, sums_ref, back_ref, previous_ref, *refs):
+    pieces, (rest_ref, total, scaled) = refs[:-3], refs[-3:]
     total[...] = sums_ref[...] * (2.0 / HALF_WIDTH) - previous_ref[...].astype(F32)
-    add_back(nodes, total, back_ref, 2.0 / HALF_WIDTH)
+    add_back(nodes, total, back_ref, 2.0 / HALF_WIDTH, scaled)
     count = len(pieces)
     rows = total.shape[0] // count
     for k, piece in enumerate(pieces):
-        start = pl.multiple_of(lax.rem(band[0] + k, count) * rows, rows)
+        start = pl.multiple_of(lax.rem(lax.axis_index("band") + k, count) * rows, rows)
         part = total[pl.ds(start, rows), :].astype(BF16)
         piece[...] = part
         if k:
             rest_ref[(k - 1) * rows : k * rows, :] = part
 
 
-def second_term(band, nodes, sums, back, previous, count):
+def second_term(nodes, sums, back, previous, count):
     owned = sums.shape[0]
     rows = owned // count
     made = pl.pallas_call(
         second_kernel,
         out_shape=[jax.ShapeDtypeStruct((rows, LANES), BF16)] * count
         + [jax.ShapeDtypeStruct((owned - rows, LANES), BF16)],
-        in_specs=[SM, SM, VM, VM, VM],
+        in_specs=[SM, VM, VM, VM],
         out_specs=[VM] * (count + 1),
-        scratch_shapes=[pltpu.VMEM(sums.shape, F32)],
+        scratch_shapes=[pltpu.VMEM(sums.shape, F32), pltpu.VMEM(back.shape, F32)],
         compiler_params=params(16),
         cost_estimate=cost(0, 6 << 20),
         name="second_term",
-    )(band, nodes, sums, back, previous)
+    )(nodes, sums, back, previous)
     return made[:count], made[count]
 
 
-def gram_kernel(place, *refs):
-    pieces, (keep_ref, send_ref, held, whole) = refs[:-4], refs[-4:]
+def gram_kernel(*refs):
+    pieces, (keep_ref, send_ref, held) = refs[:-3], refs[-3:]
     count = len(pieces)
     for s, piece in enumerate(pieces):
-        held[lax.rem(place[0] + (count - s), count)] = piece[...]
-    at = 0
-    for i in range(count):
-        for j in range(i + 1):
-            whole[at : at + LANES, :] = lax.dot_general(
-                held[i], held[j], (((0,), (0,)), ((), ())), preferred_element_type=F32
-            )
-            at += LANES
-    half = at // 2
-    mine = pl.multiple_of(place[1] * half, half)
-    keep_ref[...] = whole[pl.ds(mine, half), :]
-    send_ref[...] = whole[pl.ds(half - mine, half), :]
-
-
-def partial_gram(place, pieces):
+        held[lax.rem(lax.axis_index("band") + (count - s), count)] = piece[...]
+    half = keep_ref.shape[0]
+
+    def write(*halves):
+        at = 0
+        for i in range(count):
+            for j in range(i + 1):
+                halves[at // half][at % half : at % half + LANES, :] = lax.dot_general(
+                    held[i], held[j], (((0,), (0,)), ((), ())), preferred_element_type=F32
+                )
+                at += LANES
+
+    side = lax.rem(lax.axis_index("domain"), 2)
+    pl.when(side == 0)(lambda: write(keep_ref, send_ref))
+    pl.when(side != 0)(lambda: write(send_ref, keep_ref))
+
+
+def partial_gram(pieces):
     count = len(pieces)
     rows = count * (count + 1) // 2 * LANES
     return pl.pallas_call(
         gram_kernel,
         out_shape=[jax.ShapeDtypeStruct((rows // 2, LANES), F32)] * 2,
-        in_specs=[SM] + [VM] * count,
+        in_specs=[VM] * count,
         out_specs=[VM] * 2,
-        scratch_shapes=[
-            pltpu.VMEM((count,) + pieces[0].shape, BF16),
-            pltpu.VMEM((rows, LANES), F32),
-        ],
+        scratch_shapes=[pltpu.VMEM((count,) + pieces[0].shape, BF16)],
         compiler_params=params(16),
         cost_estimate=cost(0, 4 << 20),
         name="partial_gram",
-    )(place, *pieces)
-
-
-def quarters_kernel(place, a_ref, b_ref, *refs):
+    )(*pieces)
+
+
+def quarters_kernel(a_ref, b_ref, *refs):
     outs, total = refs[:-1], refs[-1]
     total[...] = a_ref[...] + b_ref[...]
     rows = outs[0].shape[0]
+    place = lax.axis_index("domain") // 2
     for m, out in enumerate(outs):
-        out[...] = total[pl.ds(pl.multiple_of((place[2] ^ m) * rows, rows), rows), :]
-
-
-def quarters(place, a, b, count):
+        out[...] = total[pl.ds(pl.multiple_of((place ^ m) * rows, rows), rows), :]
+
+
+def quarters(a, b, count):
     rows = a.shape[0] // count
     return pl.pallas_call(
         quarters_kernel,
         out_shape=[jax.ShapeDtypeStruct((rows, LANES), F32)] * count,
-        in_specs=[SM, VM, VM],
+        in_specs=[VM, VM],
         out_specs=[VM] * count,
         scratch_shapes=[pltpu.VMEM(a.shape, F32)],
         compiler_params=params(4),
         cost_estimate=cost(0, 1 << 20),
         name="quarters",
-    )(place, a, b)
-
-
-def joined_kernel(place, *refs):
+    )(a, b)
+
+
+def joined_kernel(*refs):
     parts, out_ref = refs[:-1], refs[-1]
     rows = parts[0].shape[0]
+    place = lax.axis_index("domain") // 2
     for m, part in enumerate(parts):
-        out_ref[pl.ds(pl.multiple_of((place[2] ^ m) * rows, rows), rows), :] = part[...]
-
-
-def joined(place, parts):
+        out_ref[pl.ds(pl.multiple_of((place ^ m) * rows, rows), rows), :] = part[...]
+
+
+def joined(parts):
     rows = parts[0].shape[0] * len(parts)
     return pl.pallas_call(
         joined_kernel,
         out_shape=jax.ShapeDtypeStruct((rows, LANES), F32),
-        in_specs=[SM] + [VM] * len(parts),
+        in_specs=[VM] * len(parts),
         out_specs=VM,
         compiler_params=params(4),
         cost_estimate=cost(0, 1 << 20),
         name="joined",
-    )(place, *parts)
+    )(*parts)
 
 
 def paired(value, axis, mask):
@@ -396,7 +400,7 @@
     return lax.optimization_barrier(values)
 
 
-def summed_beside(place, keep, send, rests, firsts):
+def summed_beside(keep, send, rests, firsts):
     count = lax.axis_size("band")
     half = keep + paired(send, "domain", 1)
     if lax.axis_size("domain") != 8 or count != 4:
@@ -407,7 +411,7 @@
         both = lax.psum(jnp.where(side == 0, both, both[::-1]) * 1.0, ("domain", "band"))
         return both[side], both[1 - side]
     rests.append(passed_up(rests, firsts, 0))
-    total, *others = quarters(place, keep, paired(send, "domain", 1), 4)
+    total, *others = quarters(keep, paired(send, "domain", 1), 4)
     for part in [paired(other, "domain", 2 * m) for m, other in enumerate(others, 1)]:
         total = total + part
     parts = [total] + [shifted(total, "band", s) for s in range(1, count)]
@@ -417,7 +421,7 @@
     skipping = jnp.concatenate([rests[1][2 * rows :], firsts[1], rests[1][:rows]])
     rests.append(lax.ppermute(skipping, "band", [(1, 3)]))
     total = sum(parts[1:], parts[0])
-    half = joined(place, [total] + [paired(total, "domain", 2 * m) for m in (1, 2, 3)])
+    half = joined([total] + [paired(total, "domain", 2 * m) for m in (1, 2, 3)])
     return half, paired(half, "domain", 1)
 
 
@@ -506,17 +510,16 @@
     return done
 
 
-def inverse_kernel(over, place, mine_ref, other_ref, out_ref, packed_ref, work, small):
+def inverse_kernel(over, mine_ref, other_ref, out_ref, work, small):
     half = mine_ref.shape[0]
-    mine = pl.multiple_of(place[1] * half, half)
-    packed_ref[pl.ds(mine, half), :] = mine_ref[...]
-    packed_ref[pl.ds(half - mine, half), :] = other_ref[...]
+    side = lax.rem(lax.axis_index("domain"), 2)
     size = work.shape[0]
     blocks = size // LANES
     at = 0
     for i in range(blocks):
         for j in range(i + 1):
-            block = packed_ref[at : at + LANES, :] * over
+            here = slice(at % half, at % half + LANES)
+            block = jnp.where(side == at // half, mine_ref[here, :], other_ref[here, :]) * over
             work[i * LANES : (i + 1) * LANES, j * LANES : (j + 1) * LANES] = block
             if i != j:
                 work[j * LANES : (j + 1) * LANES, i * LANES : (i + 1) * LANES] = block.T
@@ -555,99 +558,92 @@
     lax.fori_loop(0, blocks, step, 0)
 
 
-def inverse_factor(place, mine, other, size, over):
+def inverse_factor(mine, other, size, over):
     return pl.pallas_call(
         functools.partial(inverse_kernel, over),
         out_shape=jax.ShapeDtypeStruct((size, size), F32),
-        in_specs=[SM, VM, VM],
+        in_specs=[VM, VM],
         out_specs=VM,
         scratch_shapes=[
-            pltpu.VMEM((2 * mine.shape[0], LANES), F32),
             pltpu.VMEM((size, size), F32),
             pltpu.VMEM((LANES, LANES), F32),
         ],
         compiler_params=params(16),
         cost_estimate=cost(0, 70 << 20),
         name="inverse_factor",
-    )(place, mine, other)
-
-
-def output_kernel(band, factor_ref, *refs):
-    out_ref, blocks_ref = refs[-2:]
+    )(mine, other)
+
+
+def output_kernel(factor_ref, *refs):
+    band = lax.axis_index("band")
+    out_ref, blocks_ref, made_ref, sems = refs[-4:]
     count = factor_ref.shape[0] // LANES
-    firsts, rests = refs[:count], refs[count:-2]
-    j = pl.program_id(0)
-
-    @pl.when(j == 0)
-    def _():
-        row = pl.ds(pl.multiple_of(band[0] * LANES, LANES), LANES)
-        for s in range(count):
-            source = band[0] - s
-            column = pl.ds(pl.multiple_of(jnp.maximum(source, 0) * LANES, LANES), LANES)
-            block = jnp.where(source >= 0, factor_ref[row, column], 0.0).T
-            high = block.astype(BF16)
-            here = slice(s * LANES, (s + 1) * LANES)
-            blocks_ref[here, 0:LANES] = high
-            blocks_ref[here, LANES:] = (block - high.astype(F32)).astype(BF16)
-
-    def put(pieces):
-        rows = jnp.concatenate(pieces, axis=1)
-        made = jnp.dot(rows, blocks_ref[...], preferred_element_type=F32)
-        out_ref[...] = made[:, 0:LANES] + made[:, LANES:]
-
-    rows = out_ref.shape[0]
-
-    @pl.when(j == 0)
-    def _():
-        put([piece[...] for piece in firsts])
-
-    @pl.when(j > 0)
-    def _():
-        here = pl.ds(pl.multiple_of((j - 1) * rows, rows), rows)
-        put([piece[here, :] for piece in rests])
-
-
-def output(band, factor, firsts, rests):
+    firsts, rests = refs[:count], refs[count:-4]
+    rows = firsts[0].shape[0]
+    row = pl.ds(pl.multiple_of(band * LANES, LANES), LANES)
+    for s in range(count):
+        source = band - s
+        column = pl.ds(pl.multiple_of(jnp.maximum(source, 0) * LANES, LANES), LANES)
+        block = jnp.where(source >= 0, factor_ref[row, column], 0.0).T
+        high = block.astype(BF16)
+        here = slice(s * LANES, (s + 1) * LANES)
+        blocks_ref[here, 0:LANES] = high
+        blocks_ref[here, LANES:] = (block - high.astype(F32)).astype(BF16)
+    copies = []
+    for j in range(count):
+        here = slice((j - 1) * rows, j * rows)
+        pieces = [piece[...] for piece in firsts] if j == 0 else [piece[here, :] for piece in rests]
+        made = jnp.dot(
+            jnp.concatenate(pieces, axis=1), blocks_ref[...], preferred_element_type=F32
+        )
+        made_ref[j] = made[:, 0:LANES] + made[:, LANES:]
+        start = pl.multiple_of(lax.rem(band + j, count) * rows, rows)
+        copies.append(
+            pltpu.make_async_copy(made_ref.at[j], out_ref.at[pl.ds(start, rows), :], sems.at[j])
+        )
+        copies[-1].start()
+    for copy in copies:
+        copy.wait()
+
+
+def output(factor, firsts, rests):
     count = len(firsts)
     rows = firsts[0].shape[0]
     return pl.pallas_call(
         output_kernel,
         out_shape=jax.ShapeDtypeStruct((rows * count, LANES), F32),
-        grid_spec=pltpu.PrefetchScalarGridSpec(
-            num_scalar_prefetch=1,
-            grid=(count,),
-            in_specs=[VM] * (1 + 2 * count),
-            out_specs=pl.BlockSpec((rows, LANES), lambda j, band: (lax.rem(band[0] + j, count), 0)),
-            scratch_shapes=[pltpu.VMEM((count * LANES, 2 * LANES), BF16)],
-        ),
+        in_specs=[VM] * (1 + 2 * count),
+        out_specs=pl.BlockSpec(memory_space=pl.ANY),
+        scratch_shapes=[
+            pltpu.VMEM((count * LANES, 2 * LANES), BF16),
+            pltpu.VMEM((count, rows, LANES), F32),
+            pltpu.SemaphoreType.DMA((count,)),
+        ],
         compiler_params=params(24),
         cost_estimate=cost(0, 10 << 20),
         name="output",
-    )(band, factor, *firsts, *rests)
+    )(factor, *firsts, *rests)
 
 
 def shards(states_block, cell_matrix, cell_scale, potential, connectivity, boundary_nodes):
     owned = states_block.shape[0]
     count = lax.axis_size("band")
-    band = lax.axis_index("band").astype(jnp.int32).reshape(1)
     levels = potential.reshape(owned // LANES, LANES)
 
     start, words = prepare(boundary_nodes, states_block, connectivity)
     operator = functools.partial(apply_operator, words, cell_scale, cell_matrix, levels)
     sums, back = operator(*start)
     sums, back = operator(*first_term(boundary_nodes, sums, back))
-    pieces, rest = second_term(band, boundary_nodes, sums, back, states_block, count)
+    pieces, rest = second_term(boundary_nodes, sums, back, states_block, count)
 
     firsts = [pieces[0]] + [shifted(pieces[s], "band", s) for s in range(1, count)]
     firsts = list(ordered(*firsts))
     rests = [rest]
-    domain = lax.axis_index("domain")
-    place = jnp.stack([lax.axis_index("band"), domain % 2, domain // 2]).astype(jnp.int32)
-    keep, send = partial_gram(place, firsts)
-    mine, other = summed_beside(place, keep, send, rests, firsts)
+    keep, send = partial_gram(firsts)
+    mine, other = summed_beside(keep, send, rests, firsts)
     over = 1.0 / (owned * lax.axis_size("domain"))
-    factor = inverse_factor(place, mine, other, count * LANES, over)
-    return output(band, factor, firsts, rests)
+    factor = inverse_factor(mine, other, count * LANES, over)
+    return output(factor, firsts, rests)
 
 
 def solution(mesh):

time: 123 us -> 122 us (level)
  Pallas kernels: 52.9 us -> 50.3 us
  waiting for transfers between devices: 43.3 us -> 44.6 us
    unnamed x18 -> x20, local copies, waits for them, and re-layouts: 4.2 us -> 4.21 us
  transfers between devices with their start and end apart: 21 -> 21, of which waited for: 12 -> 12; matrix products, arithmetic and copies ran while one was open for 0% -> 0% of each run, Pallas kernels for 24% -> 23%
where the time goes in v7:
time: 122 us
  Pallas kernels  50.3 us (41%)
  waiting for transfers between devices  44.6 us (37%)
  starting transfers between devices  22 us (18%)
  local copies, waits for them, and re-layouts  4.3 us (4%)
    ppermute x10, waiting for transfers between devices, shifted(): lax.ppermute(value, axis, [(i, (i + steps) % count) for i in range(count)])  29.7 us
    pallas_call x2, Pallas kernels, apply_operator(): pl.pallas_call(far_cells_kernel, out_shape=(jax.ShapeDtypeStruct((owned,...  15 us
    pallas_call x1, Pallas kernels, inverse_factor(): pl.pallas_call(functools.partial(inverse_kernel, over), out_shape=jax.Sha...  13.4 us
    ppermute x10, starting transfers between devices, shifted(): lax.ppermute(value, axis, [(i, (i + steps) % count) for i in range(count)])  10.6 us
    ppermute x8, waiting for transfers between devices, paired(): return lax.ppermute(value, axis, [(i, i ^ mask) for i in range(count)])  8.98 us
    pallas_call x2, Pallas kernels, apply_operator(): pl.pallas_call(functools.partial(near_sums_kernel, npc), out_shape=jax.Sh...  7.65 us
    ppermute x8, starting transfers between devices, paired(): return lax.ppermute(value, axis, [(i, i ^ mask) for i in range(count)])  7.57 us
    pallas_call x2, Pallas kernels, apply_operator(): pl.pallas_call(near_products_kernel, out_shape=jax.ShapeDtypeStruct(held,...  7.11 us
  transfers between devices with their start and end apart: 21, of which 12 were waited for; matrix products, arithmetic and copies ran while one was open for 0% of the time, Pallas kernels for 23%

profile of v7, /device:TPU:26, one launch (start us, length us, event | category | flops | bytes accessed | tf_op | source)
XLA Modules:
  0.0 121.9 jit_solution(13700183902802961193)
XLA Ops:
  0.0 1.2 copy-done.2
  2.6 1.0 prepare.1
  5.3 3.6 %near_products.2.products_ref = f32[8,344,128]{2,1,0:T(8,128)S(1)} custom-call(s32[4096]{0:T(1024)S(1)} %bitcast.2, f32[16]{0:T(128)S(1)} %copy-done.8, f32[3744,128]{1,0:T(8,128)S(1)} %get-tuple-element.38.ext_ref.wide_ref, bf16[343,343]{1,0:T(8,128)(2,1)S(1)} %copy-done), custom_call_target="tpu_custom_call" | custom-call | bytes 14680064 | tf_op jit(solution)/shard_map/near_products/pallas_call | solution.py:194
  8.9 7.5 %far_cells.2 = (f32[3456,128]{1,0:T(8,128)S(1)}, bf16[288,128]{1,0:T(8,128)(2,1)S(1)}) custom-call(s32[4096]{0:T(1024)S(1)} %bitcast.3, f32[16]{0:T(128)S(1)} %copy-done.8, f32[3744,128]{1,0:T(8,128)S(1)} %get-tuple-element.38.ext_ref.wide_ref, bf16[288,128]{1,0:T(8,128)(2,1)S(1)} %collective-permute-done.ghost_ref, bf16[343,343]{1,0:T(8,128)(2,1)S(1)} %copy-done.1, ...), custom_call_target="tpu_custom_call" | custom-call | bytes 29360128 | tf_op jit(solution)/shard_map/far_cells/pallas_call | solution.py:205
  16.9 3.9 %near_sums.2.sums_ref = f32[3456,128]{1,0:T(8,128)S(1)} custom-call(s32[4096]{0:T(1024)S(1)} %bitcast.4, f32[8,344,128]{2,1,0:T(8,128)S(1)} %near_products.2.products_ref, f32[3456,128]{1,0:T(8,128)S(1)} %get-tuple-element.41.start_ref), custom_call_target="tpu_custom_call" | custom-call | bytes 14680064 | tf_op jit(solution)/shard_map/near_sums/pallas_call | solution.py:221
  20.9 1.5 %first_term.1 = (f32[3456,128]{1,0:T(8,128)S(1)}, f32[3744,128]{1,0:T(8,128)S(1)}, bf16[288,128]{1,0:T(8,128)(2,1)S(1)}) custom-call(s32[288]{0:T(512)S(1)} %copy-done.7, f32[3456,128]{1,0:T(8,128)S(1)} %near_sums.2.sums_ref, bf16[288,128]{1,0:T(8,128)(2,1)S(1)} %collective-permute-done.1.back_ref), custom_call_target="tpu_custom_call" | custom-call | bytes 8388608 | tf_op jit(solution)/shard_map/first_term/pallas_call | solution.py:260
  22.3 1.3 %collective-permute-start.2 = (bf16[288,128]{1,0:T(8,128)(2,1)S(1)}, bf16[288,128]{1,0:T(8,128)(2,1)S(1)}, u32[]{:S(2)}, u32[]{:S(2)}) collective-permute-start(bf16[288,128]{1,0:T(8,128)(2,1)S(1)} %get-tuple-element.43), channel_id=1, source_target_pairs={{0,28},{4,0},{8,4},{12,8},{16,12},{20,16},{24,20},{28,24},{1,29},{... | collective-permute-start | bytes 221192 | tf_op jit(solution)/shard_map/ppermute | solution.py:30
  23.7 3.6 %near_products.3.products_ref = f32[8,344,128]{2,1,0:T(8,128)S(1)} custom-call(s32[4096]{0:T(1024)S(1)} %bitcast.5, f32[16]{0:T(128)S(1)} %copy-done.9, f32[3744,128]{1,0:T(8,128)S(1)} %get-tuple-element.44.ext_ref, bf16[343,343]{1,0:T(8,128)(2,1)S(1)} %copy-done.1), custom_call_target="tpu_custom_call" | custom-call | bytes 14680064 | tf_op jit(solution)/shard_map/near_products/pallas_call | solution.py:194
  27.2 7.5 %far_cells.3 = (f32[3456,128]{1,0:T(8,128)S(1)}, bf16[288,128]{1,0:T(8,128)(2,1)S(1)}) custom-call(s32[4096]{0:T(1024)S(1)} %bitcast.6, f32[16]{0:T(128)S(1)} %copy-done.9, f32[3744,128]{1,0:T(8,128)S(1)} %get-tuple-element.44.ext_ref, bf16[288,128]{1,0:T(8,128)(2,1)S(1)} %collective-permute-done.2.ghost_ref, bf16[343,343]{1,0:T(8,128)(2,1)S(1)} %copy-done.1, ...), custom_call_target="tpu_custom_call" | custom-call | bytes 29360128 | tf_op jit(solution)/shard_map/far_cells/pallas_call | solution.py:205
  34.7 1.9 %collective-permute-start.3 = (bf16[288,128]{1,0:T(8,128)(2,1)S(1)}, bf16[288,128]{1,0:T(8,128)(2,1)S(1)}, u32[]{:S(2)}, u32[]{:S(2)}) collective-permute-start(bf16[288,128]{1,0:T(8,128)(2,1)S(1)} %get-tuple-element.49), channel_id=1, source_target_pairs={{0,4},{4,8},{8,12},{12,16},{16,20},{20,24},{24,28},{28,0},{1,5},{5... | collective-permute-start | bytes 221192 | tf_op jit(solution)/shard_map/ppermute | solution.py:30
  36.6 3.7 %near_sums.3.sums_ref = f32[3456,128]{1,0:T(8,128)S(1)} custom-call(s32[4096]{0:T(1024)S(1)} %bitcast.7, f32[8,344,128]{2,1,0:T(8,128)S(1)} %near_products.3.products_ref, f32[3456,128]{1,0:T(8,128)S(1)} %get-tuple-element.48.start_ref), custom_call_target="tpu_custom_call" | custom-call | bytes 14680064 | tf_op jit(solution)/shard_map/near_sums/pallas_call | solution.py:221
  40.3 1.4 %second_term.1 = (bf16[864,128]{1,0:T(8,128)(2,1)S(1)}, bf16[864,128]{1,0:T(8,128)(2,1)S(1)}, bf16[864,128]{1,0:T(8,128)(2,1)S(1)}, bf16[864,128]{1,0:T(8,128)(2,1)S(1)}, bf16[2592,128]{1,0:T(8,128)(2,1)S(1)}) custom-call(s32[288]{0:T(512)S(1)} %copy-done.7, f32[3456,128]{1,0:T(8,128)S(1)} %near_sums.3.sums_ref, ...), custom_call_target="tpu_custom_call" | custom-call | bytes 6291456 | tf_op jit(solution)/shard_map/second_term/pallas_call | solution.py:293
  42.0 1.7 %collective-permute-start.5 = (bf16[864,128]{1,0:T(8,128)(2,1)S(1)}, bf16[864,128]{1,0:T(8,128)(2,1)S(1)}, u32[]{:S(2)}, u32[]{:S(2)}) collective-permute-start(bf16[864,128]{1,0:T(8,128)(2,1)S(1)} %get-tuple-element.52), channel_id=1, source_target_pairs={{0,2},{1,3},{2,0},{3,1},{4,6},{5,7},{6,4},{7,5},{8,10},{9,11},{10,... | collective-permute-start | bytes 663560 | tf_op jit(solution)/shard_map/ppermute | solution.py:30
  44.2 5.4 %collective-permute-done.4.refs_1_ = bf16[864,128]{1,0:T(8,128)(2,1)S(1)} collective-permute-done((bf16[864,128]{1,0:T(8,128)(2,1)S(1)}, bf16[864,128]{1,0:T(8,128)(2,1)S(1)}, u32[]{:S(2)}, u32[]{:S(2)}) %collective-permute-start.4) | collective-permute-done | bytes 221216 | tf_op jit(solution)/shard_map/ppermute | solution.py:30
  49.5 14.1 %collective-permute-done.5.refs_2_ = bf16[864,128]{1,0:T(8,128)(2,1)S(1)} collective-permute-done((bf16[864,128]{1,0:T(8,128)(2,1)S(1)}, bf16[864,128]{1,0:T(8,128)(2,1)S(1)}, u32[]{:S(2)}, u32[]{:S(2)}) %collective-permute-start.5) | collective-permute-done | bytes 221216 | tf_op jit(solution)/shard_map/ppermute | solution.py:30
  63.6 1.1 partial_gram.1
  65.2 1.3 %collective-permute-start.12 = (bf16[2592,128]{1,0:T(8,128)(2,1)S(1)}, bf16[2592,128]{1,0:T(8,128)(2,1)S(1)}, u32[]{:S(2)}, u32[]{:S(2)}) collective-permute-start(bf16[2592,128]{1,0:T(8,128)(2,1)S(1)} %pad_maximum_fusion), channel_id=1, source_target_pairs={{0,1},{1,2},{2,3},{4,5},{5,6},{6,7},{8,9},{9,10},{10,11},{12,13},{... | collective-permute-start | bytes 1990664 | tf_op jit(solution)/shard_map/ppermute | solution.py:396
  68.2 1.9 %collective-permute-start.8 = (f32[160,128]{1,0:T(8,128)S(1)}, f32[160,128]{1,0:T(8,128)S(1)}, u32[]{:S(2)}, u32[]{:S(2)}) collective-permute-start(f32[160,128]{1,0:T(8,128)S(1)} %get-tuple-element.61), channel_id=1, source_target_pairs={{0,8},{4,12},{8,0},{12,4},{16,24},{20,28},{24,16},{28,20},{1,9},{5... | collective-permute-start | bytes 245768 | tf_op jit(solution)/shard_map/ppermute | solution.py:389
  70.1 2.6 %collective-permute-done.10 = f32[160,128]{1,0:T(8,128)S(1)} collective-permute-done((f32[160,128]{1,0:T(8,128)S(1)}, f32[160,128]{1,0:T(8,128)S(1)}, u32[]{:S(2)}, u32[]{:S(2)}) %collective-permute-start.10) | collective-permute-done | bytes 81952 | tf_op jit(solution)/shard_map/ppermute | solution.py:389
  74.0 3.6 %collective-permute-start.11 = (f32[160,128]{1,0:T(8,128)S(1)}, f32[160,128]{1,0:T(8,128)S(1)}, u32[]{:S(2)}, u32[]{:S(2)}) collective-permute-start(f32[160,128]{1,0:T(8,128)S(1)} %add_add_fusion.1), channel_id=1, source_target_pairs={{0,1},{1,2},{2,3},{3,0},{4,5},{5,6},{6,7},{7,4},{8,9},{9,10},{10,1... | collective-permute-start | bytes 245768 | tf_op jit(solution)/shard_map/ppermute | solution.py:30
  78.4 7.6 %collective-permute-done.11 = f32[160,128]{1,0:T(8,128)S(1)} collective-permute-done((f32[160,128]{1,0:T(8,128)S(1)}, f32[160,128]{1,0:T(8,128)S(1)}, u32[]{:S(2)}, u32[]{:S(2)}) %collective-permute-start.11) | collective-permute-done | bytes 81952 | tf_op jit(solution)/shard_map/ppermute | solution.py:30
  86.2 1.3 %collective-permute-start.19 = (bf16[2592,128]{1,0:T(8,128)(2,1)S(1)}, bf16[2592,128]{1,0:T(8,128)(2,1)S(1)}, u32[]{:S(2)}, u32[]{:S(2)}) collective-permute-start(bf16[2592,128]{1,0:T(8,128)(2,1)S(1)} %get-tuple-element.70), channel_id=1, source_target_pairs={{1,2},{2,3},{5,6},{6,7},{9,10},{10,11},{13,14},{14,15},{17,18},{18... | collective-permute-start | bytes 1990664 | tf_op jit(solution)/shard_map/ppermute | solution.py:396
  87.5 1.3 %collective-permute-start.20 = (bf16[2592,128]{1,0:T(8,128)(2,1)S(1)}, bf16[2592,128]{1,0:T(8,128)(2,1)S(1)}, u32[]{:S(2)}, u32[]{:S(2)}) collective-permute-start(bf16[2592,128]{1,0:T(8,128)(2,1)S(1)} %get-tuple-element.69), channel_id=1, source_target_pairs={{1,3},{5,7},{9,11},{13,15},{17,19},{21,23},{25,27},{29,31}} | collective-permute-start | bytes 1990664 | tf_op jit(solution)/shard_map/ppermute | solution.py:422
  89.4 2.0 %collective-permute-done.13 = f32[160,128]{1,0:T(8,128)S(1)} collective-permute-done((f32[160,128]{1,0:T(8,128)S(1)}, f32[160,128]{1,0:T(8,128)S(1)}, u32[]{:S(2)}, u32[]{:S(2)}) %collective-permute-start.13) | collective-permute-done | bytes 81952 | tf_op jit(solution)/shard_map/ppermute | solution.py:30
  91.5 1.6 %collective-permute-start.16 = (f32[160,128]{1,0:T(8,128)S(1)}, f32[160,128]{1,0:T(8,128)S(1)}, u32[]{:S(2)}, u32[]{:S(2)}) collective-permute-start(f32[160,128]{1,0:T(8,128)S(1)} %add_add_fusion.refs_0_), channel_id=1, source_target_pairs={{0,16},{4,20},{8,24},{12,28},{16,0},{20,4},{24,8},{28,12},{1,17},{... | collective-permute-start | bytes 245768 | tf_op jit(solution)/shard_map/ppermute | solution.py:389
  93.1 1.9 %collective-permute-start.17 = (f32[160,128]{1,0:T(8,128)S(1)}, f32[160,128]{1,0:T(8,128)S(1)}, u32[]{:S(2)}, u32[]{:S(2)}) collective-permute-start(f32[160,128]{1,0:T(8,128)S(1)} %add_add_fusion.refs_0_), channel_id=1, source_target_pairs={{0,24},{4,28},{8,16},{12,20},{16,8},{20,12},{24,0},{28,4},{1,25},{... | collective-permute-start | bytes 245768 | tf_op jit(solution)/shard_map/ppermute | solution.py:389
  95.0 1.7 %collective-permute-done.15.refs_1_ = f32[160,128]{1,0:T(8,128)S(1)} collective-permute-done((f32[160,128]{1,0:T(8,128)S(1)}, f32[160,128]{1,0:T(8,128)S(1)}, u32[]{:S(2)}, u32[]{:S(2)}) %collective-permute-start.15) | collective-permute-done | bytes 81952 | tf_op jit(solution)/shard_map/ppermute | solution.py:389
  96.6 1.8 %collective-permute-done.17.refs_3_ = f32[160,128]{1,0:T(8,128)S(1)} collective-permute-done((f32[160,128]{1,0:T(8,128)S(1)}, f32[160,128]{1,0:T(8,128)S(1)}, u32[]{:S(2)}, u32[]{:S(2)}) %collective-permute-start.17) | collective-permute-done | bytes 81952 | tf_op jit(solution)/shard_map/ppermute | solution.py:389
  98.6 1.6 %collective-permute-done.18.other_ref = f32[640,128]{1,0:T(8,128)S(1)} collective-permute-done((f32[640,128]{1,0:T(8,128)S(1)}, f32[640,128]{1,0:T(8,128)S(1)}, u32[]{:S(2)}, u32[]{:S(2)}) %collective-permute-start.18) | collective-permute-done | bytes 327712 | tf_op jit(solution)/shard_map/ppermute | solution.py:389
  100.2 13.4 %inverse_factor.1.factor_ref = f32[512,512]{1,0:T(8,128)S(1)} custom-call(f32[640,128]{1,0:T(8,128)S(1)} %joined.1.mine_ref, f32[640,128]{1,0:T(8,128)S(1)} %collective-permute-done.18.other_ref), custom_call_target="tpu_custom_call" | custom-call | bytes 73400320 | tf_op jit(solution)/shard_map/inverse_factor/pallas_call | solution.py:562
  113.6 5.9 %collective-permute-done.20.refs_7_ = bf16[2592,128]{1,0:T(8,128)(2,1)S(1)} collective-permute-done((bf16[2592,128]{1,0:T(8,128)(2,1)S(1)}, bf16[2592,128]{1,0:T(8,128)(2,1)S(1)}, u32[]{:S(2)}, u32[]{:S(2)}) %collective-permute-start.20) | collective-permute-done | bytes 663584 | tf_op jit(solution)/shard_map/ppermute | solution.py:422
  119.5 2.2 %output.1 = f32[3456,128]{1,0:T(8,128)} custom-call(f32[512,512]{1,0:T(8,128)S(1)} %inverse_factor.1.factor_ref, bf16[864,128]{1,0:T(8,128)(2,1)S(1)} %get-tuple-element.54.refs_0_, bf16[864,128]{1,0:T(8,128)(2,1)S(1)} %collective-permute-done.4.refs_1_, bf16[864,128]{1,0:T(8,128)(2,1)S(1)} %collective-permute-done.5.refs_2_, ...), custom_call_target="tpu_custom_call" | custom-call | bytes 10485760 | tf_op jit(solution)/shard_map/output/pallas_call | solution.py:612
  (51 shorter events, 9.6 us)
Async XLA Ops:
  0.0 1.2 copy-start.2
  1.2 0.7 copy-start.5
  1.9 0.7 copy-start.6
  3.6 5.2 %collective-permute-start = (bf16[288,128]{1,0:T(8,128)(2,1)S(1)}, bf16[288,128]{1,0:T(8,128)(2,1)S(1)}, u32[]{:S(2)}, u32[]{:S(2)}) collective-permute-start(bf16[288,128]{1,0:T(8,128)(2,1)S(1)} %get-tuple-element.37), channel_id=1, source_target_pairs={{0,28},{4,0},{8,4},{12,8},{16,12},{20,16},{24,20},{28,24},{1,29},{... | collective-permute-start | bytes 221192 | tf_op jit(solution)/shard_map/ppermute | solution.py:30
  3.6 1.0 copy-start
  4.6 0.7 copy-start.8
  5.3 3.6 %copy-start.1 = (bf16[343,343]{1,0:T(8,128)(2,1)S(1)}, bf16[343,343]{1,0:T(8,128)(2,1)}, u32[]{:S(2)}) copy-start(bf16[343,343]{1,0:T(8,128)(2,1)} %matrix_ref.7) | copy-start | bytes 705898
  5.3 3.6 %copy-start.4 = (f32[3456]{0:T(1024)S(1)}, f32[3456]{0:T(1024)}, u32[]{:S(2)}) copy-start(f32[3456]{0:T(1024)} %param.9) | copy-start | bytes 41476
  16.4 4.5 %collective-permute-start.1 = (bf16[288,128]{1,0:T(8,128)(2,1)S(1)}, bf16[288,128]{1,0:T(8,128)(2,1)S(1)}, u32[]{:S(2)}, u32[]{:S(2)}) collective-permute-start(bf16[288,128]{1,0:T(8,128)(2,1)S(1)} %get-tuple-element.42), channel_id=1, source_target_pairs={{0,4},{4,8},{8,12},{12,16},{16,20},{20,24},{24,28},{28,0},{1,5},{5... | collective-permute-start | bytes 221192 | tf_op jit(solution)/shard_map/ppermute | solution.py:30
  16.9 4.0 %copy-start.7 = (s32[288]{0:T(512)S(1)}, s32[288]{0:T(512)}, u32[]{:S(2)}) copy-start(s32[288]{0:T(512)} %nodes.5) | copy-start | bytes 3460
  20.8 2.8 %copy-start.9 = (f32[16]{0:T(128)S(1)}, f32[16]{0:T(128)}, u32[]{:S(2)}) copy-start(f32[16]{0:T(128)} %scale.7) | copy-start | bytes 196
  22.3 4.9 %collective-permute-start.2 = (bf16[288,128]{1,0:T(8,128)(2,1)S(1)}, bf16[288,128]{1,0:T(8,128)(2,1)S(1)}, u32[]{:S(2)}, u32[]{:S(2)}) collective-permute-start(bf16[288,128]{1,0:T(8,128)(2,1)S(1)} %get-tuple-element.43), channel_id=1, source_target_pairs={{0,28},{4,0},{8,4},{12,8},{16,12},{20,16},{24,20},{28,24},{1,29},{... | collective-permute-start | bytes 221192 | tf_op jit(solution)/shard_map/ppermute | solution.py:30
  34.7 5.6 %collective-permute-start.3 = (bf16[288,128]{1,0:T(8,128)(2,1)S(1)}, bf16[288,128]{1,0:T(8,128)(2,1)S(1)}, u32[]{:S(2)}, u32[]{:S(2)}) collective-permute-start(bf16[288,128]{1,0:T(8,128)(2,1)S(1)} %get-tuple-element.49), channel_id=1, source_target_pairs={{0,4},{4,8},{8,12},{12,16},{16,20},{20,24},{24,28},{28,0},{1,5},{5... | collective-permute-start | bytes 221192 | tf_op jit(solution)/shard_map/ppermute | solution.py:30
  36.6 3.7 %copy-start.3 = (bf16[3456,128]{1,0:T(8,128)(2,1)S(1)}, bf16[3456,128]{1,0:T(8,128)(2,1)}, u32[]{:S(2)}) copy-start(bf16[3456,128]{1,0:T(8,128)(2,1)} %previous_ref.1) | copy-start | bytes 2654212
  41.7 7.8 %collective-permute-start.4 = (bf16[864,128]{1,0:T(8,128)(2,1)S(1)}, bf16[864,128]{1,0:T(8,128)(2,1)S(1)}, u32[]{:S(2)}, u32[]{:S(2)}) collective-permute-start(bf16[864,128]{1,0:T(8,128)(2,1)S(1)} %get-tuple-element.51), channel_id=1, source_target_pairs={{0,1},{1,2},{2,3},{3,0},{4,5},{5,6},{6,7},{7,4},{8,9},{9,10},{10,1... | collective-permute-start | bytes 663560 | tf_op jit(solution)/shard_map/ppermute | solution.py:30
  42.0 21.7 %collective-permute-start.5 = (bf16[864,128]{1,0:T(8,128)(2,1)S(1)}, bf16[864,128]{1,0:T(8,128)(2,1)S(1)}, u32[]{:S(2)}, u32[]{:S(2)}) collective-permute-start(bf16[864,128]{1,0:T(8,128)(2,1)S(1)} %get-tuple-element.52), channel_id=1, source_target_pairs={{0,2},{1,3},{2,0},{3,1},{4,6},{5,7},{6,4},{7,5},{8,10},{9,11},{10,... | collective-permute-start | bytes 663560 | tf_op jit(solution)/shard_map/ppermute | solution.py:30
  43.7 20.0 %collective-permute-start.6 = (bf16[864,128]{1,0:T(8,128)(2,1)S(1)}, bf16[864,128]{1,0:T(8,128)(2,1)S(1)}, u32[]{:S(2)}, u32[]{:S(2)}) collective-permute-start(bf16[864,128]{1,0:T(8,128)(2,1)S(1)} %get-tuple-element.53), channel_id=1, source_target_pairs={{0,3},{1,0},{2,1},{3,2},{4,7},{5,4},{6,5},{7,6},{8,11},{9,8},{10,9... | collective-permute-start | bytes 663560 | tf_op jit(solution)/shard_map/ppermute | solution.py:30
  64.7 1.8 %collective-permute-start.7 = (f32[640,128]{1,0:T(8,128)S(1)}, f32[640,128]{1,0:T(8,128)S(1)}, u32[]{:S(2)}, u32[]{:S(2)}) collective-permute-start(f32[640,128]{1,0:T(8,128)S(1)} %get-tuple-element.59), channel_id=1, source_target_pairs={{0,4},{4,0},{8,12},{12,8},{16,20},{20,16},{24,28},{28,24},{1,5},{5... | collective-permute-start | bytes 983048 | tf_op jit(solution)/shard_map/ppermute | solution.py:389
  65.2 20.9 %collective-permute-start.12 = (bf16[2592,128]{1,0:T(8,128)(2,1)S(1)}, bf16[2592,128]{1,0:T(8,128)(2,1)S(1)}, u32[]{:S(2)}, u32[]{:S(2)}) collective-permute-start(bf16[2592,128]{1,0:T(8,128)(2,1)S(1)} %pad_maximum_fusion), channel_id=1, source_target_pairs={{0,1},{1,2},{2,3},{4,5},{5,6},{6,7},{8,9},{9,10},{10,11},{12,13},{... | collective-permute-start | bytes 1990664 | tf_op jit(solution)/shard_map/ppermute | solution.py:396
  66.5 6.2 %collective-permute-start.10 = (f32[160,128]{1,0:T(8,128)S(1)}, f32[160,128]{1,0:T(8,128)S(1)}, u32[]{:S(2)}, u32[]{:S(2)}) collective-permute-start(f32[160,128]{1,0:T(8,128)S(1)} %get-tuple-element.63), channel_id=1, source_target_pairs={{0,24},{4,28},{8,16},{12,20},{16,8},{20,12},{24,0},{28,4},{1,25},{... | collective-permute-start | bytes 245768 | tf_op jit(solution)/shard_map/ppermute | solution.py:389
  67.4 6.1 %collective-permute-start.9 = (f32[160,128]{1,0:T(8,128)S(1)}, f32[160,128]{1,0:T(8,128)S(1)}, u32[]{:S(2)}, u32[]{:S(2)}) collective-permute-start(f32[160,128]{1,0:T(8,128)S(1)} %get-tuple-element.62), channel_id=1, source_target_pairs={{0,16},{4,20},{8,24},{12,28},{16,0},{20,4},{24,8},{28,12},{1,17},{... | collective-permute-start | bytes 245768 | tf_op jit(solution)/shard_map/ppermute | solution.py:389
  68.2 5.8 %collective-permute-start.8 = (f32[160,128]{1,0:T(8,128)S(1)}, f32[160,128]{1,0:T(8,128)S(1)}, u32[]{:S(2)}, u32[]{:S(2)}) collective-permute-start(f32[160,128]{1,0:T(8,128)S(1)} %get-tuple-element.61), channel_id=1, source_target_pairs={{0,8},{4,12},{8,0},{12,4},{16,24},{20,28},{24,16},{28,20},{1,9},{5... | collective-permute-start | bytes 245768 | tf_op jit(solution)/shard_map/ppermute | solution.py:389
  74.0 12.1 %collective-permute-start.11 = (f32[160,128]{1,0:T(8,128)S(1)}, f32[160,128]{1,0:T(8,128)S(1)}, u32[]{:S(2)}, u32[]{:S(2)}) collective-permute-start(f32[160,128]{1,0:T(8,128)S(1)} %add_add_fusion.1), channel_id=1, source_target_pairs={{0,1},{1,2},{2,3},{3,0},{4,5},{5,6},{6,7},{7,4},{8,9},{9,10},{10,1... | collective-permute-start | bytes 245768 | tf_op jit(solution)/shard_map/ppermute | solution.py:30
  77.6 11.8 %collective-permute-start.14 = (f32[160,128]{1,0:T(8,128)S(1)}, f32[160,128]{1,0:T(8,128)S(1)}, u32[]{:S(2)}, u32[]{:S(2)}) collective-permute-start(f32[160,128]{1,0:T(8,128)S(1)} %add_add_fusion.1), channel_id=1, source_target_pairs={{0,3},{1,0},{2,1},{3,2},{4,7},{5,4},{6,5},{7,6},{8,11},{9,8},{10,9... | collective-permute-start | bytes 245768 | tf_op jit(solution)/shard_map/ppermute | solution.py:30
  77.6 13.8 %collective-permute-start.13 = (f32[160,128]{1,0:T(8,128)S(1)}, f32[160,128]{1,0:T(8,128)S(1)}, u32[]{:S(2)}, u32[]{:S(2)}) collective-permute-start(f32[160,128]{1,0:T(8,128)S(1)} %add_add_fusion.1), channel_id=1, source_target_pairs={{0,2},{1,3},{2,0},{3,1},{4,6},{5,7},{6,4},{7,5},{8,10},{9,11},{10,... | collective-permute-start | bytes 245768 | tf_op jit(solution)/shard_map/ppermute | solution.py:30
  86.2 27.4 %collective-permute-start.19 = (bf16[2592,128]{1,0:T(8,128)(2,1)S(1)}, bf16[2592,128]{1,0:T(8,128)(2,1)S(1)}, u32[]{:S(2)}, u32[]{:S(2)}) collective-permute-start(bf16[2592,128]{1,0:T(8,128)(2,1)S(1)} %get-tuple-element.70), channel_id=1, source_target_pairs={{1,2},{2,3},{5,6},{6,7},{9,10},{10,11},{13,14},{14,15},{17,18},{18... | collective-permute-start | bytes 1990664 | tf_op jit(solution)/shard_map/ppermute | solution.py:396
  87.5 32.0 %collective-permute-start.20 = (bf16[2592,128]{1,0:T(8,128)(2,1)S(1)}, bf16[2592,128]{1,0:T(8,128)(2,1)S(1)}, u32[]{:S(2)}, u32[]{:S(2)}) collective-permute-start(bf16[2592,128]{1,0:T(8,128)(2,1)S(1)} %get-tuple-element.69), channel_id=1, source_target_pairs={{1,3},{5,7},{9,11},{13,15},{17,19},{21,23},{25,27},{29,31}} | collective-permute-start | bytes 1990664 | tf_op jit(solution)/shard_map/ppermute | solution.py:422
  91.4 5.2 %collective-permute-start.15 = (f32[160,128]{1,0:T(8,128)S(1)}, f32[160,128]{1,0:T(8,128)S(1)}, u32[]{:S(2)}, u32[]{:S(2)}) collective-permute-start(f32[160,128]{1,0:T(8,128)S(1)} %add_add_fusion.refs_0_), channel_id=1, source_target_pairs={{0,8},{4,12},{8,0},{12,4},{16,24},{20,28},{24,16},{28,20},{1,9},{5... | collective-permute-start | bytes 245768 | tf_op jit(solution)/shard_map/ppermute | solution.py:389
  91.5 5.1 %collective-permute-start.16 = (f32[160,128]{1,0:T(8,128)S(1)}, f32[160,128]{1,0:T(8,128)S(1)}, u32[]{:S(2)}, u32[]{:S(2)}) collective-permute-start(f32[160,128]{1,0:T(8,128)S(1)} %add_add_fusion.refs_0_), channel_id=1, source_target_pairs={{0,16},{4,20},{8,24},{12,28},{16,0},{20,4},{24,8},{28,12},{1,17},{... | collective-permute-start | bytes 245768 | tf_op jit(solution)/shard_map/ppermute | solution.py:389
  93.1 5.4 %collective-permute-start.17 = (f32[160,128]{1,0:T(8,128)S(1)}, f32[160,128]{1,0:T(8,128)S(1)}, u32[]{:S(2)}, u32[]{:S(2)}) collective-permute-start(f32[160,128]{1,0:T(8,128)S(1)} %add_add_fusion.refs_0_), channel_id=1, source_target_pairs={{0,24},{4,28},{8,16},{12,20},{16,8},{20,12},{24,0},{28,4},{1,25},{... | collective-permute-start | bytes 245768 | tf_op jit(solution)/shard_map/ppermute | solution.py:389
  98.5 1.7 %collective-permute-start.18 = (f32[640,128]{1,0:T(8,128)S(1)}, f32[640,128]{1,0:T(8,128)S(1)}, u32[]{:S(2)}, u32[]{:S(2)}) collective-permute-start(f32[640,128]{1,0:T(8,128)S(1)} %joined.1.mine_ref), channel_id=1, source_target_pairs={{0,4},{4,0},{8,12},{12,8},{16,20},{20,16},{24,28},{28,24},{1,5},{5... | collective-permute-start | bytes 983048 | tf_op jit(solution)/shard_map/ppermute | solution.py:389

commit v8 on v7

--- a/solution.py
+++ b/solution.py
@@ -10,7 +10,7 @@
 CENTER = 1.5
 HALF_WIDTH = 1.25
 LANES = 128
-CHAINS = 6
+CHAINS = 7
 F32 = jnp.float32
 BF16 = jnp.bfloat16
 VM = pl.BlockSpec(memory_space=pltpu.VMEM)
@@ -574,34 +574,54 @@
     )(mine, other)
 
 
-def output_kernel(factor_ref, *refs):
+def factor_blocks(factor_ref, blocks_ref, sources):
     band = lax.axis_index("band")
-    out_ref, blocks_ref, made_ref, sems = refs[-4:]
-    count = factor_ref.shape[0] // LANES
-    firsts, rests = refs[:count], refs[count:-4]
-    rows = firsts[0].shape[0]
     row = pl.ds(pl.multiple_of(band * LANES, LANES), LANES)
-    for s in range(count):
+    for k, s in enumerate(sources):
         source = band - s
         column = pl.ds(pl.multiple_of(jnp.maximum(source, 0) * LANES, LANES), LANES)
         block = jnp.where(source >= 0, factor_ref[row, column], 0.0).T
         high = block.astype(BF16)
-        here = slice(s * LANES, (s + 1) * LANES)
+        here = slice(k * LANES, (k + 1) * LANES)
         blocks_ref[here, 0:LANES] = high
         blocks_ref[here, LANES:] = (block - high.astype(F32)).astype(BF16)
-    copies = []
-    for j in range(count):
-        here = slice((j - 1) * rows, j * rows)
-        pieces = [piece[...] for piece in firsts] if j == 0 else [piece[here, :] for piece in rests]
-        made = jnp.dot(
-            jnp.concatenate(pieces, axis=1), blocks_ref[...], preferred_element_type=F32
-        )
-        made_ref[j] = made[:, 0:LANES] + made[:, LANES:]
+
+
+def both_parts(pieces, blocks):
+    made = jnp.dot(jnp.concatenate(pieces, axis=1), blocks, preferred_element_type=F32)
+    return made[:, 0:LANES] + made[:, LANES:]
+
+
+def early_kernel(factor_ref, *refs):
+    made_ref, blocks_ref = refs[-2:]
+    count = made_ref.shape[0]
+    firsts, rests = refs[:count], refs[count:-2]
+    rows = made_ref.shape[1]
+    factor_blocks(factor_ref, blocks_ref, range(count))
+    made_ref[0] = both_parts([first[...] for first in firsts], blocks_ref[...])
+    for j in range(1, count):
+        pieces = [rest[(j - 1) * rows : j * rows, :] for rest in rests]
+        made_ref[j] = both_parts(pieces, blocks_ref[0 : len(rests) * LANES, :])
+
+
+def late_kernel(factor_ref, early_ref, *refs):
+    out_ref, blocks_ref, made_ref, sems = refs[-4:]
+    rests = refs[:-4]
+    count, rows = early_ref.shape[:2]
+    band = lax.axis_index("band")
+
+    def put(source, j):
         start = pl.multiple_of(lax.rem(band + j, count) * rows, rows)
-        copies.append(
-            pltpu.make_async_copy(made_ref.at[j], out_ref.at[pl.ds(start, rows), :], sems.at[j])
-        )
-        copies[-1].start()
+        copy = pltpu.make_async_copy(source, out_ref.at[pl.ds(start, rows), :], sems.at[j])
+        copy.start()
+        return copy
+
+    copies = [put(early_ref.at[0], 0)]
+    factor_blocks(factor_ref, blocks_ref, range(count - len(rests), count))
+    for j in range(1, count):
+        pieces = [rest[(j - 1) * rows : j * rows, :] for rest in rests]
+        made_ref[j - 1] = early_ref[j] + both_parts(pieces, blocks_ref[...])
+        copies.append(put(made_ref.at[j - 1], j))
     for copy in copies:
         copy.wait()
 
@@ -609,20 +629,31 @@
 def output(factor, firsts, rests):
     count = len(firsts)
     rows = firsts[0].shape[0]
+    soon = (count + 1) // 2
+    early = pl.pallas_call(
+        early_kernel,
+        out_shape=jax.ShapeDtypeStruct((count, rows, LANES), F32),
+        in_specs=[VM] * (1 + count + soon),
+        out_specs=VM,
+        scratch_shapes=[pltpu.VMEM((count * LANES, 2 * LANES), BF16)],
+        compiler_params=params(16),
+        cost_estimate=cost(0, 6 << 20),
+        name="output_early",
+    )(factor, *firsts, *rests[:soon])
     return pl.pallas_call(
-        output_kernel,
+        late_kernel,
         out_shape=jax.ShapeDtypeStruct((rows * count, LANES), F32),
-        in_specs=[VM] * (1 + 2 * count),
+        in_specs=[VM] * (2 + count - soon),
         out_specs=pl.BlockSpec(memory_space=pl.ANY),
         scratch_shapes=[
-            pltpu.VMEM((count * LANES, 2 * LANES), BF16),
-            pltpu.VMEM((count, rows, LANES), F32),
+            pltpu.VMEM(((count - soon) * LANES, 2 * LANES), BF16),
+            pltpu.VMEM((count - 1, rows, LANES), F32),
             pltpu.SemaphoreType.DMA((count,)),
         ],
-        compiler_params=params(24),
-        cost_estimate=cost(0, 10 << 20),
-        name="output",
-    )(factor, *firsts, *rests)
+        compiler_params=params(16),
+        cost_estimate=cost(0, 6 << 20),
+        name="output_late",
+    )(factor, early, *rests[soon:])
 
 
 def shards(states_block, cell_matrix, cell_scale, potential, connectivity, boundary_nodes):

time: 122 us -> 121 us (level)
    pallas_call x1 -> x2, Pallas kernels: 2.18 us -> 2.45 us  [the longest x1 1.58 us: output(): pl.pallas_call(late_kernel, out_shape=jax.ShapeDtypeStruct((rows * count,...]
  transfers between devices with their start and end apart: 21 -> 21, of which waited for: 12 -> 12; matrix products, arithmetic and copies ran while one was open for 0% -> 0% of each run, Pallas kernels for 23% -> 24%
where the time goes in v8:
time: 121 us
  Pallas kernels  50.2 us (41%)
  waiting for transfers between devices  43.7 us (36%)
  starting transfers between devices  22.2 us (18%)
  local copies, waits for them, and re-layouts  4.3 us (4%)
    ppermute x10, waiting for transfers between devices, shifted(): lax.ppermute(value, axis, [(i, (i + steps) % count) for i in range(count)])  29.7 us
    pallas_call x2, Pallas kernels, apply_operator(): pl.pallas_call(far_cells_kernel, out_shape=(jax.ShapeDtypeStruct((owned,...  14.9 us
    pallas_call x1, Pallas kernels, inverse_factor(): pl.pallas_call(functools.partial(inverse_kernel, over), out_shape=jax.Sha...  13.4 us
    ppermute x10, starting transfers between devices, shifted(): lax.ppermute(value, axis, [(i, (i + steps) % count) for i in range(count)])  10.8 us
    ppermute x8, waiting for transfers between devices, paired(): return lax.ppermute(value, axis, [(i, i ^ mask) for i in range(count)])  8.99 us
    ppermute x8, starting transfers between devices, paired(): return lax.ppermute(value, axis, [(i, i ^ mask) for i in range(count)])  7.58 us
    pallas_call x2, Pallas kernels, apply_operator(): pl.pallas_call(functools.partial(near_sums_kernel, npc), out_shape=jax.Sh...  7.5 us
    pallas_call x2, Pallas kernels, apply_operator(): pl.pallas_call(near_products_kernel, out_shape=jax.ShapeDtypeStruct(held,...  7.11 us
  transfers between devices with their start and end apart: 21, of which 12 were waited for; matrix products, arithmetic and copies ran while one was open for 0% of the time, Pallas kernels for 24%

profile of v8, /device:TPU:26, one launch (start us, length us, event | category | flops | bytes accessed | tf_op | source)
XLA Modules:
  0.0 121.1 jit_solution(8383841078631218953)
XLA Ops:
  0.0 1.2 copy-done.2
  2.6 1.0 prepare.1
  3.7 0.9 copy-done
  5.3 3.6 %near_products.2.products_ref = f32[8,344,128]{2,1,0:T(8,128)S(1)} custom-call(s32[4096]{0:T(1024)S(1)} %bitcast.2, f32[16]{0:T(128)S(1)} %copy-done.8, f32[3744,128]{1,0:T(8,128)S(1)} %get-tuple-element.38.ext_ref.wide_ref, bf16[343,343]{1,0:T(8,128)(2,1)S(1)} %copy-done), custom_call_target="tpu_custom_call" | custom-call | bytes 14680064 | tf_op jit(solution)/shard_map/near_products/pallas_call | solution.py:194
  8.9 7.5 %far_cells.2 = (f32[3456,128]{1,0:T(8,128)S(1)}, bf16[288,128]{1,0:T(8,128)(2,1)S(1)}) custom-call(s32[4096]{0:T(1024)S(1)} %bitcast.3, f32[16]{0:T(128)S(1)} %copy-done.8, f32[3744,128]{1,0:T(8,128)S(1)} %get-tuple-element.38.ext_ref.wide_ref, bf16[288,128]{1,0:T(8,128)(2,1)S(1)} %collective-permute-done.ghost_ref, bf16[343,343]{1,0:T(8,128)(2,1)S(1)} %copy-done.1, ...), custom_call_target="tpu_custom_call" | custom-call | bytes 29360128 | tf_op jit(solution)/shard_map/far_cells/pallas_call | solution.py:205
  16.9 3.8 %near_sums.2.sums_ref = f32[3456,128]{1,0:T(8,128)S(1)} custom-call(s32[4096]{0:T(1024)S(1)} %bitcast.4, f32[8,344,128]{2,1,0:T(8,128)S(1)} %near_products.2.products_ref, f32[3456,128]{1,0:T(8,128)S(1)} %get-tuple-element.41.start_ref), custom_call_target="tpu_custom_call" | custom-call | bytes 14680064 | tf_op jit(solution)/shard_map/near_sums/pallas_call | solution.py:221
  20.7 1.5 %first_term.1 = (f32[3456,128]{1,0:T(8,128)S(1)}, f32[3744,128]{1,0:T(8,128)S(1)}, bf16[288,128]{1,0:T(8,128)(2,1)S(1)}) custom-call(s32[288]{0:T(512)S(1)} %copy-done.7, f32[3456,128]{1,0:T(8,128)S(1)} %near_sums.2.sums_ref, bf16[288,128]{1,0:T(8,128)(2,1)S(1)} %collective-permute-done.1.back_ref), custom_call_target="tpu_custom_call" | custom-call | bytes 8388608 | tf_op jit(solution)/shard_map/first_term/pallas_call | solution.py:260
  22.2 1.3 %collective-permute-start.2 = (bf16[288,128]{1,0:T(8,128)(2,1)S(1)}, bf16[288,128]{1,0:T(8,128)(2,1)S(1)}, u32[]{:S(2)}, u32[]{:S(2)}) collective-permute-start(bf16[288,128]{1,0:T(8,128)(2,1)S(1)} %get-tuple-element.43), channel_id=1, source_target_pairs={{0,28},{4,0},{8,4},{12,8},{16,12},{20,16},{24,20},{28,24},{1,29},{... | collective-permute-start | bytes 221192 | tf_op jit(solution)/shard_map/ppermute | solution.py:30
  23.5 3.6 %near_products.3.products_ref = f32[8,344,128]{2,1,0:T(8,128)S(1)} custom-call(s32[4096]{0:T(1024)S(1)} %bitcast.5, f32[16]{0:T(128)S(1)} %copy-done.9, f32[3744,128]{1,0:T(8,128)S(1)} %get-tuple-element.44.ext_ref, bf16[343,343]{1,0:T(8,128)(2,1)S(1)} %copy-done.1), custom_call_target="tpu_custom_call" | custom-call | bytes 14680064 | tf_op jit(solution)/shard_map/near_products/pallas_call | solution.py:194
  27.1 7.5 %far_cells.3 = (f32[3456,128]{1,0:T(8,128)S(1)}, bf16[288,128]{1,0:T(8,128)(2,1)S(1)}) custom-call(s32[4096]{0:T(1024)S(1)} %bitcast.6, f32[16]{0:T(128)S(1)} %copy-done.9, f32[3744,128]{1,0:T(8,128)S(1)} %get-tuple-element.44.ext_ref, bf16[288,128]{1,0:T(8,128)(2,1)S(1)} %collective-permute-done.2.ghost_ref, bf16[343,343]{1,0:T(8,128)(2,1)S(1)} %copy-done.1, ...), custom_call_target="tpu_custom_call" | custom-call | bytes 29360128 | tf_op jit(solution)/shard_map/far_cells/pallas_call | solution.py:205
  34.5 2.0 %collective-permute-start.3 = (bf16[288,128]{1,0:T(8,128)(2,1)S(1)}, bf16[288,128]{1,0:T(8,128)(2,1)S(1)}, u32[]{:S(2)}, u32[]{:S(2)}) collective-permute-start(bf16[288,128]{1,0:T(8,128)(2,1)S(1)} %get-tuple-element.49), channel_id=1, source_target_pairs={{0,4},{4,8},{8,12},{12,16},{16,20},{20,24},{24,28},{28,0},{1,5},{5... | collective-permute-start | bytes 221192 | tf_op jit(solution)/shard_map/ppermute | solution.py:30
  36.6 3.7 %near_sums.3.sums_ref = f32[3456,128]{1,0:T(8,128)S(1)} custom-call(s32[4096]{0:T(1024)S(1)} %bitcast.7, f32[8,344,128]{2,1,0:T(8,128)S(1)} %near_products.3.products_ref, f32[3456,128]{1,0:T(8,128)S(1)} %get-tuple-element.48.start_ref), custom_call_target="tpu_custom_call" | custom-call | bytes 14680064 | tf_op jit(solution)/shard_map/near_sums/pallas_call | solution.py:221
  40.3 1.4 %second_term.1 = (bf16[864,128]{1,0:T(8,128)(2,1)S(1)}, bf16[864,128]{1,0:T(8,128)(2,1)S(1)}, bf16[864,128]{1,0:T(8,128)(2,1)S(1)}, bf16[864,128]{1,0:T(8,128)(2,1)S(1)}, bf16[2592,128]{1,0:T(8,128)(2,1)S(1)}) custom-call(s32[288]{0:T(512)S(1)} %copy-done.7, f32[3456,128]{1,0:T(8,128)S(1)} %near_sums.3.sums_ref, ...), custom_call_target="tpu_custom_call" | custom-call | bytes 6291456 | tf_op jit(solution)/shard_map/second_term/pallas_call | solution.py:293
  41.9 1.7 %collective-permute-start.5 = (bf16[864,128]{1,0:T(8,128)(2,1)S(1)}, bf16[864,128]{1,0:T(8,128)(2,1)S(1)}, u32[]{:S(2)}, u32[]{:S(2)}) collective-permute-start(bf16[864,128]{1,0:T(8,128)(2,1)S(1)} %get-tuple-element.52), channel_id=1, source_target_pairs={{0,2},{1,3},{2,0},{3,1},{4,6},{5,7},{6,4},{7,5},{8,10},{9,11},{10,... | collective-permute-start | bytes 663560 | tf_op jit(solution)/shard_map/ppermute | solution.py:30
  44.1 5.4 %collective-permute-done.4.refs_1_ = bf16[864,128]{1,0:T(8,128)(2,1)S(1)} collective-permute-done((bf16[864,128]{1,0:T(8,128)(2,1)S(1)}, bf16[864,128]{1,0:T(8,128)(2,1)S(1)}, u32[]{:S(2)}, u32[]{:S(2)}) %collective-permute-start.4) | collective-permute-done | bytes 221216 | tf_op jit(solution)/shard_map/ppermute | solution.py:30
  49.5 14.1 %collective-permute-done.5.refs_2_ = bf16[864,128]{1,0:T(8,128)(2,1)S(1)} collective-permute-done((bf16[864,128]{1,0:T(8,128)(2,1)S(1)}, bf16[864,128]{1,0:T(8,128)(2,1)S(1)}, u32[]{:S(2)}, u32[]{:S(2)}) %collective-permute-start.5) | collective-permute-done | bytes 221216 | tf_op jit(solution)/shard_map/ppermute | solution.py:30
  65.0 1.3 %collective-permute-start.12 = (bf16[2592,128]{1,0:T(8,128)(2,1)S(1)}, bf16[2592,128]{1,0:T(8,128)(2,1)S(1)}, u32[]{:S(2)}, u32[]{:S(2)}) collective-permute-start(bf16[2592,128]{1,0:T(8,128)(2,1)S(1)} %pad_maximum_fusion), channel_id=1, source_target_pairs={{0,1},{1,2},{2,3},{4,5},{5,6},{6,7},{8,9},{9,10},{10,11},{12,13},{... | collective-permute-start | bytes 1990664 | tf_op jit(solution)/shard_map/ppermute | solution.py:396
  68.0 1.9 %collective-permute-start.8 = (f32[160,128]{1,0:T(8,128)S(1)}, f32[160,128]{1,0:T(8,128)S(1)}, u32[]{:S(2)}, u32[]{:S(2)}) collective-permute-start(f32[160,128]{1,0:T(8,128)S(1)} %get-tuple-element.61), channel_id=1, source_target_pairs={{0,8},{4,12},{8,0},{12,4},{16,24},{20,28},{24,16},{28,20},{1,9},{5... | collective-permute-start | bytes 245768 | tf_op jit(solution)/shard_map/ppermute | solution.py:389
  69.9 2.6 %collective-permute-done.10 = f32[160,128]{1,0:T(8,128)S(1)} collective-permute-done((f32[160,128]{1,0:T(8,128)S(1)}, f32[160,128]{1,0:T(8,128)S(1)}, u32[]{:S(2)}, u32[]{:S(2)}) %collective-permute-start.10) | collective-permute-done | bytes 81952 | tf_op jit(solution)/shard_map/ppermute | solution.py:389
  73.8 3.6 %collective-permute-start.11 = (f32[160,128]{1,0:T(8,128)S(1)}, f32[160,128]{1,0:T(8,128)S(1)}, u32[]{:S(2)}, u32[]{:S(2)}) collective-permute-start(f32[160,128]{1,0:T(8,128)S(1)} %add_add_fusion.1), channel_id=1, source_target_pairs={{0,1},{1,2},{2,3},{3,0},{4,5},{5,6},{6,7},{7,4},{8,9},{9,10},{10,1... | collective-permute-start | bytes 245768 | tf_op jit(solution)/shard_map/ppermute | solution.py:30
  78.2 7.6 %collective-permute-done.11 = f32[160,128]{1,0:T(8,128)S(1)} collective-permute-done((f32[160,128]{1,0:T(8,128)S(1)}, f32[160,128]{1,0:T(8,128)S(1)}, u32[]{:S(2)}, u32[]{:S(2)}) %collective-permute-start.11) | collective-permute-done | bytes 81952 | tf_op jit(solution)/shard_map/ppermute | solution.py:30
  86.0 1.3 %collective-permute-start.19 = (bf16[2592,128]{1,0:T(8,128)(2,1)S(1)}, bf16[2592,128]{1,0:T(8,128)(2,1)S(1)}, u32[]{:S(2)}, u32[]{:S(2)}) collective-permute-start(bf16[2592,128]{1,0:T(8,128)(2,1)S(1)} %get-tuple-element.70), channel_id=1, source_target_pairs={{1,2},{2,3},{5,6},{6,7},{9,10},{10,11},{13,14},{14,15},{17,18},{18... | collective-permute-start | bytes 1990664 | tf_op jit(solution)/shard_map/ppermute | solution.py:396
  87.3 1.3 %collective-permute-start.20 = (bf16[2592,128]{1,0:T(8,128)(2,1)S(1)}, bf16[2592,128]{1,0:T(8,128)(2,1)S(1)}, u32[]{:S(2)}, u32[]{:S(2)}) collective-permute-start(bf16[2592,128]{1,0:T(8,128)(2,1)S(1)} %get-tuple-element.69), channel_id=1, source_target_pairs={{1,3},{5,7},{9,11},{13,15},{17,19},{21,23},{25,27},{29,31}} | collective-permute-start | bytes 1990664 | tf_op jit(solution)/shard_map/ppermute | solution.py:422
  89.2 2.0 %collective-permute-done.13 = f32[160,128]{1,0:T(8,128)S(1)} collective-permute-done((f32[160,128]{1,0:T(8,128)S(1)}, f32[160,128]{1,0:T(8,128)S(1)}, u32[]{:S(2)}, u32[]{:S(2)}) %collective-permute-start.13) | collective-permute-done | bytes 81952 | tf_op jit(solution)/shard_map/ppermute | solution.py:30
  91.3 1.6 %collective-permute-start.16 = (f32[160,128]{1,0:T(8,128)S(1)}, f32[160,128]{1,0:T(8,128)S(1)}, u32[]{:S(2)}, u32[]{:S(2)}) collective-permute-start(f32[160,128]{1,0:T(8,128)S(1)} %add_add_fusion.refs_0_), channel_id=1, source_target_pairs={{0,16},{4,20},{8,24},{12,28},{16,0},{20,4},{24,8},{28,12},{1,17},{... | collective-permute-start | bytes 245768 | tf_op jit(solution)/shard_map/ppermute | solution.py:389
  92.9 1.9 %collective-permute-start.17 = (f32[160,128]{1,0:T(8,128)S(1)}, f32[160,128]{1,0:T(8,128)S(1)}, u32[]{:S(2)}, u32[]{:S(2)}) collective-permute-start(f32[160,128]{1,0:T(8,128)S(1)} %add_add_fusion.refs_0_), channel_id=1, source_target_pairs={{0,24},{4,28},{8,16},{12,20},{16,8},{20,12},{24,0},{28,4},{1,25},{... | collective-permute-start | bytes 245768 | tf_op jit(solution)/shard_map/ppermute | solution.py:389
  94.8 1.7 %collective-permute-done.15.refs_1_ = f32[160,128]{1,0:T(8,128)S(1)} collective-permute-done((f32[160,128]{1,0:T(8,128)S(1)}, f32[160,128]{1,0:T(8,128)S(1)}, u32[]{:S(2)}, u32[]{:S(2)}) %collective-permute-start.15) | collective-permute-done | bytes 81952 | tf_op jit(solution)/shard_map/ppermute | solution.py:389
  96.4 1.8 %collective-permute-done.17.refs_3_ = f32[160,128]{1,0:T(8,128)S(1)} collective-permute-done((f32[160,128]{1,0:T(8,128)S(1)}, f32[160,128]{1,0:T(8,128)S(1)}, u32[]{:S(2)}, u32[]{:S(2)}) %collective-permute-start.17) | collective-permute-done | bytes 81952 | tf_op jit(solution)/shard_map/ppermute | solution.py:389
  98.4 1.6 %collective-permute-done.18.other_ref = f32[640,128]{1,0:T(8,128)S(1)} collective-permute-done((f32[640,128]{1,0:T(8,128)S(1)}, f32[640,128]{1,0:T(8,128)S(1)}, u32[]{:S(2)}, u32[]{:S(2)}) %collective-permute-start.18) | collective-permute-done | bytes 327712 | tf_op jit(solution)/shard_map/ppermute | solution.py:389
  100.0 13.4 %inverse_factor.1.factor_ref = f32[512,512]{1,0:T(8,128)S(1)} custom-call(f32[640,128]{1,0:T(8,128)S(1)} %joined.1.mine_ref, f32[640,128]{1,0:T(8,128)S(1)} %collective-permute-done.18.other_ref), custom_call_target="tpu_custom_call" | custom-call | bytes 73400320 | tf_op jit(solution)/shard_map/inverse_factor/pallas_call | solution.py:562
  114.3 5.0 %collective-permute-done.20.refs_1_ = bf16[2592,128]{1,0:T(8,128)(2,1)S(1)} collective-permute-done((bf16[2592,128]{1,0:T(8,128)(2,1)S(1)}, bf16[2592,128]{1,0:T(8,128)(2,1)S(1)}, u32[]{:S(2)}, u32[]{:S(2)}) %collective-permute-start.20) | collective-permute-done | bytes 663584 | tf_op jit(solution)/shard_map/ppermute | solution.py:422
  119.3 1.6 %output_late.1 = f32[3456,128]{1,0:T(8,128)} custom-call(f32[512,512]{1,0:T(8,128)S(1)} %inverse_factor.1.factor_ref, f32[4,864,128]{2,1,0:T(8,128)S(1)} %output_early.1.early_ref, bf16[2592,128]{1,0:T(8,128)(2,1)S(1)} %collective-permute-done.19.refs_0_, bf16[2592,128]{1,0:T(8,128)(2,1)S(1)} %collective-permute-done.20.refs_1_), custom_call_target="tpu_custom_call" | custom-call | bytes 6291456 | tf_op jit(solution)/shard_map/output_late/pallas_call | solution.py:643
  (52 shorter events, 10.4 us)
Async XLA Ops:
  0.0 1.2 copy-start.2
  1.2 0.7 copy-start.5
  1.9 0.7 copy-start.6
  3.6 5.2 %collective-permute-start = (bf16[288,128]{1,0:T(8,128)(2,1)S(1)}, bf16[288,128]{1,0:T(8,128)(2,1)S(1)}, u32[]{:S(2)}, u32[]{:S(2)}) collective-permute-start(bf16[288,128]{1,0:T(8,128)(2,1)S(1)} %get-tuple-element.37), channel_id=1, source_target_pairs={{0,28},{4,0},{8,4},{12,8},{16,12},{20,16},{24,20},{28,24},{1,29},{... | collective-permute-start | bytes 221192 | tf_op jit(solution)/shard_map/ppermute | solution.py:30
  3.6 1.0 copy-start
  4.6 0.7 copy-start.8
  5.3 3.6 %copy-start.1 = (bf16[343,343]{1,0:T(8,128)(2,1)S(1)}, bf16[343,343]{1,0:T(8,128)(2,1)}, u32[]{:S(2)}) copy-start(bf16[343,343]{1,0:T(8,128)(2,1)} %matrix_ref.7) | copy-start | bytes 705898
  5.3 3.6 %copy-start.4 = (f32[3456]{0:T(1024)S(1)}, f32[3456]{0:T(1024)}, u32[]{:S(2)}) copy-start(f32[3456]{0:T(1024)} %param.9) | copy-start | bytes 41476
  16.3 4.4 %collective-permute-start.1 = (bf16[288,128]{1,0:T(8,128)(2,1)S(1)}, bf16[288,128]{1,0:T(8,128)(2,1)S(1)}, u32[]{:S(2)}, u32[]{:S(2)}) collective-permute-start(bf16[288,128]{1,0:T(8,128)(2,1)S(1)} %get-tuple-element.42), channel_id=1, source_target_pairs={{0,4},{4,8},{8,12},{12,16},{16,20},{20,24},{24,28},{28,0},{1,5},{5... | collective-permute-start | bytes 221192 | tf_op jit(solution)/shard_map/ppermute | solution.py:30
  16.9 3.8 %copy-start.7 = (s32[288]{0:T(512)S(1)}, s32[288]{0:T(512)}, u32[]{:S(2)}) copy-start(s32[288]{0:T(512)} %nodes.5) | copy-start | bytes 3460
  20.7 2.8 %copy-start.9 = (f32[16]{0:T(128)S(1)}, f32[16]{0:T(128)}, u32[]{:S(2)}) copy-start(f32[16]{0:T(128)} %scale.7) | copy-start | bytes 196
  22.2 4.9 %collective-permute-start.2 = (bf16[288,128]{1,0:T(8,128)(2,1)S(1)}, bf16[288,128]{1,0:T(8,128)(2,1)S(1)}, u32[]{:S(2)}, u32[]{:S(2)}) collective-permute-start(bf16[288,128]{1,0:T(8,128)(2,1)S(1)} %get-tuple-element.43), channel_id=1, source_target_pairs={{0,28},{4,0},{8,4},{12,8},{16,12},{20,16},{24,20},{28,24},{1,29},{... | collective-permute-start | bytes 221192 | tf_op jit(solution)/shard_map/ppermute | solution.py:30
  34.5 5.8 %collective-permute-start.3 = (bf16[288,128]{1,0:T(8,128)(2,1)S(1)}, bf16[288,128]{1,0:T(8,128)(2,1)S(1)}, u32[]{:S(2)}, u32[]{:S(2)}) collective-permute-start(bf16[288,128]{1,0:T(8,128)(2,1)S(1)} %get-tuple-element.49), channel_id=1, source_target_pairs={{0,4},{4,8},{8,12},{12,16},{16,20},{20,24},{24,28},{28,0},{1,5},{5... | collective-permute-start | bytes 221192 | tf_op jit(solution)/shard_map/ppermute | solution.py:30
  36.6 3.7 %copy-start.3 = (bf16[3456,128]{1,0:T(8,128)(2,1)S(1)}, bf16[3456,128]{1,0:T(8,128)(2,1)}, u32[]{:S(2)}) copy-start(bf16[3456,128]{1,0:T(8,128)(2,1)} %previous_ref.1) | copy-start | bytes 2654212
  41.7 7.8 %collective-permute-start.4 = (bf16[864,128]{1,0:T(8,128)(2,1)S(1)}, bf16[864,128]{1,0:T(8,128)(2,1)S(1)}, u32[]{:S(2)}, u32[]{:S(2)}) collective-permute-start(bf16[864,128]{1,0:T(8,128)(2,1)S(1)} %get-tuple-element.51), channel_id=1, source_target_pairs={{0,1},{1,2},{2,3},{3,0},{4,5},{5,6},{6,7},{7,4},{8,9},{9,10},{10,1... | collective-permute-start | bytes 663560 | tf_op jit(solution)/shard_map/ppermute | solution.py:30
  41.9 21.7 %collective-permute-start.5 = (bf16[864,128]{1,0:T(8,128)(2,1)S(1)}, bf16[864,128]{1,0:T(8,128)(2,1)S(1)}, u32[]{:S(2)}, u32[]{:S(2)}) collective-permute-start(bf16[864,128]{1,0:T(8,128)(2,1)S(1)} %get-tuple-element.52), channel_id=1, source_target_pairs={{0,2},{1,3},{2,0},{3,1},{4,6},{5,7},{6,4},{7,5},{8,10},{9,11},{10,... | collective-permute-start | bytes 663560 | tf_op jit(solution)/shard_map/ppermute | solution.py:30
  43.6 20.0 %collective-permute-start.6 = (bf16[864,128]{1,0:T(8,128)(2,1)S(1)}, bf16[864,128]{1,0:T(8,128)(2,1)S(1)}, u32[]{:S(2)}, u32[]{:S(2)}) collective-permute-start(bf16[864,128]{1,0:T(8,128)(2,1)S(1)} %get-tuple-element.53), channel_id=1, source_target_pairs={{0,3},{1,0},{2,1},{3,2},{4,7},{5,4},{6,5},{7,6},{8,11},{9,8},{10,9... | collective-permute-start | bytes 663560 | tf_op jit(solution)/shard_map/ppermute | solution.py:30
  64.5 1.8 %collective-permute-start.7 = (f32[640,128]{1,0:T(8,128)S(1)}, f32[640,128]{1,0:T(8,128)S(1)}, u32[]{:S(2)}, u32[]{:S(2)}) collective-permute-start(f32[640,128]{1,0:T(8,128)S(1)} %get-tuple-element.59), channel_id=1, source_target_pairs={{0,4},{4,0},{8,12},{12,8},{16,20},{20,16},{24,28},{28,24},{1,5},{5... | collective-permute-start | bytes 983048 | tf_op jit(solution)/shard_map/ppermute | solution.py:389
  65.0 20.9 %collective-permute-start.12 = (bf16[2592,128]{1,0:T(8,128)(2,1)S(1)}, bf16[2592,128]{1,0:T(8,128)(2,1)S(1)}, u32[]{:S(2)}, u32[]{:S(2)}) collective-permute-start(bf16[2592,128]{1,0:T(8,128)(2,1)S(1)} %pad_maximum_fusion), channel_id=1, source_target_pairs={{0,1},{1,2},{2,3},{4,5},{5,6},{6,7},{8,9},{9,10},{10,11},{12,13},{... | collective-permute-start | bytes 1990664 | tf_op jit(solution)/shard_map/ppermute | solution.py:396
  66.3 6.2 %collective-permute-start.10 = (f32[160,128]{1,0:T(8,128)S(1)}, f32[160,128]{1,0:T(8,128)S(1)}, u32[]{:S(2)}, u32[]{:S(2)}) collective-permute-start(f32[160,128]{1,0:T(8,128)S(1)} %get-tuple-element.63), channel_id=1, source_target_pairs={{0,24},{4,28},{8,16},{12,20},{16,8},{20,12},{24,0},{28,4},{1,25},{... | collective-permute-start | bytes 245768 | tf_op jit(solution)/shard_map/ppermute | solution.py:389
  67.2 6.1 %collective-permute-start.9 = (f32[160,128]{1,0:T(8,128)S(1)}, f32[160,128]{1,0:T(8,128)S(1)}, u32[]{:S(2)}, u32[]{:S(2)}) collective-permute-start(f32[160,128]{1,0:T(8,128)S(1)} %get-tuple-element.62), channel_id=1, source_target_pairs={{0,16},{4,20},{8,24},{12,28},{16,0},{20,4},{24,8},{28,12},{1,17},{... | collective-permute-start | bytes 245768 | tf_op jit(solution)/shard_map/ppermute | solution.py:389
  68.0 5.8 %collective-permute-start.8 = (f32[160,128]{1,0:T(8,128)S(1)}, f32[160,128]{1,0:T(8,128)S(1)}, u32[]{:S(2)}, u32[]{:S(2)}) collective-permute-start(f32[160,128]{1,0:T(8,128)S(1)} %get-tuple-element.61), channel_id=1, source_target_pairs={{0,8},{4,12},{8,0},{12,4},{16,24},{20,28},{24,16},{28,20},{1,9},{5... | collective-permute-start | bytes 245768 | tf_op jit(solution)/shard_map/ppermute | solution.py:389
  73.8 12.0 %collective-permute-start.11 = (f32[160,128]{1,0:T(8,128)S(1)}, f32[160,128]{1,0:T(8,128)S(1)}, u32[]{:S(2)}, u32[]{:S(2)}) collective-permute-start(f32[160,128]{1,0:T(8,128)S(1)} %add_add_fusion.1), channel_id=1, source_target_pairs={{0,1},{1,2},{2,3},{3,0},{4,5},{5,6},{6,7},{7,4},{8,9},{9,10},{10,1... | collective-permute-start | bytes 245768 | tf_op jit(solution)/shard_map/ppermute | solution.py:30
  77.4 11.8 %collective-permute-start.14 = (f32[160,128]{1,0:T(8,128)S(1)}, f32[160,128]{1,0:T(8,128)S(1)}, u32[]{:S(2)}, u32[]{:S(2)}) collective-permute-start(f32[160,128]{1,0:T(8,128)S(1)} %add_add_fusion.1), channel_id=1, source_target_pairs={{0,3},{1,0},{2,1},{3,2},{4,7},{5,4},{6,5},{7,6},{8,11},{9,8},{10,9... | collective-permute-start | bytes 245768 | tf_op jit(solution)/shard_map/ppermute | solution.py:30
  77.4 13.8 %collective-permute-start.13 = (f32[160,128]{1,0:T(8,128)S(1)}, f32[160,128]{1,0:T(8,128)S(1)}, u32[]{:S(2)}, u32[]{:S(2)}) collective-permute-start(f32[160,128]{1,0:T(8,128)S(1)} %add_add_fusion.1), channel_id=1, source_target_pairs={{0,2},{1,3},{2,0},{3,1},{4,6},{5,7},{6,4},{7,5},{8,10},{9,11},{10,... | collective-permute-start | bytes 245768 | tf_op jit(solution)/shard_map/ppermute | solution.py:30
  86.0 28.3 %collective-permute-start.19 = (bf16[2592,128]{1,0:T(8,128)(2,1)S(1)}, bf16[2592,128]{1,0:T(8,128)(2,1)S(1)}, u32[]{:S(2)}, u32[]{:S(2)}) collective-permute-start(bf16[2592,128]{1,0:T(8,128)(2,1)S(1)} %get-tuple-element.70), channel_id=1, source_target_pairs={{1,2},{2,3},{5,6},{6,7},{9,10},{10,11},{13,14},{14,15},{17,18},{18... | collective-permute-start | bytes 1990664 | tf_op jit(solution)/shard_map/ppermute | solution.py:396
  87.3 32.0 %collective-permute-start.20 = (bf16[2592,128]{1,0:T(8,128)(2,1)S(1)}, bf16[2592,128]{1,0:T(8,128)(2,1)S(1)}, u32[]{:S(2)}, u32[]{:S(2)}) collective-permute-start(bf16[2592,128]{1,0:T(8,128)(2,1)S(1)} %get-tuple-element.69), channel_id=1, source_target_pairs={{1,3},{5,7},{9,11},{13,15},{17,19},{21,23},{25,27},{29,31}} | collective-permute-start | bytes 1990664 | tf_op jit(solution)/shard_map/ppermute | solution.py:422
  91.2 5.2 %collective-permute-start.15 = (f32[160,128]{1,0:T(8,128)S(1)}, f32[160,128]{1,0:T(8,128)S(1)}, u32[]{:S(2)}, u32[]{:S(2)}) collective-permute-start(f32[160,128]{1,0:T(8,128)S(1)} %add_add_fusion.refs_0_), channel_id=1, source_target_pairs={{0,8},{4,12},{8,0},{12,4},{16,24},{20,28},{24,16},{28,20},{1,9},{5... | collective-permute-start | bytes 245768 | tf_op jit(solution)/shard_map/ppermute | solution.py:389
  91.3 5.1 %collective-permute-start.16 = (f32[160,128]{1,0:T(8,128)S(1)}, f32[160,128]{1,0:T(8,128)S(1)}, u32[]{:S(2)}, u32[]{:S(2)}) collective-permute-start(f32[160,128]{1,0:T(8,128)S(1)} %add_add_fusion.refs_0_), channel_id=1, source_target_pairs={{0,16},{4,20},{8,24},{12,28},{16,0},{20,4},{24,8},{28,12},{1,17},{... | collective-permute-start | bytes 245768 | tf_op jit(solution)/shard_map/ppermute | solution.py:389
  92.9 5.4 %collective-permute-start.17 = (f32[160,128]{1,0:T(8,128)S(1)}, f32[160,128]{1,0:T(8,128)S(1)}, u32[]{:S(2)}, u32[]{:S(2)}) collective-permute-start(f32[160,128]{1,0:T(8,128)S(1)} %add_add_fusion.refs_0_), channel_id=1, source_target_pairs={{0,24},{4,28},{8,16},{12,20},{16,8},{20,12},{24,0},{28,4},{1,25},{... | collective-permute-start | bytes 245768 | tf_op jit(solution)/shard_map/ppermute | solution.py:389
  98.3 1.7 %collective-permute-start.18 = (f32[640,128]{1,0:T(8,128)S(1)}, f32[640,128]{1,0:T(8,128)S(1)}, u32[]{:S(2)}, u32[]{:S(2)}) collective-permute-start(f32[640,128]{1,0:T(8,128)S(1)} %joined.1.mine_ref), channel_id=1, source_target_pairs={{0,4},{4,0},{8,12},{12,8},{16,20},{20,16},{24,28},{28,24},{1,5},{5... | collective-permute-start | bytes 983048 | tf_op jit(solution)/shard_map/ppermute | solution.py:389

commit v9 on v8

--- a/solution.py
+++ b/solution.py
@@ -113,7 +113,7 @@
     lax.fori_loop(0, gathered.shape[0], cell, 0)
 
 
-def multiply_cells(scale, matrix_ref, gathered, products, first):
+def multiply_cells(matrix_ref, gathered, products):
     cells, npc = gathered.shape[0], matrix_ref.shape[0]
     for c in range(0, cells, 2):
         both = jnp.concatenate(
@@ -121,19 +121,18 @@
         )
         made = jnp.dot(matrix_ref[...], both, preferred_element_type=F32)
         for half in range(2):
-            products[c + half, 0:npc, :] = (
-                made[:, half * LANES : (half + 1) * LANES] * scale[first + c + half]
-            )
-
-
-def scatter_cells(words, cells, npc, products, sums, first):
+            products[c + half, 0:npc, :] = made[:, half * LANES : (half + 1) * LANES]
+
+
+def scatter_cells(words, scale, cells, npc, products, sums, first):
     def cell(c, _):
         seen = []
+        factor = jnp.full((1, LANES), scale[first + c], F32)
 
         def visit(r, row):
             total = sums[len(seen) % len(sums)]
             seen.append(r)
-            total[row, :] = total[row, :] + products[c, r : r + 1, :]
+            total[row, :] = total[row, :] + factor * products[c, r : r + 1, :]
 
         each_row(words, cells, npc, first + c, visit)
         return 0
@@ -141,9 +140,9 @@
     lax.fori_loop(0, products.shape[0], cell, 0)
 
 
-def near_products_kernel(words, scale, ext_ref, matrix_ref, out_ref, gathered):
+def near_products_kernel(words, ext_ref, matrix_ref, out_ref, gathered):
     gather_cells(words, 2 * gathered.shape[0], matrix_ref.shape[0], ext_ref, gathered, 0)
-    multiply_cells(scale, matrix_ref, gathered, out_ref, 0)
+    multiply_cells(matrix_ref, gathered, out_ref)
 
 
 def far_cells_kernel(
@@ -164,21 +163,26 @@
         total[...] = jnp.zeros_like(total)
     copy.wait()
     gather_cells(words, 2 * half, npc, ext, gathered, half)
-    multiply_cells(scale, matrix_ref, gathered, products, half)
-    scatter_cells(words, 2 * half, npc, products, sums, half)
+    multiply_cells(matrix_ref, gathered, products)
+    scatter_cells(words, scale, 2 * half, npc, products, sums, half)
     back_ref[...] = sum(total[owned:, :] for total in sums).astype(BF16)
     out_ref[...] = sum(total[0:owned, :] for total in sums)
 
 
-def near_sums_kernel(npc, words_ref, products_ref, start_ref, out_ref, words, sem, *sums):
+def near_sums_kernel(
+    npc, words_ref, scale_ref, products_ref, start_ref, out_ref, words, sem, scale, scale_sem, *sums
+):
     copy = pltpu.make_async_copy(words_ref, words, sem)
     copy.start()
+    scale_copy = pltpu.make_async_copy(scale_ref, scale, scale_sem)
+    scale_copy.start()
     sums = (out_ref,) + sums
     out_ref[...] = start_ref[...]
     for total in sums[1:]:
         total[...] = jnp.zeros_like(total)
     copy.wait()
-    scatter_cells(words, 2 * products_ref.shape[0], npc, products_ref, sums, 0)
+    scale_copy.wait()
+    scatter_cells(words, scale, 2 * products_ref.shape[0], npc, products_ref, sums, 0)
     out_ref[...] = sum(total[...] for total in sums)
 
 
@@ -194,13 +198,13 @@
     products = pl.pallas_call(
         near_products_kernel,
         out_shape=jax.ShapeDtypeStruct(held, F32),
-        in_specs=[SM, SM, VM, VM],
+        in_specs=[SM, VM, VM],
         out_specs=VM,
         scratch_shapes=[pltpu.VMEM(held, F32)],
         compiler_params=params(16),
         cost_estimate=cost(0, 14 << 20),
         name="near_products",
-    )(links, scale, ext, matrix)
+    )(links, ext, matrix)
     ghost, products = ordered(ghost, products)
     sums, back = pl.pallas_call(
         far_cells_kernel,
@@ -221,13 +225,15 @@
     sums = pl.pallas_call(
         functools.partial(near_sums_kernel, npc),
         out_shape=jax.ShapeDtypeStruct((owned, LANES), F32),
-        in_specs=[VM] * 3,
+        in_specs=[VM] * 4,
         out_specs=VM,
-        scratch_shapes=index + [pltpu.VMEM((owned, LANES), F32)] * (CHAINS - 1),
+        scratch_shapes=index
+        + [pltpu.SMEM(scale.shape, F32), pltpu.SemaphoreType.DMA]
+        + [pltpu.VMEM((owned, LANES), F32)] * (CHAINS - 1),
         compiler_params=params(16),
         cost_estimate=cost(0, 14 << 20),
         name="near_sums",
-    )(links, products, sums)
+    )(links, scale, products, sums)
     return sums, back
 
 
@@ -394,6 +400,11 @@
     count = lax.axis_size("band")
     onward = jnp.concatenate([rests[held][rows:], firsts[held]])
     return lax.ppermute(onward, "band", [(i, i + 1) for i in range(held, count - 1)])
+
+
+def passed_up_last(rows):
+    count = lax.axis_size("band")
+    return lax.ppermute(rows, "band", [(count - 2, count - 1)])
 
 
 def ordered(*values):
@@ -418,8 +429,9 @@
     parts[1], rests[1] = ordered(parts[1], rests[1])
     rests.append(passed_up(rests, firsts, 1))
     rows = firsts[1].shape[0]
-    skipping = jnp.concatenate([rests[1][2 * rows :], firsts[1], rests[1][:rows]])
-    rests.append(lax.ppermute(skipping, "band", [(1, 3)]))
+    skipping = jnp.concatenate([rests[1][2 * rows :], firsts[1]])
+    relayed = ordered(parts[1], firsts[2])[1]
+    rests.append((lax.ppermute(skipping, "band", [(1, 3)]), passed_up_last(relayed)))
     total = sum(parts[1:], parts[0])
     half = joined([total] + [paired(total, "domain", 2 * m) for m in (1, 2, 3)])
     return half, paired(half, "domain", 1)
@@ -604,10 +616,18 @@
         made_ref[j] = both_parts(pieces, blocks_ref[0 : len(rests) * LANES, :])
 
 
-def late_kernel(factor_ref, early_ref, *refs):
+def late_kernel(shape, factor_ref, early_ref, *refs):
     out_ref, blocks_ref, made_ref, sems = refs[-4:]
-    rests = refs[:-4]
+    others = list(refs[:-4])
     count, rows = early_ref.shape[:2]
+    rests = [
+        [
+            ref.at[k : k + rows, :]
+            for ref in [others.pop(0) for _ in range(size)]
+            for k in range(0, ref.shape[0], rows)
+        ]
+        for size in shape
+    ]
     band = lax.axis_index("band")
 
     def put(source, j):
@@ -619,7 +639,7 @@
     copies = [put(early_ref.at[0], 0)]
     factor_blocks(factor_ref, blocks_ref, range(count - len(rests), count))
     for j in range(1, count):
-        pieces = [rest[(j - 1) * rows : j * rows, :] for rest in rests]
+        pieces = [rest[j - 1][...] for rest in rests]
         made_ref[j - 1] = early_ref[j] + both_parts(pieces, blocks_ref[...])
         copies.append(put(made_ref.at[j - 1], j))
     for copy in copies:
@@ -640,10 +660,12 @@
         cost_estimate=cost(0, 6 << 20),
         name="output_early",
     )(factor, *firsts, *rests[:soon])
+    late = [rest if isinstance(rest, tuple) else (rest,) for rest in rests[soon:]]
+    flat = [part for rest in late for part in rest]
     return pl.pallas_call(
-        late_kernel,
+        functools.partial(late_kernel, [len(rest) for rest in late]),
         out_shape=jax.ShapeDtypeStruct((rows * count, LANES), F32),
-        in_specs=[VM] * (2 + count - soon),
+        in_specs=[VM] * (2 + len(flat)),
         out_specs=pl.BlockSpec(memory_space=pl.ANY),
         scratch_shapes=[
             pltpu.VMEM(((count - soon) * LANES, 2 * LANES), BF16),
@@ -653,7 +675,7 @@
         compiler_params=params(16),
         cost_estimate=cost(0, 6 << 20),
         name="output_late",
-    )(factor, early, *rests[soon:])
+    )(factor, early, *flat)
 
 
 def shards(states_block, cell_matrix, cell_scale, potential, connectivity, boundary_nodes):

time: 121 us -> 120 us (level)
  waiting for transfers between devices: 43.7 us -> 41.6 us
  starting transfers between devices: 22.2 us -> 23.5 us
    ppermute x8, waiting for transfers between devices: 8.99 us -> 7.69 us  [paired(): return lax.ppermute(value, axis, [(i, i ^ mask) for i in range(count)])]
    ppermute x1 -> x2, starting transfers between devices: 1.29 us -> 2.58 us  [the longest x1 1.29 us: passed_up_last(): return lax.ppermute(rows, 'band', [(count - 2, count - 1)])]
    ppermute x1 -> x2, waiting for transfers between devices: 5.01 us -> 4.18 us  [the longest x1 4.17 us: passed_up_last(): return lax.ppermute(rows, 'band', [(count - 2, count - 1)])]
    unnamed x20 -> x18, local copies, waits for them, and re-layouts: 4.21 us -> 3.55 us
  transfers between devices with their start and end apart: 21 -> 22, of which waited for: 12 -> 12; matrix products, arithmetic and copies ran while one was open for 0% -> 0% of each run, Pallas kernels for 24% -> 24%
where the time goes in v9:
time: 120 us
  Pallas kernels  50.2 us (42%)
  waiting for transfers between devices  41.6 us (35%)
  starting transfers between devices  23.5 us (20%)
  local copies, waits for them, and re-layouts  3.62 us (3%)
    ppermute x10, waiting for transfers between devices, shifted(): lax.ppermute(value, axis, [(i, (i + steps) % count) for i in range(count)])  29.7 us
    pallas_call x2, Pallas kernels, apply_operator(): pl.pallas_call(far_cells_kernel, out_shape=(jax.ShapeDtypeStruct((owned,...  14.9 us
    pallas_call x1, Pallas kernels, inverse_factor(): pl.pallas_call(functools.partial(inverse_kernel, over), out_shape=jax.Sha...  13.4 us
    ppermute x10, starting transfers between devices, shifted(): lax.ppermute(value, axis, [(i, (i + steps) % count) for i in range(count)])  10.8 us
    ppermute x8, waiting for transfers between devices, paired(): return lax.ppermute(value, axis, [(i, i ^ mask) for i in range(count)])  7.69 us
    pallas_call x2, Pallas kernels, apply_operator(): pl.pallas_call(functools.partial(near_sums_kernel, npc), out_shape=jax.Sh...  7.55 us
    ppermute x8, starting transfers between devices, paired(): return lax.ppermute(value, axis, [(i, i ^ mask) for i in range(count)])  7.55 us
    pallas_call x2, Pallas kernels, apply_operator(): pl.pallas_call(near_products_kernel, out_shape=jax.ShapeDtypeStruct(held,...  7.09 us
  transfers between devices with their start and end apart: 22, of which 12 were waited for; matrix products, arithmetic and copies ran while one was open for 0% of the time, Pallas kernels for 24%

profile of v9, /device:TPU:26, one launch (start us, length us, event | category | flops | bytes accessed | tf_op | source)
XLA Modules:
  0.0 119.6 jit_solution(9974013438051938253)
XLA Ops:
  0.0 1.2 copy-done.2
  2.6 1.0 prepare.1
  3.7 0.9 copy-done
  4.6 3.5 %near_products.2.products_ref = f32[8,344,128]{2,1,0:T(8,128)S(1)} custom-call(s32[4096]{0:T(1024)S(1)} %bitcast.2, f32[3744,128]{1,0:T(8,128)S(1)} %get-tuple-element.39.ext_ref.wide_ref, bf16[343,343]{1,0:T(8,128)(2,1)S(1)} %copy-done), custom_call_target="tpu_custom_call" | custom-call | bytes 14680064 | tf_op jit(solution)/shard_map/near_products/pallas_call | solution.py:198
  8.2 7.5 %far_cells.2 = (f32[3456,128]{1,0:T(8,128)S(1)}, bf16[288,128]{1,0:T(8,128)(2,1)S(1)}) custom-call(s32[4096]{0:T(1024)S(1)} %bitcast.3, f32[16]{0:T(128)S(1)} %copy-done.8, f32[3744,128]{1,0:T(8,128)S(1)} %get-tuple-element.39.ext_ref.wide_ref, bf16[288,128]{1,0:T(8,128)(2,1)S(1)} %collective-permute-done.ghost_ref, bf16[343,343]{1,0:T(8,128)(2,1)S(1)} %copy-done.1, ...), custom_call_target="tpu_custom_call" | custom-call | bytes 29360128 | tf_op jit(solution)/shard_map/far_cells/pallas_call | solution.py:209
  16.2 3.8 %near_sums.2.sums_ref = f32[3456,128]{1,0:T(8,128)S(1)} custom-call(s32[4096]{0:T(1024)S(1)} %bitcast.4, f32[16]{0:T(128)S(1)} %copy-done.8, f32[8,344,128]{2,1,0:T(8,128)S(1)} %near_products.2.products_ref, f32[3456,128]{1,0:T(8,128)S(1)} %get-tuple-element.42.start_ref), custom_call_target="tpu_custom_call" | custom-call | bytes 14680064 | tf_op jit(solution)/shard_map/near_sums/pallas_call | solution.py:225
  20.1 1.5 %first_term.1 = (f32[3456,128]{1,0:T(8,128)S(1)}, f32[3744,128]{1,0:T(8,128)S(1)}, bf16[288,128]{1,0:T(8,128)(2,1)S(1)}) custom-call(s32[288]{0:T(512)S(1)} %copy-done.7, f32[3456,128]{1,0:T(8,128)S(1)} %near_sums.2.sums_ref, bf16[288,128]{1,0:T(8,128)(2,1)S(1)} %collective-permute-done.1.back_ref), custom_call_target="tpu_custom_call" | custom-call | bytes 8388608 | tf_op jit(solution)/shard_map/first_term/pallas_call | solution.py:266
  21.5 1.3 %collective-permute-start.2 = (bf16[288,128]{1,0:T(8,128)(2,1)S(1)}, bf16[288,128]{1,0:T(8,128)(2,1)S(1)}, u32[]{:S(2)}, u32[]{:S(2)}) collective-permute-start(bf16[288,128]{1,0:T(8,128)(2,1)S(1)} %get-tuple-element.44), channel_id=1, source_target_pairs={{0,28},{4,0},{8,4},{12,8},{16,12},{20,16},{24,20},{28,24},{1,29},{... | collective-permute-start | bytes 221192 | tf_op jit(solution)/shard_map/ppermute | solution.py:30
  22.8 3.5 %near_products.3.products_ref = f32[8,344,128]{2,1,0:T(8,128)S(1)} custom-call(s32[4096]{0:T(1024)S(1)} %bitcast.5, f32[3744,128]{1,0:T(8,128)S(1)} %get-tuple-element.45.ext_ref, bf16[343,343]{1,0:T(8,128)(2,1)S(1)} %copy-done.1), custom_call_target="tpu_custom_call" | custom-call | bytes 14680064 | tf_op jit(solution)/shard_map/near_products/pallas_call | solution.py:198
  26.4 7.5 %far_cells.3 = (f32[3456,128]{1,0:T(8,128)S(1)}, bf16[288,128]{1,0:T(8,128)(2,1)S(1)}) custom-call(s32[4096]{0:T(1024)S(1)} %bitcast.6, f32[16]{0:T(128)S(1)} %copy-done.8, f32[3744,128]{1,0:T(8,128)S(1)} %get-tuple-element.45.ext_ref, bf16[288,128]{1,0:T(8,128)(2,1)S(1)} %collective-permute-done.2.ghost_ref, bf16[343,343]{1,0:T(8,128)(2,1)S(1)} %copy-done.1, ...), custom_call_target="tpu_custom_call" | custom-call | bytes 29360128 | tf_op jit(solution)/shard_map/far_cells/pallas_call | solution.py:209
  33.9 1.9 %collective-permute-start.3 = (bf16[288,128]{1,0:T(8,128)(2,1)S(1)}, bf16[288,128]{1,0:T(8,128)(2,1)S(1)}, u32[]{:S(2)}, u32[]{:S(2)}) collective-permute-start(bf16[288,128]{1,0:T(8,128)(2,1)S(1)} %get-tuple-element.50), channel_id=1, source_target_pairs={{0,4},{4,8},{8,12},{12,16},{16,20},{20,24},{24,28},{28,0},{1,5},{5... | collective-permute-start | bytes 221192 | tf_op jit(solution)/shard_map/ppermute | solution.py:30
  35.7 3.7 %near_sums.3.sums_ref = f32[3456,128]{1,0:T(8,128)S(1)} custom-call(s32[4096]{0:T(1024)S(1)} %bitcast.7, f32[16]{0:T(128)S(1)} %copy-done.8, f32[8,344,128]{2,1,0:T(8,128)S(1)} %near_products.3.products_ref, f32[3456,128]{1,0:T(8,128)S(1)} %get-tuple-element.49.start_ref), custom_call_target="tpu_custom_call" | custom-call | bytes 14680064 | tf_op jit(solution)/shard_map/near_sums/pallas_call | solution.py:225
  39.5 1.3 %second_term.1 = (bf16[864,128]{1,0:T(8,128)(2,1)S(1)}, bf16[864,128]{1,0:T(8,128)(2,1)S(1)}, bf16[864,128]{1,0:T(8,128)(2,1)S(1)}, bf16[864,128]{1,0:T(8,128)(2,1)S(1)}, bf16[2592,128]{1,0:T(8,128)(2,1)S(1)}) custom-call(s32[288]{0:T(512)S(1)} %copy-done.7, f32[3456,128]{1,0:T(8,128)S(1)} %near_sums.3.sums_ref, ...), custom_call_target="tpu_custom_call" | custom-call | bytes 6291456 | tf_op jit(solution)/shard_map/second_term/pallas_call | solution.py:299
  41.3 1.7 %collective-permute-start.5 = (bf16[864,128]{1,0:T(8,128)(2,1)S(1)}, bf16[864,128]{1,0:T(8,128)(2,1)S(1)}, u32[]{:S(2)}, u32[]{:S(2)}) collective-permute-start(bf16[864,128]{1,0:T(8,128)(2,1)S(1)} %get-tuple-element.53), channel_id=1, source_target_pairs={{0,2},{1,3},{2,0},{3,1},{4,6},{5,7},{6,4},{7,5},{8,10},{9,11},{10,... | collective-permute-start | bytes 663560 | tf_op jit(solution)/shard_map/ppermute | solution.py:30
  43.5 5.4 %collective-permute-done.4.refs_1_ = bf16[864,128]{1,0:T(8,128)(2,1)S(1)} collective-permute-done((bf16[864,128]{1,0:T(8,128)(2,1)S(1)}, bf16[864,128]{1,0:T(8,128)(2,1)S(1)}, u32[]{:S(2)}, u32[]{:S(2)}) %collective-permute-start.4) | collective-permute-done | bytes 221216 | tf_op jit(solution)/shard_map/ppermute | solution.py:30
  48.9 14.1 %collective-permute-done.5.refs_2_ = bf16[864,128]{1,0:T(8,128)(2,1)S(1)} collective-permute-done((bf16[864,128]{1,0:T(8,128)(2,1)S(1)}, bf16[864,128]{1,0:T(8,128)(2,1)S(1)}, u32[]{:S(2)}, u32[]{:S(2)}) %collective-permute-start.5) | collective-permute-done | bytes 221216 | tf_op jit(solution)/shard_map/ppermute | solution.py:30
  64.3 1.3 %collective-permute-start.12 = (bf16[2592,128]{1,0:T(8,128)(2,1)S(1)}, bf16[2592,128]{1,0:T(8,128)(2,1)S(1)}, u32[]{:S(2)}, u32[]{:S(2)}) collective-permute-start(bf16[2592,128]{1,0:T(8,128)(2,1)S(1)} %pad_maximum_fusion), channel_id=1, source_target_pairs={{0,1},{1,2},{2,3},{4,5},{5,6},{6,7},{8,9},{9,10},{10,11},{12,13},{... | collective-permute-start | bytes 1990664 | tf_op jit(solution)/shard_map/ppermute | solution.py:402
  67.4 1.9 %collective-permute-start.8 = (f32[160,128]{1,0:T(8,128)S(1)}, f32[160,128]{1,0:T(8,128)S(1)}, u32[]{:S(2)}, u32[]{:S(2)}) collective-permute-start(f32[160,128]{1,0:T(8,128)S(1)} %get-tuple-element.62), channel_id=1, source_target_pairs={{0,8},{4,12},{8,0},{12,4},{16,24},{20,28},{24,16},{28,20},{1,9},{5... | collective-permute-start | bytes 245768 | tf_op jit(solution)/shard_map/ppermute | solution.py:395
  69.3 2.6 %collective-permute-done.10 = f32[160,128]{1,0:T(8,128)S(1)} collective-permute-done((f32[160,128]{1,0:T(8,128)S(1)}, f32[160,128]{1,0:T(8,128)S(1)}, u32[]{:S(2)}, u32[]{:S(2)}) %collective-permute-start.10) | collective-permute-done | bytes 81952 | tf_op jit(solution)/shard_map/ppermute | solution.py:395
  73.2 3.6 %collective-permute-start.11 = (f32[160,128]{1,0:T(8,128)S(1)}, f32[160,128]{1,0:T(8,128)S(1)}, u32[]{:S(2)}, u32[]{:S(2)}) collective-permute-start(f32[160,128]{1,0:T(8,128)S(1)} %add_add_fusion.1), channel_id=1, source_target_pairs={{0,1},{1,2},{2,3},{3,0},{4,5},{5,6},{6,7},{7,4},{8,9},{9,10},{10,1... | collective-permute-start | bytes 245768 | tf_op jit(solution)/shard_map/ppermute | solution.py:30
  77.6 7.7 %collective-permute-done.11 = f32[160,128]{1,0:T(8,128)S(1)} collective-permute-done((f32[160,128]{1,0:T(8,128)S(1)}, f32[160,128]{1,0:T(8,128)S(1)}, u32[]{:S(2)}, u32[]{:S(2)}) %collective-permute-start.11) | collective-permute-done | bytes 81952 | tf_op jit(solution)/shard_map/ppermute | solution.py:30
  85.4 1.3 %collective-permute-start.19 = (bf16[2592,128]{1,0:T(8,128)(2,1)S(1)}, bf16[2592,128]{1,0:T(8,128)(2,1)S(1)}, u32[]{:S(2)}, u32[]{:S(2)}) collective-permute-start(bf16[2592,128]{1,0:T(8,128)(2,1)S(1)} %pad_maximum_fusion.1), channel_id=1, source_target_pairs={{1,2},{2,3},{5,6},{6,7},{9,10},{10,11},{13,14},{14,15},{17,18},{18... | collective-permute-start | bytes 1990664 | tf_op jit(solution)/shard_map/ppermute | solution.py:402
  86.7 1.3 %collective-permute-start.20 = (bf16[1728,128]{1,0:T(8,128)(2,1)S(1)}, bf16[1728,128]{1,0:T(8,128)(2,1)S(1)}, u32[]{:S(2)}, u32[]{:S(2)}) collective-permute-start(bf16[1728,128]{1,0:T(8,128)(2,1)S(1)} %pad_maximum_fusion.2), channel_id=1, source_target_pairs={{1,3},{5,7},{9,11},{13,15},{17,19},{21,23},{25,27},{29,31}} | collective-permute-start | bytes 1327112 | tf_op jit(solution)/shard_map/ppermute | solution.py:434
  88.5 2.0 %collective-permute-done.13 = f32[160,128]{1,0:T(8,128)S(1)} collective-permute-done((f32[160,128]{1,0:T(8,128)S(1)}, f32[160,128]{1,0:T(8,128)S(1)}, u32[]{:S(2)}, u32[]{:S(2)}) %collective-permute-start.13) | collective-permute-done | bytes 81952 | tf_op jit(solution)/shard_map/ppermute | solution.py:30
  90.6 1.6 %collective-permute-start.16 = (f32[160,128]{1,0:T(8,128)S(1)}, f32[160,128]{1,0:T(8,128)S(1)}, u32[]{:S(2)}, u32[]{:S(2)}) collective-permute-start(f32[160,128]{1,0:T(8,128)S(1)} %add_add_fusion.refs_0_), channel_id=1, source_target_pairs={{0,16},{4,20},{8,24},{12,28},{16,0},{20,4},{24,8},{28,12},{1,17},{... | collective-permute-start | bytes 245768 | tf_op jit(solution)/shard_map/ppermute | solution.py:395
  92.2 1.9 %collective-permute-start.17 = (f32[160,128]{1,0:T(8,128)S(1)}, f32[160,128]{1,0:T(8,128)S(1)}, u32[]{:S(2)}, u32[]{:S(2)}) collective-permute-start(f32[160,128]{1,0:T(8,128)S(1)} %add_add_fusion.refs_0_), channel_id=1, source_target_pairs={{0,24},{4,28},{8,16},{12,20},{16,8},{20,12},{24,0},{28,4},{1,25},{... | collective-permute-start | bytes 245768 | tf_op jit(solution)/shard_map/ppermute | solution.py:395
  94.1 1.7 %collective-permute-done.15.refs_1_ = f32[160,128]{1,0:T(8,128)S(1)} collective-permute-done((f32[160,128]{1,0:T(8,128)S(1)}, f32[160,128]{1,0:T(8,128)S(1)}, u32[]{:S(2)}, u32[]{:S(2)}) %collective-permute-start.15) | collective-permute-done | bytes 81952 | tf_op jit(solution)/shard_map/ppermute | solution.py:395
  95.8 1.8 %collective-permute-done.17.refs_3_ = f32[160,128]{1,0:T(8,128)S(1)} collective-permute-done((f32[160,128]{1,0:T(8,128)S(1)}, f32[160,128]{1,0:T(8,128)S(1)}, u32[]{:S(2)}, u32[]{:S(2)}) %collective-permute-start.17) | collective-permute-done | bytes 81952 | tf_op jit(solution)/shard_map/ppermute | solution.py:395
  97.7 1.3 %collective-permute-start.21 = (bf16[864,128]{1,0:T(8,128)(2,1)S(1)}, bf16[864,128]{1,0:T(8,128)(2,1)S(1)}, u32[]{:S(2)}, u32[]{:S(2)}) collective-permute-start(bf16[864,128]{1,0:T(8,128)(2,1)S(1)} %collective-permute-done.5.refs_2_), channel_id=1, source_target_pairs={{2,3},{6,7},{10,11},{14,15},{18,19},{22,23},{26,27},{30,31}} | collective-permute-start | bytes 663560 | tf_op jit(solution)/shard_map/ppermute | solution.py:407
  99.3 13.4 %inverse_factor.1.factor_ref = f32[512,512]{1,0:T(8,128)S(1)} custom-call(f32[640,128]{1,0:T(8,128)S(1)} %joined.1.mine_ref, f32[640,128]{1,0:T(8,128)S(1)} %collective-permute-done.18.other_ref), custom_call_target="tpu_custom_call" | custom-call | bytes 73400320 | tf_op jit(solution)/shard_map/inverse_factor/pallas_call | solution.py:574
  113.7 4.2 %collective-permute-done.21.refs_2_ = bf16[864,128]{1,0:T(8,128)(2,1)S(1)} collective-permute-done((bf16[864,128]{1,0:T(8,128)(2,1)S(1)}, bf16[864,128]{1,0:T(8,128)(2,1)S(1)}, u32[]{:S(2)}, u32[]{:S(2)}) %collective-permute-start.21) | collective-permute-done | bytes 221216 | tf_op jit(solution)/shard_map/ppermute | solution.py:407
  117.8 1.6 %output_late.1 = f32[3456,128]{1,0:T(8,128)} custom-call(f32[512,512]{1,0:T(8,128)S(1)} %inverse_factor.1.factor_ref, f32[4,864,128]{2,1,0:T(8,128)S(1)} %output_early.1.early_ref, bf16[2592,128]{1,0:T(8,128)(2,1)S(1)} %collective-permute-done.19.refs_0_, bf16[1728,128]{1,0:T(8,128)(2,1)S(1)} %collective-permute-done.20.refs_1_, ...), custom_call_target="tpu_custom_call" | custom-call | bytes 6291456 | tf_op jit(solution)/shard_map/output_late/pallas_call | solution.py:665
  (53 shorter events, 10.2 us)
Async XLA Ops:
  0.0 1.2 copy-start.2
  1.2 0.7 copy-start.5
  1.9 0.7 copy-start.6
  3.6 4.6 %collective-permute-start = (bf16[288,128]{1,0:T(8,128)(2,1)S(1)}, bf16[288,128]{1,0:T(8,128)(2,1)S(1)}, u32[]{:S(2)}, u32[]{:S(2)}) collective-permute-start(bf16[288,128]{1,0:T(8,128)(2,1)S(1)} %get-tuple-element.38), channel_id=1, source_target_pairs={{0,28},{4,0},{8,4},{12,8},{16,12},{20,16},{24,20},{28,24},{1,29},{... | collective-permute-start | bytes 221192 | tf_op jit(solution)/shard_map/ppermute | solution.py:30
  3.6 1.0 copy-start
  4.6 3.6 %copy-start.1 = (bf16[343,343]{1,0:T(8,128)(2,1)S(1)}, bf16[343,343]{1,0:T(8,128)(2,1)}, u32[]{:S(2)}) copy-start(bf16[343,343]{1,0:T(8,128)(2,1)} %matrix_ref.7) | copy-start | bytes 705898
  4.6 3.6 %copy-start.4 = (f32[3456]{0:T(1024)S(1)}, f32[3456]{0:T(1024)}, u32[]{:S(2)}) copy-start(f32[3456]{0:T(1024)} %param.9) | copy-start | bytes 41476
  4.6 3.6 %copy-start.8 = (f32[16]{0:T(128)S(1)}, f32[16]{0:T(128)}, u32[]{:S(2)}) copy-start(f32[16]{0:T(128)} %scale_ref.3) | copy-start | bytes 196
  15.7 4.4 %collective-permute-start.1 = (bf16[288,128]{1,0:T(8,128)(2,1)S(1)}, bf16[288,128]{1,0:T(8,128)(2,1)S(1)}, u32[]{:S(2)}, u32[]{:S(2)}) collective-permute-start(bf16[288,128]{1,0:T(8,128)(2,1)S(1)} %get-tuple-element.43), channel_id=1, source_target_pairs={{0,4},{4,8},{8,12},{12,16},{16,20},{20,24},{24,28},{28,0},{1,5},{5... | collective-permute-start | bytes 221192 | tf_op jit(solution)/shard_map/ppermute | solution.py:30
  16.2 3.8 %copy-start.7 = (s32[288]{0:T(512)S(1)}, s32[288]{0:T(512)}, u32[]{:S(2)}) copy-start(s32[288]{0:T(512)} %nodes.5) | copy-start | bytes 3460
  21.5 4.9 %collective-permute-start.2 = (bf16[288,128]{1,0:T(8,128)(2,1)S(1)}, bf16[288,128]{1,0:T(8,128)(2,1)S(1)}, u32[]{:S(2)}, u32[]{:S(2)}) collective-permute-start(bf16[288,128]{1,0:T(8,128)(2,1)S(1)} %get-tuple-element.44), channel_id=1, source_target_pairs={{0,28},{4,0},{8,4},{12,8},{16,12},{20,16},{24,20},{28,24},{1,29},{... | collective-permute-start | bytes 221192 | tf_op jit(solution)/shard_map/ppermute | solution.py:30
  33.9 5.6 %collective-permute-start.3 = (bf16[288,128]{1,0:T(8,128)(2,1)S(1)}, bf16[288,128]{1,0:T(8,128)(2,1)S(1)}, u32[]{:S(2)}, u32[]{:S(2)}) collective-permute-start(bf16[288,128]{1,0:T(8,128)(2,1)S(1)} %get-tuple-element.50), channel_id=1, source_target_pairs={{0,4},{4,8},{8,12},{12,16},{16,20},{20,24},{24,28},{28,0},{1,5},{5... | collective-permute-start | bytes 221192 | tf_op jit(solution)/shard_map/ppermute | solution.py:30
  35.7 3.8 %copy-start.3 = (bf16[3456,128]{1,0:T(8,128)(2,1)S(1)}, bf16[3456,128]{1,0:T(8,128)(2,1)}, u32[]{:S(2)}) copy-start(bf16[3456,128]{1,0:T(8,128)(2,1)} %previous_ref.1) | copy-start | bytes 2654212
  40.9 8.0 %collective-permute-start.4 = (bf16[864,128]{1,0:T(8,128)(2,1)S(1)}, bf16[864,128]{1,0:T(8,128)(2,1)S(1)}, u32[]{:S(2)}, u32[]{:S(2)}) collective-permute-start(bf16[864,128]{1,0:T(8,128)(2,1)S(1)} %get-tuple-element.52), channel_id=1, source_target_pairs={{0,1},{1,2},{2,3},{3,0},{4,5},{5,6},{6,7},{7,4},{8,9},{9,10},{10,1... | collective-permute-start | bytes 663560 | tf_op jit(solution)/shard_map/ppermute | solution.py:30
  41.3 21.7 %collective-permute-start.5 = (bf16[864,128]{1,0:T(8,128)(2,1)S(1)}, bf16[864,128]{1,0:T(8,128)(2,1)S(1)}, u32[]{:S(2)}, u32[]{:S(2)}) collective-permute-start(bf16[864,128]{1,0:T(8,128)(2,1)S(1)} %get-tuple-element.53), channel_id=1, source_target_pairs={{0,2},{1,3},{2,0},{3,1},{4,6},{5,7},{6,4},{7,5},{8,10},{9,11},{10,... | collective-permute-start | bytes 663560 | tf_op jit(solution)/shard_map/ppermute | solution.py:30
  43.0 20.0 %collective-permute-start.6 = (bf16[864,128]{1,0:T(8,128)(2,1)S(1)}, bf16[864,128]{1,0:T(8,128)(2,1)S(1)}, u32[]{:S(2)}, u32[]{:S(2)}) collective-permute-start(bf16[864,128]{1,0:T(8,128)(2,1)S(1)} %get-tuple-element.54), channel_id=1, source_target_pairs={{0,3},{1,0},{2,1},{3,2},{4,7},{5,4},{6,5},{7,6},{8,11},{9,8},{10,9... | collective-permute-start | bytes 663560 | tf_op jit(solution)/shard_map/ppermute | solution.py:30
  63.9 1.7 %collective-permute-start.7 = (f32[640,128]{1,0:T(8,128)S(1)}, f32[640,128]{1,0:T(8,128)S(1)}, u32[]{:S(2)}, u32[]{:S(2)}) collective-permute-start(f32[640,128]{1,0:T(8,128)S(1)} %get-tuple-element.60), channel_id=1, source_target_pairs={{0,4},{4,0},{8,12},{12,8},{16,20},{20,16},{24,28},{28,24},{1,5},{5... | collective-permute-start | bytes 983048 | tf_op jit(solution)/shard_map/ppermute | solution.py:395
  64.3 20.9 %collective-permute-start.12 = (bf16[2592,128]{1,0:T(8,128)(2,1)S(1)}, bf16[2592,128]{1,0:T(8,128)(2,1)S(1)}, u32[]{:S(2)}, u32[]{:S(2)}) collective-permute-start(bf16[2592,128]{1,0:T(8,128)(2,1)S(1)} %pad_maximum_fusion), channel_id=1, source_target_pairs={{0,1},{1,2},{2,3},{4,5},{5,6},{6,7},{8,9},{9,10},{10,11},{12,13},{... | collective-permute-start | bytes 1990664 | tf_op jit(solution)/shard_map/ppermute | solution.py:402
  65.7 6.2 %collective-permute-start.10 = (f32[160,128]{1,0:T(8,128)S(1)}, f32[160,128]{1,0:T(8,128)S(1)}, u32[]{:S(2)}, u32[]{:S(2)}) collective-permute-start(f32[160,128]{1,0:T(8,128)S(1)} %get-tuple-element.64), channel_id=1, source_target_pairs={{0,24},{4,28},{8,16},{12,20},{16,8},{20,12},{24,0},{28,4},{1,25},{... | collective-permute-start | bytes 245768 | tf_op jit(solution)/shard_map/ppermute | solution.py:395
  66.5 6.1 %collective-permute-start.9 = (f32[160,128]{1,0:T(8,128)S(1)}, f32[160,128]{1,0:T(8,128)S(1)}, u32[]{:S(2)}, u32[]{:S(2)}) collective-permute-start(f32[160,128]{1,0:T(8,128)S(1)} %get-tuple-element.63), channel_id=1, source_target_pairs={{0,16},{4,20},{8,24},{12,28},{16,0},{20,4},{24,8},{28,12},{1,17},{... | collective-permute-start | bytes 245768 | tf_op jit(solution)/shard_map/ppermute | solution.py:395
  67.4 5.8 %collective-permute-start.8 = (f32[160,128]{1,0:T(8,128)S(1)}, f32[160,128]{1,0:T(8,128)S(1)}, u32[]{:S(2)}, u32[]{:S(2)}) collective-permute-start(f32[160,128]{1,0:T(8,128)S(1)} %get-tuple-element.62), channel_id=1, source_target_pairs={{0,8},{4,12},{8,0},{12,4},{16,24},{20,28},{24,16},{28,20},{1,9},{5... | collective-permute-start | bytes 245768 | tf_op jit(solution)/shard_map/ppermute | solution.py:395
  73.2 12.1 %collective-permute-start.11 = (f32[160,128]{1,0:T(8,128)S(1)}, f32[160,128]{1,0:T(8,128)S(1)}, u32[]{:S(2)}, u32[]{:S(2)}) collective-permute-start(f32[160,128]{1,0:T(8,128)S(1)} %add_add_fusion.1), channel_id=1, source_target_pairs={{0,1},{1,2},{2,3},{3,0},{4,5},{5,6},{6,7},{7,4},{8,9},{9,10},{10,1... | collective-permute-start | bytes 245768 | tf_op jit(solution)/shard_map/ppermute | solution.py:30
  76.7 11.8 %collective-permute-start.14 = (f32[160,128]{1,0:T(8,128)S(1)}, f32[160,128]{1,0:T(8,128)S(1)}, u32[]{:S(2)}, u32[]{:S(2)}) collective-permute-start(f32[160,128]{1,0:T(8,128)S(1)} %add_add_fusion.1), channel_id=1, source_target_pairs={{0,3},{1,0},{2,1},{3,2},{4,7},{5,4},{6,5},{7,6},{8,11},{9,8},{10,9... | collective-permute-start | bytes 245768 | tf_op jit(solution)/shard_map/ppermute | solution.py:30
  76.8 13.8 %collective-permute-start.13 = (f32[160,128]{1,0:T(8,128)S(1)}, f32[160,128]{1,0:T(8,128)S(1)}, u32[]{:S(2)}, u32[]{:S(2)}) collective-permute-start(f32[160,128]{1,0:T(8,128)S(1)} %add_add_fusion.1), channel_id=1, source_target_pairs={{0,2},{1,3},{2,0},{3,1},{4,6},{5,7},{6,4},{7,5},{8,10},{9,11},{10,... | collective-permute-start | bytes 245768 | tf_op jit(solution)/shard_map/ppermute | solution.py:30
  85.4 32.5 %collective-permute-start.19 = (bf16[2592,128]{1,0:T(8,128)(2,1)S(1)}, bf16[2592,128]{1,0:T(8,128)(2,1)S(1)}, u32[]{:S(2)}, u32[]{:S(2)}) collective-permute-start(bf16[2592,128]{1,0:T(8,128)(2,1)S(1)} %pad_maximum_fusion.1), channel_id=1, source_target_pairs={{1,2},{2,3},{5,6},{6,7},{9,10},{10,11},{13,14},{14,15},{17,18},{18... | collective-permute-start | bytes 1990664 | tf_op jit(solution)/shard_map/ppermute | solution.py:402
  86.7 31.1 %collective-permute-start.20 = (bf16[1728,128]{1,0:T(8,128)(2,1)S(1)}, bf16[1728,128]{1,0:T(8,128)(2,1)S(1)}, u32[]{:S(2)}, u32[]{:S(2)}) collective-permute-start(bf16[1728,128]{1,0:T(8,128)(2,1)S(1)} %pad_maximum_fusion.2), channel_id=1, source_target_pairs={{1,3},{5,7},{9,11},{13,15},{17,19},{21,23},{25,27},{29,31}} | collective-permute-start | bytes 1327112 | tf_op jit(solution)/shard_map/ppermute | solution.py:434
  90.6 5.2 %collective-permute-start.15 = (f32[160,128]{1,0:T(8,128)S(1)}, f32[160,128]{1,0:T(8,128)S(1)}, u32[]{:S(2)}, u32[]{:S(2)}) collective-permute-start(f32[160,128]{1,0:T(8,128)S(1)} %add_add_fusion.refs_0_), channel_id=1, source_target_pairs={{0,8},{4,12},{8,0},{12,4},{16,24},{20,28},{24,16},{28,20},{1,9},{5... | collective-permute-start | bytes 245768 | tf_op jit(solution)/shard_map/ppermute | solution.py:395
  90.6 5.1 %collective-permute-start.16 = (f32[160,128]{1,0:T(8,128)S(1)}, f32[160,128]{1,0:T(8,128)S(1)}, u32[]{:S(2)}, u32[]{:S(2)}) collective-permute-start(f32[160,128]{1,0:T(8,128)S(1)} %add_add_fusion.refs_0_), channel_id=1, source_target_pairs={{0,16},{4,20},{8,24},{12,28},{16,0},{20,4},{24,8},{28,12},{1,17},{... | collective-permute-start | bytes 245768 | tf_op jit(solution)/shard_map/ppermute | solution.py:395
  92.2 5.4 %collective-permute-start.17 = (f32[160,128]{1,0:T(8,128)S(1)}, f32[160,128]{1,0:T(8,128)S(1)}, u32[]{:S(2)}, u32[]{:S(2)}) collective-permute-start(f32[160,128]{1,0:T(8,128)S(1)} %add_add_fusion.refs_0_), channel_id=1, source_target_pairs={{0,24},{4,28},{8,16},{12,20},{16,8},{20,12},{24,0},{28,4},{1,25},{... | collective-permute-start | bytes 245768 | tf_op jit(solution)/shard_map/ppermute | solution.py:395
  97.6 1.7 %collective-permute-start.18 = (f32[640,128]{1,0:T(8,128)S(1)}, f32[640,128]{1,0:T(8,128)S(1)}, u32[]{:S(2)}, u32[]{:S(2)}) collective-permute-start(f32[640,128]{1,0:T(8,128)S(1)} %joined.1.mine_ref), channel_id=1, source_target_pairs={{0,4},{4,0},{8,12},{12,8},{16,20},{20,16},{24,28},{28,24},{1,5},{5... | collective-permute-start | bytes 983048 | tf_op jit(solution)/shard_map/ppermute | solution.py:395
  97.7 20.1 %collective-permute-start.21 = (bf16[864,128]{1,0:T(8,128)(2,1)S(1)}, bf16[864,128]{1,0:T(8,128)(2,1)S(1)}, u32[]{:S(2)}, u32[]{:S(2)}) collective-permute-start(bf16[864,128]{1,0:T(8,128)(2,1)S(1)} %collective-permute-done.5.refs_2_), channel_id=1, source_target_pairs={{2,3},{6,7},{10,11},{14,15},{18,19},{22,23},{26,27},{30,31}} | collective-permute-start | bytes 663560 | tf_op jit(solution)/shard_map/ppermute | solution.py:407

commit v10 on v9

--- a/solution.py
+++ b/solution.py
@@ -49,12 +49,12 @@
     pack_links(links_ref, words_ref)
 
     def body(step, _):
-        for k in range(16):
-            i = step * 16 + k
+        for k in range(48):
+            i = step * 48 + k
             picked[pl.ds(i, 1), :] = ext_ref[pl.ds(nodes[i], 1), :]
         return 0
 
-    lax.fori_loop(0, nodes.shape[0] // 16, body, 0)
+    lax.fori_loop(0, nodes.shape[0] // 48, body, 0)
     edge_ref[...] = picked[...].astype(BF16)
 
 
@@ -280,17 +280,14 @@
 
 
 def second_kernel(nodes, sums_ref, back_ref, previous_ref, *refs):
-    pieces, (rest_ref, total, scaled) = refs[:-3], refs[-3:]
+    pieces, (total, scaled) = refs[:-2], refs[-2:]
     total[...] = sums_ref[...] * (2.0 / HALF_WIDTH) - previous_ref[...].astype(F32)
     add_back(nodes, total, back_ref, 2.0 / HALF_WIDTH, scaled)
     count = len(pieces)
     rows = total.shape[0] // count
     for k, piece in enumerate(pieces):
         start = pl.multiple_of(lax.rem(lax.axis_index("band") + k, count) * rows, rows)
-        part = total[pl.ds(start, rows), :].astype(BF16)
-        piece[...] = part
-        if k:
-            rest_ref[(k - 1) * rows : k * rows, :] = part
+        piece[...] = total[pl.ds(start, rows), :].astype(BF16)
 
 
 def second_term(nodes, sums, back, previous, count):
@@ -298,16 +295,15 @@
     rows = owned // count
     made = pl.pallas_call(
         second_kernel,
-        out_shape=[jax.ShapeDtypeStruct((rows, LANES), BF16)] * count
-        + [jax.ShapeDtypeStruct((owned - rows, LANES), BF16)],
+        out_shape=[jax.ShapeDtypeStruct((rows, LANES), BF16)] * count,
         in_specs=[SM, VM, VM, VM],
-        out_specs=[VM] * (count + 1),
+        out_specs=[VM] * count,
         scratch_shapes=[pltpu.VMEM(sums.shape, F32), pltpu.VMEM(back.shape, F32)],
         compiler_params=params(16),
         cost_estimate=cost(0, 6 << 20),
         name="second_term",
     )(nodes, sums, back, previous)
-    return made[:count], made[count]
+    return made
 
 
 def gram_kernel(*refs):
@@ -687,11 +683,11 @@
     operator = functools.partial(apply_operator, words, cell_scale, cell_matrix, levels)
     sums, back = operator(*start)
     sums, back = operator(*first_term(boundary_nodes, sums, back))
-    pieces, rest = second_term(boundary_nodes, sums, back, states_block, count)
+    pieces = second_term(boundary_nodes, sums, back, states_block, count)
 
     firsts = [pieces[0]] + [shifted(pieces[s], "band", s) for s in range(1, count)]
     firsts = list(ordered(*firsts))
-    rests = [rest]
+    rests = [jnp.concatenate(pieces[1:])]
     keep, send = partial_gram(firsts)
     mine, other = summed_beside(keep, send, rests, firsts)
     over = 1.0 / (owned * lax.axis_size("domain"))

time: 120 us -> 120 us (level)
  no operation moved by 1% of the time
where the time goes in v10:
time: 120 us
  Pallas kernels  50.3 us (42%)
  waiting for transfers between devices  41.6 us (35%)
  starting transfers between devices  23.6 us (20%)
  local copies, waits for them, and re-layouts  3.59 us (3%)
    ppermute x10, waiting for transfers between devices, shifted(): lax.ppermute(value, axis, [(i, (i + steps) % count) for i in range(count)])  29.8 us
    pallas_call x2, Pallas kernels, apply_operator(): pl.pallas_call(far_cells_kernel, out_shape=(jax.ShapeDtypeStruct((owned,...  14.9 us
    pallas_call x1, Pallas kernels, inverse_factor(): pl.pallas_call(functools.partial(inverse_kernel, over), out_shape=jax.Sha...  13.4 us
    ppermute x10, starting transfers between devices, shifted(): lax.ppermute(value, axis, [(i, (i + steps) % count) for i in range(count)])  10.8 us
    ppermute x8, waiting for transfers between devices, paired(): return lax.ppermute(value, axis, [(i, i ^ mask) for i in range(count)])  7.65 us
    pallas_call x2, Pallas kernels, apply_operator(): pl.pallas_call(functools.partial(near_sums_kernel, npc), out_shape=jax.Sh...  7.62 us
    ppermute x8, starting transfers between devices, paired(): return lax.ppermute(value, axis, [(i, i ^ mask) for i in range(count)])  7.55 us
    pallas_call x2, Pallas kernels, apply_operator(): pl.pallas_call(near_products_kernel, out_shape=jax.ShapeDtypeStruct(held,...  7.09 us
  transfers between devices with their start and end apart: 22, of which 12 were waited for; matrix products, arithmetic and copies ran while one was open for 0% of the time, Pallas kernels for 24%

profile of v10, /device:TPU:26, one launch (start us, length us, event | category | flops | bytes accessed | tf_op | source)
XLA Modules:
  0.0 119.7 jit_solution(10620100488087472179)
XLA Ops:
  0.0 1.2 copy-done.2
  2.6 0.9 prepare.1
  3.6 0.9 copy-done
  4.6 3.5 %near_products.2.products_ref = f32[8,344,128]{2,1,0:T(8,128)S(1)} custom-call(s32[4096]{0:T(1024)S(1)} %bitcast.2, f32[3744,128]{1,0:T(8,128)S(1)} %get-tuple-element.38.ext_ref.wide_ref, bf16[343,343]{1,0:T(8,128)(2,1)S(1)} %copy-done), custom_call_target="tpu_custom_call" | custom-call | bytes 14680064 | tf_op jit(solution)/shard_map/near_products/pallas_call | solution.py:198
  8.1 7.5 %far_cells.2 = (f32[3456,128]{1,0:T(8,128)S(1)}, bf16[288,128]{1,0:T(8,128)(2,1)S(1)}) custom-call(s32[4096]{0:T(1024)S(1)} %bitcast.3, f32[16]{0:T(128)S(1)} %copy-done.8, f32[3744,128]{1,0:T(8,128)S(1)} %get-tuple-element.38.ext_ref.wide_ref, bf16[288,128]{1,0:T(8,128)(2,1)S(1)} %collective-permute-done.ghost_ref, bf16[343,343]{1,0:T(8,128)(2,1)S(1)} %copy-done.1, ...), custom_call_target="tpu_custom_call" | custom-call | bytes 29360128 | tf_op jit(solution)/shard_map/far_cells/pallas_call | solution.py:209
  16.2 3.8 %near_sums.2.sums_ref = f32[3456,128]{1,0:T(8,128)S(1)} custom-call(s32[4096]{0:T(1024)S(1)} %bitcast.4, f32[16]{0:T(128)S(1)} %copy-done.8, f32[8,344,128]{2,1,0:T(8,128)S(1)} %near_products.2.products_ref, f32[3456,128]{1,0:T(8,128)S(1)} %get-tuple-element.41.start_ref), custom_call_target="tpu_custom_call" | custom-call | bytes 14680064 | tf_op jit(solution)/shard_map/near_sums/pallas_call | solution.py:225
  20.0 1.5 %first_term.1 = (f32[3456,128]{1,0:T(8,128)S(1)}, f32[3744,128]{1,0:T(8,128)S(1)}, bf16[288,128]{1,0:T(8,128)(2,1)S(1)}) custom-call(s32[288]{0:T(512)S(1)} %copy-done.7, f32[3456,128]{1,0:T(8,128)S(1)} %near_sums.2.sums_ref, bf16[288,128]{1,0:T(8,128)(2,1)S(1)} %collective-permute-done.1.back_ref), custom_call_target="tpu_custom_call" | custom-call | bytes 8388608 | tf_op jit(solution)/shard_map/first_term/pallas_call | solution.py:266
  21.5 1.3 %collective-permute-start.2 = (bf16[288,128]{1,0:T(8,128)(2,1)S(1)}, bf16[288,128]{1,0:T(8,128)(2,1)S(1)}, u32[]{:S(2)}, u32[]{:S(2)}) collective-permute-start(bf16[288,128]{1,0:T(8,128)(2,1)S(1)} %get-tuple-element.43), channel_id=1, source_target_pairs={{0,28},{4,0},{8,4},{12,8},{16,12},{20,16},{24,20},{28,24},{1,29},{... | collective-permute-start | bytes 221192 | tf_op jit(solution)/shard_map/ppermute | solution.py:30
  22.8 3.5 %near_products.3.products_ref = f32[8,344,128]{2,1,0:T(8,128)S(1)} custom-call(s32[4096]{0:T(1024)S(1)} %bitcast.5, f32[3744,128]{1,0:T(8,128)S(1)} %get-tuple-element.44.ext_ref, bf16[343,343]{1,0:T(8,128)(2,1)S(1)} %copy-done.1), custom_call_target="tpu_custom_call" | custom-call | bytes 14680064 | tf_op jit(solution)/shard_map/near_products/pallas_call | solution.py:198
  26.3 7.5 %far_cells.3 = (f32[3456,128]{1,0:T(8,128)S(1)}, bf16[288,128]{1,0:T(8,128)(2,1)S(1)}) custom-call(s32[4096]{0:T(1024)S(1)} %bitcast.6, f32[16]{0:T(128)S(1)} %copy-done.8, f32[3744,128]{1,0:T(8,128)S(1)} %get-tuple-element.44.ext_ref, bf16[288,128]{1,0:T(8,128)(2,1)S(1)} %collective-permute-done.2.ghost_ref, bf16[343,343]{1,0:T(8,128)(2,1)S(1)} %copy-done.1, ...), custom_call_target="tpu_custom_call" | custom-call | bytes 29360128 | tf_op jit(solution)/shard_map/far_cells/pallas_call | solution.py:209
  33.8 1.9 %collective-permute-start.3 = (bf16[288,128]{1,0:T(8,128)(2,1)S(1)}, bf16[288,128]{1,0:T(8,128)(2,1)S(1)}, u32[]{:S(2)}, u32[]{:S(2)}) collective-permute-start(bf16[288,128]{1,0:T(8,128)(2,1)S(1)} %get-tuple-element.49), channel_id=1, source_target_pairs={{0,4},{4,8},{8,12},{12,16},{16,20},{20,24},{24,28},{28,0},{1,5},{5... | collective-permute-start | bytes 221192 | tf_op jit(solution)/shard_map/ppermute | solution.py:30
  35.7 3.8 %near_sums.3.sums_ref = f32[3456,128]{1,0:T(8,128)S(1)} custom-call(s32[4096]{0:T(1024)S(1)} %bitcast.7, f32[16]{0:T(128)S(1)} %copy-done.8, f32[8,344,128]{2,1,0:T(8,128)S(1)} %near_products.3.products_ref, f32[3456,128]{1,0:T(8,128)S(1)} %get-tuple-element.48.start_ref), custom_call_target="tpu_custom_call" | custom-call | bytes 14680064 | tf_op jit(solution)/shard_map/near_sums/pallas_call | solution.py:225
  39.5 1.4 %second_term.1 = (bf16[864,128]{1,0:T(8,128)(2,1)S(1)}, bf16[864,128]{1,0:T(8,128)(2,1)S(1)}, bf16[864,128]{1,0:T(8,128)(2,1)S(1)}, bf16[864,128]{1,0:T(8,128)(2,1)S(1)}) custom-call(s32[288]{0:T(512)S(1)} %copy-done.7, f32[3456,128]{1,0:T(8,128)S(1)} %near_sums.3.sums_ref, bf16[288,128]{1,0:T(8,128)(2,1)S(1)} %collective-permute-done.3.back_ref, ...), custom_call_target="tpu_custom_call" | custom-call | bytes 6291456 | tf_op jit(solution)/shard_map/second_term/pallas_call | solution.py:296
  41.4 1.7 %collective-permute-start.5 = (bf16[864,128]{1,0:T(8,128)(2,1)S(1)}, bf16[864,128]{1,0:T(8,128)(2,1)S(1)}, u32[]{:S(2)}, u32[]{:S(2)}) collective-permute-start(bf16[864,128]{1,0:T(8,128)(2,1)S(1)} %get-tuple-element.52), channel_id=1, source_target_pairs={{0,2},{1,3},{2,0},{3,1},{4,6},{5,7},{6,4},{7,5},{8,10},{9,11},{10,... | collective-permute-start | bytes 663560 | tf_op jit(solution)/shard_map/ppermute | solution.py:30
  43.5 5.4 %collective-permute-done.4.refs_1_ = bf16[864,128]{1,0:T(8,128)(2,1)S(1)} collective-permute-done((bf16[864,128]{1,0:T(8,128)(2,1)S(1)}, bf16[864,128]{1,0:T(8,128)(2,1)S(1)}, u32[]{:S(2)}, u32[]{:S(2)}) %collective-permute-start.4) | collective-permute-done | bytes 221216 | tf_op jit(solution)/shard_map/ppermute | solution.py:30
  49.0 14.1 %collective-permute-done.5.refs_2_ = bf16[864,128]{1,0:T(8,128)(2,1)S(1)} collective-permute-done((bf16[864,128]{1,0:T(8,128)(2,1)S(1)}, bf16[864,128]{1,0:T(8,128)(2,1)S(1)}, u32[]{:S(2)}, u32[]{:S(2)}) %collective-permute-start.5) | collective-permute-done | bytes 221216 | tf_op jit(solution)/shard_map/ppermute | solution.py:30
  64.4 1.3 %collective-permute-start.12 = (bf16[2592,128]{1,0:T(8,128)(2,1)S(1)}, bf16[2592,128]{1,0:T(8,128)(2,1)S(1)}, u32[]{:S(2)}, u32[]{:S(2)}) collective-permute-start(bf16[2592,128]{1,0:T(8,128)(2,1)S(1)} %get-tuple-element.68), channel_id=1, source_target_pairs={{0,1},{1,2},{2,3},{4,5},{5,6},{6,7},{8,9},{9,10},{10,11},{12,13},{... | collective-permute-start | bytes 1990664 | tf_op jit(solution)/shard_map/ppermute | solution.py:398
  67.5 1.9 %collective-permute-start.8 = (f32[160,128]{1,0:T(8,128)S(1)}, f32[160,128]{1,0:T(8,128)S(1)}, u32[]{:S(2)}, u32[]{:S(2)}) collective-permute-start(f32[160,128]{1,0:T(8,128)S(1)} %get-tuple-element.61), channel_id=1, source_target_pairs={{0,8},{4,12},{8,0},{12,4},{16,24},{20,28},{24,16},{28,20},{1,9},{5... | collective-permute-start | bytes 245768 | tf_op jit(solution)/shard_map/ppermute | solution.py:391
  69.4 2.6 %collective-permute-done.10 = f32[160,128]{1,0:T(8,128)S(1)} collective-permute-done((f32[160,128]{1,0:T(8,128)S(1)}, f32[160,128]{1,0:T(8,128)S(1)}, u32[]{:S(2)}, u32[]{:S(2)}) %collective-permute-start.10) | collective-permute-done | bytes 81952 | tf_op jit(solution)/shard_map/ppermute | solution.py:391
  73.2 3.6 %collective-permute-start.11 = (f32[160,128]{1,0:T(8,128)S(1)}, f32[160,128]{1,0:T(8,128)S(1)}, u32[]{:S(2)}, u32[]{:S(2)}) collective-permute-start(f32[160,128]{1,0:T(8,128)S(1)} %add_add_fusion.1), channel_id=1, source_target_pairs={{0,1},{1,2},{2,3},{3,0},{4,5},{5,6},{6,7},{7,4},{8,9},{9,10},{10,1... | collective-permute-start | bytes 245768 | tf_op jit(solution)/shard_map/ppermute | solution.py:30
  77.7 7.7 %collective-permute-done.11 = f32[160,128]{1,0:T(8,128)S(1)} collective-permute-done((f32[160,128]{1,0:T(8,128)S(1)}, f32[160,128]{1,0:T(8,128)S(1)}, u32[]{:S(2)}, u32[]{:S(2)}) %collective-permute-start.11) | collective-permute-done | bytes 81952 | tf_op jit(solution)/shard_map/ppermute | solution.py:30
  85.5 1.3 %collective-permute-start.19 = (bf16[2592,128]{1,0:T(8,128)(2,1)S(1)}, bf16[2592,128]{1,0:T(8,128)(2,1)S(1)}, u32[]{:S(2)}, u32[]{:S(2)}) collective-permute-start(bf16[2592,128]{1,0:T(8,128)(2,1)S(1)} %pad_maximum_fusion.2), channel_id=1, source_target_pairs={{1,2},{2,3},{5,6},{6,7},{9,10},{10,11},{13,14},{14,15},{17,18},{18... | collective-permute-start | bytes 1990664 | tf_op jit(solution)/shard_map/ppermute | solution.py:398
  86.8 1.3 %collective-permute-start.20 = (bf16[1728,128]{1,0:T(8,128)(2,1)S(1)}, bf16[1728,128]{1,0:T(8,128)(2,1)S(1)}, u32[]{:S(2)}, u32[]{:S(2)}) collective-permute-start(bf16[1728,128]{1,0:T(8,128)(2,1)S(1)} %pad_maximum_fusion.3), channel_id=1, source_target_pairs={{1,3},{5,7},{9,11},{13,15},{17,19},{21,23},{25,27},{29,31}} | collective-permute-start | bytes 1327112 | tf_op jit(solution)/shard_map/ppermute | solution.py:430
  88.6 2.0 %collective-permute-done.13 = f32[160,128]{1,0:T(8,128)S(1)} collective-permute-done((f32[160,128]{1,0:T(8,128)S(1)}, f32[160,128]{1,0:T(8,128)S(1)}, u32[]{:S(2)}, u32[]{:S(2)}) %collective-permute-start.13) | collective-permute-done | bytes 81952 | tf_op jit(solution)/shard_map/ppermute | solution.py:30
  90.8 1.6 %collective-permute-start.16 = (f32[160,128]{1,0:T(8,128)S(1)}, f32[160,128]{1,0:T(8,128)S(1)}, u32[]{:S(2)}, u32[]{:S(2)}) collective-permute-start(f32[160,128]{1,0:T(8,128)S(1)} %add_add_fusion.refs_0_), channel_id=1, source_target_pairs={{0,16},{4,20},{8,24},{12,28},{16,0},{20,4},{24,8},{28,12},{1,17},{... | collective-permute-start | bytes 245768 | tf_op jit(solution)/shard_map/ppermute | solution.py:391
  92.3 1.9 %collective-permute-start.17 = (f32[160,128]{1,0:T(8,128)S(1)}, f32[160,128]{1,0:T(8,128)S(1)}, u32[]{:S(2)}, u32[]{:S(2)}) collective-permute-start(f32[160,128]{1,0:T(8,128)S(1)} %add_add_fusion.refs_0_), channel_id=1, source_target_pairs={{0,24},{4,28},{8,16},{12,20},{16,8},{20,12},{24,0},{28,4},{1,25},{... | collective-permute-start | bytes 245768 | tf_op jit(solution)/shard_map/ppermute | solution.py:391
  94.2 1.7 %collective-permute-done.15.refs_1_ = f32[160,128]{1,0:T(8,128)S(1)} collective-permute-done((f32[160,128]{1,0:T(8,128)S(1)}, f32[160,128]{1,0:T(8,128)S(1)}, u32[]{:S(2)}, u32[]{:S(2)}) %collective-permute-start.15) | collective-permute-done | bytes 81952 | tf_op jit(solution)/shard_map/ppermute | solution.py:391
  95.9 1.8 %collective-permute-done.17.refs_3_ = f32[160,128]{1,0:T(8,128)S(1)} collective-permute-done((f32[160,128]{1,0:T(8,128)S(1)}, f32[160,128]{1,0:T(8,128)S(1)}, u32[]{:S(2)}, u32[]{:S(2)}) %collective-permute-start.17) | collective-permute-done | bytes 81952 | tf_op jit(solution)/shard_map/ppermute | solution.py:391
  97.8 1.3 %collective-permute-start.21 = (bf16[864,128]{1,0:T(8,128)(2,1)S(1)}, bf16[864,128]{1,0:T(8,128)(2,1)S(1)}, u32[]{:S(2)}, u32[]{:S(2)}) collective-permute-start(bf16[864,128]{1,0:T(8,128)(2,1)S(1)} %collective-permute-done.5.refs_2_), channel_id=1, source_target_pairs={{2,3},{6,7},{10,11},{14,15},{18,19},{22,23},{26,27},{30,31}} | collective-permute-start | bytes 663560 | tf_op jit(solution)/shard_map/ppermute | solution.py:403
  99.5 13.4 %inverse_factor.1.factor_ref = f32[512,512]{1,0:T(8,128)S(1)} custom-call(f32[640,128]{1,0:T(8,128)S(1)} %joined.1.mine_ref, f32[640,128]{1,0:T(8,128)S(1)} %collective-permute-done.18.other_ref), custom_call_target="tpu_custom_call" | custom-call | bytes 73400320 | tf_op jit(solution)/shard_map/inverse_factor/pallas_call | solution.py:570
  113.8 4.2 %collective-permute-done.21.refs_2_ = bf16[864,128]{1,0:T(8,128)(2,1)S(1)} collective-permute-done((bf16[864,128]{1,0:T(8,128)(2,1)S(1)}, bf16[864,128]{1,0:T(8,128)(2,1)S(1)}, u32[]{:S(2)}, u32[]{:S(2)}) %collective-permute-start.21) | collective-permute-done | bytes 221216 | tf_op jit(solution)/shard_map/ppermute | solution.py:403
  118.0 1.6 %output_late.1 = f32[3456,128]{1,0:T(8,128)} custom-call(f32[512,512]{1,0:T(8,128)S(1)} %inverse_factor.1.factor_ref, f32[4,864,128]{2,1,0:T(8,128)S(1)} %output_early.1.early_ref, bf16[2592,128]{1,0:T(8,128)(2,1)S(1)} %collective-permute-done.19.refs_0_, bf16[1728,128]{1,0:T(8,128)(2,1)S(1)} %collective-permute-done.20.refs_1_, ...), custom_call_target="tpu_custom_call" | custom-call | bytes 6291456 | tf_op jit(solution)/shard_map/output_late/pallas_call | solution.py:661
  (52 shorter events, 10.2 us)
Async XLA Ops:
  0.0 1.2 copy-start.2
  1.2 0.7 copy-start.5
  1.9 0.7 copy-start.6
  3.5 4.6 %collective-permute-start = (bf16[288,128]{1,0:T(8,128)(2,1)S(1)}, bf16[288,128]{1,0:T(8,128)(2,1)S(1)}, u32[]{:S(2)}, u32[]{:S(2)}) collective-permute-start(bf16[288,128]{1,0:T(8,128)(2,1)S(1)} %get-tuple-element.37), channel_id=1, source_target_pairs={{0,28},{4,0},{8,4},{12,8},{16,12},{20,16},{24,20},{28,24},{1,29},{... | collective-permute-start | bytes 221192 | tf_op jit(solution)/shard_map/ppermute | solution.py:30
  3.6 1.0 copy-start
  4.6 3.6 %copy-start.1 = (bf16[343,343]{1,0:T(8,128)(2,1)S(1)}, bf16[343,343]{1,0:T(8,128)(2,1)}, u32[]{:S(2)}) copy-start(bf16[343,343]{1,0:T(8,128)(2,1)} %matrix_ref.7) | copy-start | bytes 705898
  4.6 3.6 %copy-start.4 = (f32[3456]{0:T(1024)S(1)}, f32[3456]{0:T(1024)}, u32[]{:S(2)}) copy-start(f32[3456]{0:T(1024)} %param.9) | copy-start | bytes 41476
  4.6 3.6 %copy-start.8 = (f32[16]{0:T(128)S(1)}, f32[16]{0:T(128)}, u32[]{:S(2)}) copy-start(f32[16]{0:T(128)} %scale_ref.3) | copy-start | bytes 196
  15.6 4.4 %collective-permute-start.1 = (bf16[288,128]{1,0:T(8,128)(2,1)S(1)}, bf16[288,128]{1,0:T(8,128)(2,1)S(1)}, u32[]{:S(2)}, u32[]{:S(2)}) collective-permute-start(bf16[288,128]{1,0:T(8,128)(2,1)S(1)} %get-tuple-element.42), channel_id=1, source_target_pairs={{0,4},{4,8},{8,12},{12,16},{16,20},{20,24},{24,28},{28,0},{1,5},{5... | collective-permute-start | bytes 221192 | tf_op jit(solution)/shard_map/ppermute | solution.py:30
  16.2 3.8 %copy-start.7 = (s32[288]{0:T(512)S(1)}, s32[288]{0:T(512)}, u32[]{:S(2)}) copy-start(s32[288]{0:T(512)} %nodes.5) | copy-start | bytes 3460
  21.5 4.9 %collective-permute-start.2 = (bf16[288,128]{1,0:T(8,128)(2,1)S(1)}, bf16[288,128]{1,0:T(8,128)(2,1)S(1)}, u32[]{:S(2)}, u32[]{:S(2)}) collective-permute-start(bf16[288,128]{1,0:T(8,128)(2,1)S(1)} %get-tuple-element.43), channel_id=1, source_target_pairs={{0,28},{4,0},{8,4},{12,8},{16,12},{20,16},{24,20},{28,24},{1,29},{... | collective-permute-start | bytes 221192 | tf_op jit(solution)/shard_map/ppermute | solution.py:30
  33.8 5.7 %collective-permute-start.3 = (bf16[288,128]{1,0:T(8,128)(2,1)S(1)}, bf16[288,128]{1,0:T(8,128)(2,1)S(1)}, u32[]{:S(2)}, u32[]{:S(2)}) collective-permute-start(bf16[288,128]{1,0:T(8,128)(2,1)S(1)} %get-tuple-element.49), channel_id=1, source_target_pairs={{0,4},{4,8},{8,12},{12,16},{16,20},{20,24},{24,28},{28,0},{1,5},{5... | collective-permute-start | bytes 221192 | tf_op jit(solution)/shard_map/ppermute | solution.py:30
  35.7 3.8 %copy-start.3 = (bf16[3456,128]{1,0:T(8,128)(2,1)S(1)}, bf16[3456,128]{1,0:T(8,128)(2,1)}, u32[]{:S(2)}) copy-start(bf16[3456,128]{1,0:T(8,128)(2,1)} %previous_ref.1) | copy-start | bytes 2654212
  40.9 8.0 %collective-permute-start.4 = (bf16[864,128]{1,0:T(8,128)(2,1)S(1)}, bf16[864,128]{1,0:T(8,128)(2,1)S(1)}, u32[]{:S(2)}, u32[]{:S(2)}) collective-permute-start(bf16[864,128]{1,0:T(8,128)(2,1)S(1)} %get-tuple-element.51), channel_id=1, source_target_pairs={{0,1},{1,2},{2,3},{3,0},{4,5},{5,6},{6,7},{7,4},{8,9},{9,10},{10,1... | collective-permute-start | bytes 663560 | tf_op jit(solution)/shard_map/ppermute | solution.py:30
  41.4 21.7 %collective-permute-start.5 = (bf16[864,128]{1,0:T(8,128)(2,1)S(1)}, bf16[864,128]{1,0:T(8,128)(2,1)S(1)}, u32[]{:S(2)}, u32[]{:S(2)}) collective-permute-start(bf16[864,128]{1,0:T(8,128)(2,1)S(1)} %get-tuple-element.52), channel_id=1, source_target_pairs={{0,2},{1,3},{2,0},{3,1},{4,6},{5,7},{6,4},{7,5},{8,10},{9,11},{10,... | collective-permute-start | bytes 663560 | tf_op jit(solution)/shard_map/ppermute | solution.py:30
  43.1 20.0 %collective-permute-start.6 = (bf16[864,128]{1,0:T(8,128)(2,1)S(1)}, bf16[864,128]{1,0:T(8,128)(2,1)S(1)}, u32[]{:S(2)}, u32[]{:S(2)}) collective-permute-start(bf16[864,128]{1,0:T(8,128)(2,1)S(1)} %get-tuple-element.53), channel_id=1, source_target_pairs={{0,3},{1,0},{2,1},{3,2},{4,7},{5,4},{6,5},{7,6},{8,11},{9,8},{10,9... | collective-permute-start | bytes 663560 | tf_op jit(solution)/shard_map/ppermute | solution.py:30
  64.0 1.8 %collective-permute-start.7 = (f32[640,128]{1,0:T(8,128)S(1)}, f32[640,128]{1,0:T(8,128)S(1)}, u32[]{:S(2)}, u32[]{:S(2)}) collective-permute-start(f32[640,128]{1,0:T(8,128)S(1)} %get-tuple-element.59), channel_id=1, source_target_pairs={{0,4},{4,0},{8,12},{12,8},{16,20},{20,16},{24,28},{28,24},{1,5},{5... | collective-permute-start | bytes 983048 | tf_op jit(solution)/shard_map/ppermute | solution.py:391
  64.4 20.9 %collective-permute-start.12 = (bf16[2592,128]{1,0:T(8,128)(2,1)S(1)}, bf16[2592,128]{1,0:T(8,128)(2,1)S(1)}, u32[]{:S(2)}, u32[]{:S(2)}) collective-permute-start(bf16[2592,128]{1,0:T(8,128)(2,1)S(1)} %get-tuple-element.68), channel_id=1, source_target_pairs={{0,1},{1,2},{2,3},{4,5},{5,6},{6,7},{8,9},{9,10},{10,11},{12,13},{... | collective-permute-start | bytes 1990664 | tf_op jit(solution)/shard_map/ppermute | solution.py:398
  65.8 6.1 %collective-permute-start.10 = (f32[160,128]{1,0:T(8,128)S(1)}, f32[160,128]{1,0:T(8,128)S(1)}, u32[]{:S(2)}, u32[]{:S(2)}) collective-permute-start(f32[160,128]{1,0:T(8,128)S(1)} %get-tuple-element.63), channel_id=1, source_target_pairs={{0,24},{4,28},{8,16},{12,20},{16,8},{20,12},{24,0},{28,4},{1,25},{... | collective-permute-start | bytes 245768 | tf_op jit(solution)/shard_map/ppermute | solution.py:391
  66.6 6.1 %collective-permute-start.9 = (f32[160,128]{1,0:T(8,128)S(1)}, f32[160,128]{1,0:T(8,128)S(1)}, u32[]{:S(2)}, u32[]{:S(2)}) collective-permute-start(f32[160,128]{1,0:T(8,128)S(1)} %get-tuple-element.62), channel_id=1, source_target_pairs={{0,16},{4,20},{8,24},{12,28},{16,0},{20,4},{24,8},{28,12},{1,17},{... | collective-permute-start | bytes 245768 | tf_op jit(solution)/shard_map/ppermute | solution.py:391
  67.5 5.7 %collective-permute-start.8 = (f32[160,128]{1,0:T(8,128)S(1)}, f32[160,128]{1,0:T(8,128)S(1)}, u32[]{:S(2)}, u32[]{:S(2)}) collective-permute-start(f32[160,128]{1,0:T(8,128)S(1)} %get-tuple-element.61), channel_id=1, source_target_pairs={{0,8},{4,12},{8,0},{12,4},{16,24},{20,28},{24,16},{28,20},{1,9},{5... | collective-permute-start | bytes 245768 | tf_op jit(solution)/shard_map/ppermute | solution.py:391
  73.2 12.1 %collective-permute-start.11 = (f32[160,128]{1,0:T(8,128)S(1)}, f32[160,128]{1,0:T(8,128)S(1)}, u32[]{:S(2)}, u32[]{:S(2)}) collective-permute-start(f32[160,128]{1,0:T(8,128)S(1)} %add_add_fusion.1), channel_id=1, source_target_pairs={{0,1},{1,2},{2,3},{3,0},{4,5},{5,6},{6,7},{7,4},{8,9},{9,10},{10,1... | collective-permute-start | bytes 245768 | tf_op jit(solution)/shard_map/ppermute | solution.py:30
  76.9 11.8 %collective-permute-start.14 = (f32[160,128]{1,0:T(8,128)S(1)}, f32[160,128]{1,0:T(8,128)S(1)}, u32[]{:S(2)}, u32[]{:S(2)}) collective-permute-start(f32[160,128]{1,0:T(8,128)S(1)} %add_add_fusion.1), channel_id=1, source_target_pairs={{0,3},{1,0},{2,1},{3,2},{4,7},{5,4},{6,5},{7,6},{8,11},{9,8},{10,9... | collective-permute-start | bytes 245768 | tf_op jit(solution)/shard_map/ppermute | solution.py:30
  76.9 13.8 %collective-permute-start.13 = (f32[160,128]{1,0:T(8,128)S(1)}, f32[160,128]{1,0:T(8,128)S(1)}, u32[]{:S(2)}, u32[]{:S(2)}) collective-permute-start(f32[160,128]{1,0:T(8,128)S(1)} %add_add_fusion.1), channel_id=1, source_target_pairs={{0,2},{1,3},{2,0},{3,1},{4,6},{5,7},{6,4},{7,5},{8,10},{9,11},{10,... | collective-permute-start | bytes 245768 | tf_op jit(solution)/shard_map/ppermute | solution.py:30
  85.5 32.5 %collective-permute-start.19 = (bf16[2592,128]{1,0:T(8,128)(2,1)S(1)}, bf16[2592,128]{1,0:T(8,128)(2,1)S(1)}, u32[]{:S(2)}, u32[]{:S(2)}) collective-permute-start(bf16[2592,128]{1,0:T(8,128)(2,1)S(1)} %pad_maximum_fusion.2), channel_id=1, source_target_pairs={{1,2},{2,3},{5,6},{6,7},{9,10},{10,11},{13,14},{14,15},{17,18},{18... | collective-permute-start | bytes 1990664 | tf_op jit(solution)/shard_map/ppermute | solution.py:398
  86.8 31.1 %collective-permute-start.20 = (bf16[1728,128]{1,0:T(8,128)(2,1)S(1)}, bf16[1728,128]{1,0:T(8,128)(2,1)S(1)}, u32[]{:S(2)}, u32[]{:S(2)}) collective-permute-start(bf16[1728,128]{1,0:T(8,128)(2,1)S(1)} %pad_maximum_fusion.3), channel_id=1, source_target_pairs={{1,3},{5,7},{9,11},{13,15},{17,19},{21,23},{25,27},{29,31}} | collective-permute-start | bytes 1327112 | tf_op jit(solution)/shard_map/ppermute | solution.py:430
  90.7 5.2 %collective-permute-start.15 = (f32[160,128]{1,0:T(8,128)S(1)}, f32[160,128]{1,0:T(8,128)S(1)}, u32[]{:S(2)}, u32[]{:S(2)}) collective-permute-start(f32[160,128]{1,0:T(8,128)S(1)} %add_add_fusion.refs_0_), channel_id=1, source_target_pairs={{0,8},{4,12},{8,0},{12,4},{16,24},{20,28},{24,16},{28,20},{1,9},{5... | collective-permute-start | bytes 245768 | tf_op jit(solution)/shard_map/ppermute | solution.py:391
  90.8 5.1 %collective-permute-start.16 = (f32[160,128]{1,0:T(8,128)S(1)}, f32[160,128]{1,0:T(8,128)S(1)}, u32[]{:S(2)}, u32[]{:S(2)}) collective-permute-start(f32[160,128]{1,0:T(8,128)S(1)} %add_add_fusion.refs_0_), channel_id=1, source_target_pairs={{0,16},{4,20},{8,24},{12,28},{16,0},{20,4},{24,8},{28,12},{1,17},{... | collective-permute-start | bytes 245768 | tf_op jit(solution)/shard_map/ppermute | solution.py:391
  92.3 5.4 %collective-permute-start.17 = (f32[160,128]{1,0:T(8,128)S(1)}, f32[160,128]{1,0:T(8,128)S(1)}, u32[]{:S(2)}, u32[]{:S(2)}) collective-permute-start(f32[160,128]{1,0:T(8,128)S(1)} %add_add_fusion.refs_0_), channel_id=1, source_target_pairs={{0,24},{4,28},{8,16},{12,20},{16,8},{20,12},{24,0},{28,4},{1,25},{... | collective-permute-start | bytes 245768 | tf_op jit(solution)/shard_map/ppermute | solution.py:391
  97.8 1.7 %collective-permute-start.18 = (f32[640,128]{1,0:T(8,128)S(1)}, f32[640,128]{1,0:T(8,128)S(1)}, u32[]{:S(2)}, u32[]{:S(2)}) collective-permute-start(f32[640,128]{1,0:T(8,128)S(1)} %joined.1.mine_ref), channel_id=1, source_target_pairs={{0,4},{4,0},{8,12},{12,8},{16,20},{20,16},{24,28},{28,24},{1,5},{5... | collective-permute-start | bytes 983048 | tf_op jit(solution)/shard_map/ppermute | solution.py:391
  97.8 20.1 %collective-permute-start.21 = (bf16[864,128]{1,0:T(8,128)(2,1)S(1)}, bf16[864,128]{1,0:T(8,128)(2,1)S(1)}, u32[]{:S(2)}, u32[]{:S(2)}) collective-permute-start(bf16[864,128]{1,0:T(8,128)(2,1)S(1)} %collective-permute-done.5.refs_2_), channel_id=1, source_target_pairs={{2,3},{6,7},{10,11},{14,15},{18,19},{22,23},{26,27},{30,31}} | collective-permute-start | bytes 663560 | tf_op jit(solution)/shard_map/ppermute | solution.py:403

commit v11 on v9

--- a/solution.py
+++ b/solution.py
@@ -241,7 +241,7 @@
     scaled[...] = back_ref[...].astype(F32) * factor
 
     def body(step, _):
-        at = [step * 16 + k for k in range(16)]
+        at = [step * 8 + k for k in range(8)]
         rows = [pl.ds(nodes[i], 1) for i in at]
         new = [target[r, :] + scaled[pl.ds(i, 1), :] for i, r in zip(at, rows)]
         for i, r, value in zip(at, rows, new):
@@ -250,7 +250,7 @@
                 picked[pl.ds(i, 1), :] = value
         return 0
 
-    lax.fori_loop(0, nodes.shape[0] // 16, body, 0)
+    lax.fori_loop(0, nodes.shape[0] // 8, body, 0)
 
 
 def first_kernel(nodes, sums_ref, back_ref, term_ref, ext_ref, edge_ref, scaled, picked):

time: 120 us -> 120 us (level)
  no operation moved by 1% of the time
where the time goes in v11:
time: 120 us
  Pallas kernels  50.2 us (42%)
  waiting for transfers between devices  41.6 us (35%)
  starting transfers between devices  23.5 us (20%)
  local copies, waits for them, and re-layouts  3.62 us (3%)
    ppermute x10, waiting for transfers between devices, shifted(): lax.ppermute(value, axis, [(i, (i + steps) % count) for i in range(count)])  29.7 us
    pallas_call x2, Pallas kernels, apply_operator(): pl.pallas_call(far_cells_kernel, out_shape=(jax.ShapeDtypeStruct((owned,...  14.9 us
    pallas_call x1, Pallas kernels, inverse_factor(): pl.pallas_call(functools.partial(inverse_kernel, over), out_shape=jax.Sha...  13.4 us
    ppermute x10, starting transfers between devices, shifted(): lax.ppermute(value, axis, [(i, (i + steps) % count) for i in range(count)])  10.8 us
    ppermute x8, waiting for transfers between devices, paired(): return lax.ppermute(value, axis, [(i, i ^ mask) for i in range(count)])  7.69 us
    ppermute x8, starting transfers between devices, paired(): return lax.ppermute(value, axis, [(i, i ^ mask) for i in range(count)])  7.56 us
    pallas_call x2, Pallas kernels, apply_operator(): pl.pallas_call(functools.partial(near_sums_kernel, npc), out_shape=jax.Sh...  7.55 us
    pallas_call x2, Pallas kernels, apply_operator(): pl.pallas_call(near_products_kernel, out_shape=jax.ShapeDtypeStruct(held,...  7.09 us
  transfers between devices with their start and end apart: 22, of which 12 were waited for; matrix products, arithmetic and copies ran while one was open for 0% of the time, Pallas kernels for 24%

profile of v11, /device:TPU:26, one launch (start us, length us, event | category | flops | bytes accessed | tf_op | source)
XLA Modules:
  0.0 119.5 jit_solution(14168005551130094327)
XLA Ops:
  0.0 1.2 copy-done.2
  2.6 1.0 prepare.1
  3.7 0.9 copy-done
  4.6 3.5 %near_products.2.products_ref = f32[8,344,128]{2,1,0:T(8,128)S(1)} custom-call(s32[4096]{0:T(1024)S(1)} %bitcast.2, f32[3744,128]{1,0:T(8,128)S(1)} %get-tuple-element.39.ext_ref.wide_ref, bf16[343,343]{1,0:T(8,128)(2,1)S(1)} %copy-done), custom_call_target="tpu_custom_call" | custom-call | bytes 14680064 | tf_op jit(solution)/shard_map/near_products/pallas_call | solution.py:198
  8.2 7.5 %far_cells.2 = (f32[3456,128]{1,0:T(8,128)S(1)}, bf16[288,128]{1,0:T(8,128)(2,1)S(1)}) custom-call(s32[4096]{0:T(1024)S(1)} %bitcast.3, f32[16]{0:T(128)S(1)} %copy-done.8, f32[3744,128]{1,0:T(8,128)S(1)} %get-tuple-element.39.ext_ref.wide_ref, bf16[288,128]{1,0:T(8,128)(2,1)S(1)} %collective-permute-done.ghost_ref, bf16[343,343]{1,0:T(8,128)(2,1)S(1)} %copy-done.1, ...), custom_call_target="tpu_custom_call" | custom-call | bytes 29360128 | tf_op jit(solution)/shard_map/far_cells/pallas_call | solution.py:209
  16.2 3.8 %near_sums.2.sums_ref = f32[3456,128]{1,0:T(8,128)S(1)} custom-call(s32[4096]{0:T(1024)S(1)} %bitcast.4, f32[16]{0:T(128)S(1)} %copy-done.8, f32[8,344,128]{2,1,0:T(8,128)S(1)} %near_products.2.products_ref, f32[3456,128]{1,0:T(8,128)S(1)} %get-tuple-element.42.start_ref), custom_call_target="tpu_custom_call" | custom-call | bytes 14680064 | tf_op jit(solution)/shard_map/near_sums/pallas_call | solution.py:225
  20.1 1.4 %first_term.1 = (f32[3456,128]{1,0:T(8,128)S(1)}, f32[3744,128]{1,0:T(8,128)S(1)}, bf16[288,128]{1,0:T(8,128)(2,1)S(1)}) custom-call(s32[288]{0:T(512)S(1)} %copy-done.7, f32[3456,128]{1,0:T(8,128)S(1)} %near_sums.2.sums_ref, bf16[288,128]{1,0:T(8,128)(2,1)S(1)} %collective-permute-done.1.back_ref), custom_call_target="tpu_custom_call" | custom-call | bytes 8388608 | tf_op jit(solution)/shard_map/first_term/pallas_call | solution.py:266
  21.4 1.3 %collective-permute-start.2 = (bf16[288,128]{1,0:T(8,128)(2,1)S(1)}, bf16[288,128]{1,0:T(8,128)(2,1)S(1)}, u32[]{:S(2)}, u32[]{:S(2)}) collective-permute-start(bf16[288,128]{1,0:T(8,128)(2,1)S(1)} %get-tuple-element.44), channel_id=1, source_target_pairs={{0,28},{4,0},{8,4},{12,8},{16,12},{20,16},{24,20},{28,24},{1,29},{... | collective-permute-start | bytes 221192 | tf_op jit(solution)/shard_map/ppermute | solution.py:30
  22.7 3.5 %near_products.3.products_ref = f32[8,344,128]{2,1,0:T(8,128)S(1)} custom-call(s32[4096]{0:T(1024)S(1)} %bitcast.5, f32[3744,128]{1,0:T(8,128)S(1)} %get-tuple-element.45.ext_ref, bf16[343,343]{1,0:T(8,128)(2,1)S(1)} %copy-done.1), custom_call_target="tpu_custom_call" | custom-call | bytes 14680064 | tf_op jit(solution)/shard_map/near_products/pallas_call | solution.py:198
  26.3 7.5 %far_cells.3 = (f32[3456,128]{1,0:T(8,128)S(1)}, bf16[288,128]{1,0:T(8,128)(2,1)S(1)}) custom-call(s32[4096]{0:T(1024)S(1)} %bitcast.6, f32[16]{0:T(128)S(1)} %copy-done.8, f32[3744,128]{1,0:T(8,128)S(1)} %get-tuple-element.45.ext_ref, bf16[288,128]{1,0:T(8,128)(2,1)S(1)} %collective-permute-done.2.ghost_ref, bf16[343,343]{1,0:T(8,128)(2,1)S(1)} %copy-done.1, ...), custom_call_target="tpu_custom_call" | custom-call | bytes 29360128 | tf_op jit(solution)/shard_map/far_cells/pallas_call | solution.py:209
  33.8 1.9 %collective-permute-start.3 = (bf16[288,128]{1,0:T(8,128)(2,1)S(1)}, bf16[288,128]{1,0:T(8,128)(2,1)S(1)}, u32[]{:S(2)}, u32[]{:S(2)}) collective-permute-start(bf16[288,128]{1,0:T(8,128)(2,1)S(1)} %get-tuple-element.50), channel_id=1, source_target_pairs={{0,4},{4,8},{8,12},{12,16},{16,20},{20,24},{24,28},{28,0},{1,5},{5... | collective-permute-start | bytes 221192 | tf_op jit(solution)/shard_map/ppermute | solution.py:30
  35.7 3.7 %near_sums.3.sums_ref = f32[3456,128]{1,0:T(8,128)S(1)} custom-call(s32[4096]{0:T(1024)S(1)} %bitcast.7, f32[16]{0:T(128)S(1)} %copy-done.8, f32[8,344,128]{2,1,0:T(8,128)S(1)} %near_products.3.products_ref, f32[3456,128]{1,0:T(8,128)S(1)} %get-tuple-element.49.start_ref), custom_call_target="tpu_custom_call" | custom-call | bytes 14680064 | tf_op jit(solution)/shard_map/near_sums/pallas_call | solution.py:225
  39.4 1.4 %second_term.1 = (bf16[864,128]{1,0:T(8,128)(2,1)S(1)}, bf16[864,128]{1,0:T(8,128)(2,1)S(1)}, bf16[864,128]{1,0:T(8,128)(2,1)S(1)}, bf16[864,128]{1,0:T(8,128)(2,1)S(1)}, bf16[2592,128]{1,0:T(8,128)(2,1)S(1)}) custom-call(s32[288]{0:T(512)S(1)} %copy-done.7, f32[3456,128]{1,0:T(8,128)S(1)} %near_sums.3.sums_ref, ...), custom_call_target="tpu_custom_call" | custom-call | bytes 6291456 | tf_op jit(solution)/shard_map/second_term/pallas_call | solution.py:299
  41.3 1.7 %collective-permute-start.5 = (bf16[864,128]{1,0:T(8,128)(2,1)S(1)}, bf16[864,128]{1,0:T(8,128)(2,1)S(1)}, u32[]{:S(2)}, u32[]{:S(2)}) collective-permute-start(bf16[864,128]{1,0:T(8,128)(2,1)S(1)} %get-tuple-element.53), channel_id=1, source_target_pairs={{0,2},{1,3},{2,0},{3,1},{4,6},{5,7},{6,4},{7,5},{8,10},{9,11},{10,... | collective-permute-start | bytes 663560 | tf_op jit(solution)/shard_map/ppermute | solution.py:30
  43.4 5.4 %collective-permute-done.4.refs_1_ = bf16[864,128]{1,0:T(8,128)(2,1)S(1)} collective-permute-done((bf16[864,128]{1,0:T(8,128)(2,1)S(1)}, bf16[864,128]{1,0:T(8,128)(2,1)S(1)}, u32[]{:S(2)}, u32[]{:S(2)}) %collective-permute-start.4) | collective-permute-done | bytes 221216 | tf_op jit(solution)/shard_map/ppermute | solution.py:30
  48.8 14.1 %collective-permute-done.5.refs_2_ = bf16[864,128]{1,0:T(8,128)(2,1)S(1)} collective-permute-done((bf16[864,128]{1,0:T(8,128)(2,1)S(1)}, bf16[864,128]{1,0:T(8,128)(2,1)S(1)}, u32[]{:S(2)}, u32[]{:S(2)}) %collective-permute-start.5) | collective-permute-done | bytes 221216 | tf_op jit(solution)/shard_map/ppermute | solution.py:30
  64.3 1.3 %collective-permute-start.12 = (bf16[2592,128]{1,0:T(8,128)(2,1)S(1)}, bf16[2592,128]{1,0:T(8,128)(2,1)S(1)}, u32[]{:S(2)}, u32[]{:S(2)}) collective-permute-start(bf16[2592,128]{1,0:T(8,128)(2,1)S(1)} %pad_maximum_fusion), channel_id=1, source_target_pairs={{0,1},{1,2},{2,3},{4,5},{5,6},{6,7},{8,9},{9,10},{10,11},{12,13},{... | collective-permute-start | bytes 1990664 | tf_op jit(solution)/shard_map/ppermute | solution.py:402
  67.3 1.9 %collective-permute-start.8 = (f32[160,128]{1,0:T(8,128)S(1)}, f32[160,128]{1,0:T(8,128)S(1)}, u32[]{:S(2)}, u32[]{:S(2)}) collective-permute-start(f32[160,128]{1,0:T(8,128)S(1)} %get-tuple-element.62), channel_id=1, source_target_pairs={{0,8},{4,12},{8,0},{12,4},{16,24},{20,28},{24,16},{28,20},{1,9},{5... | collective-permute-start | bytes 245768 | tf_op jit(solution)/shard_map/ppermute | solution.py:395
  69.2 2.6 %collective-permute-done.10 = f32[160,128]{1,0:T(8,128)S(1)} collective-permute-done((f32[160,128]{1,0:T(8,128)S(1)}, f32[160,128]{1,0:T(8,128)S(1)}, u32[]{:S(2)}, u32[]{:S(2)}) %collective-permute-start.10) | collective-permute-done | bytes 81952 | tf_op jit(solution)/shard_map/ppermute | solution.py:395
  73.1 3.6 %collective-permute-start.11 = (f32[160,128]{1,0:T(8,128)S(1)}, f32[160,128]{1,0:T(8,128)S(1)}, u32[]{:S(2)}, u32[]{:S(2)}) collective-permute-start(f32[160,128]{1,0:T(8,128)S(1)} %add_add_fusion.1), channel_id=1, source_target_pairs={{0,1},{1,2},{2,3},{3,0},{4,5},{5,6},{6,7},{7,4},{8,9},{9,10},{10,1... | collective-permute-start | bytes 245768 | tf_op jit(solution)/shard_map/ppermute | solution.py:30
  77.5 7.7 %collective-permute-done.11 = f32[160,128]{1,0:T(8,128)S(1)} collective-permute-done((f32[160,128]{1,0:T(8,128)S(1)}, f32[160,128]{1,0:T(8,128)S(1)}, u32[]{:S(2)}, u32[]{:S(2)}) %collective-permute-start.11) | collective-permute-done | bytes 81952 | tf_op jit(solution)/shard_map/ppermute | solution.py:30
  85.3 1.3 %collective-permute-start.19 = (bf16[2592,128]{1,0:T(8,128)(2,1)S(1)}, bf16[2592,128]{1,0:T(8,128)(2,1)S(1)}, u32[]{:S(2)}, u32[]{:S(2)}) collective-permute-start(bf16[2592,128]{1,0:T(8,128)(2,1)S(1)} %pad_maximum_fusion.1), channel_id=1, source_target_pairs={{1,2},{2,3},{5,6},{6,7},{9,10},{10,11},{13,14},{14,15},{17,18},{18... | collective-permute-start | bytes 1990664 | tf_op jit(solution)/shard_map/ppermute | solution.py:402
  86.6 1.3 %collective-permute-start.20 = (bf16[1728,128]{1,0:T(8,128)(2,1)S(1)}, bf16[1728,128]{1,0:T(8,128)(2,1)S(1)}, u32[]{:S(2)}, u32[]{:S(2)}) collective-permute-start(bf16[1728,128]{1,0:T(8,128)(2,1)S(1)} %pad_maximum_fusion.2), channel_id=1, source_target_pairs={{1,3},{5,7},{9,11},{13,15},{17,19},{21,23},{25,27},{29,31}} | collective-permute-start | bytes 1327112 | tf_op jit(solution)/shard_map/ppermute | solution.py:434
  88.5 2.0 %collective-permute-done.13 = f32[160,128]{1,0:T(8,128)S(1)} collective-permute-done((f32[160,128]{1,0:T(8,128)S(1)}, f32[160,128]{1,0:T(8,128)S(1)}, u32[]{:S(2)}, u32[]{:S(2)}) %collective-permute-start.13) | collective-permute-done | bytes 81952 | tf_op jit(solution)/shard_map/ppermute | solution.py:30
  90.6 1.6 %collective-permute-start.16 = (f32[160,128]{1,0:T(8,128)S(1)}, f32[160,128]{1,0:T(8,128)S(1)}, u32[]{:S(2)}, u32[]{:S(2)}) collective-permute-start(f32[160,128]{1,0:T(8,128)S(1)} %add_add_fusion.refs_0_), channel_id=1, source_target_pairs={{0,16},{4,20},{8,24},{12,28},{16,0},{20,4},{24,8},{28,12},{1,17},{... | collective-permute-start | bytes 245768 | tf_op jit(solution)/shard_map/ppermute | solution.py:395
  92.2 1.9 %collective-permute-start.17 = (f32[160,128]{1,0:T(8,128)S(1)}, f32[160,128]{1,0:T(8,128)S(1)}, u32[]{:S(2)}, u32[]{:S(2)}) collective-permute-start(f32[160,128]{1,0:T(8,128)S(1)} %add_add_fusion.refs_0_), channel_id=1, source_target_pairs={{0,24},{4,28},{8,16},{12,20},{16,8},{20,12},{24,0},{28,4},{1,25},{... | collective-permute-start | bytes 245768 | tf_op jit(solution)/shard_map/ppermute | solution.py:395
  94.1 1.6 %collective-permute-done.15.refs_1_ = f32[160,128]{1,0:T(8,128)S(1)} collective-permute-done((f32[160,128]{1,0:T(8,128)S(1)}, f32[160,128]{1,0:T(8,128)S(1)}, u32[]{:S(2)}, u32[]{:S(2)}) %collective-permute-start.15) | collective-permute-done | bytes 81952 | tf_op jit(solution)/shard_map/ppermute | solution.py:395
  95.7 1.8 %collective-permute-done.17.refs_3_ = f32[160,128]{1,0:T(8,128)S(1)} collective-permute-done((f32[160,128]{1,0:T(8,128)S(1)}, f32[160,128]{1,0:T(8,128)S(1)}, u32[]{:S(2)}, u32[]{:S(2)}) %collective-permute-start.17) | collective-permute-done | bytes 81952 | tf_op jit(solution)/shard_map/ppermute | solution.py:395
  97.7 1.3 %collective-permute-start.21 = (bf16[864,128]{1,0:T(8,128)(2,1)S(1)}, bf16[864,128]{1,0:T(8,128)(2,1)S(1)}, u32[]{:S(2)}, u32[]{:S(2)}) collective-permute-start(bf16[864,128]{1,0:T(8,128)(2,1)S(1)} %collective-permute-done.5.refs_2_), channel_id=1, source_target_pairs={{2,3},{6,7},{10,11},{14,15},{18,19},{22,23},{26,27},{30,31}} | collective-permute-start | bytes 663560 | tf_op jit(solution)/shard_map/ppermute | solution.py:407
  99.3 13.4 %inverse_factor.1.factor_ref = f32[512,512]{1,0:T(8,128)S(1)} custom-call(f32[640,128]{1,0:T(8,128)S(1)} %joined.1.mine_ref, f32[640,128]{1,0:T(8,128)S(1)} %collective-permute-done.18.other_ref), custom_call_target="tpu_custom_call" | custom-call | bytes 73400320 | tf_op jit(solution)/shard_map/inverse_factor/pallas_call | solution.py:574
  113.6 4.1 %collective-permute-done.21.refs_2_ = bf16[864,128]{1,0:T(8,128)(2,1)S(1)} collective-permute-done((bf16[864,128]{1,0:T(8,128)(2,1)S(1)}, bf16[864,128]{1,0:T(8,128)(2,1)S(1)}, u32[]{:S(2)}, u32[]{:S(2)}) %collective-permute-start.21) | collective-permute-done | bytes 221216 | tf_op jit(solution)/shard_map/ppermute | solution.py:407
  117.8 1.6 %output_late.1 = f32[3456,128]{1,0:T(8,128)} custom-call(f32[512,512]{1,0:T(8,128)S(1)} %inverse_factor.1.factor_ref, f32[4,864,128]{2,1,0:T(8,128)S(1)} %output_early.1.early_ref, bf16[2592,128]{1,0:T(8,128)(2,1)S(1)} %collective-permute-done.19.refs_0_, bf16[1728,128]{1,0:T(8,128)(2,1)S(1)} %collective-permute-done.20.refs_1_, ...), custom_call_target="tpu_custom_call" | custom-call | bytes 6291456 | tf_op jit(solution)/shard_map/output_late/pallas_call | solution.py:665
  (53 shorter events, 10.2 us)
Async XLA Ops:
  0.0 1.2 copy-start.2
  1.2 0.7 copy-start.5
  1.9 0.7 copy-start.6
  3.6 4.6 %collective-permute-start = (bf16[288,128]{1,0:T(8,128)(2,1)S(1)}, bf16[288,128]{1,0:T(8,128)(2,1)S(1)}, u32[]{:S(2)}, u32[]{:S(2)}) collective-permute-start(bf16[288,128]{1,0:T(8,128)(2,1)S(1)} %get-tuple-element.38), channel_id=1, source_target_pairs={{0,28},{4,0},{8,4},{12,8},{16,12},{20,16},{24,20},{28,24},{1,29},{... | collective-permute-start | bytes 221192 | tf_op jit(solution)/shard_map/ppermute | solution.py:30
  3.6 1.0 copy-start
  4.6 3.6 %copy-start.1 = (bf16[343,343]{1,0:T(8,128)(2,1)S(1)}, bf16[343,343]{1,0:T(8,128)(2,1)}, u32[]{:S(2)}) copy-start(bf16[343,343]{1,0:T(8,128)(2,1)} %matrix_ref.7) | copy-start | bytes 705898
  4.6 3.6 %copy-start.4 = (f32[3456]{0:T(1024)S(1)}, f32[3456]{0:T(1024)}, u32[]{:S(2)}) copy-start(f32[3456]{0:T(1024)} %param.9) | copy-start | bytes 41476
  4.6 3.6 %copy-start.8 = (f32[16]{0:T(128)S(1)}, f32[16]{0:T(128)}, u32[]{:S(2)}) copy-start(f32[16]{0:T(128)} %scale_ref.3) | copy-start | bytes 196
  15.7 4.4 %collective-permute-start.1 = (bf16[288,128]{1,0:T(8,128)(2,1)S(1)}, bf16[288,128]{1,0:T(8,128)(2,1)S(1)}, u32[]{:S(2)}, u32[]{:S(2)}) collective-permute-start(bf16[288,128]{1,0:T(8,128)(2,1)S(1)} %get-tuple-element.43), channel_id=1, source_target_pairs={{0,4},{4,8},{8,12},{12,16},{16,20},{20,24},{24,28},{28,0},{1,5},{5... | collective-permute-start | bytes 221192 | tf_op jit(solution)/shard_map/ppermute | solution.py:30
  16.2 3.8 %copy-start.7 = (s32[288]{0:T(512)S(1)}, s32[288]{0:T(512)}, u32[]{:S(2)}) copy-start(s32[288]{0:T(512)} %nodes.5) | copy-start | bytes 3460
  21.4 4.9 %collective-permute-start.2 = (bf16[288,128]{1,0:T(8,128)(2,1)S(1)}, bf16[288,128]{1,0:T(8,128)(2,1)S(1)}, u32[]{:S(2)}, u32[]{:S(2)}) collective-permute-start(bf16[288,128]{1,0:T(8,128)(2,1)S(1)} %get-tuple-element.44), channel_id=1, source_target_pairs={{0,28},{4,0},{8,4},{12,8},{16,12},{20,16},{24,20},{28,24},{1,29},{... | collective-permute-start | bytes 221192 | tf_op jit(solution)/shard_map/ppermute | solution.py:30
  33.8 5.6 %collective-permute-start.3 = (bf16[288,128]{1,0:T(8,128)(2,1)S(1)}, bf16[288,128]{1,0:T(8,128)(2,1)S(1)}, u32[]{:S(2)}, u32[]{:S(2)}) collective-permute-start(bf16[288,128]{1,0:T(8,128)(2,1)S(1)} %get-tuple-element.50), channel_id=1, source_target_pairs={{0,4},{4,8},{8,12},{12,16},{16,20},{20,24},{24,28},{28,0},{1,5},{5... | collective-permute-start | bytes 221192 | tf_op jit(solution)/shard_map/ppermute | solution.py:30
  35.7 3.8 %copy-start.3 = (bf16[3456,128]{1,0:T(8,128)(2,1)S(1)}, bf16[3456,128]{1,0:T(8,128)(2,1)}, u32[]{:S(2)}) copy-start(bf16[3456,128]{1,0:T(8,128)(2,1)} %previous_ref.1) | copy-start | bytes 2654212
  40.8 8.0 %collective-permute-start.4 = (bf16[864,128]{1,0:T(8,128)(2,1)S(1)}, bf16[864,128]{1,0:T(8,128)(2,1)S(1)}, u32[]{:S(2)}, u32[]{:S(2)}) collective-permute-start(bf16[864,128]{1,0:T(8,128)(2,1)S(1)} %get-tuple-element.52), channel_id=1, source_target_pairs={{0,1},{1,2},{2,3},{3,0},{4,5},{5,6},{6,7},{7,4},{8,9},{9,10},{10,1... | collective-permute-start | bytes 663560 | tf_op jit(solution)/shard_map/ppermute | solution.py:30
  41.3 21.7 %collective-permute-start.5 = (bf16[864,128]{1,0:T(8,128)(2,1)S(1)}, bf16[864,128]{1,0:T(8,128)(2,1)S(1)}, u32[]{:S(2)}, u32[]{:S(2)}) collective-permute-start(bf16[864,128]{1,0:T(8,128)(2,1)S(1)} %get-tuple-element.53), channel_id=1, source_target_pairs={{0,2},{1,3},{2,0},{3,1},{4,6},{5,7},{6,4},{7,5},{8,10},{9,11},{10,... | collective-permute-start | bytes 663560 | tf_op jit(solution)/shard_map/ppermute | solution.py:30
  42.9 20.0 %collective-permute-start.6 = (bf16[864,128]{1,0:T(8,128)(2,1)S(1)}, bf16[864,128]{1,0:T(8,128)(2,1)S(1)}, u32[]{:S(2)}, u32[]{:S(2)}) collective-permute-start(bf16[864,128]{1,0:T(8,128)(2,1)S(1)} %get-tuple-element.54), channel_id=1, source_target_pairs={{0,3},{1,0},{2,1},{3,2},{4,7},{5,4},{6,5},{7,6},{8,11},{9,8},{10,9... | collective-permute-start | bytes 663560 | tf_op jit(solution)/shard_map/ppermute | solution.py:30
  63.8 1.7 %collective-permute-start.7 = (f32[640,128]{1,0:T(8,128)S(1)}, f32[640,128]{1,0:T(8,128)S(1)}, u32[]{:S(2)}, u32[]{:S(2)}) collective-permute-start(f32[640,128]{1,0:T(8,128)S(1)} %get-tuple-element.60), channel_id=1, source_target_pairs={{0,4},{4,0},{8,12},{12,8},{16,20},{20,16},{24,28},{28,24},{1,5},{5... | collective-permute-start | bytes 983048 | tf_op jit(solution)/shard_map/ppermute | solution.py:395
  64.3 20.9 %collective-permute-start.12 = (bf16[2592,128]{1,0:T(8,128)(2,1)S(1)}, bf16[2592,128]{1,0:T(8,128)(2,1)S(1)}, u32[]{:S(2)}, u32[]{:S(2)}) collective-permute-start(bf16[2592,128]{1,0:T(8,128)(2,1)S(1)} %pad_maximum_fusion), channel_id=1, source_target_pairs={{0,1},{1,2},{2,3},{4,5},{5,6},{6,7},{8,9},{9,10},{10,11},{12,13},{... | collective-permute-start | bytes 1990664 | tf_op jit(solution)/shard_map/ppermute | solution.py:402
  65.6 6.2 %collective-permute-start.10 = (f32[160,128]{1,0:T(8,128)S(1)}, f32[160,128]{1,0:T(8,128)S(1)}, u32[]{:S(2)}, u32[]{:S(2)}) collective-permute-start(f32[160,128]{1,0:T(8,128)S(1)} %get-tuple-element.64), channel_id=1, source_target_pairs={{0,24},{4,28},{8,16},{12,20},{16,8},{20,12},{24,0},{28,4},{1,25},{... | collective-permute-start | bytes 245768 | tf_op jit(solution)/shard_map/ppermute | solution.py:395
  66.4 6.1 %collective-permute-start.9 = (f32[160,128]{1,0:T(8,128)S(1)}, f32[160,128]{1,0:T(8,128)S(1)}, u32[]{:S(2)}, u32[]{:S(2)}) collective-permute-start(f32[160,128]{1,0:T(8,128)S(1)} %get-tuple-element.63), channel_id=1, source_target_pairs={{0,16},{4,20},{8,24},{12,28},{16,0},{20,4},{24,8},{28,12},{1,17},{... | collective-permute-start | bytes 245768 | tf_op jit(solution)/shard_map/ppermute | solution.py:395
  67.3 5.8 %collective-permute-start.8 = (f32[160,128]{1,0:T(8,128)S(1)}, f32[160,128]{1,0:T(8,128)S(1)}, u32[]{:S(2)}, u32[]{:S(2)}) collective-permute-start(f32[160,128]{1,0:T(8,128)S(1)} %get-tuple-element.62), channel_id=1, source_target_pairs={{0,8},{4,12},{8,0},{12,4},{16,24},{20,28},{24,16},{28,20},{1,9},{5... | collective-permute-start | bytes 245768 | tf_op jit(solution)/shard_map/ppermute | solution.py:395
  73.1 12.1 %collective-permute-start.11 = (f32[160,128]{1,0:T(8,128)S(1)}, f32[160,128]{1,0:T(8,128)S(1)}, u32[]{:S(2)}, u32[]{:S(2)}) collective-permute-start(f32[160,128]{1,0:T(8,128)S(1)} %add_add_fusion.1), channel_id=1, source_target_pairs={{0,1},{1,2},{2,3},{3,0},{4,5},{5,6},{6,7},{7,4},{8,9},{9,10},{10,1... | collective-permute-start | bytes 245768 | tf_op jit(solution)/shard_map/ppermute | solution.py:30
  76.7 11.8 %collective-permute-start.14 = (f32[160,128]{1,0:T(8,128)S(1)}, f32[160,128]{1,0:T(8,128)S(1)}, u32[]{:S(2)}, u32[]{:S(2)}) collective-permute-start(f32[160,128]{1,0:T(8,128)S(1)} %add_add_fusion.1), channel_id=1, source_target_pairs={{0,3},{1,0},{2,1},{3,2},{4,7},{5,4},{6,5},{7,6},{8,11},{9,8},{10,9... | collective-permute-start | bytes 245768 | tf_op jit(solution)/shard_map/ppermute | solution.py:30
  76.7 13.8 %collective-permute-start.13 = (f32[160,128]{1,0:T(8,128)S(1)}, f32[160,128]{1,0:T(8,128)S(1)}, u32[]{:S(2)}, u32[]{:S(2)}) collective-permute-start(f32[160,128]{1,0:T(8,128)S(1)} %add_add_fusion.1), channel_id=1, source_target_pairs={{0,2},{1,3},{2,0},{3,1},{4,6},{5,7},{6,4},{7,5},{8,10},{9,11},{10,... | collective-permute-start | bytes 245768 | tf_op jit(solution)/shard_map/ppermute | solution.py:30
  85.3 32.5 %collective-permute-start.19 = (bf16[2592,128]{1,0:T(8,128)(2,1)S(1)}, bf16[2592,128]{1,0:T(8,128)(2,1)S(1)}, u32[]{:S(2)}, u32[]{:S(2)}) collective-permute-start(bf16[2592,128]{1,0:T(8,128)(2,1)S(1)} %pad_maximum_fusion.1), channel_id=1, source_target_pairs={{1,2},{2,3},{5,6},{6,7},{9,10},{10,11},{13,14},{14,15},{17,18},{18... | collective-permute-start | bytes 1990664 | tf_op jit(solution)/shard_map/ppermute | solution.py:402
  86.6 31.1 %collective-permute-start.20 = (bf16[1728,128]{1,0:T(8,128)(2,1)S(1)}, bf16[1728,128]{1,0:T(8,128)(2,1)S(1)}, u32[]{:S(2)}, u32[]{:S(2)}) collective-permute-start(bf16[1728,128]{1,0:T(8,128)(2,1)S(1)} %pad_maximum_fusion.2), channel_id=1, source_target_pairs={{1,3},{5,7},{9,11},{13,15},{17,19},{21,23},{25,27},{29,31}} | collective-permute-start | bytes 1327112 | tf_op jit(solution)/shard_map/ppermute | solution.py:434
  90.5 5.2 %collective-permute-start.15 = (f32[160,128]{1,0:T(8,128)S(1)}, f32[160,128]{1,0:T(8,128)S(1)}, u32[]{:S(2)}, u32[]{:S(2)}) collective-permute-start(f32[160,128]{1,0:T(8,128)S(1)} %add_add_fusion.refs_0_), channel_id=1, source_target_pairs={{0,8},{4,12},{8,0},{12,4},{16,24},{20,28},{24,16},{28,20},{1,9},{5... | collective-permute-start | bytes 245768 | tf_op jit(solution)/shard_map/ppermute | solution.py:395
  90.6 5.1 %collective-permute-start.16 = (f32[160,128]{1,0:T(8,128)S(1)}, f32[160,128]{1,0:T(8,128)S(1)}, u32[]{:S(2)}, u32[]{:S(2)}) collective-permute-start(f32[160,128]{1,0:T(8,128)S(1)} %add_add_fusion.refs_0_), channel_id=1, source_target_pairs={{0,16},{4,20},{8,24},{12,28},{16,0},{20,4},{24,8},{28,12},{1,17},{... | collective-permute-start | bytes 245768 | tf_op jit(solution)/shard_map/ppermute | solution.py:395
  92.2 5.4 %collective-permute-start.17 = (f32[160,128]{1,0:T(8,128)S(1)}, f32[160,128]{1,0:T(8,128)S(1)}, u32[]{:S(2)}, u32[]{:S(2)}) collective-permute-start(f32[160,128]{1,0:T(8,128)S(1)} %add_add_fusion.refs_0_), channel_id=1, source_target_pairs={{0,24},{4,28},{8,16},{12,20},{16,8},{20,12},{24,0},{28,4},{1,25},{... | collective-permute-start | bytes 245768 | tf_op jit(solution)/shard_map/ppermute | solution.py:395
  97.6 1.7 %collective-permute-start.18 = (f32[640,128]{1,0:T(8,128)S(1)}, f32[640,128]{1,0:T(8,128)S(1)}, u32[]{:S(2)}, u32[]{:S(2)}) collective-permute-start(f32[640,128]{1,0:T(8,128)S(1)} %joined.1.mine_ref), channel_id=1, source_target_pairs={{0,4},{4,0},{8,12},{12,8},{16,20},{20,16},{24,28},{28,24},{1,5},{5... | collective-permute-start | bytes 983048 | tf_op jit(solution)/shard_map/ppermute | solution.py:395
  97.7 20.1 %collective-permute-start.21 = (bf16[864,128]{1,0:T(8,128)(2,1)S(1)}, bf16[864,128]{1,0:T(8,128)(2,1)S(1)}, u32[]{:S(2)}, u32[]{:S(2)}) collective-permute-start(bf16[864,128]{1,0:T(8,128)(2,1)S(1)} %collective-permute-done.5.refs_2_), channel_id=1, source_target_pairs={{2,3},{6,7},{10,11},{14,15},{18,19},{22,23},{26,27},{30,31}} | collective-permute-start | bytes 663560 | tf_op jit(solution)/shard_map/ppermute | solution.py:407
